TPU v7x, 32 devices: a whole 2x2x4 slice. The times are simulated.
32 devices in a mesh: seq: 2 (over x), fsdp: 16 (over z, y, core).
Axes of the slice: x: 2, y: 2, z: 4, core: 2. Of those that a mesh axis runs over, the one named last changes fastest.
Arguments:
- tokens: bfloat16 [16, 1024, 1536], P('fsdp', 'seq'), may hold values from -6 to 6
- lengths: int32 [16], P('fsdp'), may hold values from 513 to 1024, as said below
- routes: int32 [16, 1024, 8], P('fsdp', 'seq'), may hold values from 0 to 15, all different within a row; in each aligned block of 512 rows (0 to 511, 512 to 1023, ..., all dimensions but the last counted through in order) at most 320 rows name the same one
- route_gates: float32 [16, 1024, 8], P('fsdp', 'seq'), may hold values from 0.25 to 0.75
- cotangent: bfloat16 [16, 1024, 1536], P('fsdp', 'seq'), may hold values from -6 to 6
- norm_first: bfloat16 [1536], P('fsdp'), may hold values from 0.5 to 1.5
- attention_in: bfloat16 [1536, 2560], P('fsdp'), may hold values from -0.15625 to 0.15625
- attention_out: bfloat16 [1536, 1536], P('fsdp'), may hold values from -1.25 to 1.25
- norm_second: bfloat16 [1536], P('fsdp'), may hold values from 0.5 to 1.5
- expert_gate: bfloat16 [1536, 16, 512], P('fsdp'), may hold values from -0.15625 to 0.15625
- expert_lift: bfloat16 [1536, 16, 512], P('fsdp'), may hold values from -0.15625 to 0.15625
- expert_down: bfloat16 [1536, 16, 512], P('fsdp'), may hold values from -0.25 to 0.25
Outputs:
- block_output: bfloat16 [16, 1024, 1536], P('fsdp', 'seq')
- grad_tokens: float32 [16, 1024, 1536], P('fsdp', 'seq')
- grad_gates: float32 [16, 1024, 8], P('fsdp', 'seq')
- grad_norm_first: float32 [1536], P('fsdp')
- grad_attention_in: float32 [1536, 2560], P('fsdp')
- grad_attention_out: float32 [1536, 1536], P('fsdp')
- grad_norm_second: float32 [1536], P('fsdp')
- grad_expert_gate: float32 [1536, 16, 512], P('fsdp')
- grad_expert_lift: float32 [1536, 16, 512], P('fsdp')
- grad_expert_down: float32 [1536, 16, 512], P('fsdp')
Inputs may be any that keep to these rules, and one draw needn't show every extreme that they name: `lengths`: each slot's sequence covers more than its first 512 positions; some slot is full. `routes`: each position names 8 different experts; among the 512 positions of one device no expert is named more than 320 times.
All inputs are finite; a program needn't handle non-finite values.
Results may differ from a plain program's by a relative error of at most 0.013.
Values may be sent and summed in bfloat16 or wider, within the bound.
No kernel may reach another device: no remote copies, remote signals or barrier semaphores. Data moves between devices by JAX's collectives and lax.ppermute only.
A program may use at most 448 MiB of HBM per device.

v0:
```python
import jax
import jax.numpy as jnp
from jax import lax
from jax.sharding import PartitionSpec as P

HEADS = 24
KV_HEADS = 8
HEAD_DIM = 64
EXPERTS = 16


EPS = 1e-06


def norm_rows(values, gain_vector):
    inverse = lax.rsqrt(jnp.mean(values * values, axis=-1, keepdims=True) + EPS)
    normed = values * inverse
    return (normed, inverse, (normed * gain_vector).astype(jnp.bfloat16))


def norm_back(upstream, normed, inverse, gain_vector):
    scaled = upstream * gain_vector
    spread = jnp.mean(scaled * normed, axis=-1, keepdims=True)
    return (inverse * (scaled - normed * spread), jnp.sum(upstream * normed, axis=0))


def score_block(query_all, key_heads, first_row, block_rows, length):
    length_all = key_heads.shape[0]
    groups = key_heads.shape[1]
    query_rows = lax.dynamic_slice_in_dim(query_all, first_row, block_rows, 0).reshape(
        block_rows, groups, HEADS // KV_HEADS, HEAD_DIM
    )
    scores = jnp.einsum(
        "qgrd,kgd->grqk", query_rows, key_heads, preferred_element_type=jnp.float32
    ) * HEAD_DIM ** (-0.5)
    query_place = first_row + jnp.arange(block_rows, dtype=jnp.int32)
    key_place = jnp.arange(length_all, dtype=jnp.int32)
    allowed = (key_place[None, :] <= query_place[:, None]) & (key_place[None, :] < length)
    return (query_rows, jnp.where(allowed, scores, -jnp.inf))


def attend(query_all, key_all, value_all, length):
    length_all = query_all.shape[0]
    block_rows = min(512, length_all)
    key_heads = key_all.reshape(length_all, -1, HEAD_DIM)
    value_heads = value_all.reshape(length_all, -1, HEAD_DIM)

    def one_block(first_row):
        query_rows, scores = score_block(query_all, key_heads, first_row, block_rows, length)
        row_peak = jnp.max(scores, axis=-1, keepdims=True)
        lifted = jnp.exp(scores - row_peak)
        row_total = jnp.sum(lifted, axis=-1, keepdims=True)
        shares = (lifted / row_total).astype(jnp.bfloat16)
        mixed_rows = jnp.einsum(
            "grqk,kgd->qgrd", shares, value_heads, preferred_element_type=jnp.float32
        )
        return (mixed_rows.reshape(block_rows, -1).astype(jnp.bfloat16), row_peak, row_total)

    starts = jnp.arange(length_all // block_rows, dtype=jnp.int32) * block_rows
    mixed_rows, row_peaks, totals = lax.map(one_block, starts)
    return (mixed_rows.reshape(length_all, -1), starts, row_peaks, totals)


def attend_back(query_all, key_all, value_all, grad_all, starts, row_peaks, totals, length):
    length_all = query_all.shape[0]
    block_rows = min(512, length_all)
    key_heads = key_all.reshape(length_all, -1, HEAD_DIM)
    value_heads = value_all.reshape(length_all, -1, HEAD_DIM)
    groups = key_heads.shape[1]

    def one_block(running, block_item):
        first_row, row_peak, row_total = block_item
        key_sum, value_sum = running
        query_rows, scores = score_block(query_all, key_heads, first_row, block_rows, length)
        chances = jnp.exp(scores - row_peak) / row_total
        grad_rows = lax.dynamic_slice_in_dim(grad_all, first_row, block_rows, 0).reshape(
            block_rows, groups, HEADS // KV_HEADS, HEAD_DIM
        )
        chance_grad = jnp.einsum(
            "qgrd,kgd->grqk", grad_rows, value_heads, preferred_element_type=jnp.float32
        )
        inner = jnp.sum(chances * chance_grad, axis=-1, keepdims=True)
        score_grad = (chances * (chance_grad - inner)).astype(jnp.bfloat16)
        query_grad = jnp.einsum(
            "grqk,kgd->qgrd", score_grad, key_heads, preferred_element_type=jnp.float32
        ) * HEAD_DIM ** (-0.5)
        key_sum = key_sum + jnp.einsum(
            "grqk,qgrd->kgd", score_grad, query_rows, preferred_element_type=jnp.float32
        ) * HEAD_DIM ** (-0.5)
        value_sum = value_sum + jnp.einsum(
            "grqk,qgrd->kgd",
            chances.astype(jnp.bfloat16),
            grad_rows,
            preferred_element_type=jnp.float32,
        )
        return ((key_sum, value_sum), query_grad.reshape(block_rows, -1).astype(jnp.bfloat16))

    empty = jnp.zeros((length_all, groups, HEAD_DIM), jnp.float32)
    (key_sum, value_sum), query_grad = lax.scan(
        one_block, (empty, empty), (starts, row_peaks, totals)
    )
    return (
        query_grad.reshape(length_all, -1),
        key_sum.reshape(length_all, -1).astype(jnp.bfloat16),
        value_sum.reshape(length_all, -1).astype(jnp.bfloat16),
    )


def dispatch_plan(route_rows, live_rows, capacity):
    token_count, choose = route_rows.shape
    flat_routes = route_rows.reshape(-1)
    live_pairs = jnp.repeat(live_rows, choose)
    matches = (
        (flat_routes[:, None] == jnp.arange(EXPERTS, dtype=jnp.int32)[None, :])
        & live_pairs[:, None]
    ).astype(jnp.int32)
    within = jnp.sum(matches * (jnp.cumsum(matches, axis=0) - 1), axis=1)
    spare_slot = EXPERTS * capacity
    slot_index = jnp.where(live_pairs, flat_routes * capacity + within, spare_slot)
    owners = jnp.arange(token_count * choose, dtype=jnp.int32) // choose
    source = jnp.zeros((spare_slot + 1,), jnp.int32).at[slot_index].set(owners)[:spare_slot]
    filled = (
        jnp.zeros((spare_slot + 1,), jnp.int32)
        .at[slot_index]
        .set(live_pairs.astype(jnp.int32))[:spare_slot]
    )
    return (slot_index, source, filled)


def body(
    tokens,
    lengths,
    routes,
    route_gates,
    cotangent,
    norm_first,
    attention_in,
    attention_out,
    norm_second,
    expert_gate,
    expert_lift,
    expert_down,
):
    token_count = tokens.shape[1]
    model_width = tokens.shape[2]
    choose = routes.shape[2]
    fsdp_count = lax.axis_size("fsdp")
    copies = fsdp_count // EXPERTS
    capacity = copies * (
        (token_count * choose * 5 + 4 * EXPERTS * copies - 1) // (4 * EXPERTS * copies)
    )
    share = capacity // copies
    query_width = HEADS * HEAD_DIM
    key_width = KV_HEADS * HEAD_DIM
    length = lengths[0]
    positions = lax.axis_index("seq") * token_count + jnp.arange(token_count, dtype=jnp.int32)
    live_rows = positions < length
    inputs = tokens[0].astype(jnp.float32)

    def to_experts(rows):
        return lax.all_to_all(
            rows.reshape(fsdp_count, share, model_width),
            "fsdp",
            split_axis=0,
            concat_axis=0,
            tiled=True,
        ).reshape(-1, model_width)

    def from_experts(rows):
        return lax.all_to_all(
            rows.reshape(fsdp_count, share, model_width),
            "fsdp",
            split_axis=0,
            concat_axis=0,
            tiled=True,
        ).reshape(EXPERTS, capacity, model_width)

    first_gain, second_gain, project_in, project_out = (
        lax.all_gather(norm_first, "fsdp", axis=0, tiled=True),
        lax.all_gather(norm_second, "fsdp", axis=0, tiled=True),
        lax.all_gather(attention_in, "fsdp", axis=0, tiled=True),
        lax.all_gather(attention_out, "fsdp", axis=0, tiled=True),
    )
    first_gain = first_gain.astype(jnp.float32)
    second_gain = second_gain.astype(jnp.float32)
    normed_one, inverse_one, lowered_one = norm_rows(inputs, first_gain)
    projected = jnp.dot(lowered_one, project_in, preferred_element_type=jnp.float32).astype(
        jnp.bfloat16
    )
    query_all, key_all, value_all = (
        lax.all_to_all(projected[:, :query_width], "seq", split_axis=1, concat_axis=0, tiled=True),
        lax.all_to_all(
            projected[:, query_width : query_width + key_width],
            "seq",
            split_axis=1,
            concat_axis=0,
            tiled=True,
        ),
        lax.all_to_all(
            projected[:, query_width + key_width :], "seq", split_axis=1, concat_axis=0, tiled=True
        ),
    )
    mixed_heads, starts, row_peaks, totals = attend(query_all, key_all, value_all, length)
    mixed_rows = lax.all_to_all(mixed_heads, "seq", split_axis=0, concat_axis=1, tiled=True)
    middle = inputs + jnp.dot(mixed_rows, project_out, preferred_element_type=jnp.float32)
    normed_two, inverse_two, lowered_two = norm_rows(middle, second_gain)
    slot_index, source, filled = dispatch_plan(routes[0], live_rows, capacity)
    gate_rows = route_gates[0]
    slot_gate = (
        jnp.zeros((EXPERTS * capacity + 1,), jnp.float32)
        .at[slot_index]
        .set(gate_rows.reshape(-1))[: EXPERTS * capacity]
    )
    occupied = filled[:, None] > 0
    expert_rows = jnp.where(occupied, lowered_two[source], jnp.zeros((), jnp.bfloat16)).reshape(
        EXPERTS, capacity, model_width
    )
    gate_one, lift_one, down_one = (
        lax.all_to_all(
            jnp.repeat(expert_gate, copies, axis=1), "fsdp", split_axis=1, concat_axis=0, tiled=True
        ),
        lax.all_to_all(
            jnp.repeat(expert_lift, copies, axis=1), "fsdp", split_axis=1, concat_axis=0, tiled=True
        ),
        lax.all_to_all(
            jnp.repeat(expert_down, copies, axis=1), "fsdp", split_axis=1, concat_axis=0, tiled=True
        ),
    )
    gate_one = gate_one[:, 0, :]
    lift_one = lift_one[:, 0, :]
    down_one = down_one[:, 0, :]
    taken = to_experts(expert_rows)
    gate_local = jnp.dot(taken, gate_one, preferred_element_type=jnp.float32)
    lift_local = jnp.dot(taken, lift_one, preferred_element_type=jnp.float32)
    sigmoid_local = jax.nn.sigmoid(gate_local)
    silu_local = gate_local * sigmoid_local
    hidden_local = (silu_local * lift_local).astype(jnp.bfloat16)
    made = jnp.einsum("mf,df->md", hidden_local, down_one, preferred_element_type=jnp.float32)
    expert_result = from_experts(made).reshape(-1, model_width)
    padded_result = jnp.concatenate(
        [expert_result, jnp.zeros((1, model_width), jnp.float32)], axis=0
    )
    pair_result = padded_result[slot_index].reshape(token_count, choose, model_width)
    combined = jnp.sum(pair_result * gate_rows[:, :, None], axis=1)
    block_output = (middle + combined).astype(jnp.bfloat16)[None]
    upstream = cotangent[0].astype(jnp.float32)
    grad_gates = jnp.sum(pair_result * upstream[:, None, :], axis=-1)[None]
    result_grad = (
        jnp.where(occupied, slot_gate[:, None] * upstream[source], 0.0)
        .astype(jnp.bfloat16)
        .reshape(EXPERTS, capacity, model_width)
    )
    returned_in = to_experts(result_grad)
    hidden_grad_local = jnp.einsum(
        "md,df->mf", returned_in, down_one, preferred_element_type=jnp.float32
    )
    gate_grad_local = (
        hidden_grad_local * lift_local * sigmoid_local * (1.0 + gate_local * (1.0 - sigmoid_local))
    ).astype(jnp.bfloat16)
    lift_grad_local = (hidden_grad_local * silu_local).astype(jnp.bfloat16)
    rows_back = jnp.einsum(
        "mf,df->md", gate_grad_local, gate_one, preferred_element_type=jnp.float32
    ) + jnp.einsum("mf,df->md", lift_grad_local, lift_one, preferred_element_type=jnp.float32)
    rows_grad = from_experts(rows_back)
    local_grads = jnp.stack(
        [
            jnp.einsum("md,mf->df", taken, gate_grad_local, preferred_element_type=jnp.float32),
            jnp.einsum("md,mf->df", taken, lift_grad_local, preferred_element_type=jnp.float32),
            jnp.einsum("md,mf->df", returned_in, hidden_local, preferred_element_type=jnp.float32),
        ],
        axis=1,
    )[:, :, None, :]
    homed = lax.all_to_all(local_grads, "fsdp", split_axis=0, concat_axis=2, tiled=True)
    expert_part = jnp.sum(homed.reshape(homed.shape[0], 3, EXPERTS, copies, homed.shape[3]), axis=3)
    padded_grad = jnp.concatenate(
        [rows_grad.reshape(-1, model_width), jnp.zeros((1, model_width), jnp.float32)], axis=0
    )
    normed_grad_two = jnp.sum(
        padded_grad[slot_index].reshape(token_count, choose, model_width), axis=1
    )
    middle_norm_grad, second_gain_grad = norm_back(
        normed_grad_two, normed_two, inverse_two, second_gain
    )
    middle_grad = upstream + middle_norm_grad
    branch_grad = middle_grad.astype(jnp.bfloat16)
    project_in_back, project_out_back = (
        lax.all_gather(attention_in, "fsdp", axis=0, tiled=True),
        lax.all_gather(attention_out, "fsdp", axis=0, tiled=True),
    )
    mixed_grad = jnp.einsum(
        "td,qd->tq", branch_grad, project_out_back, preferred_element_type=jnp.float32
    ).astype(jnp.bfloat16)
    out_weight_grad = jnp.einsum(
        "tq,td->qd", mixed_rows, branch_grad, preferred_element_type=jnp.float32
    )
    mixed_grad_heads = lax.all_to_all(mixed_grad, "seq", split_axis=1, concat_axis=0, tiled=True)
    query_grad, key_grad, value_grad = attend_back(
        query_all, key_all, value_all, mixed_grad_heads, starts, row_peaks, totals, length
    )
    query_rows_grad, key_rows_grad, value_rows_grad = (
        lax.all_to_all(query_grad, "seq", split_axis=0, concat_axis=1, tiled=True),
        lax.all_to_all(key_grad, "seq", split_axis=0, concat_axis=1, tiled=True),
        lax.all_to_all(value_grad, "seq", split_axis=0, concat_axis=1, tiled=True),
    )
    projected_grad = jnp.concatenate([query_rows_grad, key_rows_grad, value_rows_grad], axis=1)
    normed_grad_one = jnp.einsum(
        "tq,dq->td", projected_grad, project_in_back, preferred_element_type=jnp.float32
    )
    in_weight_grad = jnp.einsum(
        "td,tq->dq", lowered_one, projected_grad, preferred_element_type=jnp.float32
    )
    input_norm_grad, first_gain_grad = norm_back(
        normed_grad_one, normed_one, inverse_one, first_gain
    )
    grad_tokens = (middle_grad + input_norm_grad)[None]
    in_part, out_part, first_part, second_part = (
        lax.psum_scatter(in_weight_grad, "fsdp", scatter_dimension=0, tiled=True),
        lax.psum_scatter(out_weight_grad, "fsdp", scatter_dimension=0, tiled=True),
        lax.psum_scatter(first_gain_grad, "fsdp", scatter_dimension=0, tiled=True),
        lax.psum_scatter(second_gain_grad, "fsdp", scatter_dimension=0, tiled=True),
    )
    in_part, out_part, first_part, second_part, expert_part = lax.psum(
        (in_part, out_part, first_part, second_part, expert_part), "seq"
    )
    return (
        block_output,
        grad_tokens,
        grad_gates,
        first_part,
        in_part,
        out_part,
        second_part,
        expert_part[:, 0],
        expert_part[:, 1],
        expert_part[:, 2],
    )


def solution(mesh):
    return jax.shard_map(
        body,
        mesh=mesh,
        in_specs=(
            P("fsdp", "seq", None),
            P("fsdp"),
            P("fsdp", "seq", None),
            P("fsdp", "seq", None),
            P("fsdp", "seq", None),
            P("fsdp"),
            P("fsdp", None),
            P("fsdp", None),
            P("fsdp"),
            P("fsdp", None, None),
            P("fsdp", None, None),
            P("fsdp", None, None),
        ),
        out_specs=(
            P("fsdp", "seq", None),
            P("fsdp", "seq", None),
            P("fsdp", "seq", None),
            P("fsdp"),
            P("fsdp", None),
            P("fsdp", None),
            P("fsdp"),
            P("fsdp", None, None),
            P("fsdp", None, None),
            P("fsdp", None, None),
        ),
        check_vma=False,
    )
```

profile of v0, /device:TPU:0, one launch (start us, length us, event | category | flops | bytes accessed | tf_op | source)
XLA Modules:
  0.0 3472.0 jit_solution(339653852598011142)
XLA Ops:
  11.6 36.7 %all-reduce.9 = (bf16[1536]{0:T(1024)(128)(2,1)S(1)}, bf16[1536]{0:T(1024)(128)(2,1)}) all-reduce(bf16[1536]{0:T(1024)(128)(2,1)S(1)} %dynamic-update-slice, bf16[1536]{0:T(1024)(128)(2,1)S(1)} %dynamic-update-slice.1), channel_id=1, replica_groups=mesh['seq'=2,'fsdp'=16] {'fsdp'}, use_global_device_ids=true, to_apply=%add.2 | all-reduce | flops 3072 | bytes 12288
  50.1 34.9 %all-gather.3.cloned.1.call-done = bf16[1536,2560]{1,0:T(8,128)(2,1)} async-done(((bf16[96,2560]{1,0:T(8,128)(2,1)}), bf16[1536,2560]{1,0:T(8,128)(2,1)}) %all-gather.3.cloned.1.call-update) | async-done | bytes 7864336 | tf_op jit(solution)/shard_map/all_gather | solution.py:181
  163.6 23.4 all-to-all-done.5
  202.3 79.8 %while.29 = (s32[]{:T(128)}, bf16[2,512,768]{1,2,0:T(8,128)(2,1)}, f32[2,4,3,512,1]{3,2,1,4,0:T(4,128)S(1)}, f32[2,4,3,512,1]{3,2,1,4,0:T(4,128)S(1)}, s32[2]{0:...) while((s32[]{:T(128)}, bf16[2,512,768]{1,2,0:T(8,128)(2,1)}, ...), condition=%wide.region_4.5_spmd, body=%wide.region_1.4_spmd.sunk | while | flops 1687541248 | bytes 83622584 | solution.py:60
  336.5 23.8 gather_fusion
  381.8 25.8 gather_fusion.2
  440.7 217.7 %all-to-all-done.4 = bf16[16,320,1536]{2,1,0:T(8,128)(2,1)} async-done(((bf16[16,320,1536]{2,1,0:T(8,128)(2,1)}), bf16[16,320,1536]{2,1,0:T(8,128)(2,1)}, u32[]{:S(2)}, u32[]{:S(2)}) %all-to-all-start.4) | async-done | bytes 15728672 | tf_op jit(solution)/shard_map/all_to_all | solution.py:161
  658.4 66.0 %all-to-all-start.9 = ((bf16[16,320,1536]{2,1,0:T(8,128)(2,1)}), bf16[16,320,1536]{2,1,0:T(8,128)(2,1)}, u32[]{:S(2)}, u32[]{:S(2)}) async-start(bf16[16,320,1536]{2,1,0:T(8,128)(2,1)} %select_convert_fusion), calls=%async_computation.9 | async-start | bytes 31457280 | tf_op jit(solution)/shard_map/all_to_all | solution.py:161
  753.5 249.5 %all-to-all-done.9 = bf16[16,320,1536]{2,1,0:T(8,128)(2,1)} async-done(((bf16[16,320,1536]{2,1,0:T(8,128)(2,1)}), bf16[16,320,1536]{2,1,0:T(8,128)(2,1)}, u32[]{:S(2)}, u32[]{:S(2)}) %all-to-all-start.9) | async-done | bytes 15728672 | tf_op jit(solution)/shard_map/all_to_all | solution.py:161
  1003.0 24.8 multiply_convert_fusion.1
  1027.8 17.5 fusion.76
  1045.3 25.6 convolution_add_fusion
  1070.9 66.0 %all-to-all-start.10 = ((f32[16,320,1536]{2,1,0:T(8,128)}), f32[16,320,1536]{2,1,0:T(8,128)}, u32[]{:S(2)}, u32[]{:S(2)}) async-start(f32[16,320,1536]{2,1,0:T(8,128)} %bitcast.323), calls=%async_computation.10 | async-start | bytes 62914560 | tf_op jit(solution)/shard_map/all_to_all | solution.py:170
  1136.9 17.3 fusion.75
  1154.2 535.1 %all-to-all-done.10 = f32[16,320,1536]{2,1,0:T(8,128)} async-done(((f32[16,320,1536]{2,1,0:T(8,128)}), f32[16,320,1536]{2,1,0:T(8,128)}, u32[]{:S(2)}, u32[]{:S(2)}) %all-to-all-start.10) | async-done | bytes 31457312 | tf_op jit(solution)/shard_map/all_to_all | solution.py:170
  1689.3 129.8 %all-to-all-start.8 = ((f32[16,320,1536]{2,1,0:T(8,128)}), f32[16,320,1536]{2,1,0:T(8,128)}, u32[]{:S(2)}, u32[]{:S(2)}) async-start(f32[16,320,1536]{2,1,0:T(8,128)} %fusion.75), calls=%async_computation.8 | async-start | bytes 62914560 | tf_op jit(solution)/shard_map/all_to_all | solution.py:170
  1820.0 21.7 concatenate.10
  1841.7 37.3 %gather_fusion.3 = f32[4096,1536]{1,0:T(8,128)} fusion(f32[5121,1536]{1,0:T(8,128)} %concatenate.10, s32[4096]{0:T(1024)S(1)} %broadcast_clamp_fusion), kind=kCustom, calls=%fused_computation.3 | custom fusion | bytes 50348032 | tf_op jit(solution)/shard_map/gather | solution.py:279
  1894.8 477.1 %all-to-all-done.8 = f32[16,320,1536]{2,1,0:T(8,128)} async-done(((f32[16,320,1536]{2,1,0:T(8,128)}), f32[16,320,1536]{2,1,0:T(8,128)}, u32[]{:S(2)}, u32[]{:S(2)}) %all-to-all-start.8) | async-done | bytes 31457312 | tf_op jit(solution)/shard_map/all_to_all | solution.py:170
  2371.9 21.7 concatenate.9
  2393.6 37.4 %gather_fusion.1 = f32[4096,1536]{1,0:T(8,128)} fusion(f32[5121,1536]{1,0:T(8,128)} %concatenate.9, s32[4096]{0:T(1024)S(1)} %broadcast_clamp_fusion), kind=kCustom, calls=%fused_computation.1 | custom fusion | bytes 50348032 | tf_op jit(solution)/shard_map/gather | solution.py:243
  2431.0 33.1 fusion.32
  2500.0 176.3 %while.30 = (s32[]{:T(128)}, f32[1024,4,64]{0,2,1:T(8,128)}, f32[1024,4,64]{0,2,1:T(8,128)}, bf16[2,512,768]{1,2,0:T(8,128)(2,1)}, s32[2]{0:T(128)S(1)}, /*index...) while((s32[]{:T(128)}, f32[1024,4,64]{0,2,1:T(8,128)}, ...), condition=%wide.region_17.18_spmd.clone, body=%wide.region_15.17_spmd.clone.sunk | while | flops 4092587520 | bytes 212278032 | solution.py:99
  2516.5 19.6 fusion.144
  2536.2 21.2 fusion.145
  2602.5 20.2 fusion.144
  2622.7 23.8 fusion.145
  2702.8 20.4 all_to_all.215
  2771.7 21.4 copy.113
  2793.1 396.6 %all_to_all.216 = f32[1536,3,1,512]{3,2,1,0:T(1,128)S(1)} all-to-all(f32[1536,3,1,512]{3,2,1,0:T(1,128)S(1)} %copy.113), channel_id=1, replica_groups=mesh['seq'=2,'fsdp'=16] {'fsdp'}, dimensions={0} | all-to-all | bytes 18874368 | tf_op jit(solution)/shard_map/all_to_all | solution.py:273
  3211.9 60.2 %all-reduce.6 = (f32[1536]{0:T(1024)S(1)}, f32[1536]{0:T(1024)S(1)}) all-reduce(f32[1536]{0:T(1024)S(1)} %get-tuple-element.265, f32[1536]{0:T(1024)S(1)} %copy-done.44), channel_id=2, replica_groups=mesh['seq'=2,'fsdp'=16] {'fsdp'}, use_global_device_ids=true, to_apply=%region_21.22.clone | all-reduce | flops 3072 | bytes 24576
  3282.7 172.1 %all-reduce.12.cloned.1.call-done = (f32[96,2560]{1,0:T(8,128)}, f32[96,1536]{1,0:T(8,128)}, f32[96,3,16,512]{3,2,0,1:T(8,128)}) async-done(((f32[96,2560]{1,0:T(8,128)}, f32[96,1536]{1,0:T(8,128)}, f32[96,3,16,512]{3,2,0,1:T(8,128)}), (f32[96,2560]{1,0:T(8,128)}, f32[96,1536]{1,0:T(8,128)}, f32[96,3,16,512]{3,2,0,1:T(8,128)})) %all-reduce.12.cloned.1.call-update) | async-done | bytes 11010064 | tf_op jit(solution)/shard_map/psum | solution.py:322
  (290 shorter events, 568.8 us)
Async XLA Ops:
  7.2 77.9 %all-gather.3.cloned.1.call-start = ((), (), s32[]{:S(2)}) async-start(), calls=%async_computation.18 | async-start | bytes 8355840 | tf_op jit(solution)/shard_map/all_gather | solution.py:181
  48.3 44.8 %copy-start.45 = (f32[1536]{0:T(1024)}, f32[1536]{0:T(1024)S(1)}, u32[]{:S(2)}) copy-start(f32[1536]{0:T(1024)S(1)} %convert_element_type.118) | copy-start | bytes 18436
  94.8 12.2 all-to-all-start.1
  107.0 12.2 all-to-all-start.2
  119.2 22.0 all-to-all-start
  141.1 45.9 %all-to-all-start.5 = ((bf16[96,16,512]{2,0,1:T(8,128)(2,1)}), bf16[96,16,512]{2,0,1:T(8,128)(2,1)}, u32[]{:S(2)}, u32[]{:S(2)}) async-start(bf16[96,16,512]{2,0,1:T(8,128)(2,1)} %copy.103), calls=%async_computation.5 | async-start | bytes 3145728 | tf_op jit(solution)/shard_map/all_to_all | solution.py:219
  145.6 182.6 %all-gather.5.cloned.1.call-start = ((), (), s32[]{:S(2)}) async-start(), calls=%async_computation.19 | async-start | bytes 5013504 | tf_op jit(solution)/shard_map/all_gather | solution.py:182
  187.0 95.2 %all-to-all-start.6 = ((bf16[96,16,512]{2,0,1:T(8,128)(2,1)}), bf16[96,16,512]{2,0,1:T(8,128)(2,1)}, u32[]{:S(2)}, u32[]{:S(2)}) async-start(bf16[96,16,512]{2,0,1:T(8,128)(2,1)} %copy.104), calls=%async_computation.6 | async-start | bytes 3145728 | tf_op jit(solution)/shard_map/all_to_all | solution.py:222
  202.3 84.6 %copy-start.35 = (pred[4096,1]{0,1:T(4,128)(4,1)S(1)}, pred[4096,1]{0,1:T(4,128)(4,1)}, u32[]{:S(2)}) copy-start(pred[4096,1]{0,1:T(4,128)(4,1)} %reshape.294) | copy-start | bytes 12292
  202.3 84.6 %copy-start.36 = (s32[4096,1]{0,1:T(1,128)S(1)}, s32[4096,1]{0,1:T(1,128)}, u32[]{:S(2)}) copy-start(s32[4096,1]{0,1:T(1,128)} %mul.204) | copy-start | bytes 49156
  202.3 84.6 %copy-start.37 = (s32[4096]{0:T(1024)S(1)}, s32[4096]{0:T(1024)}, u32[]{:S(2)}) copy-start(s32[4096]{0:T(1024)} %fusion.55) | copy-start | bytes 49156
  202.3 84.6 %copy-start.41 = (pred[4096]{0:T(1024)(128)(4,1)S(1)}, pred[4096]{0:T(1024)(128)(4,1)}, u32[]{:S(2)}) copy-start(pred[4096]{0:T(1024)(128)(4,1)} %copy-done.40) | copy-start | bytes 12292
  202.3 84.7 %copy-start.49 = (bf16[1536]{0:T(1024)(128)(2,1)S(1)}, bf16[1536]{0:T(1024)(128)(2,1)}, u32[]{:S(2)}) copy-start(bf16[1536]{0:T(1024)(128)(2,1)} %get-tuple-element.317) | copy-start | bytes 9220
  282.2 39.5 %all-to-all-start.3 = ((bf16[2,512,768]{1,2,0:T(8,128)(2,1)}), bf16[2,512,768]{1,2,0:T(8,128)(2,1)}, u32[]{:S(2)}, u32[]{:S(2)}) async-start(bf16[2,512,768]{1,2,0:T(8,128)(2,1)} %get-tuple-element.123), calls=%async_computation.3 | async-start | bytes 3145728 | tf_op jit(solution)/shard_map/all_to_all | solution.py:204
  286.9 121.0 %copy-start.38 = (s32[4096,1]{0,1:T(1,128)}, s32[4096,1]{0,1:T(1,128)S(1)}, u32[]{:S(2)}) copy-start(s32[4096,1]{0,1:T(1,128)S(1)} %compare_select_fusion) | copy-start | bytes 49156
  287.0 47.6 %copy-start.30 = (f32[1536]{0:T(1024)}, f32[1536]{0:T(1024)S(1)}, u32[]{:S(2)}) copy-start(f32[1536]{0:T(1024)S(1)} %convert_element_type.123) | copy-start | bytes 18436
  321.7 52.1 %all-to-all-start.7 = ((bf16[96,16,512]{2,0,1:T(8,128)(2,1)}), bf16[96,16,512]{2,0,1:T(8,128)(2,1)}, u32[]{:S(2)}, u32[]{:S(2)}) async-start(bf16[96,16,512]{2,0,1:T(8,128)(2,1)} %copy.105), calls=%async_computation.7 | async-start | bytes 3145728 | tf_op jit(solution)/shard_map/all_to_all | solution.py:225
  373.8 284.7 %all-to-all-start.4 = ((bf16[16,320,1536]{2,1,0:T(8,128)(2,1)}), bf16[16,320,1536]{2,1,0:T(8,128)(2,1)}, u32[]{:S(2)}, u32[]{:S(2)}) async-start(bf16[16,320,1536]{2,1,0:T(8,128)(2,1)} %broadcast_select_fusion), calls=%async_computation.4 | async-start | bytes 31457280 | tf_op jit(solution)/shard_map/all_to_all | solution.py:161
  658.4 344.6 %all-to-all-start.9 = ((bf16[16,320,1536]{2,1,0:T(8,128)(2,1)}), bf16[16,320,1536]{2,1,0:T(8,128)(2,1)}, u32[]{:S(2)}, u32[]{:S(2)}) async-start(bf16[16,320,1536]{2,1,0:T(8,128)(2,1)} %select_convert_fusion), calls=%async_computation.9 | async-start | bytes 31457280 | tf_op jit(solution)/shard_map/all_to_all | solution.py:161
  1070.9 618.4 %all-to-all-start.10 = ((f32[16,320,1536]{2,1,0:T(8,128)}), f32[16,320,1536]{2,1,0:T(8,128)}, u32[]{:S(2)}, u32[]{:S(2)}) async-start(f32[16,320,1536]{2,1,0:T(8,128)} %bitcast.323), calls=%async_computation.10 | async-start | bytes 62914560 | tf_op jit(solution)/shard_map/all_to_all | solution.py:170
  1154.2 664.9 %copy-start.33 = (f32[1,512,8]{1,2,0:T(8,128)S(1)}, f32[1,512,8]{1,2,0:T(8,128)}, u32[]{:S(2)}) copy-start(f32[1,512,8]{1,2,0:T(8,128)} %param.19) | copy-start | bytes 49156
  1154.2 665.8 %copy-start.39 = (s32[4096,1]{0,1:T(1,128)S(1)}, s32[4096,1]{0,1:T(1,128)}, u32[]{:S(2)}) copy-start(s32[4096,1]{0,1:T(1,128)} %copy-done.38) | copy-start | bytes 49156
  1689.3 682.6 %all-to-all-start.8 = ((f32[16,320,1536]{2,1,0:T(8,128)}), f32[16,320,1536]{2,1,0:T(8,128)}, u32[]{:S(2)}, u32[]{:S(2)}) async-start(f32[16,320,1536]{2,1,0:T(8,128)} %fusion.75), calls=%async_computation.8 | async-start | bytes 62914560 | tf_op jit(solution)/shard_map/all_to_all | solution.py:170
  2473.7 25.0 all-to-all-start.11
  2478.3 720.4 %reduce-scatter.5.cloned.1.call-start = ((), (), s32[]{:S(2)}) async-start(), calls=%async_computation.21 | async-start | bytes 10027008 | tf_op jit(solution)/shard_map/reduce_scatter | solution.py:318
  2678.9 45.4 %copy-start.18 = (bf16[1,512,1536]{2,1,0:T(8,128)(2,1)S(1)}, bf16[1,512,1536]{2,1,0:T(8,128)(2,1)}, u32[]{:S(2)}) copy-start(bf16[1,512,1536]{2,1,0:T(8,128)(2,1)} %param.16) | copy-start | bytes 4718596
  2678.9 45.4 %copy-start.46 = (f32[1536]{0:T(1024)S(1)}, f32[1536]{0:T(1024)}, u32[]{:S(2)}) copy-start(f32[1536]{0:T(1024)} %copy-done.45) | copy-start | bytes 18436
  2678.9 45.4 %copy-start.48 = (f32[512]{0:T(512)S(1)}, f32[512]{0:T(512)}, u32[]{:S(2)}) copy-start(f32[512]{0:T(512)} %copy-done.47) | copy-start | bytes 6148
  2678.9 12.9 all-to-all-start.13
  2683.3 515.4 %reduce-scatter.3.cloned.1.call-start = ((), (), s32[]{:S(2)}) async-start(), calls=%async_computation.20 | async-start | bytes 16711680 | tf_op jit(solution)/shard_map/reduce_scatter | solution.py:317
  2733.5 721.3 %all-reduce.12.cloned.1.call-start = ((), (), s32[]{:S(2)}) async-start(), calls=%async_computation.22 | async-start | bytes 22020096 | tf_op jit(solution)/shard_map/psum | solution.py:322
  3200.4 77.4 %copy-start.12 = (f32[512,1536]{1,0:T(8,128)S(1)}, f32[512,1536]{1,0:T(8,128)}, u32[]{:S(2)}) copy-start(f32[512,1536]{1,0:T(8,128)} %copy-done.11) | copy-start | bytes 9437188
  (41 other events, 842.5 us)
Sparse Core Ops, SparseCore 0:
  10.3 74.7 all-gather.2
  148.7 78.3 all-gather.4
  2485.0 236.3 reduce-scatter.4
  2733.6 375.2 reduce-scatter.2
  3198.9 255.8 all-reduce.11
where the time goes:
time: 3480 us; the launch traced here: 3470 us
  waiting for transfers between devices  1760 us (51%)
  blocking collectives  530 us (15%)
  matrix products  360 us (10%)
  starting transfers between devices  318 us (9%)
  local copies, waits for them, and re-layouts  307 us (9%)
  other arithmetic  175 us (5%)
    all_to_all x2, waiting for transfers between devices, from_experts(): lax.all_to_all(rows.reshape(fsdp_count, share, model_width), 'fsdp', spli...  1010 us
    all_to_all x2, waiting for transfers between devices, to_experts(): lax.all_to_all(rows.reshape(fsdp_count, share, model_width), 'fsdp', spli...  467 us
    all_to_all x1, blocking collectives, body(): lax.all_to_all(local_grads, 'fsdp', split_axis=0, concat_axis=2, tiled=True)  397 us
    all_to_all x2, starting transfers between devices, from_experts(): lax.all_to_all(rows.reshape(fsdp_count, share, model_width), 'fsdp', spli...  196 us
    psum x1, waiting for transfers between devices, body(): lax.psum((in_part, out_part, first_part, second_part, expert_part), 'seq')  172 us
    unnamed x2, blocking collectives  96.9 us
    all_to_all x2, starting transfers between devices, to_experts(): lax.all_to_all(rows.reshape(fsdp_count, share, model_width), 'fsdp', spli...  72.2 us
  transfers between devices with their start and end apart: 18, of which 12 were waited for; matrix products, arithmetic and copies ran while one was open for 19% of the time, Pallas kernels for 0%

commit v1 on v0

v1 whole, which is shorter than its diff:
```python
import functools

import jax
import jax.numpy as jnp
from jax import lax
from jax.experimental import pallas as pl
from jax.experimental.pallas import tpu as pltpu
from jax.sharding import PartitionSpec as P

HEADS = 24
KV_HEADS = 8
HEAD_DIM = 64
EXPERTS = 16
GROUP = HEADS // KV_HEADS
EPS = 1e-06
BF = jnp.bfloat16
F32 = jnp.float32
ROWS = ("outer", "inner")
VMEM_LIMIT = 60 * 1024 * 1024


def norm_rows(values, gain_vector):
    inverse = lax.rsqrt(jnp.mean(values * values, axis=-1, keepdims=True) + EPS)
    normed = values * inverse
    return (normed, inverse, (normed * gain_vector).astype(BF))


def norm_back(upstream, normed, inverse, gain_vector):
    scaled = upstream * gain_vector
    spread = jnp.mean(scaled * normed, axis=-1, keepdims=True)
    return (inverse * (scaled - normed * spread), jnp.sum(upstream * normed, axis=0))


def swap(x, axis, bit):
    return lax.ppermute(x, axis, [(i, i ^ bit) for i in range(lax.axis_size(axis))])


def core_swap(x):
    return swap(x, "inner", 1)


def side_swap(x):
    return swap(x, "inner", 2)


def seq_swap(x):
    return swap(x, "seq", 1)


def layer_gather(block):
    half = block.shape[0] // 2
    across = seq_swap(block)
    beside = side_swap(block)
    sibling = core_swap(block)
    far_top = seq_swap(beside[:half])
    far_low = side_swap(across[half:])
    far = jnp.concatenate([far_top, far_low], axis=0)
    return [
        (block, sibling),
        (across, core_swap(across)),
        (beside, core_swap(beside)),
        (far, core_swap(far)),
    ]


def layer_scatter(own, across, beside, far):
    def plus(a, b):
        return (a.astype(F32) + b.astype(F32)).astype(BF)

    far_sum = plus(far[0], core_swap(far[1]))
    across_sum = plus(across[0], core_swap(across[1]))
    beside_sum = plus(beside[0], core_swap(beside[1]))
    half = far_sum.shape[0] // 2
    top = seq_swap(far_sum[:half])
    low = side_swap(far_sum[half:])
    beside_in = side_swap(jnp.concatenate([plus(beside_sum[:half], top), beside_sum[half:]]))
    across_in = seq_swap(jnp.concatenate([across_sum[:half], plus(across_sum[half:], low)]))
    own_sum = own[0].astype(F32) + core_swap(own[1]).astype(F32)
    return own_sum + across_in.astype(F32) + beside_in.astype(F32)


def dot_nt(a, b):
    return lax.dot_general(a, b, (((1,), (1,)), ((), ())), preferred_element_type=F32)


def dot_nn(a, b):
    return lax.dot_general(a, b, (((1,), (0,)), ((), ())), preferred_element_type=F32)


def dot_tn(a, b):
    return lax.dot_general(a, b, (((0,), (0,)), ((), ())), preferred_element_type=F32)


def attend_kernel(place_ref, q_ref, k_ref, v_ref, kr_ref, vr_ref, mixed_ref, stat_ref, bias_ref, col_ref):
    count = q_ref.shape[0]
    half = count // 2
    seq_at = place_ref[0]
    live = place_ref[1]

    @pl.when(pl.program_id(0) == 0)
    def _():
        row = lax.broadcasted_iota(jnp.int32, (count, count), 0)
        col = lax.broadcasted_iota(jnp.int32, (count, count), 1)
        bias_ref[...] = jnp.where((col <= row) & (col < live), 0.0, -jnp.inf)
        col_ref[...] = jnp.zeros_like(col_ref)

    def run(with_past):
        for g in range(2):
            lanes = slice(g * HEAD_DIM, (g + 1) * HEAD_DIM)
            key = k_ref[:, lanes]
            value = v_ref[:, lanes]
            if with_past:
                key_past = kr_ref[:, lanes]
                value_past = vr_ref[:, lanes]
            for r in range(GROUP):
                h = g * GROUP + r
                for part in range(2):
                    rows = slice(part * half, (part + 1) * half)
                    span = (part + 1) * half
                    query = q_ref[rows, h * HEAD_DIM : (h + 1) * HEAD_DIM] * BF(HEAD_DIM**-0.5)
                    scores = dot_nt(query, key[:span]) + bias_ref[rows, :span]
                    peak = jnp.max(scores, axis=-1, keepdims=True)
                    if with_past:
                        past = dot_nt(query, key_past)
                        peak = jnp.maximum(peak, jnp.max(past, axis=-1, keepdims=True))
                    lifted = jnp.exp(scores - peak)
                    total = jnp.sum(lifted, axis=-1, keepdims=True)
                    mixed = dot_nn(lifted.astype(BF), value[:span])
                    if with_past:
                        lifted_past = jnp.exp(past - peak)
                        total = total + jnp.sum(lifted_past, axis=-1, keepdims=True)
                        mixed = mixed + dot_nn(lifted_past.astype(BF), value_past)
                    mixed_ref[rows, h * HEAD_DIM : (h + 1) * HEAD_DIM] = (mixed / total).astype(BF)
                    col_ref[rows, h : h + 1] = peak + jnp.log(total)

    @pl.when(seq_at == 0)
    def _():
        run(False)

    @pl.when(seq_at != 0)
    def _():
        run(True)

    stat_ref[...] = col_ref[...].T[:8, :]


def attend(place, projected, past):
    count = projected.shape[0]
    steps = KV_HEADS // 2
    wide = 2 * GROUP * HEAD_DIM
    first_key = HEADS * HEAD_DIM // 128
    first_value = first_key + KV_HEADS * HEAD_DIM // 128
    return pl.pallas_call(
        attend_kernel,
        grid_spec=pltpu.PrefetchScalarGridSpec(
            num_scalar_prefetch=1,
            grid=(steps,),
            in_specs=[
                pl.BlockSpec((count, wide), lambda j, place: (0, j)),
                pl.BlockSpec((count, 128), lambda j, place: (0, first_key + j)),
                pl.BlockSpec((count, 128), lambda j, place: (0, first_value + j)),
                pl.BlockSpec((count, 128), lambda j, place: (0, j)),
                pl.BlockSpec((count, 128), lambda j, place: (0, steps + j)),
            ],
            out_specs=[
                pl.BlockSpec((count, wide), lambda j, place: (0, j)),
                pl.BlockSpec((None, 8, count), lambda j, place: (j, 0, 0)),
            ],
            scratch_shapes=[pltpu.VMEM((count, count), F32), pltpu.VMEM((count, 128), F32)],
        ),
        out_shape=[
            jax.ShapeDtypeStruct((count, HEADS * HEAD_DIM), BF),
            jax.ShapeDtypeStruct((steps, 8, count), F32),
        ],
        compiler_params=pltpu.CompilerParams(vmem_limit_bytes=VMEM_LIMIT),
        cost_estimate=pl.CostEstimate(flops=30_000_000_000, bytes_accessed=5_000_000, transcendentals=0),
        name="attend",
    )(place, projected, projected, projected, past, past)


def attend_back_kernel(
    place_ref, q_ref, k_ref, v_ref, kr_ref, vr_ref, mixed_ref, grad_ref, stat_ref,
    dq_ref, dk_ref, dv_ref, dkr_ref, dvr_ref, bias_ref,
):
    count = q_ref.shape[0]
    half = count // 2
    seq_at = place_ref[0]
    live = place_ref[1]
    scale = HEAD_DIM**-0.5

    @pl.when(pl.program_id(0) == 0)
    def _():
        key_at = lax.broadcasted_iota(jnp.int32, (count, count), 0)
        query_at = lax.broadcasted_iota(jnp.int32, (count, count), 1)
        bias_ref[...] = jnp.where((key_at <= query_at) & (key_at < live), 0.0, -jnp.inf)

    def run(with_past):
        for g in range(2):
            lanes = slice(g * HEAD_DIM, (g + 1) * HEAD_DIM)
            key = k_ref[:, lanes]
            value = v_ref[:, lanes]
            sums = [[jnp.zeros((half, HEAD_DIM), F32) for _ in range(2)] for _ in range(2)]
            if with_past:
                key_past = kr_ref[:, lanes]
                value_past = vr_ref[:, lanes]
                past_sums = [jnp.zeros((count, HEAD_DIM), F32) for _ in range(2)]
            for r in range(GROUP):
                h = g * GROUP + r
                cols = slice(h * HEAD_DIM, (h + 1) * HEAD_DIM)
                query = q_ref[:, cols] * BF(scale)
                grad = grad_ref[:, cols]
                product = grad.astype(F32) * mixed_ref[:, cols].astype(F32)
                delta = lax.dot_general(
                    jnp.ones((8, HEAD_DIM), F32), product, (((1,), (1,)), ((), ())),
                    precision=lax.Precision.HIGHEST, preferred_element_type=F32,
                )[:1]
                stat = stat_ref[h : h + 1, :]

                def piece(keys, values, queries, grads, stats, deltas, bias):
                    scores = dot_nt(keys, queries)
                    if bias is not None:
                        scores = scores + bias
                    chances = jnp.exp(scores - stats)
                    chance_grad = dot_nt(values, grads)
                    score_grad = (chances * (chance_grad - deltas)).astype(BF)
                    return chances.astype(BF), score_grad

                p0, s0 = piece(key[:half], value[:half], query, grad, stat, delta, bias_ref[:half, :])
                p1, s1 = piece(
                    key[half:], value[half:], query[half:], grad[half:], stat[:, half:], delta[:, half:],
                    bias_ref[half:, half:],
                )
                dq = dot_tn(s0, key[:half])
                dq_late = dot_tn(s1, key[half:])
                sums[0][0] += dot_nn(s0, query)
                sums[0][1] += dot_nn(s1, query[half:])
                sums[1][0] += dot_nn(p0, grad)
                sums[1][1] += dot_nn(p1, grad[half:])
                if with_past:
                    pp, sp = piece(key_past, value_past, query, grad, stat, delta, None)
                    dq = dq + dot_tn(sp, key_past)
                    past_sums[0] += dot_nn(sp, query)
                    past_sums[1] += dot_nn(pp, grad)
                dq_ref[:half, cols] = (dq[:half] * scale).astype(BF)
                dq_ref[half:, cols] = ((dq[half:] + dq_late) * scale).astype(BF)
            for where, out in ((0, dk_ref), (1, dv_ref)):
                out[:half, lanes] = sums[where][0].astype(BF)
                out[half:, lanes] = sums[where][1].astype(BF)
            if with_past:
                dkr_ref[:, lanes] = past_sums[0].astype(BF)
                dvr_ref[:, lanes] = past_sums[1].astype(BF)

    @pl.when(seq_at == 0)
    def _():
        run(False)
        dkr_ref[...] = jnp.zeros_like(dkr_ref)
        dvr_ref[...] = jnp.zeros_like(dvr_ref)

    @pl.when(seq_at != 0)
    def _():
        run(True)


def attend_back(place, projected, past, mixed, mixed_grad, stats):
    count = projected.shape[0]
    steps = KV_HEADS // 2
    wide = 2 * GROUP * HEAD_DIM
    first_key = HEADS * HEAD_DIM // 128
    first_value = first_key + KV_HEADS * HEAD_DIM // 128
    narrow = jax.ShapeDtypeStruct((count, KV_HEADS * HEAD_DIM), BF)
    head_spec = pl.BlockSpec((count, wide), lambda j, place: (0, j))
    pair_spec = pl.BlockSpec((count, 128), lambda j, place: (0, j))
    return pl.pallas_call(
        attend_back_kernel,
        grid_spec=pltpu.PrefetchScalarGridSpec(
            num_scalar_prefetch=1,
            grid=(steps,),
            in_specs=[
                head_spec,
                pl.BlockSpec((count, 128), lambda j, place: (0, first_key + j)),
                pl.BlockSpec((count, 128), lambda j, place: (0, first_value + j)),
                pair_spec,
                pl.BlockSpec((count, 128), lambda j, place: (0, steps + j)),
                head_spec,
                head_spec,
                pl.BlockSpec((None, 8, count), lambda j, place: (j, 0, 0)),
            ],
            out_specs=[head_spec, pair_spec, pair_spec, pair_spec, pair_spec],
            scratch_shapes=[pltpu.VMEM((count, count), F32)],
        ),
        out_shape=[jax.ShapeDtypeStruct((count, HEADS * HEAD_DIM), BF), narrow, narrow, narrow, narrow],
        compiler_params=pltpu.CompilerParams(vmem_limit_bytes=VMEM_LIMIT),
        cost_estimate=pl.CostEstimate(flops=60_000_000_000, bytes_accessed=10_000_000, transcendentals=0),
        name="attend_back",
    )(place, projected, projected, projected, past, past, mixed, mixed_grad, stats)


def expert_kernel(
    n_ref, c_ref, w_ref, wg_ref, wl_ref, wd_ref, ch_ref, gg_ref, lg_ref, out_ref, back_ref, dot_ref
):
    ff = wg_ref.shape[1] // 2
    rows = n_ref[...]
    up = c_ref[...]
    gate = dot_nn(rows, wg_ref[...])
    lift = dot_nn(rows, wl_ref[...])
    push = dot_nn(up, wd_ref[...])
    for e in range(2):
        cols = slice(e * ff, (e + 1) * ff)
        weight = w_ref[:, e : e + 1]
        g, l, u = gate[:, cols], lift[:, cols], push[:, cols]
        sig = 1.0 / (1.0 + jnp.exp(-g))
        silu = g * sig
        hidden = silu * l
        hidden = hidden.astype(BF).astype(F32)
        dot_ref[:, e : e + 1] = jnp.sum(hidden * u, axis=-1, keepdims=True)
        grad = u * weight
        ch_ref[:, cols] = (hidden * weight).astype(BF)
        gg_ref[:, cols] = (grad * l * sig * (1.0 + g * (1.0 - sig))).astype(BF)
        lg_ref[:, cols] = (grad * silu).astype(BF)
    out_ref[...] = dot_nt(ch_ref[...], wd_ref[...]).astype(BF)
    back_ref[...] = (dot_nt(gg_ref[...], wg_ref[...]) + dot_nt(lg_ref[...], wl_ref[...])).astype(BF)


def expert_rows(rows, up, weight, gate, lift, down):
    count, width = rows.shape
    ff = gate.shape[1]
    tile = 256
    row_spec = pl.BlockSpec((tile, width), lambda i: (i, 0))
    ff_spec = pl.BlockSpec((tile, ff), lambda i: (i, 0))
    lane_spec = pl.BlockSpec((tile, 2), lambda i: (i, 0))
    weight_spec = pl.BlockSpec((width, ff), lambda i: (0, 0), pipeline_mode=pl.Buffered(1))
    mid = jax.ShapeDtypeStruct((count, ff), BF)
    wide = jax.ShapeDtypeStruct((count, width), BF)
    return pl.pallas_call(
        expert_kernel,
        grid=(count // tile,),
        in_specs=[row_spec, row_spec, lane_spec, weight_spec, weight_spec, weight_spec],
        out_specs=[ff_spec, ff_spec, ff_spec, row_spec, row_spec, lane_spec],
        out_shape=[mid, mid, mid, wide, wide, jax.ShapeDtypeStruct((count, 2), F32)],
        compiler_params=pltpu.CompilerParams(vmem_limit_bytes=VMEM_LIMIT),
        cost_estimate=pl.CostEstimate(
            flops=12 * count * width * ff, bytes_accessed=count * (8 * width + 6 * ff), transcendentals=0
        ),
        name="expert_rows",
    )(rows, up, weight, gate, lift, down)


def body(
    tokens,
    lengths,
    routes,
    route_gates,
    cotangent,
    norm_first,
    attention_in,
    attention_out,
    norm_second,
    expert_gate,
    expert_lift,
    expert_down,
):
    count = tokens.shape[1]
    width = tokens.shape[2]
    choose = routes.shape[2]
    seq_count = lax.axis_size("seq")
    inner_count = lax.axis_size("inner")
    owners = seq_count * inner_count
    per_owner = EXPERTS // owners
    ff = expert_gate.shape[2]
    query_width = HEADS * HEAD_DIM
    seq_at = lax.axis_index("seq")
    layer_at = seq_at * inner_count + lax.axis_index("inner")
    length = lengths[0]
    place = jnp.stack([seq_at.astype(jnp.int32), length - seq_at.astype(jnp.int32) * count])
    live_rows = seq_at * count + jnp.arange(count, dtype=jnp.int32) < length
    inputs = tokens[0].astype(F32)
    upstream_low = cotangent[0]
    upstream = upstream_low.astype(F32)

    shard = width // (lax.axis_size("outer") * inner_count)
    gains = jnp.concatenate(
        [norm_first[:, None], norm_second[:, None], jnp.zeros((shard, 126), BF)], axis=1
    )
    project_in = lax.all_gather(
        jnp.concatenate([attention_in, gains], axis=1), ROWS, axis=0, tiled=True
    )
    project_out = lax.all_gather(attention_out, ROWS, axis=0, tiled=True)
    qkv = attention_in.shape[1]
    first_gain = project_in[:, qkv].astype(F32)
    second_gain = project_in[:, qkv + 1].astype(F32)
    project_in = project_in[:, :qkv]

    def fetch(weight):
        mine = lax.dynamic_slice_in_dim(
            weight, seq_at * (inner_count * per_owner), inner_count * per_owner, 1
        ).reshape(shard, inner_count, per_owner * ff).transpose(1, 0, 2)
        local = lax.all_to_all(mine, "inner", split_axis=0, concat_axis=0, tiled=True)
        local = local.reshape(inner_count * shard, per_owner * ff)
        return lax.all_gather(local, "outer", axis=0, tiled=True)

    gate_two, lift_two, down_two = fetch(expert_gate), fetch(expert_lift), fetch(expert_down)

    route_rows = routes[0]
    gate_rows = route_gates[0]
    chosen = (
        route_rows.T[:, None, :] == jnp.arange(EXPERTS, dtype=jnp.int32)[None, :, None]
    ) & live_rows[None, None, :]
    combine = jnp.sum(jnp.where(chosen, gate_rows.T[:, None, :], 0.0), axis=0)
    combine = lax.all_to_all(
        combine.reshape(owners, per_owner, count), ("seq", "inner"), split_axis=0, concat_axis=0, tiled=True
    )
    combine = combine.transpose(0, 2, 1)

    def partner(at):
        return layer_at ^ at

    chips = (0, inner_count, 2, inner_count + 2)
    weights = [
        jnp.concatenate([combine[partner(chip)], combine[partner(chip + 1)]], axis=0) for chip in chips
    ]
    up_rows = [jnp.concatenate(pair, axis=0) for pair in layer_gather(upstream_low)]

    normed_one, inverse_one, lowered_one = norm_rows(inputs, first_gain)
    projected = jnp.dot(lowered_one, project_in, preferred_element_type=F32).astype(BF)
    past = lax.ppermute(projected[:, query_width:], "seq", [(0, 1)])
    mixed, stats = attend(place, projected, past)
    middle = inputs + jnp.dot(mixed, project_out, preferred_element_type=F32)
    normed_two, inverse_two, lowered_two = norm_rows(middle, second_gain)

    row_pairs = [jnp.concatenate(pair, axis=0) for pair in layer_gather(lowered_two)]
    made = [
        expert_rows(rows, up, weight, gate_two, lift_two, down_two)
        for rows, up, weight in zip(row_pairs, up_rows, weights)
    ]

    def pairs(at):
        return [(part[at][:count], part[at][count:]) for part in made]

    normed_grad_two = layer_scatter(*pairs(4))
    combined = layer_scatter(*pairs(3))
    block_output = (middle + combined).astype(BF)[None]
    dots = jnp.zeros((owners, count, per_owner), F32)
    for chip, part in zip(chips, made):
        dots = dots.at[partner(chip)].set(part[5][:count]).at[partner(chip + 1)].set(part[5][count:])
    dots = lax.all_to_all(
        dots.transpose(0, 2, 1), ("seq", "inner"), split_axis=0, concat_axis=0, tiled=True
    ).reshape(EXPERTS, count)
    grad_gates = jnp.sum(jnp.where(chosen, dots[None], 0.0), axis=1).T[None]

    all_rows = jnp.concatenate(row_pairs, axis=0)
    all_up = jnp.concatenate(up_rows, axis=0)
    mids = [jnp.concatenate([part[at] for part in made], axis=0) for at in range(3)]

    def give_back(left, right):
        total = lax.dot_general(left, right, (((0,), (0,)), ((), ())), preferred_element_type=F32).astype(BF)
        local = lax.psum_scatter(total, "outer", scatter_dimension=0, tiled=True)
        local = local.reshape(inner_count, shard, per_owner * ff)
        mine = lax.all_to_all(local, "inner", split_axis=0, concat_axis=0, tiled=True)
        mine = mine.reshape(inner_count, shard, per_owner, ff)
        other = seq_swap(mine)
        both = jnp.where(seq_at == 0, jnp.stack([mine, other]), jnp.stack([other, mine]))
        return both.transpose(2, 0, 1, 3, 4).reshape(shard, EXPERTS, ff).astype(F32)

    grad_gate = give_back(all_rows, mids[1])
    grad_lift = give_back(all_rows, mids[2])
    grad_down = give_back(all_up, mids[0])

    middle_norm_grad, second_gain_grad = norm_back(normed_grad_two, normed_two, inverse_two, second_gain)
    middle_grad = upstream + middle_norm_grad
    branch_grad = middle_grad.astype(BF)
    mixed_grad = dot_nt(branch_grad, project_out).astype(BF)
    out_weight_grad = dot_tn(mixed, branch_grad)
    query_grad, key_grad, value_grad, key_past, value_past = attend_back(
        place, projected, past, mixed, mixed_grad, stats
    )
    late = lax.ppermute(jnp.concatenate([key_past, value_past], axis=1), "seq", [(1, 0)])
    pair_grad = jnp.concatenate([key_grad, value_grad], axis=1)
    pair_grad = (pair_grad.astype(F32) + late.astype(F32)).astype(BF)
    projected_grad = jnp.concatenate([query_grad, pair_grad], axis=1)
    normed_grad_one = dot_nt(projected_grad, project_in)
    in_weight_grad = dot_tn(lowered_one, projected_grad)
    input_norm_grad, first_gain_grad = norm_back(normed_grad_one, normed_one, inverse_one, first_gain)
    grad_tokens = (middle_grad + input_norm_grad)[None]

    def home(total):
        part = lax.psum_scatter(total.astype(BF), ROWS, scatter_dimension=0, tiled=True)
        return part.astype(F32) + seq_swap(part).astype(F32)

    gain_grads = jnp.concatenate(
        [first_gain_grad[:, None], second_gain_grad[:, None], jnp.zeros((width, 126), F32)], axis=1
    )
    in_part = home(jnp.concatenate([in_weight_grad, gain_grads], axis=1))
    out_part = home(out_weight_grad)
    return (
        block_output,
        grad_tokens,
        grad_gates,
        in_part[:, qkv],
        in_part[:, :qkv],
        out_part,
        in_part[:, qkv + 1],
        grad_gate,
        grad_lift,
        grad_down,
    )


def solution(mesh):
    seq_count, fsdp_count = mesh.devices.shape
    inner_count = EXPERTS // (2 * seq_count)
    fine = jax.sharding.Mesh(
        mesh.devices.reshape(seq_count, fsdp_count // inner_count, inner_count), ("seq", "outer", "inner")
    )
    return jax.shard_map(
        body,
        mesh=fine,
        in_specs=(
            P(ROWS, "seq", None),
            P(ROWS),
            P(ROWS, "seq", None),
            P(ROWS, "seq", None),
            P(ROWS, "seq", None),
            P(ROWS),
            P(ROWS, None),
            P(ROWS, None),
            P(ROWS),
            P(ROWS, None, None),
            P(ROWS, None, None),
            P(ROWS, None, None),
        ),
        out_specs=(
            P(ROWS, "seq", None),
            P(ROWS, "seq", None),
            P(ROWS, "seq", None),
            P(ROWS),
            P(ROWS, None),
            P(ROWS, None),
            P(ROWS),
            P(ROWS, None, None),
            P(ROWS, None, None),
            P(ROWS, None, None),
        ),
        check_vma=False,
    )
```

time: 3480 us -> 990 us (0.28)
  waiting for transfers between devices: 1760 us -> 371 us
  blocking collectives: 530 us -> 42 us
  matrix products: 360 us -> 102 us
  starting transfers between devices: 318 us -> 70.4 us
  local copies, waits for them, and re-layouts: 307 us -> 135 us
  Pallas kernels: 0 us -> 159 us
  other arithmetic: 175 us -> 85.9 us
    all_to_all x13 -> x5, waiting for transfers between devices: 1550 us -> 53.1 us  [the longest x3 30.6 us: give_back(): lax.all_to_all(local, 'inner', split_axis=0, concat_axis=0, tiled=True)]
    all_to_all x3, blocking collectives: 428 us -> 42 us  [the longest x2 34.9 us: fetch(): lax.all_to_all(mine, 'inner', split_axis=0, concat_axis=0, tiled=True)]
    all_to_all x13 -> x5, starting transfers between devices: 318 us -> 20.6 us  [the longest x3 13 us: give_back(): lax.all_to_all(local, 'inner', split_axis=0, concat_axis=0, tiled=True)]
    dot_general x29 -> x9, matrix products: 360 us -> 102 us  [the longest x3 61.2 us: give_back(): lax.dot_general(left, right, (((0,), (0,)), ((), ())), preferred_element_...]
    ppermute x0 -> x39, waiting for transfers between devices: none -> 214 us  [the longest x37 174 us: swap(): lax.ppermute(x, axis, [(i, i ^ bit) for i in range(lax.axis_size(axis))])]
    psum x1 -> x0, waiting for transfers between devices: 172 us -> none  [body(): lax.psum((in_part, out_part, first_part, second_part, expert_part), 'seq')]
    pallas_call x0 -> x6, Pallas kernels: none -> 159 us  [the longest x4 112 us: expert_rows(): pl.pallas_call(expert_kernel, grid=(count // tile,), in_specs=[row_spec,...]
    gather x4 -> x0, local copies, waits for them, and re-layouts: 124 us -> none  [the longest x1 37.4 us: body(): padded_result[slot_index].reshape(token_count, choose, model_width)]
  transfers between devices with their start and end apart: 18 -> 54, of which waited for: 12 -> 17; matrix products, arithmetic and copies ran while one was open for 19% -> 28% of each run, Pallas kernels for 0% -> 13%
where the time goes in v1:
time: 990 us; the launch traced here: 982 us
  waiting for transfers between devices  371 us (37%)
  Pallas kernels  159 us (16%)
  local copies, waits for them, and re-layouts  135 us (14%)
  matrix products  102 us (10%)
  other arithmetic  85.9 us (9%)
  starting transfers between devices  70.4 us (7%)
  blocking collectives  42 us (4%)
  between operations  16.2 us (2%)
    ppermute x37, waiting for transfers between devices, swap(): lax.ppermute(x, axis, [(i, i ^ bit) for i in range(lax.axis_size(axis))])  174 us
    pallas_call x4, Pallas kernels, expert_rows(): pl.pallas_call(expert_kernel, grid=(count // tile,), in_specs=[row_spec,...  112 us
    all_gather x3, waiting for transfers between devices, fetch(): return lax.all_gather(local, 'outer', axis=0, tiled=True)  103 us
    dot_general x3, matrix products, give_back(): lax.dot_general(left, right, (((0,), (0,)), ((), ())), preferred_element_...  61.2 us
    ppermute x37, starting transfers between devices, swap(): lax.ppermute(x, axis, [(i, i ^ bit) for i in range(lax.axis_size(axis))])  44 us
    ppermute x1, waiting for transfers between devices, body(): lax.ppermute(jnp.concatenate([key_past, value_past], axis=1), 'seq', [(1,...  40.3 us
    unnamed x133, local copies, waits for them, and re-layouts  39.6 us
    all_to_all x2, blocking collectives, fetch(): lax.all_to_all(mine, 'inner', split_axis=0, concat_axis=0, tiled=True)  34.9 us
  transfers between devices with their start and end apart: 54, of which 17 were waited for; matrix products, arithmetic and copies ran while one was open for 28% of the time, Pallas kernels for 13%

profile of v1, /device:TPU:0, one launch (start us, length us, event | category | flops | bytes accessed | tf_op | source)
XLA Modules:
  0.0 981.5 jit_solution(9205277397393084289)
XLA Ops:
  12.4 20.1 %all_to_all.40 = bf16[4,96,1024]{2,1,0:T(8,128)(2,1)} all-to-all(bf16[4,96,1024]{2,1,0:T(8,128)(2,1)S(1)} %copy.74), channel_id=1, replica_groups=mesh['seq'=2,'outer'=4,'inner'=4] {'inner'}, dimensions={0} | all-to-all | bytes 1572864 | tf_op jit(solution)/shard_map/all_to_all | solution.py:397
  35.6 14.8 %all_to_all.41 = bf16[4,96,1024]{2,1,0:T(8,128)(2,1)} all-to-all(bf16[4,96,1024]{2,1,0:T(8,128)(2,1)S(1)} %copy.76), channel_id=1, replica_groups=mesh['seq'=2,'outer'=4,'inner'=4] {'inner'}, dimensions={0} | all-to-all | bytes 1572864 | tf_op jit(solution)/shard_map/all_to_all | solution.py:397
  55.6 51.4 %collective-permute-done.13 = bf16[512,1536]{1,0:T(8,128)(2,1)S(1)} collective-permute-done((bf16[512,1536]{1,0:T(8,128)(2,1)S(1)}, bf16[512,1536]{1,0:T(8,128)(2,1)S(1)}, u32[]{:S(2)}, u32[]{:S(2)}) %collective-permute-start.13) | collective-permute-done | bytes 1572896 | tf_op jit(solution)/shard_map/ppermute | solution.py:35
  113.8 8.1 fusion.32.q_ref.k_ref.v_ref
  137.3 11.9 %all-to-all-done = f32[8,2,512]{2,1,0:T(2,128)S(1)} async-done(((f32[8,2,512]{2,1,0:T(2,128)}), f32[8,2,512]{2,1,0:T(2,128)S(1)}, u32[]{:S(2)}, u32[]{:S(2)}) %all-to-all-start) | async-done | bytes 32800 | tf_op jit(solution)/shard_map/all_to_all | solution.py:409
  154.5 10.6 %all-to-all-done.2 = bf16[4,96,1024]{2,1,0:T(8,128)(2,1)} async-done(((bf16[4,96,1024]{2,1,0:T(8,128)(2,1)}), bf16[4,96,1024]{2,1,0:T(8,128)(2,1)}, u32[]{:S(2)}, u32[]{:S(2)}) %all-to-all-start.2) | async-done | bytes 786464 | tf_op jit(solution)/shard_map/all_to_all | solution.py:397
  169.0 19.8 %attend.1 = (bf16[512,1536]{1,0:T(8,128)(2,1)}, f32[4,8,512]{2,1,0:T(8,128)}) custom-call(s32[2]{0:T(128)} %pad_add_fusion.16.place_ref, bf16[512,2560]{1,0:T(8,128)(2,1)} %copy-done.34, bf16[512,2560]{1,0:T(8,128)(2,1)} %copy-done.34, bf16[512,2560]{1,0:T(8,128)(2,1)} %copy-done.34, bf16[512,1024]{1,0:T(8,128)(2,1)} %collective-permute-done.kr_ref.vr_ref, ...), custom_call_target="tpu_custom_call" | custom-call | flops 30000001024 | bytes 5000000 | tf_op jit(solution)/shard_map/attend/pallas_call | solution.py:153
  197.9 10.8 %collective-permute-start.4 = (bf16[512,1536]{1,0:T(8,128)(2,1)}, bf16[512,1536]{1,0:T(8,128)(2,1)}, u32[]{:S(2)}, u32[]{:S(2)}) collective-permute-start(bf16[512,1536]{1,0:T(8,128)(2,1)} %get-tuple-element.185), channel_id=1, source_target_pairs={{0,16},{16,0},{1,17},{17,1},{2,18},{18,2},{3,19},{19,3},{4,20},{20... | collective-permute-start | bytes 4718600 | tf_op jit(solution)/shard_map/ppermute | solution.py:35
  226.8 7.7 collective-permute-done.9
  236.6 10.9 %collective-permute-start.10 = (bf16[256,1536]{1,0:T(8,128)(2,1)}, bf16[256,1536]{1,0:T(8,128)(2,1)S(1)}, u32[]{:S(2)}, u32[]{:S(2)}) collective-permute-start(bf16[256,1536]{1,0:T(8,128)(2,1)} %slice.346), channel_id=1, source_target_pairs={{0,16},{16,0},{1,17},{17,1},{2,18},{18,2},{3,19},{19,3},{4,20},{20... | collective-permute-start | bytes 2359304 | tf_op jit(solution)/shard_map/ppermute | solution.py:35
  254.1 39.3 %all-gather.14.cloned.1.call-done.wd_ref = bf16[1536,1024]{1,0:T(8,128)(2,1)} async-done(((bf16[384,1024]{1,0:T(8,128)(2,1)}), bf16[1536,1024]{1,0:T(8,128)(2,1)}) %all-gather.14.cloned.1.call-update) | async-done | bytes 3145744 | tf_op jit(solution)/shard_map/all_gather | solution.py:399
  293.4 63.6 %all-gather.12.cloned.1.call-done.wl_ref = bf16[1536,1024]{1,0:T(8,128)(2,1)} async-done(((bf16[384,1024]{1,0:T(8,128)(2,1)}), bf16[1536,1024]{1,0:T(8,128)(2,1)}) %all-gather.12.cloned.1.call-update) | async-done | bytes 3145744 | tf_op jit(solution)/shard_map/all_gather | solution.py:399
  357.0 27.9 %expert_rows.4 = (bf16[1024,1024]{1,0:T(8,128)(2,1)}, bf16[1024,1024]{1,0:T(8,128)(2,1)}, bf16[1024,1024]{1,0:T(8,128)(2,1)}, bf16[1024,1536]{1,0:T(8,128)(2,1)}...) custom-call(bf16[1024,1536]{1,0:T(8,128)(2,1)} %pad_maximum_fusion.n_ref, bf16[1024,1536]{1,0:T(8,128)(2,1)} %pad_maximum_fusion.1.c_ref, ...), custom_call_target="tpu_custom_call" | custom-call | flops 19327352832 | bytes 18874368 | tf_op jit(solution)/shard_map/expert_rows/pallas_call | solution.py:334
  407.1 28.1 %expert_rows.7 = (bf16[1024,1024]{1,0:T(8,128)(2,1)}, bf16[1024,1024]{1,0:T(8,128)(2,1)}, bf16[1024,1024]{1,0:T(8,128)(2,1)}, bf16[1024,1536]{1,0:T(8,128)(2,1)}...) custom-call(bf16[1024,1536]{1,0:T(8,128)(2,1)} %pad_maximum_fusion.6.n_ref, bf16[1024,1536]{1,0:T(8,128)(2,1)} %pad_maximum_fusion.7.c_ref, ...), custom_call_target="tpu_custom_call" | custom-call | flops 19327352832 | bytes 18874368 | tf_op jit(solution)/shard_map/expert_rows/pallas_call | solution.py:334
  435.2 27.9 %expert_rows.5 = (bf16[1024,1024]{1,0:T(8,128)(2,1)}, bf16[1024,1024]{1,0:T(8,128)(2,1)}, bf16[1024,1024]{1,0:T(8,128)(2,1)}, bf16[1024,1536]{1,0:T(8,128)(2,1)}...) custom-call(bf16[1024,1536]{1,0:T(8,128)(2,1)} %pad_maximum_fusion.2.n_ref, bf16[1024,1536]{1,0:T(8,128)(2,1)} %pad_maximum_fusion.3.c_ref, ...), custom_call_target="tpu_custom_call" | custom-call | flops 19327352832 | bytes 18874368 | tf_op jit(solution)/shard_map/expert_rows/pallas_call | solution.py:334
  469.1 28.4 %expert_rows.6 = (bf16[1024,1024]{1,0:T(8,128)(2,1)}, bf16[1024,1024]{1,0:T(8,128)(2,1)}, bf16[1024,1024]{1,0:T(8,128)(2,1)}, bf16[1024,1536]{1,0:T(8,128)(2,1)}...) custom-call(bf16[1024,1536]{1,0:T(8,128)(2,1)} %pad_maximum_fusion.4.n_ref, bf16[1024,1536]{1,0:T(8,128)(2,1)} %pad_maximum_fusion.5.c_ref, ...), custom_call_target="tpu_custom_call" | custom-call | flops 19327352832 | bytes 18874368 | tf_op jit(solution)/shard_map/expert_rows/pallas_call | solution.py:334
  497.5 20.4 %fusion.41 = bf16[1536,1024]{1,0:T(8,128)(2,1)} fusion(bf16[4096,1536]{1,0:T(8,128)(2,1)} %constant_dynamic-update-slice_fusion, bf16[1024,1024]{1,0:T(8,128)(2,1)} %get-tuple-element.159, bf16[1024,1024]{1,0:T(8,128)(2,1)} %get-tuple-element.158, bf16[1024,1024]{1,0:T(8,128)(2,1)} %get-tuple-element.157, bf16[1024,1024]{1,0:T(8,128)(2,1)S(1)} %copy-done.58), kind=kOutput, calls=%fused_computation.40 | convolution fusion | flops 12920029184 | bytes 24117248 | tf_op jit(solution)/shard_map/dot_general | solution.py:455
  519.4 21.0 %fusion.38 = bf16[1536,1024]{1,0:T(8,128)(2,1)} fusion(bf16[4096,1536]{1,0:T(8,128)(2,1)} %constant_dynamic-update-slice_fusion, bf16[1024,1024]{1,0:T(8,128)(2,1)} %get-tuple-element.163, bf16[1024,1024]{1,0:T(8,128)(2,1)} %get-tuple-element.162, bf16[1024,1024]{1,0:T(8,128)(2,1)} %get-tuple-element.161, bf16[1024,1024]{1,0:T(8,128)(2,1)S(1)} %copy-done.57), kind=kOutput, calls=%fused_computation.39 | convolution fusion | flops 12920029184 | bytes 24117248 | tf_op jit(solution)/shard_map/dot_general | solution.py:455
  567.4 19.9 %fusion.35 = bf16[1536,1024]{1,0:T(8,128)(2,1)} fusion(bf16[4096,1536]{1,0:T(8,128)(2,1)} %copy-done.37, bf16[1024,1024]{1,0:T(8,128)(2,1)} %get-tuple-element.167, bf16[1024,1024]{1,0:T(8,128)(2,1)S(1)} %copy-done.55, bf16[1024,1024]{1,0:T(8,128)(2,1)S(1)} %copy-done.56, bf16[1024,1024]{1,0:T(8,128)(2,1)S(1)} %copy-done.54), kind=kOutput, calls=%fused_computation.38 | convolution fusion | flops 12920029184 | bytes 24117248 | tf_op jit(solution)/shard_map/dot_general | solution.py:455
  606.5 16.7 %collective-permute-done.31 = bf16[256,1536]{1,0:T(8,128)(2,1)S(1)} collective-permute-done((bf16[256,1536]{1,0:T(8,128)(2,1)S(1)}, bf16[256,1536]{1,0:T(8,128)(2,1)S(1)}, u32[]{:S(2)}, u32[]{:S(2)}) %collective-permute-start.31) | collective-permute-done | bytes 786464 | tf_op jit(solution)/shard_map/ppermute | solution.py:35
  626.0 15.8 %collective-permute-done.23 = bf16[256,1536]{1,0:T(8,128)(2,1)S(1)} collective-permute-done((bf16[256,1536]{1,0:T(8,128)(2,1)S(1)}, bf16[256,1536]{1,0:T(8,128)(2,1)S(1)}, u32[]{:S(2)}, u32[]{:S(2)}) %collective-permute-start.23) | collective-permute-done | bytes 786464 | tf_op jit(solution)/shard_map/ppermute | solution.py:35
  645.1 28.3 %collective-permute-done.32 = bf16[512,1536]{1,0:T(8,128)(2,1)S(1)} collective-permute-done((bf16[512,1536]{1,0:T(8,128)(2,1)S(1)}, bf16[512,1536]{1,0:T(8,128)(2,1)S(1)}, u32[]{:S(2)}, u32[]{:S(2)}) %collective-permute-start.32) | collective-permute-done | bytes 1572896 | tf_op jit(solution)/shard_map/ppermute | solution.py:35
  680.6 25.7 %collective-permute-done.24 = bf16[512,1536]{1,0:T(8,128)(2,1)S(1)} collective-permute-done((bf16[512,1536]{1,0:T(8,128)(2,1)S(1)}, bf16[512,1536]{1,0:T(8,128)(2,1)S(1)}, u32[]{:S(2)}, u32[]{:S(2)}) %collective-permute-start.24) | collective-permute-done | bytes 1572896 | tf_op jit(solution)/shard_map/ppermute | solution.py:35
  728.8 26.7 %attend_back.1 = (bf16[512,1536]{1,0:T(8,128)(2,1)}, bf16[512,512]{1,0:T(8,128)(2,1)}, bf16[512,512]{1,0:T(8,128)(2,1)}, bf16[512,512]{1,0:T(8,128)(2,1)}, bf16[512,512]{1,0:T(8,128)(2,1)}) custom-call(s32[2]{0:T(128)} %pad_add_fusion.16.place_ref, bf16[512,2560]{1,0:T(8,128)(2,1)} %copy-done.34, bf16[512,2560]{1,0:T(8,128)(2,1)} %copy-done.34, ...), custom_call_target="tpu_custom_call" | custom-call | flops 60000002048 | bytes 10000000 | tf_op jit(solution)/shard_map/attend_back/pallas_call | solution.py:273
  758.5 40.3 %collective-permute-done.33 = bf16[512,1024]{1,0:T(8,128)(2,1)S(1)} collective-permute-done((bf16[512,1024]{1,0:T(8,128)(2,1)S(1)}, bf16[512,1024]{1,0:T(8,128)(2,1)S(1)}, u32[]{:S(2)}, u32[]{:S(2)}) %collective-permute-start.33) | collective-permute-done | bytes 1048608 | tf_op jit(solution)/shard_map/ppermute | solution.py:476
  800.4 9.3 fusion.50
  816.9 13.1 %concatenate.151 = bf16[1536,2688]{1,0:T(8,128)(2,1)} concatenate(bf16[1536,2560]{1,0:T(8,128)(2,1)} %convolution_convert_fusion, bf16[1536,1]{1,0:T(8,128)(2,1)S(1)} %broadcast_in_dim.90, bf16[1536,1]{1,0:T(8,128)(2,1)S(1)} %broadcast_in_dim.91, bf16[1536,126]{1,0:T(8,128)(2,1)S(1)} %broadcast_in_dim.89), dimensions={1} | concatenate | bytes 16515072 | tf_op jit(solution)/shard_map/concatenate | solution.py:492
  838.4 7.1 all_to_all.42
  849.8 12.6 %all-to-all-done.5 = bf16[4,96,1024]{2,1,0:T(8,128)(2,1)} async-done(((bf16[4,96,1024]{2,1,0:T(8,128)(2,1)}), bf16[4,96,1024]{2,1,0:T(8,128)(2,1)}, u32[]{:S(2)}, u32[]{:S(2)}) %all-to-all-start.5) | async-done | bytes 786464 | tf_op jit(solution)/shard_map/all_to_all | solution.py:458
  873.4 7.6 all-to-all-done.6
  894.1 10.4 %all-to-all-done.7 = bf16[4,96,1024]{2,1,0:T(8,128)(2,1)} async-done(((bf16[4,96,1024]{2,1,0:T(8,128)(2,1)}), bf16[4,96,1024]{2,1,0:T(8,128)(2,1)}, u32[]{:S(2)}, u32[]{:S(2)}) %all-to-all-start.7) | async-done | bytes 786464 | tf_op jit(solution)/shard_map/all_to_all | solution.py:458
  924.6 19.2 %collective-permute-done.37 = bf16[4,96,2,512]{3,2,0,1:T(2,128)(2,1)} collective-permute-done((bf16[4,96,2,512]{3,2,0,1:T(2,128)(2,1)}, bf16[4,96,2,512]{3,2,0,1:T(2,128)(2,1)}, u32[]{:S(2)}, u32[]{:S(2)}) %collective-permute-start.37) | collective-permute-done | bytes 786464 | tf_op jit(solution)/shard_map/ppermute | solution.py:35
  (356 shorter events, 290.2 us)
Async XLA Ops:
  7.2 104.9 %all-gather.6.cloned.1.call-start = ((), (), s32[]{:S(2)}) async-start(), calls=%async_computation.13 | async-start | bytes 8773632 | tf_op jit(solution)/shard_map/all_gather | solution.py:384
  10.8 178.1 %all-gather.8.cloned.1.call-start = ((), (), s32[]{:S(2)}) async-start(), calls=%async_computation.14 | async-start | bytes 5013504 | tf_op jit(solution)/shard_map/all_gather | solution.py:387
  11.5 242.6 %all-gather.10.cloned.1.call-start = ((), (), s32[]{:S(2)}) async-start(), calls=%async_computation.15 | async-start | bytes 3932160 | tf_op jit(solution)/shard_map/all_gather | solution.py:399
  32.6 260.8 %all-gather.14.cloned.1.call-start = ((), (), s32[]{:S(2)}) async-start(), calls=%async_computation.17 | async-start | bytes 3932160 | tf_op jit(solution)/shard_map/all_gather | solution.py:399
  50.4 56.6 %collective-permute-start.13 = (bf16[512,1536]{1,0:T(8,128)(2,1)S(1)}, bf16[512,1536]{1,0:T(8,128)(2,1)S(1)}, u32[]{:S(2)}, u32[]{:S(2)}) collective-permute-start(bf16[512,1536]{1,0:T(8,128)(2,1)S(1)} %bitcast.130), channel_id=1, source_target_pairs={{0,2},{1,3},{2,0},{3,1},{4,6},{5,7},{6,4},{7,5},{8,10},{9,11},{10,... | collective-permute-start | bytes 4718600 | tf_op jit(solution)/shard_map/ppermute | solution.py:35
  50.8 58.7 %collective-permute-start.6 = (bf16[512,1536]{1,0:T(8,128)(2,1)S(1)}, bf16[512,1536]{1,0:T(8,128)(2,1)}, u32[]{:S(2)}, u32[]{:S(2)}) collective-permute-start(bf16[512,1536]{1,0:T(8,128)(2,1)S(1)} %bitcast.131), channel_id=1, source_target_pairs={{0,16},{16,0},{1,17},{17,1},{2,18},{18,2},{3,19},{19,3},{4,20},{20... | collective-permute-start | bytes 4718600 | tf_op jit(solution)/shard_map/ppermute | solution.py:35
  108.0 57.8 %collective-permute-start.14 = (bf16[256,1536]{1,0:T(8,128)(2,1)}, bf16[256,1536]{1,0:T(8,128)(2,1)}, u32[]{:S(2)}, u32[]{:S(2)}) collective-permute-start(bf16[256,1536]{1,0:T(8,128)(2,1)} %slice.348), channel_id=1, source_target_pairs={{0,16},{16,0},{1,17},{17,1},{2,18},{18,2},{3,19},{19,3},{4,20},{20... | collective-permute-start | bytes 2359304 | tf_op jit(solution)/shard_map/ppermute | solution.py:35
  111.5 54.7 %collective-permute-start.15 = (bf16[256,1536]{1,0:T(8,128)(2,1)}, bf16[256,1536]{1,0:T(8,128)(2,1)}, u32[]{:S(2)}, u32[]{:S(2)}) collective-permute-start(bf16[256,1536]{1,0:T(8,128)(2,1)} %slice.349), channel_id=1, source_target_pairs={{0,2},{1,3},{2,0},{3,1},{4,6},{5,7},{6,4},{7,5},{8,10},{9,11},{10,... | collective-permute-start | bytes 2359304 | tf_op jit(solution)/shard_map/ppermute | solution.py:35
  124.6 44.4 %collective-permute-start = (bf16[512,1024]{1,0:T(8,128)(2,1)}, bf16[512,1024]{1,0:T(8,128)(2,1)}, u32[]{:S(2)}, u32[]{:S(2)}) collective-permute-start(bf16[512,1024]{1,0:T(8,128)(2,1)} %slice.342), channel_id=1, source_target_pairs={{0,16},{1,17},{2,18},{3,19},{4,20},{5,21},{6,22},{7,23},{8,24},{9,... | collective-permute-start | bytes 3145736 | tf_op jit(solution)/shard_map/ppermute | solution.py:425
  153.4 203.6 %all-gather.12.cloned.1.call-start = ((), (), s32[]{:S(2)}) async-start(), calls=%async_computation.16 | async-start | bytes 3932160 | tf_op jit(solution)/shard_map/all_gather | solution.py:399
  153.4 44.5 %collective-permute-start.2 = (bf16[512,1536]{1,0:T(8,128)(2,1)S(1)}, bf16[512,1536]{1,0:T(8,128)(2,1)}, u32[]{:S(2)}, u32[]{:S(2)}) collective-permute-start(bf16[512,1536]{1,0:T(8,128)(2,1)S(1)} %bitcast.132), channel_id=1, source_target_pairs={{0,1},{1,0},{2,3},{3,2},{4,5},{5,4},{6,7},{7,6},{8,9},{9,8},{10,11... | collective-permute-start | bytes 4718600 | tf_op jit(solution)/shard_map/ppermute | solution.py:35
  165.1 680.4 %reduce-scatter.10.cloned.1.call-start = ((), (), s32[]{:S(2)}) async-start(), calls=%async_computation.20 | async-start | bytes 3932160 | tf_op jit(solution)/shard_map/reduce_scatter | solution.py:456
  165.7 54.1 %collective-permute-start.21 = (bf16[512,1536]{1,0:T(8,128)(2,1)S(1)}, bf16[512,1536]{1,0:T(8,128)(2,1)}, u32[]{:S(2)}, u32[]{:S(2)}) collective-permute-start(bf16[512,1536]{1,0:T(8,128)(2,1)S(1)} %collective-permute-done.13), channel_id=1, source_target_pairs={{0,1},{1,0},{2,3},{3,2},{4,5},{5,4},{6,7},{7,6},{8,9},{9,8},{10,11... | collective-permute-start | bytes 4718600 | tf_op jit(solution)/shard_map/ppermute | solution.py:35
  165.8 42.9 %collective-permute-start.7 = (bf16[512,1536]{1,0:T(8,128)(2,1)}, bf16[512,1536]{1,0:T(8,128)(2,1)}, u32[]{:S(2)}, u32[]{:S(2)}) collective-permute-start(bf16[512,1536]{1,0:T(8,128)(2,1)} %collective-permute-done.6), channel_id=1, source_target_pairs={{0,1},{1,0},{2,3},{3,2},{4,5},{5,4},{6,7},{7,6},{8,9},{9,8},{10,11... | collective-permute-start | bytes 4718600 | tf_op jit(solution)/shard_map/ppermute | solution.py:35
  168.9 54.2 %collective-permute-start.16 = (bf16[512,1536]{1,0:T(8,128)(2,1)}, bf16[512,1536]{1,0:T(8,128)(2,1)}, u32[]{:S(2)}, u32[]{:S(2)}) collective-permute-start(bf16[512,1536]{1,0:T(8,128)(2,1)} %pad_maximum_fusion.12), channel_id=1, source_target_pairs={{0,1},{1,0},{2,3},{3,2},{4,5},{5,4},{6,7},{7,6},{8,9},{9,8},{10,11... | collective-permute-start | bytes 4718600 | tf_op jit(solution)/shard_map/ppermute | solution.py:35
  197.9 49.6 %collective-permute-start.4 = (bf16[512,1536]{1,0:T(8,128)(2,1)}, bf16[512,1536]{1,0:T(8,128)(2,1)}, u32[]{:S(2)}, u32[]{:S(2)}) collective-permute-start(bf16[512,1536]{1,0:T(8,128)(2,1)} %get-tuple-element.185), channel_id=1, source_target_pairs={{0,16},{16,0},{1,17},{17,1},{2,18},{18,2},{3,19},{19,3},{4,20},{20... | collective-permute-start | bytes 4718600 | tf_op jit(solution)/shard_map/ppermute | solution.py:35
  236.6 153.6 %collective-permute-start.10 = (bf16[256,1536]{1,0:T(8,128)(2,1)}, bf16[256,1536]{1,0:T(8,128)(2,1)S(1)}, u32[]{:S(2)}, u32[]{:S(2)}) collective-permute-start(bf16[256,1536]{1,0:T(8,128)(2,1)} %slice.346), channel_id=1, source_target_pairs={{0,16},{16,0},{1,17},{17,1},{2,18},{18,2},{3,19},{19,3},{4,20},{20... | collective-permute-start | bytes 2359304 | tf_op jit(solution)/shard_map/ppermute | solution.py:35
  249.6 140.7 %collective-permute-start.11 = (bf16[256,1536]{1,0:T(8,128)(2,1)}, bf16[256,1536]{1,0:T(8,128)(2,1)S(1)}, u32[]{:S(2)}, u32[]{:S(2)}) collective-permute-start(bf16[256,1536]{1,0:T(8,128)(2,1)} %slice.347), channel_id=1, source_target_pairs={{0,2},{1,3},{2,0},{3,1},{4,6},{5,7},{6,4},{7,5},{8,10},{9,11},{10,... | collective-permute-start | bytes 2359304 | tf_op jit(solution)/shard_map/ppermute | solution.py:35
  249.9 150.8 %collective-permute-start.20 = (bf16[512,1536]{1,0:T(8,128)(2,1)}, bf16[512,1536]{1,0:T(8,128)(2,1)S(1)}, u32[]{:S(2)}, u32[]{:S(2)}) collective-permute-start(bf16[512,1536]{1,0:T(8,128)(2,1)} %collective-permute-done.9), channel_id=1, source_target_pairs={{0,1},{1,0},{2,3},{3,2},{4,5},{5,4},{6,7},{7,6},{8,9},{9,8},{10,11... | collective-permute-start | bytes 4718600 | tf_op jit(solution)/shard_map/ppermute | solution.py:35
  249.9 141.6 %collective-permute-start.5 = (bf16[512,1536]{1,0:T(8,128)(2,1)}, bf16[512,1536]{1,0:T(8,128)(2,1)}, u32[]{:S(2)}, u32[]{:S(2)}) collective-permute-start(bf16[512,1536]{1,0:T(8,128)(2,1)} %collective-permute-done.4), channel_id=1, source_target_pairs={{0,1},{1,0},{2,3},{3,2},{4,5},{5,4},{6,7},{7,6},{8,9},{9,8},{10,11... | collective-permute-start | bytes 4718600 | tf_op jit(solution)/shard_map/ppermute | solution.py:35
  391.5 71.5 %collective-permute-start.12 = (bf16[512,1536]{1,0:T(8,128)(2,1)}, bf16[512,1536]{1,0:T(8,128)(2,1)}, u32[]{:S(2)}, u32[]{:S(2)}) collective-permute-start(bf16[512,1536]{1,0:T(8,128)(2,1)} %pad_maximum_fusion.11), channel_id=1, source_target_pairs={{0,1},{1,0},{2,3},{3,2},{4,5},{5,4},{6,7},{7,6},{8,9},{9,8},{10,11... | collective-permute-start | bytes 4718600 | tf_op jit(solution)/shard_map/ppermute | solution.py:35
  517.9 331.9 %reduce-scatter.12.cloned.1.call-start = ((), (), s32[]{:S(2)}) async-start(), calls=%async_computation.21 | async-start | bytes 3932160 | tf_op jit(solution)/shard_map/reduce_scatter | solution.py:456
  540.5 332.9 %reduce-scatter.14.cloned.1.call-start = ((), (), s32[]{:S(2)}) async-start(), calls=%async_computation.22 | async-start | bytes 3932160 | tf_op jit(solution)/shard_map/reduce_scatter | solution.py:456
  559.7 84.9 %collective-permute-start.25 = (bf16[512,1536]{1,0:T(8,128)(2,1)}, bf16[512,1536]{1,0:T(8,128)(2,1)S(1)}, u32[]{:S(2)}, u32[]{:S(2)}) collective-permute-start(bf16[512,1536]{1,0:T(8,128)(2,1)} %slice.316), channel_id=1, source_target_pairs={{0,1},{1,0},{2,3},{3,2},{4,5},{5,4},{6,7},{7,6},{8,9},{9,8},{10,11... | collective-permute-start | bytes 4718600 | tf_op jit(solution)/shard_map/ppermute | solution.py:35
  560.2 120.4 %collective-permute-start.3 = (bf16[512,1536]{1,0:T(8,128)(2,1)}, bf16[512,1536]{1,0:T(8,128)(2,1)}, u32[]{:S(2)}, u32[]{:S(2)}) collective-permute-start(bf16[512,1536]{1,0:T(8,128)(2,1)} %slice.298), channel_id=1, source_target_pairs={{0,1},{1,0},{2,3},{3,2},{4,5},{5,4},{6,7},{7,6},{8,9},{9,8},{10,11... | collective-permute-start | bytes 4718600 | tf_op jit(solution)/shard_map/ppermute | solution.py:35
  591.4 357.6 %reduce-scatter.8.cloned.1.call-start = ((), (), s32[]{:S(2)}) async-start(), calls=%async_computation.19 | async-start | bytes 5013504 | tf_op jit(solution)/shard_map/reduce_scatter | solution.py:486
  625.0 48.4 %collective-permute-start.32 = (bf16[512,1536]{1,0:T(8,128)(2,1)S(1)}, bf16[512,1536]{1,0:T(8,128)(2,1)S(1)}, u32[]{:S(2)}, u32[]{:S(2)}) collective-permute-start(bf16[512,1536]{1,0:T(8,128)(2,1)S(1)} %pad_maximum_fusion.16), channel_id=1, source_target_pairs={{0,2},{1,3},{2,0},{3,1},{4,6},{5,7},{6,4},{7,5},{8,10},{9,11},{10,... | collective-permute-start | bytes 4718600 | tf_op jit(solution)/shard_map/ppermute | solution.py:35
  643.6 62.7 %collective-permute-start.24 = (bf16[512,1536]{1,0:T(8,128)(2,1)S(1)}, bf16[512,1536]{1,0:T(8,128)(2,1)S(1)}, u32[]{:S(2)}, u32[]{:S(2)}) collective-permute-start(bf16[512,1536]{1,0:T(8,128)(2,1)S(1)} %pad_maximum_fusion.14), channel_id=1, source_target_pairs={{0,2},{1,3},{2,0},{3,1},{4,6},{5,7},{6,4},{7,5},{8,10},{9,11},{10,... | collective-permute-start | bytes 4718600 | tf_op jit(solution)/shard_map/ppermute | solution.py:35
  644.6 65.4 %collective-permute-start.19 = (bf16[512,1536]{1,0:T(8,128)(2,1)S(1)}, bf16[512,1536]{1,0:T(8,128)(2,1)S(1)}, u32[]{:S(2)}, u32[]{:S(2)}) collective-permute-start(bf16[512,1536]{1,0:T(8,128)(2,1)S(1)} %pad_maximum_fusion.13), channel_id=1, source_target_pairs={{0,16},{16,0},{1,17},{17,1},{2,18},{18,2},{3,19},{19,3},{4,20},{20... | collective-permute-start | bytes 4718600 | tf_op jit(solution)/shard_map/ppermute | solution.py:35
  720.6 228.9 %reduce-scatter.6.cloned.1.call-start = ((), (), s32[]{:S(2)}) async-start(), calls=%async_computation.18 | async-start | bytes 8773632 | tf_op jit(solution)/shard_map/reduce_scatter | solution.py:486
  873.4 47.0 %collective-permute-start.36 = (bf16[4,96,2,512]{3,2,0,1:T(2,128)(2,1)}, bf16[4,96,2,512]{3,2,0,1:T(2,128)(2,1)}, u32[]{:S(2)}, u32[]{:S(2)}) collective-permute-start(bf16[4,96,2,512]{3,2,0,1:T(2,128)(2,1)} %copy.84), channel_id=1, source_target_pairs={{0,16},{16,0},{1,17},{17,1},{2,18},{18,2},{3,19},{19,3},{4,20},{20... | collective-permute-start | bytes 2359304 | tf_op jit(solution)/shard_map/ppermute | solution.py:35
  908.5 42.4 %collective-permute-start.38 = (bf16[4,96,2,512]{3,2,0,1:T(2,128)(2,1)}, bf16[4,96,2,512]{3,2,0,1:T(2,128)(2,1)}, u32[]{:S(2)}, u32[]{:S(2)}) collective-permute-start(bf16[4,96,2,512]{3,2,0,1:T(2,128)(2,1)} %copy.90), channel_id=1, source_target_pairs={{0,16},{16,0},{1,17},{17,1},{2,18},{18,2},{3,19},{19,3},{4,20},{20... | collective-permute-start | bytes 2359304 | tf_op jit(solution)/shard_map/ppermute | solution.py:35
  (81 other events, 1561.3 us)
Sparse Core Ops, SparseCore 0:
  10.9 98.5 all-gather.5
  111.8 54.1 all-gather.7
  167.6 62.2 all-gather.9
  231.2 62.1 all-gather.13
  294.8 62.1 all-gather.11
  518.0 59.0 reduce-scatter.9
  579.4 60.2 reduce-scatter.11
  642.0 60.2 reduce-scatter.13
  720.8 73.3 reduce-scatter.7
  830.1 107.9 reduce-scatter.5

commit v2 on v1

v2 whole, which is shorter than its diff:
```python
import functools

import jax
import jax.numpy as jnp
from jax import lax
from jax.experimental import pallas as pl
from jax.experimental.pallas import tpu as pltpu
from jax.sharding import PartitionSpec as P

HEADS = 24
KV_HEADS = 8
HEAD_DIM = 64
EXPERTS = 16
GROUP = HEADS // KV_HEADS
EPS = 1e-06
BF = jnp.bfloat16
F32 = jnp.float32
ROWS = ("outer", "inner")
VMEM_LIMIT = 60 * 1024 * 1024


def cost(microseconds):
    return pl.CostEstimate(flops=int(microseconds * 0.6e9), bytes_accessed=1000, transcendentals=0)


def norm_rows(values, gain_vector):
    inverse = lax.rsqrt(jnp.mean(values * values, axis=-1, keepdims=True) + EPS)
    normed = values * inverse
    return (normed, inverse, (normed * gain_vector).astype(BF))


def norm_back(upstream, normed, inverse, gain_vector):
    scaled = upstream * gain_vector
    spread = jnp.mean(scaled * normed, axis=-1, keepdims=True)
    return (inverse * (scaled - normed * spread), jnp.sum(upstream * normed, axis=0))


def swap(x, axis, bit):
    return lax.ppermute(x, axis, [(i, i ^ bit) for i in range(lax.axis_size(axis))])


def core_swap(x):
    return swap(x, "inner", 1)


def side_swap(x):
    return swap(x, "inner", 2)


def seq_swap(x):
    return swap(x, "seq", 1)


def after(x, *others):
    return lax.optimization_barrier((x, others))[0]


def low_plus(a, b):
    return (a.astype(F32) + b.astype(F32)).astype(BF)


def exchange_start(pieces):
    at = lax.axis_index("inner")
    bits = range(1, lax.axis_size("inner"))
    return [swap(lax.dynamic_index_in_dim(pieces, at ^ bit, 0, keepdims=False), "inner", bit) for bit in bits]


def exchange_end(pieces, got):
    at = lax.axis_index("inner")
    for bit, piece in enumerate(got, 1):
        pieces = lax.dynamic_update_index_in_dim(pieces, piece, at ^ bit, 0)
    return pieces


def pick(x, at, axis):
    return lax.dynamic_index_in_dim(x, at, axis, keepdims=False)


class HomeSum:
    def __init__(self, *totals):
        rows, columns = totals[0].shape[0], sum(total.shape[1] for total in totals)
        self.n = lax.axis_size("outer")
        self.seq_at = lax.axis_index("seq")
        self.outer_at = lax.axis_index("outer")
        inner_at = lax.axis_index("inner")
        sides = lax.axis_size("inner") // 2
        self.side_at, core_at = inner_at // 2, inner_at % 2
        self.half = columns // 2
        self.split = False
        part = rows // (self.n * sides * 2)

        def half_of(at):
            return jnp.concatenate(
                [pick(total.reshape(self.n, sides, 2, part, total.shape[1]), at, 2) for total in totals], axis=-1
            )

        self.held = half_of(core_at)
        self.got = core_swap(half_of(1 - core_at))

    def beside(self):
        held = low_plus(self.held, self.got)
        self.got = side_swap(pick(held, 1 - self.side_at, 1))
        self.held = pick(held, self.side_at, 1)
        return held

    def across(self):
        held = low_plus(self.held, self.got)
        self.got = seq_swap(lax.dynamic_slice_in_dim(held, (1 - self.seq_at) * self.half, self.half, 2))
        self.held = lax.dynamic_slice_in_dim(held, self.seq_at * self.half, self.half, 2)
        self.split = True
        return held

    def along(self):
        held = low_plus(self.held, self.got)
        self.held = pick(held, self.outer_at, 0)
        self.got = []
        for step in range(1, self.n):
            piece = pick(held, lax.rem(self.outer_at + step, self.n), 0)
            self.got.append(lax.ppermute(piece, "outer", [(i, (i + step) % self.n) for i in range(self.n)]))
        return held

    def final(self):
        result = self.held.astype(F32)
        for got in self.got:
            result = result + got.astype(F32)
        self.low = result.astype(BF)
        self.other = seq_swap(self.low)
        return self.low

    def result(self):
        low, other = self.low.astype(F32), self.other.astype(F32)
        if not self.split:
            return low + other
        first = self.seq_at == 0
        return jnp.concatenate([jnp.where(first, low, other), jnp.where(first, other, low)], axis=1)


class Chain:
    def __init__(self, last):
        self.last = last

    def enter(self, x):
        return after(x, self.last)

    def leave(self, y):
        self.last = y
        return y


def dot_nt(a, b):
    return lax.dot_general(a, b, (((1,), (1,)), ((), ())), preferred_element_type=F32)


def dot_nn(a, b):
    return lax.dot_general(a, b, (((1,), (0,)), ((), ())), preferred_element_type=F32)


def dot_tn(a, b):
    return lax.dot_general(a, b, (((0,), (0,)), ((), ())), preferred_element_type=F32)


def project_in_kernel(token_ref, weight_ref, tail_ref, query_ref, pair_ref, low_ref, gain_ref):
    step = pl.program_id(0)
    queries = HEADS * HEAD_DIM // weight_ref.shape[1]

    @pl.when(step == 0)
    def _():
        row = lax.broadcasted_iota(jnp.int32, (8, 128), 0)
        lane = lax.broadcasted_iota(jnp.int32, (8, 128), 1)
        gain_ref[...] = dot_nt((row == lane).astype(BF), tail_ref[...])
        x = token_ref[...].astype(F32)
        inverse = lax.rsqrt(jnp.mean(x * x, axis=-1, keepdims=True) + EPS)
        low_ref[...] = (x * inverse * gain_ref[0:1, :]).astype(BF)

    result = dot_nn(low_ref[...], weight_ref[...]).astype(BF)

    @pl.when(step < queries)
    def _():
        query_ref[...] = result

    @pl.when(step >= queries)
    def _():
        pair_ref[...] = result


def project_rows(tokens, weight, qkv):
    count, width = tokens.shape
    tile = 512
    query_width = HEADS * HEAD_DIM
    queries = query_width // tile
    return pl.pallas_call(
        project_in_kernel,
        grid=(qkv // tile,),
        in_specs=[
            pl.BlockSpec((count, width), lambda j: (0, 0)),
            pl.BlockSpec((width, tile), lambda j: (0, j)),
            pl.BlockSpec((width, 128), lambda j: (0, qkv // 128)),
        ],
        out_specs=[
            pl.BlockSpec((count, tile), lambda j: (0, jnp.minimum(j, queries - 1))),
            pl.BlockSpec((count, tile), lambda j: (0, jnp.maximum(j - queries, 0))),
            pl.BlockSpec((count, width), lambda j: (0, 0)),
            pl.BlockSpec((8, width), lambda j: (0, 0)),
        ],
        out_shape=[
            jax.ShapeDtypeStruct((count, query_width), BF),
            jax.ShapeDtypeStruct((count, qkv - query_width), BF),
            jax.ShapeDtypeStruct((count, width), BF),
            jax.ShapeDtypeStruct((8, width), F32),
        ],
        compiler_params=pltpu.CompilerParams(vmem_limit_bytes=VMEM_LIMIT),
        cost_estimate=cost(0),
        name="project_rows",
    )(tokens, weight, weight)


def merge_kernel(mixed_ref, weight_ref, token_ref, gain_ref, middle_ref, low_ref):
    product = dot_nn(mixed_ref[...], weight_ref[...])
    step = pl.program_id(0)

    @pl.when(step == 0)
    def _():
        middle_ref[...] = token_ref[...].astype(F32) + product

    @pl.when(step > 0)
    def _():
        middle_ref[...] += product

    @pl.when(step == pl.num_programs(0) - 1)
    def _():
        x = middle_ref[...]
        inverse = lax.rsqrt(jnp.mean(x * x, axis=-1, keepdims=True) + EPS)
        low_ref[...] = (x * inverse * gain_ref[1:2, :]).astype(BF)


def merge_rows(mixed, weight, tokens, gains):
    count, width = tokens.shape
    tile = 512
    whole = pl.BlockSpec((count, width), lambda j: (0, 0))
    return pl.pallas_call(
        merge_kernel,
        grid=(mixed.shape[1] // tile,),
        in_specs=[
            pl.BlockSpec((count, tile), lambda j: (0, j)),
            pl.BlockSpec((tile, width), lambda j: (j, 0)),
            whole,
            pl.BlockSpec((8, width), lambda j: (0, 0)),
        ],
        out_specs=[whole, whole],
        out_shape=[jax.ShapeDtypeStruct((count, width), F32), jax.ShapeDtypeStruct((count, width), BF)],
        compiler_params=pltpu.CompilerParams(vmem_limit_bytes=VMEM_LIMIT),
        cost_estimate=cost(0),
        name="merge_rows",
    )(mixed, weight, tokens, gains)


def attend_kernel(place_ref, q_ref, k_ref, v_ref, kr_ref, vr_ref, mixed_ref, stat_ref, bias_ref, col_ref):
    count = q_ref.shape[0]
    half = count // 2
    seq_at = place_ref[0]
    live = place_ref[1]

    @pl.when(pl.program_id(0) == 0)
    def _():
        row = lax.broadcasted_iota(jnp.int32, (count, count), 0)
        col = lax.broadcasted_iota(jnp.int32, (count, count), 1)
        bias_ref[...] = jnp.where((col <= row) & (col < live), 0.0, -jnp.inf)
        col_ref[...] = jnp.zeros_like(col_ref)

    def run(with_past):
        for g in range(2):
            lanes = slice(g * HEAD_DIM, (g + 1) * HEAD_DIM)
            key = k_ref[:, lanes]
            value = v_ref[:, lanes]
            if with_past:
                key_past = kr_ref[:, lanes]
                value_past = vr_ref[:, lanes]
            for r in range(GROUP):
                h = g * GROUP + r
                for part in range(2):
                    rows = slice(part * half, (part + 1) * half)
                    span = (part + 1) * half
                    query = q_ref[rows, h * HEAD_DIM : (h + 1) * HEAD_DIM] * BF(HEAD_DIM**-0.5)
                    scores = dot_nt(query, key[:span]) + bias_ref[rows, :span]
                    peak = jnp.max(scores, axis=-1, keepdims=True)
                    if with_past:
                        past = dot_nt(query, key_past)
                        peak = jnp.maximum(peak, jnp.max(past, axis=-1, keepdims=True))
                    lifted = jnp.exp(scores - peak)
                    total = jnp.sum(lifted, axis=-1, keepdims=True)
                    mixed = dot_nn(lifted.astype(BF), value[:span])
                    if with_past:
                        lifted_past = jnp.exp(past - peak)
                        total = total + jnp.sum(lifted_past, axis=-1, keepdims=True)
                        mixed = mixed + dot_nn(lifted_past.astype(BF), value_past)
                    mixed_ref[rows, h * HEAD_DIM : (h + 1) * HEAD_DIM] = (mixed / total).astype(BF)
                    col_ref[rows, h : h + 1] = peak + jnp.log(total)

    @pl.when(seq_at == 0)
    def _():
        run(False)

    @pl.when(seq_at != 0)
    def _():
        run(True)

    stat_ref[...] = col_ref[...].T[:8, :]


def attend(place, query, pair, past):
    count = query.shape[0]
    steps = KV_HEADS // 2
    wide = 2 * GROUP * HEAD_DIM
    return pl.pallas_call(
        attend_kernel,
        grid_spec=pltpu.PrefetchScalarGridSpec(
            num_scalar_prefetch=1,
            grid=(steps,),
            in_specs=[
                pl.BlockSpec((count, wide), lambda j, place: (0, j)),
                pl.BlockSpec((count, 128), lambda j, place: (0, j)),
                pl.BlockSpec((count, 128), lambda j, place: (0, steps + j)),
                pl.BlockSpec((count, 128), lambda j, place: (0, j)),
                pl.BlockSpec((count, 128), lambda j, place: (0, steps + j)),
            ],
            out_specs=[
                pl.BlockSpec((count, wide), lambda j, place: (0, j)),
                pl.BlockSpec((None, 8, count), lambda j, place: (j, 0, 0)),
            ],
            scratch_shapes=[pltpu.VMEM((count, count), F32), pltpu.VMEM((count, 128), F32)],
        ),
        out_shape=[
            jax.ShapeDtypeStruct((count, HEADS * HEAD_DIM), BF),
            jax.ShapeDtypeStruct((steps, 8, count), F32),
        ],
        compiler_params=pltpu.CompilerParams(vmem_limit_bytes=VMEM_LIMIT),
        cost_estimate=cost(0),
        name="attend",
    )(place, query, pair, pair, past, past)


def attend_back_kernel(
    place_ref, q_ref, k_ref, v_ref, kr_ref, vr_ref, mixed_ref, grad_ref, stat_ref,
    dq_ref, dk_ref, dv_ref, dkr_ref, dvr_ref, bias_ref,
):
    count = q_ref.shape[0]
    half = count // 2
    seq_at = place_ref[0]
    live = place_ref[1]
    scale = HEAD_DIM**-0.5

    @pl.when(pl.program_id(0) == 0)
    def _():
        key_at = lax.broadcasted_iota(jnp.int32, (count, count), 0)
        query_at = lax.broadcasted_iota(jnp.int32, (count, count), 1)
        bias_ref[...] = jnp.where((key_at <= query_at) & (key_at < live), 0.0, -jnp.inf)

    def run(with_past):
        for g in range(2):
            lanes = slice(g * HEAD_DIM, (g + 1) * HEAD_DIM)
            key = k_ref[:, lanes]
            value = v_ref[:, lanes]
            sums = [[jnp.zeros((half, HEAD_DIM), F32) for _ in range(2)] for _ in range(2)]
            if with_past:
                key_past = kr_ref[:, lanes]
                value_past = vr_ref[:, lanes]
                past_sums = [jnp.zeros((count, HEAD_DIM), F32) for _ in range(2)]
            for r in range(GROUP):
                h = g * GROUP + r
                cols = slice(h * HEAD_DIM, (h + 1) * HEAD_DIM)
                query = q_ref[:, cols] * BF(scale)
                grad = grad_ref[:, cols]
                product = grad.astype(F32) * mixed_ref[:, cols].astype(F32)
                delta = lax.dot_general(
                    jnp.ones((8, HEAD_DIM), F32), product, (((1,), (1,)), ((), ())),
                    precision=lax.Precision.HIGHEST, preferred_element_type=F32,
                )[:1]
                stat = stat_ref[h : h + 1, :]

                def piece(keys, values, queries, grads, stats, deltas, bias):
                    scores = dot_nt(keys, queries)
                    if bias is not None:
                        scores = scores + bias
                    chances = jnp.exp(scores - stats)
                    chance_grad = dot_nt(values, grads)
                    score_grad = (chances * (chance_grad - deltas)).astype(BF)
                    return chances.astype(BF), score_grad

                p0, s0 = piece(key[:half], value[:half], query, grad, stat, delta, bias_ref[:half, :])
                p1, s1 = piece(
                    key[half:], value[half:], query[half:], grad[half:], stat[:, half:], delta[:, half:],
                    bias_ref[half:, half:],
                )
                dq = dot_tn(s0, key[:half])
                dq_late = dot_tn(s1, key[half:])
                sums[0][0] += dot_nn(s0, query)
                sums[0][1] += dot_nn(s1, query[half:])
                sums[1][0] += dot_nn(p0, grad)
                sums[1][1] += dot_nn(p1, grad[half:])
                if with_past:
                    pp, sp = piece(key_past, value_past, query, grad, stat, delta, None)
                    dq = dq + dot_tn(sp, key_past)
                    past_sums[0] += dot_nn(sp, query)
                    past_sums[1] += dot_nn(pp, grad)
                dq_ref[:half, cols] = (dq[:half] * scale).astype(BF)
                dq_ref[half:, cols] = ((dq[half:] + dq_late) * scale).astype(BF)
            for where, out in ((0, dk_ref), (1, dv_ref)):
                out[:half, lanes] = sums[where][0].astype(BF)
                out[half:, lanes] = sums[where][1].astype(BF)
            if with_past:
                dkr_ref[:, lanes] = past_sums[0].astype(BF)
                dvr_ref[:, lanes] = past_sums[1].astype(BF)

    @pl.when(seq_at == 0)
    def _():
        run(False)
        dkr_ref[...] = jnp.zeros_like(dkr_ref)
        dvr_ref[...] = jnp.zeros_like(dvr_ref)

    @pl.when(seq_at != 0)
    def _():
        run(True)


def attend_back(place, query, pair, past, mixed, mixed_grad, stats, first, steps, us):
    count = query.shape[0]
    pairs = KV_HEADS // 2
    wide = 2 * GROUP * HEAD_DIM
    narrow = jax.ShapeDtypeStruct((count, steps * 128), BF)
    head_spec = pl.BlockSpec((count, wide), lambda j, place: (0, first + j))
    pair_spec = pl.BlockSpec((count, 128), lambda j, place: (0, j))
    return pl.pallas_call(
        attend_back_kernel,
        grid_spec=pltpu.PrefetchScalarGridSpec(
            num_scalar_prefetch=1,
            grid=(steps,),
            in_specs=[
                head_spec,
                pl.BlockSpec((count, 128), lambda j, place: (0, first + j)),
                pl.BlockSpec((count, 128), lambda j, place: (0, pairs + first + j)),
                pl.BlockSpec((count, 128), lambda j, place: (0, first + j)),
                pl.BlockSpec((count, 128), lambda j, place: (0, pairs + first + j)),
                head_spec,
                head_spec,
                pl.BlockSpec((None, 8, count), lambda j, place: (first + j, 0, 0)),
            ],
            out_specs=[pl.BlockSpec((count, wide), lambda j, place: (0, j))] + [pair_spec] * 4,
            scratch_shapes=[pltpu.VMEM((count, count), F32)],
        ),
        out_shape=[jax.ShapeDtypeStruct((count, steps * wide), BF), narrow, narrow, narrow, narrow],
        compiler_params=pltpu.CompilerParams(vmem_limit_bytes=VMEM_LIMIT),
        cost_estimate=cost(us),
        name="attend_back",
    )(place, query, pair, pair, past, past, mixed, mixed_grad, stats)


def pack_kernel(seq_ref, gate_ref, lift_ref, down_ref, *out_refs):
    owners, _, columns = out_refs[0].shape
    ff = columns // 3
    for seq in range(2):

        @pl.when(seq_ref[0] == seq)
        def _():
            for kind, ref in enumerate((gate_ref, lift_ref, down_ref)):
                for owner in range(owners):
                    for e in range(2):
                        out_refs[e][owner, :, kind * ff : (kind + 1) * ff] = ref[:, (seq * owners + owner) * 2 + e, :]


def pack_experts(seq, gate, lift, down, owners):
    rows, experts, ff = gate.shape
    tile = 32 if rows % 32 == 0 else rows
    in_spec = pl.BlockSpec((tile, experts, ff), lambda i, seq: (i, 0, 0))
    out_spec = pl.BlockSpec((owners, tile, 3 * ff), lambda i, seq: (0, i, 0))
    out = jax.ShapeDtypeStruct((owners, rows, 3 * ff), BF)
    return pl.pallas_call(
        pack_kernel,
        grid_spec=pltpu.PrefetchScalarGridSpec(
            num_scalar_prefetch=1, grid=(rows // tile,), in_specs=[in_spec] * 3, out_specs=[out_spec] * 2
        ),
        out_shape=[out, out],
        compiler_params=pltpu.CompilerParams(vmem_limit_bytes=VMEM_LIMIT),
        cost_estimate=cost(6),
        name="pack_experts",
    )(seq, gate, lift, down)


def unpack_kernel(seq_ref, *refs):
    out_ref = refs[-1]
    owners = refs[0].shape[0]
    for seq in range(2):

        @pl.when(seq_ref[0] == seq)
        def _():
            for e in range(2):
                for at, ref in ((seq, refs[2 * e]), (1 - seq, refs[2 * e + 1])):
                    for owner in range(owners):
                        out_ref[:, (at * owners + owner) * 2 + e, :] = ref[owner].astype(F32)


def unpack_experts(seq, parts, column, ff):
    owners, rows, _ = parts[0].shape
    in_spec = pl.BlockSpec((owners, rows, ff), lambda i, seq: (0, 0, column))
    return pl.pallas_call(
        unpack_kernel,
        grid_spec=pltpu.PrefetchScalarGridSpec(
            num_scalar_prefetch=1,
            grid=(1,),
            in_specs=[in_spec] * 4,
            out_specs=pl.BlockSpec((rows, EXPERTS, ff), lambda i, seq: (0, 0, 0)),
        ),
        out_shape=jax.ShapeDtypeStruct((rows, EXPERTS, ff), F32),
        compiler_params=pltpu.CompilerParams(vmem_limit_bytes=VMEM_LIMIT),
        cost_estimate=cost(4),
        name="unpack_experts",
    )(seq, *parts)


def expert_kernel(e, has_earlier, n, place_ref, *refs):
    na_ref, nb_ref, ca_ref, cb_ref = refs[:4]
    earlier_refs = refs[4:8] if has_earlier else (None,) * 4
    begin = 8 if has_earlier else 4
    block_refs = refs[begin : begin + n]
    (ch_ref, gl_ref, outa_ref, outb_ref, backa_ref, backb_ref) = refs[-8:-2]
    wt_ref, sems = refs[-2:]
    part = block_refs[0].shape[0]
    width = na_ref.shape[1]
    ff = wt_ref.shape[1] // 3
    step_at = pl.program_id(0)
    fresh = step_at == 0
    first = step_at < 2
    mine = 2 * place_ref[0] + e
    at = place_ref[1]

    def piece(step, kind):
        slot = lax.rem(at + n - step, n) if n > 1 else 0
        rows = pl.ds(pl.multiple_of(slot * part, part), part) if n > 1 else slice(None)
        cols = slice(kind * ff, (kind + 1) * ff)
        return pltpu.make_async_copy(block_refs[step].at[:, cols], wt_ref.at[rows, cols], sems.at[kind * n + step])

    @pl.when(fresh)
    def _():
        for kind in range(3):
            for step in range(n):
                piece(step, kind).start()

    def run(n_ref, c_ref, earlier_out, earlier_back, out_ref, back_ref, is_first):
        def arrived(kind):
            if is_first:

                @pl.when(fresh)
                def _():
                    for step in range(n):
                        piece(step, kind).wait()

        packed = c_ref[:, width:].astype(F32)
        lane = lax.broadcasted_iota(jnp.int32, packed.shape, 1)
        arrived(0)
        g = dot_nn(n_ref[...], wt_ref[:, :ff])
        arrived(1)
        l = dot_nn(n_ref[...], wt_ref[:, ff : 2 * ff])
        arrived(2)
        u = dot_nn(c_ref[:, :width], wt_ref[:, 2 * ff :])
        own_lane = (lane == mine) | (lane == EXPERTS + mine)
        weight = jnp.sum(jnp.where(own_lane, packed, 0.0), axis=-1, keepdims=True)
        sig = 1.0 / (1.0 + jnp.exp(-g))
        silu = g * sig
        hidden = silu * l
        dot = jnp.sum(hidden * u, axis=-1, keepdims=True)
        dot_high = dot.astype(BF).astype(F32)
        dots = jnp.where(lane == mine, dot_high, 0.0)
        dots = jnp.where(lane == EXPERTS + mine, dot - dot_high, dots)
        grad = u * weight
        ch_ref[...] = (hidden * weight).astype(BF)
        gl_ref[:, :ff] = (grad * l * (sig + silu * (1.0 - sig))).astype(BF)
        gl_ref[:, ff:] = (grad * silu).astype(BF)
        back = dot_nt(gl_ref[...], wt_ref[:, : 2 * ff])
        out = dot_nt(ch_ref[...], wt_ref[:, 2 * ff :])
        if has_earlier:
            out = out + earlier_out[:, :width].astype(F32)
            dots = dots + earlier_out[:, width:].astype(F32)
            back = back + earlier_back[...].astype(F32)
        back_ref[...] = back.astype(BF)
        out_ref[:, :width] = out.astype(BF)
        out_ref[:, width:] = dots.astype(BF)

    @pl.when(first)
    def _():
        run(na_ref, ca_ref, earlier_refs[0], earlier_refs[2], outa_ref, backa_ref, True)

    @pl.when(jnp.logical_not(first))
    def _():
        run(nb_ref, cb_ref, earlier_refs[1], earlier_refs[3], outb_ref, backb_ref, False)


def expert_rows(place, e, rows, up, blocks, chunk, chunks, held, earlier, us):
    count, width = rows[0].shape
    ff = blocks[0].shape[1] // 3
    tile = count // 2
    more = width + 128

    def early(i, place):
        return (jnp.minimum(i, 1), 0)

    def late(i, place):
        return (jnp.maximum(i - 2, 0), 0)

    def at_rows(i, place):
        return (4 * chunk + i, 0)

    any_spec = pl.BlockSpec(memory_space=pl.ANY)
    wide_specs = [pl.BlockSpec((tile, width), early), pl.BlockSpec((tile, width), late)]
    more_specs = [pl.BlockSpec((tile, more), early), pl.BlockSpec((tile, more), late)]
    total = 2 * count * chunks
    one = jax.ShapeDtypeStruct((count, width), BF)
    one_more = jax.ShapeDtypeStruct((count, more), BF)
    held, earlier = list(held), list(earlier)
    begin = 5 + len(earlier) + len(blocks)
    return pl.pallas_call(
        functools.partial(expert_kernel, e, len(earlier) > 0, len(blocks)),
        grid_spec=pltpu.PrefetchScalarGridSpec(
            num_scalar_prefetch=1,
            grid=(4,),
            in_specs=wide_specs
            + more_specs
            + (more_specs + wide_specs if earlier else [])
            + [any_spec] * (len(blocks) + len(held)),
            out_specs=[pl.BlockSpec((tile, ff), at_rows), pl.BlockSpec((tile, 2 * ff), at_rows)]
            + more_specs
            + wide_specs,
            scratch_shapes=[pltpu.VMEM((width, 3 * ff), BF), pltpu.SemaphoreType.DMA((3 * len(blocks),))],
        ),
        out_shape=[jax.ShapeDtypeStruct((total, ff), BF), jax.ShapeDtypeStruct((total, 2 * ff), BF)]
        + [one_more] * 2
        + [one] * 2,
        input_output_aliases={begin + at: at for at in range(len(held))},
        compiler_params=pltpu.CompilerParams(vmem_limit_bytes=VMEM_LIMIT),
        cost_estimate=cost(us),
        name="expert_rows",
    )(place, *rows, *up, *earlier, *blocks, *held)


def expert_grad_kernel(*refs):
    right_ref, out_ref, sum_ref, held_ref, sems = refs[-5:]
    sources = refs[:-5]
    width = held_ref.shape[2]
    step = pl.program_id(0)

    def fetch(at):
        return pltpu.make_async_copy(sources[at].at[:, :width], held_ref.at[at % 2], sems.at[at % 2])

    @pl.when(step == 0)
    def _():
        fetch(0).start()

    for at in range(len(sources)):

        @pl.when(step == at)
        def _():
            if at + 1 < len(sources):
                fetch(at + 1).start()
            fetch(at).wait()
            product = dot_tn(held_ref[at % 2], right_ref[...])
            if at == 0:
                sum_ref[...] = product
            elif at + 1 < len(sources):
                sum_ref[...] += product
            else:
                out_ref[...] = (sum_ref[...] + product).astype(BF)


def expert_grad(lefts, right, width, us):
    count = lefts[0].shape[0]
    columns = right.shape[1]
    return pl.pallas_call(
        expert_grad_kernel,
        grid=(len(lefts),),
        in_specs=[pl.BlockSpec(memory_space=pl.ANY)] * len(lefts) + [pl.BlockSpec((count, columns), lambda i: (i, 0))],
        out_specs=pl.BlockSpec((width, columns), lambda i: (0, 0)),
        out_shape=jax.ShapeDtypeStruct((width, columns), BF),
        scratch_shapes=[
            pltpu.VMEM((width, columns), F32),
            pltpu.VMEM((2, count, width), BF),
            pltpu.SemaphoreType.DMA((2,)),
        ],
        compiler_params=pltpu.CompilerParams(vmem_limit_bytes=VMEM_LIMIT),
        cost_estimate=cost(us),
        name="expert_grad",
    )(*lefts, right)


def body(
    tokens,
    lengths,
    routes,
    route_gates,
    cotangent,
    norm_first,
    attention_in,
    attention_out,
    norm_second,
    expert_gate,
    expert_lift,
    expert_down,
):
    count = tokens.shape[1]
    width = tokens.shape[2]
    choose = routes.shape[2]
    seq_count = lax.axis_size("seq")
    inner_count = lax.axis_size("inner")
    owners = seq_count * inner_count
    per_owner = EXPERTS // owners
    ff = expert_gate.shape[2]
    query_width = HEADS * HEAD_DIM
    seq_at = lax.axis_index("seq")
    layer_at = seq_at * inner_count + lax.axis_index("inner")
    length = lengths[0]
    place = jnp.stack([seq_at.astype(jnp.int32), length - seq_at.astype(jnp.int32) * count])
    live_rows = seq_at * count + jnp.arange(count, dtype=jnp.int32) < length
    inputs = tokens[0].astype(F32)
    upstream_low = cotangent[0]
    upstream = upstream_low.astype(F32)

    outer_count = lax.axis_size("outer")
    outer_at = lax.axis_index("outer")
    shard = width // (outer_count * inner_count)
    qkv = attention_in.shape[1]
    gains = jnp.concatenate([norm_first[:, None], norm_second[:, None], jnp.zeros((shard, 126), BF)], axis=1)
    project_in = lax.all_gather(jnp.concatenate([attention_in, gains], axis=1), ROWS, axis=0, tiled=True)
    project_out = lax.all_gather(attention_out, ROWS, axis=0, tiled=True)

    seq_place = seq_at.astype(jnp.int32)[None]
    expert_place = jnp.stack([layer_at.astype(jnp.int32), outer_at.astype(jnp.int32)])
    packed = pack_experts(seq_place, expert_gate, expert_lift, expert_down, inner_count)
    got = [exchange_start(part) for part in packed]
    packed = [exchange_end(*pair).reshape(inner_count * shard, 3 * ff) for pair in zip(packed, got)]
    if outer_count == 4:
        blocks_a = [packed[0]] + [
            lax.ppermute(packed[0], "outer", [(i, (i + step) % outer_count) for i in range(outer_count)])
            for step in range(1, outer_count)
        ]
    else:
        blocks_a = [lax.all_gather(packed[0], "outer", axis=0, tiled=True)]
    blocks = (blocks_a, [lax.all_gather(after(packed[1], project_out[:8, :128]), "outer", axis=0, tiled=True)])

    chosen = (
        routes[0][:, :, None] == jnp.arange(EXPERTS, dtype=jnp.int32)[None, None, :]
    ) & live_rows[:, None, None]
    combine = jnp.sum(jnp.where(chosen, route_gates[0][:, :, None], 0.0), axis=1)
    combine_high = combine.astype(BF)
    combine_low = (combine - combine_high.astype(F32)).astype(BF)
    up_block = jnp.concatenate(
        [upstream_low, combine_high, combine_low, jnp.zeros((count, 128 - 2 * EXPERTS), BF)], axis=1
    )
    half = count // 2
    up_block = after(up_block, packed)
    up_across, up_beside, up_sibling = seq_swap(up_block), side_swap(up_block), core_swap(up_block)

    query, pair, lowered_one, gains = project_rows(tokens[0], project_in, qkv)
    past = lax.ppermute(pair, "seq", [(0, 1)])
    past, up_across, up_beside = lax.optimization_barrier((past, up_across, up_beside))
    up_far_top, up_far_low = seq_swap(up_beside[:half]), side_swap(up_across[half:])
    mixed, stats = attend(place, query, pair, past)
    mixed, up_far_top, up_far_low = lax.optimization_barrier((mixed, up_far_top, up_far_low))
    up_pair_across = (up_across, core_swap(up_across))
    up_pair_beside = (up_beside, core_swap(up_beside))
    middle, lowered_two = merge_rows(mixed, project_out, tokens[0], gains)

    across, beside, sibling = seq_swap(lowered_two), side_swap(lowered_two), core_swap(lowered_two)

    def experts(e, at, rows, up, held, earlier=(), us=1):
        return expert_rows(expert_place, e, rows, up, blocks[e], at, 4, held, earlier, us)

    def upper(block, more):
        return jnp.concatenate([low_plus(block[:half], more), block[half:]])

    def lower(block, more):
        return jnp.concatenate([block[:half], low_plus(block[half:], more)])

    row_own, up_own = (lowered_two, sibling), (up_block, up_sibling)
    made_own = experts(0, 0, row_own, up_own, ())
    across, beside, held = lax.optimization_barrier((across, beside, made_own[:2]))
    far_top, far_low = seq_swap(beside[:half]), side_swap(across[half:])
    row_across = (across, core_swap(across))
    row_beside = (beside, core_swap(beside))
    made_across = experts(0, 1, row_across, up_pair_across, held)
    up_far = jnp.concatenate([up_far_top, up_far_low], axis=0)
    up_pair_far = (up_far, core_swap(up_far))
    made_beside = experts(0, 2, row_beside, up_pair_beside, made_across[:2])
    far_top, far_low, held = lax.optimization_barrier((far_top, far_low, made_beside[:2]))
    far = jnp.concatenate([far_top, far_low], axis=0)
    row_far = (far, core_swap(far))
    made_far = experts(0, 3, row_far, up_pair_far, held)
    hidden_a, grads_a = made_far[:2]

    row_all = (*row_own, *row_across, *row_beside, *row_far)
    up_all = (*up_own, *up_pair_across, *up_pair_beside, *up_pair_far)

    def home(total):
        return lax.psum_scatter(total, "outer", scatter_dimension=0, tiled=True)

    def slots(*locals_):
        local = jnp.concatenate(locals_, axis=1) if len(locals_) > 1 else locals_[0]
        return local.reshape(inner_count, shard, local.shape[1])

    total_a = expert_grad(row_all, grads_a, width, 1)
    home_a = home(total_a)
    hidden_a = after(hidden_a, total_a)
    down_a = expert_grad(up_all, hidden_a, width, 1)
    home_down_a = home(down_a)
    far_parts = after(made_far[2:], down_a)

    made_far = experts(1, 3, row_far, up_pair_far, (), far_parts)
    far_got, far_out_got = core_swap(made_far[5]), core_swap(made_far[3])
    made_across = experts(1, 1, row_across, up_pair_across, made_far[:2], made_across[2:])
    across_got, across_out_got = core_swap(made_across[5]), core_swap(made_across[3])
    far_got, held = lax.optimization_barrier((far_got, made_across[:2]))
    far_sum, held = lax.optimization_barrier((low_plus(made_far[4], far_got), held))
    back_low, back_top = side_swap(far_sum[half:]), seq_swap(far_sum[:half])
    made_beside = experts(1, 2, row_beside, up_pair_beside, held, made_beside[2:], 15)
    beside_got, beside_out_got = core_swap(made_beside[5]), core_swap(made_beside[3])
    across_got, back_low, back_top, held = lax.optimization_barrier(
        (across_got, back_low, back_top, made_beside[:2])
    )
    across_sum, held = lax.optimization_barrier((lower(low_plus(made_across[4], across_got), back_low), held))
    across_in = seq_swap(across_sum)
    made_own = experts(1, 0, row_own, up_own, held, made_own[2:], 15)
    hidden_b, grads_b = made_own[:2]
    own_got, own_out_got = core_swap(made_own[5]), core_swap(made_own[3])
    beside_got, far_out_got, grads_b = lax.optimization_barrier((beside_got, far_out_got, grads_b))
    beside_sum, grads_b = lax.optimization_barrier((upper(low_plus(made_beside[4], beside_got), back_top), grads_b))
    beside_in = side_swap(beside_sum)
    far_out = low_plus(made_far[2], far_out_got)
    out_low, out_top = side_swap(far_out[half:]), seq_swap(far_out[:half])

    total_b = expert_grad(row_all, grads_b, width, 1)
    home_b = home(total_b)
    across_in, hidden_b = lax.optimization_barrier((across_in, after(hidden_b, total_b)))
    down_b = expert_grad(up_all, hidden_b, width, 1)
    home_down_b = home(down_b)
    beside_in, own_got, out_top, out_low, across_out_got, beside_out_got, own_out_got, _ = lax.optimization_barrier(
        (beside_in, own_got, out_top, out_low, across_out_got, beside_out_got, own_out_got, down_b)
    )
    out_across = lower(low_plus(made_across[2], across_out_got), out_low)
    out_beside = upper(low_plus(made_beside[2], beside_out_got), out_top)
    normed_grad_two = (
        made_own[4].astype(F32) + own_got.astype(F32) + across_in.astype(F32) + beside_in.astype(F32)
    )

    normed_two, inverse_two, _ = norm_rows(middle, gains[1])
    middle_norm_grad, second_gain_grad = norm_back(normed_grad_two, normed_two, inverse_two, gains[1])
    middle_grad = upstream + middle_norm_grad
    branch_grad = middle_grad.astype(BF)
    mixed_grad = dot_nt(branch_grad, project_out).astype(BF)
    out_across, out_beside, mixed_grad = lax.optimization_barrier((out_across, out_beside, mixed_grad))
    out_across_in, out_beside_in = seq_swap(out_across), side_swap(out_beside)
    chain = Chain(mixed_grad)
    pairs = KV_HEADS // 2
    first_pairs = pairs // 2

    def back(first, steps):
        return attend_back(chain.enter(place), query, pair, past, mixed, mixed_grad, stats, first, steps, 24)

    query_a, key_a, value_a, key_past_a, value_past_a = chain.leave(back(0, first_pairs))
    late_a = lax.ppermute(jnp.concatenate([key_past_a, value_past_a], axis=1), "seq", [(1, 0)])
    out_weight_grad = chain.leave(dot_tn(chain.enter(mixed), branch_grad).astype(BF))
    out_across_in, out_beside_in = chain.enter((out_across_in, out_beside_in))
    combined = (
        made_own[2].astype(F32) + own_out_got.astype(F32) + out_across_in.astype(F32) + out_beside_in.astype(F32)
    )
    block_output = chain.leave((middle + combined[:, :width]).astype(BF))[None]
    dots = combined[:, width : width + EXPERTS] + combined[:, width + EXPERTS : width + 2 * EXPERTS]
    query_weight_a = chain.leave(dot_tn(chain.enter(lowered_one), query_a).astype(BF))
    early_home = HomeSum(out_weight_grad, query_weight_a)
    grad_gates = chain.leave(jnp.sum(jnp.where(chosen, chain.enter(dots)[:, None, :], 0.0), axis=-1))[None]
    early_home.got = chain.enter(early_home.got)
    late_a = chain.enter(late_a)
    chain.leave((early_home.beside(), late_a))
    a_slots = slots(chain.enter(home_a), chain.enter(home_down_a))
    a_got = exchange_start(a_slots)
    query_b, key_b, value_b, key_past_b, value_past_b = chain.leave(back(first_pairs, pairs - first_pairs))
    late_b = lax.ppermute(jnp.concatenate([key_past_b, value_past_b], axis=1), "seq", [(1, 0)])
    query_weight_b = chain.leave(dot_tn(chain.enter(lowered_one), query_b).astype(BF))
    a_mine = chain.leave(exchange_end(a_slots, chain.enter(a_got)))
    late_b = chain.enter(late_b)
    split_a, split_b = key_past_a.shape[1], key_past_b.shape[1]
    pair_own = jnp.concatenate([key_a, key_b, value_a, value_b], axis=1)
    pair_late = jnp.concatenate(
        [late_a[:, :split_a], late_b[:, :split_b], late_a[:, split_a:], late_b[:, split_b:]], axis=1
    )
    pair_grad = low_plus(pair_own, pair_late)
    pair_weight = chain.leave(dot_tn(lowered_one, pair_grad).astype(BF))
    final_total = chain.leave(jnp.concatenate([query_weight_b, pair_weight], axis=1))
    final_part = lax.psum_scatter(final_total, ROWS, scatter_dimension=0, tiled=True)
    early_home.got = chain.enter(early_home.got)
    chain.leave(early_home.across())
    projected_grad = jnp.concatenate([query_a, query_b, pair_grad], axis=1)
    normed_grad_one = chain.leave(dot_nt(chain.enter(projected_grad), project_in[:, :qkv]))
    normed_one, inverse_one, _ = norm_rows(inputs, gains[0])
    input_norm_grad, first_gain_grad = norm_back(chain.enter(normed_grad_one), normed_one, inverse_one, gains[0])
    grad_tokens = chain.leave(middle_grad + input_norm_grad)[None]
    gain_grads = jnp.stack([first_gain_grad, second_gain_grad])
    gain_grads = gain_grads + seq_swap(gain_grads)
    b_slots = slots(chain.enter(home_b), chain.enter(home_down_b))
    b_got = exchange_start(b_slots)
    gain_grads = chain.enter(gain_grads)
    gain_grads = chain.leave(gain_grads + core_swap(gain_grads))
    early_home.got = chain.enter(early_home.got)
    chain.leave(early_home.along())
    b_mine = chain.leave(exchange_end(b_slots, chain.enter(b_got)))
    a_other, b_other = seq_swap(a_mine), seq_swap(b_mine)

    gain_grads = chain.leave(gain_grads + side_swap(gain_grads))
    gain_grads = gain_grads.reshape(2, outer_count, inner_count * shard)
    gain_sum = pick(gain_grads, outer_at, 1)
    for step in range(1, outer_count):
        piece = pick(gain_grads, lax.rem(outer_at + step, outer_count), 1)
        gain_sum = gain_sum + lax.ppermute(
            piece, "outer", [(i, (i + step) % outer_count) for i in range(outer_count)]
        )
    gain_sum = pick(gain_sum.reshape(2, inner_count, shard), lax.axis_index("inner"), 1)
    early_home.got = chain.enter(early_home.got)
    chain.leave(early_home.final())
    early_home.other = chain.enter(early_home.other)
    early = early_home.result()
    grad_out = chain.leave(early[:, : mixed.shape[1]])
    parts = chain.enter((a_mine, a_other, b_mine, b_other))
    grad_gate, grad_lift, grad_down = [unpack_experts(seq_place, parts, kind, ff) for kind in range(3)]
    final_part = after(final_part, grad_gate, grad_lift, grad_down)
    final_sum = final_part.astype(F32) + seq_swap(final_part).astype(F32)
    grad_in = jnp.concatenate([early[:, mixed.shape[1] :], final_sum], axis=1)
    return (
        block_output,
        grad_tokens,
        grad_gates,
        gain_sum[0],
        grad_in,
        grad_out,
        gain_sum[1],
        grad_gate,
        grad_lift,
        grad_down,
    )


def solution(mesh):
    seq_count, fsdp_count = mesh.devices.shape
    inner_count = EXPERTS // (2 * seq_count)
    fine = jax.sharding.Mesh(
        mesh.devices.reshape(seq_count, fsdp_count // inner_count, inner_count), ("seq", "outer", "inner")
    )
    return jax.shard_map(
        body,
        mesh=fine,
        in_specs=(
            P(ROWS, "seq", None),
            P(ROWS),
            P(ROWS, "seq", None),
            P(ROWS, "seq", None),
            P(ROWS, "seq", None),
            P(ROWS),
            P(ROWS, None),
            P(ROWS, None),
            P(ROWS),
            P(ROWS, None, None),
            P(ROWS, None, None),
            P(ROWS, None, None),
        ),
        out_specs=(
            P(ROWS, "seq", None),
            P(ROWS, "seq", None),
            P(ROWS, "seq", None),
            P(ROWS),
            P(ROWS, None),
            P(ROWS, None),
            P(ROWS),
            P(ROWS, None, None),
            P(ROWS, None, None),
            P(ROWS, None, None),
        ),
        check_vma=False,
    )
```

time: 990 us -> 850 us (0.86)
  Pallas kernels: 159 us -> 309 us
  matrix products: 102 us -> 20.4 us
  local copies, waits for them, and re-layouts: 135 us -> 54.6 us
  waiting for transfers between devices: 371 us -> 306 us
  blocking collectives: 42 us -> 0 us
  other arithmetic: 85.9 us -> 63.5 us
    pallas_call x4 -> x18, Pallas kernels: 112 us -> 259 us  [the longest x8 153 us: expert_rows(): pl.pallas_call(functools.partial(expert_kernel, e, len(earlier) > 0, len(...]
    all_gather x3 -> x1, waiting for transfers between devices: 103 us -> 0.02 us  [body(): lax.all_gather(after(packed[1], project_out[:8, :128]), 'outer', axis=0,...]
    dot_general x5 -> x0, matrix products: 75.3 us -> none  [the longest x3 61.2 us: give_back(): lax.dot_general(left, right, (((0,), (0,)), ((), ())), preferred_element_...]
    all_to_all x5 -> x0, waiting for transfers between devices: 53.1 us -> none  [the longest x3 30.6 us: give_back(): lax.all_to_all(local, 'inner', split_axis=0, concat_axis=0, tiled=True)]
    all_gather x1, waiting for transfers between devices: 0.02 us -> 52.2 us  [body(): project_out = lax.all_gather(attention_out, ROWS, axis=0, tiled=True)]
    all_to_all x3 -> x0, blocking collectives: 42 us -> none  [the longest x2 34.9 us: fetch(): lax.all_to_all(mine, 'inner', split_axis=0, concat_axis=0, tiled=True)]
    all_gather x1, waiting for transfers between devices: 0.01 us -> 36.2 us  [body(): lax.all_gather(jnp.concatenate([attention_in, gains], axis=1), ROWS, axis...]
    ppermute x2 -> x12, waiting for transfers between devices: 40.3 us -> 63.5 us  [the longest x3 20.5 us: along(): lax.ppermute(piece, 'outer', [(i, (i + step) % self.n) for i in range(sel...]
  transfers between devices with their start and end apart: 54 -> 74, of which waited for: 17 -> 25; matrix products, arithmetic and copies ran while one was open for 28% -> 15% of each run, Pallas kernels for 13% -> 37%
where the time goes in v2:
time: 850 us; the launch traced here: 843 us
  Pallas kernels  309 us (36%)
  waiting for transfers between devices  306 us (36%)
  starting transfers between devices  72.8 us (9%)
  other arithmetic  63.5 us (7%)
  local copies, waits for them, and re-layouts  54.6 us (6%)
  matrix products  20.4 us (2%)
  between operations  16.4 us (2%)
    ppermute x54, waiting for transfers between devices, swap(): lax.ppermute(x, axis, [(i, i ^ bit) for i in range(lax.axis_size(axis))])  154 us
    pallas_call x8, Pallas kernels, expert_rows(): pl.pallas_call(functools.partial(expert_kernel, e, len(earlier) > 0, len(...  153 us
    pallas_call x4, Pallas kernels, expert_grad(): pl.pallas_call(expert_grad_kernel, grid=(len(lefts),), in_specs=[pl.Block...  67.9 us
    ppermute x54, starting transfers between devices, swap(): lax.ppermute(x, axis, [(i, i ^ bit) for i in range(lax.axis_size(axis))])  54.4 us
    all_gather x1, waiting for transfers between devices, body(): project_out = lax.all_gather(attention_out, ROWS, axis=0, tiled=True)  52.2 us
    all_gather x1, waiting for transfers between devices, body(): lax.all_gather(jnp.concatenate([attention_in, gains], axis=1), ROWS, axis...  36.2 us
    pallas_call x2, Pallas kernels, attend_back(): pl.pallas_call(attend_back_kernel, grid_spec=pltpu.PrefetchScalarGridSpec...  30.2 us
    convert_element_type x13, other arithmetic, low_plus(): return (a.astype(F32) + b.astype(F32)).astype(BF)  24.1 us
  transfers between devices with their start and end apart: 74, of which 25 were waited for; matrix products, arithmetic and copies ran while one was open for 15% of the time, Pallas kernels for 37%

profile of v2, /device:TPU:0, one launch (start us, length us, event | category | flops | bytes accessed | tf_op | source)
XLA Modules:
  0.0 842.9 jit_solution(2188024554943408353)
XLA Ops:
  33.0 10.6 %collective-permute-done.5 = bf16[96,1536]{1,0:T(8,128)(2,1)S(1)} collective-permute-done((bf16[96,1536]{1,0:T(8,128)(2,1)S(1)}, bf16[96,1536]{1,0:T(8,128)(2,1)S(1)}, u32[]{:S(2)}, u32[]{:S(2)}) %collective-permute-start.5) | collective-permute-done | bytes 294944 | tf_op jit(solution)/shard_map/ppermute | solution.py:39
  43.7 19.9 %collective-permute-done.2 = bf16[96,1536]{1,0:T(8,128)(2,1)S(1)} collective-permute-done((bf16[96,1536]{1,0:T(8,128)(2,1)S(1)}, bf16[96,1536]{1,0:T(8,128)(2,1)S(1)}, u32[]{:S(2)}, u32[]{:S(2)}) %collective-permute-start.2) | collective-permute-done | bytes 294944 | tf_op jit(solution)/shard_map/ppermute | solution.py:39
  68.8 36.2 %all-gather.4.cloned.1.call-done.weight_ref.tail_ref = bf16[1536,2688]{1,0:T(8,128)(2,1)} async-done(((bf16[96,2688]{1,0:T(8,128)(2,1)}), bf16[1536,2688]{1,0:T(8,128)(2,1)}) %all-gather.4.cloned.1.call-update) | async-done | bytes 8257552 | tf_op jit(solution)/shard_map/all_gather | solution.py:729
  105.1 10.6 %project_rows.1 = (bf16[512,1536]{1,0:T(8,128)(2,1)}, bf16[512,1024]{1,0:T(8,128)(2,1)}, bf16[512,1536]{1,0:T(8,128)(2,1)}, f32[8,1536]{1,0:T(8,128)}) custom-call(bf16[512,1536]{1,0:T(8,128)(2,1)} %bitcast.126, bf16[1536,2688]{1,0:T(8,128)(2,1)} %all-gather.4.cloned.1.call-done.weight_ref.tail_ref, ...), custom_call_target="tpu_custom_call" | custom-call | bytes 1000 | tf_op jit(solution)/shard_map/project_rows/pallas_call | solution.py:191
  122.3 20.0 %collective-permute-done.kr_ref.vr_ref = bf16[512,1024]{1,0:T(8,128)(2,1)} collective-permute-done((bf16[512,1024]{1,0:T(8,128)(2,1)}, bf16[512,1024]{1,0:T(8,128)(2,1)}, u32[]{:S(2)}, u32[]{:S(2)}) %collective-permute-start) | collective-permute-done | bytes 1048608 | tf_op jit(solution)/shard_map/ppermute | solution.py:760
  147.8 15.0 %collective-permute-done.10 = bf16[256,1664]{1,0:T(8,128)(2,1)} collective-permute-done((bf16[256,1664]{1,0:T(8,128)(2,1)S(1)}, bf16[256,1664]{1,0:T(8,128)(2,1)}, u32[]{:S(2)}, u32[]{:S(2)}) %collective-permute-start.10) | collective-permute-done | bytes 852000 | tf_op jit(solution)/shard_map/ppermute | solution.py:39
  163.4 19.6 %attend.1 = (bf16[512,1536]{1,0:T(8,128)(2,1)}, f32[4,8,512]{2,1,0:T(8,128)}) custom-call(s32[2]{0:T(128)} %pad_add_fusion.place_ref, bf16[512,1536]{1,0:T(8,128)(2,1)} %get-tuple-element.164.q_ref, bf16[512,1024]{1,0:T(8,128)(2,1)} %get-tuple-element.165.k_ref.v_ref, bf16[512,1024]{1,0:T(8,128)(2,1)} %get-tuple-element.165.k_ref.v_ref, ...), custom_call_target="tpu_custom_call" | custom-call | bytes 1000 | tf_op jit(solution)/shard_map/attend/pallas_call | solution.py:314
  183.0 52.2 %all-gather.6.cloned.1.call-done.weight_ref = bf16[1536,1536]{1,0:T(8,128)(2,1)} async-done(((bf16[96,1536]{1,0:T(8,128)(2,1)}), bf16[1536,1536]{1,0:T(8,128)(2,1)}) %all-gather.6.cloned.1.call-update) | async-done | bytes 4718608 | tf_op jit(solution)/shard_map/all_gather | solution.py:730
  235.2 8.8 %merge_rows.1 = (f32[512,1536]{1,0:T(8,128)}, bf16[512,1536]{1,0:T(8,128)(2,1)}) custom-call(bf16[512,1536]{1,0:T(8,128)(2,1)} %get-tuple-element.279.mixed_ref, bf16[1536,1536]{1,0:T(8,128)(2,1)} %all-gather.6.cloned.1.call-done.weight_ref, bf16[512,1536]{1,0:T(8,128)(2,1)} %bitcast.127, f32[8,1536]{1,0:T(8,128)} %get-tuple-element.174.gain_ref), custom_call_target="tpu_custom_call" | custom-call | bytes 1000 | tf_op jit(solution)/shard_map/merge_rows/pallas_call | solution.py:240
  254.6 19.0 %expert_rows.8 = (bf16[4096,512]{1,0:T(8,128)(2,1)}, bf16[4096,1024]{1,0:T(8,128)(2,1)}, bf16[512,1664]{1,0:T(8,128)(2,1)}, bf16[512,1664]{1,0:T(8,128)(2,1)}, b...) custom-call(s32[2]{0:T(128)} %pad_add_fusion.1.place_ref, bf16[512,1536]{1,0:T(8,128)(2,1)} %get-tuple-element.176.refs_0_, ...), custom_call_target="tpu_custom_call" | custom-call | flops 600000000 | bytes 1000 | tf_op jit(solution)/shard_map/expert_rows/pallas_call | solution.py:619
  281.2 8.7 %collective-permute-done.16.refs_0_.refs_2_ = bf16[512,1536]{1,0:T(8,128)(2,1)S(1)} collective-permute-done((bf16[512,1536]{1,0:T(8,128)(2,1)}, bf16[512,1536]{1,0:T(8,128)(2,1)S(1)}, u32[]{:S(2)}, u32[]{:S(2)}) %collective-permute-start.16) | collective-permute-done | bytes 1572896 | tf_op jit(solution)/shard_map/ppermute | solution.py:39
  297.9 18.6 %expert_rows.9 = (bf16[4096,512]{1,0:T(8,128)(2,1)}, bf16[4096,1024]{1,0:T(8,128)(2,1)}, bf16[512,1664]{1,0:T(8,128)(2,1)}, bf16[512,1664]{1,0:T(8,128)(2,1)}, b...) custom-call(s32[2]{0:T(128)} %pad_add_fusion.1.place_ref, ...), custom_call_target="tpu_custom_call", output_to_operand_aliasing={{0}: (9, {}), {1}: (10, {})} | custom-call | flops 600000000 | bytes 1000 | tf_op jit(solution)/shard_map/expert_rows/pallas_call | solution.py:619
  316.5 18.8 %expert_rows.10 = (bf16[4096,512]{1,0:T(8,128)(2,1)}, bf16[4096,1024]{1,0:T(8,128)(2,1)}, bf16[512,1664]{1,0:T(8,128)(2,1)}, bf16[512,1664]{1,0:T(8,128)(2,1)}, ...) custom-call(s32[2]{0:T(128)} %pad_add_fusion.1.place_ref, ...), custom_call_target="tpu_custom_call", output_to_operand_aliasing={{0}: (9, {}), {1}: (10, {})} | custom-call | flops 600000000 | bytes 1000 | tf_op jit(solution)/shard_map/expert_rows/pallas_call | solution.py:619
  341.5 18.7 %expert_rows.11 = (bf16[4096,512]{1,0:T(8,128)(2,1)}, bf16[4096,1024]{1,0:T(8,128)(2,1)}, bf16[512,1664]{1,0:T(8,128)(2,1)}, bf16[512,1664]{1,0:T(8,128)(2,1)}, ...) custom-call(s32[2]{0:T(128)} %pad_add_fusion.1.place_ref, ...), custom_call_target="tpu_custom_call", output_to_operand_aliasing={{0}: (9, {}), {1}: (10, {})} | custom-call | flops 600000000 | bytes 1000 | tf_op jit(solution)/shard_map/expert_rows/pallas_call | solution.py:619
  360.2 19.6 %expert_grad.4 = bf16[1536,1024]{1,0:T(8,128)(2,1)} custom-call(bf16[512,1536]{1,0:T(8,128)(2,1)} %get-tuple-element.176.refs_0_, bf16[512,1536]{1,0:T(8,128)(2,1)} %collective-permute-done.11.refs_1_, bf16[512,1536]{1,0:T(8,128)(2,1)} %copy-done.4, bf16[512,1536]{1,0:T(8,128)(2,1)} %copy-done.6, bf16[512,1536]{1,0:T(8,128)(2,1)} %collective-permute-done.17.refs_0_.refs_4_, ...), custom_call_target="tpu_custom_call" | custom-call | flops 600000000 | bytes 1000 | tf_op jit(solution)/shard_map/expert_grad/pallas_call | solution.py:675
  379.8 14.3 %expert_grad.5 = bf16[1536,512]{1,0:T(8,128)(2,1)} custom-call(bf16[512,1664]{1,0:T(8,128)(2,1)} %concatenate.61.refs_2_.refs_0_, bf16[512,1664]{1,0:T(8,128)(2,1)} %collective-permute-done.12.refs_3_.refs_1_, bf16[512,1664]{1,0:T(8,128)(2,1)} %copy-done.3, bf16[512,1664]{1,0:T(8,128)(2,1)} %collective-permute-done.19.refs_3_, bf16[512,1664]{1,0:T(8,128)(2,1)} %copy-done.7, ...), custom_call_target="tpu_custom_call" | custom-call | flops 600000000 | bytes 1000 | tf_op jit(solution)/shard_map/expert_grad/pallas_call | solution.py:675
  394.2 19.7 %expert_rows.12 = (bf16[4096,512]{1,0:T(8,128)(2,1)}, bf16[4096,1024]{1,0:T(8,128)(2,1)}, bf16[512,1664]{1,0:T(8,128)(2,1)}, bf16[512,1664]{1,0:T(8,128)(2,1)}, ...) custom-call(s32[2]{0:T(128)} %pad_add_fusion.1.place_ref, bf16[512,1536]{1,0:T(8,128)(2,1)} %copy-done.5, ...), custom_call_target="tpu_custom_call" | custom-call | flops 600000000 | bytes 1000 | tf_op jit(solution)/shard_map/expert_rows/pallas_call | solution.py:619
  414.4 19.6 %expert_rows.13 = (bf16[4096,512]{1,0:T(8,128)(2,1)}, bf16[4096,1024]{1,0:T(8,128)(2,1)}, bf16[512,1664]{1,0:T(8,128)(2,1)}, bf16[512,1664]{1,0:T(8,128)(2,1)}, ...) custom-call(s32[2]{0:T(128)} %pad_add_fusion.1.place_ref, ...), custom_call_target="tpu_custom_call", output_to_operand_aliasing={{0}: (10, {}), {1}: (11, {})} | custom-call | flops 600000000 | bytes 1000 | tf_op jit(solution)/shard_map/expert_rows/pallas_call | solution.py:619
  442.2 19.4 %expert_rows.14 = (bf16[4096,512]{1,0:T(8,128)(2,1)}, bf16[4096,1024]{1,0:T(8,128)(2,1)}, bf16[512,1664]{1,0:T(8,128)(2,1)}, bf16[512,1664]{1,0:T(8,128)(2,1)}, ...) custom-call(s32[2]{0:T(128)} %pad_add_fusion.1.place_ref, ...), custom_call_target="tpu_custom_call", output_to_operand_aliasing={{0}: (10, {}), {1}: (11, {})} | custom-call | flops 8999999488 | bytes 1000 | tf_op jit(solution)/shard_map/expert_rows/pallas_call | solution.py:619
  467.2 19.4 %expert_rows.15 = (bf16[4096,512]{1,0:T(8,128)(2,1)}, bf16[4096,1024]{1,0:T(8,128)(2,1)}, bf16[512,1664]{1,0:T(8,128)(2,1)}, bf16[512,1664]{1,0:T(8,128)(2,1)}, ...) custom-call(s32[2]{0:T(128)} %pad_add_fusion.1.place_ref, ...), custom_call_target="tpu_custom_call", output_to_operand_aliasing={{0}: (10, {}), {1}: (11, {})} | custom-call | flops 8999999488 | bytes 1000 | tf_op jit(solution)/shard_map/expert_rows/pallas_call | solution.py:619
  496.1 27.7 %collective-permute-done.39 = bf16[512,1536]{1,0:T(8,128)(2,1)} collective-permute-done((bf16[512,1536]{1,0:T(8,128)(2,1)}, bf16[512,1536]{1,0:T(8,128)(2,1)}, u32[]{:S(2)}, u32[]{:S(2)}) %collective-permute-start.39) | collective-permute-done | bytes 1572896 | tf_op jit(solution)/shard_map/ppermute | solution.py:39
  525.2 19.8 %expert_grad.6 = bf16[1536,1024]{1,0:T(8,128)(2,1)} custom-call(bf16[512,1536]{1,0:T(8,128)(2,1)} %get-tuple-element.176.refs_0_, bf16[512,1536]{1,0:T(8,128)(2,1)} %collective-permute-done.11.refs_1_, bf16[512,1536]{1,0:T(8,128)(2,1)} %copy-done.4, bf16[512,1536]{1,0:T(8,128)(2,1)} %copy-done.6, bf16[512,1536]{1,0:T(8,128)(2,1)} %collective-permute-done.17.refs_0_.refs_4_, ...), custom_call_target="tpu_custom_call" | custom-call | flops 600000000 | bytes 1000 | tf_op jit(solution)/shard_map/expert_grad/pallas_call | solution.py:675
  545.1 14.1 %expert_grad.7 = bf16[1536,512]{1,0:T(8,128)(2,1)} custom-call(bf16[512,1664]{1,0:T(8,128)(2,1)} %concatenate.61.refs_2_.refs_0_, bf16[512,1664]{1,0:T(8,128)(2,1)} %collective-permute-done.12.refs_3_.refs_1_, bf16[512,1664]{1,0:T(8,128)(2,1)} %copy-done.3, bf16[512,1664]{1,0:T(8,128)(2,1)} %collective-permute-done.19.refs_3_, bf16[512,1664]{1,0:T(8,128)(2,1)} %copy-done.7, ...), custom_call_target="tpu_custom_call" | custom-call | flops 600000000 | bytes 1000 | tf_op jit(solution)/shard_map/expert_grad/pallas_call | solution.py:675
  583.5 15.2 %attend_back.2 = (bf16[512,768]{1,0:T(8,128)(2,1)}, bf16[512,256]{1,0:T(8,128)(2,1)}, bf16[512,256]{1,0:T(8,128)(2,1)}, bf16[512,256]{1,0:T(8,128)(2,1)}, bf16[512,256]{1,0:T(8,128)(2,1)}) custom-call(s32[2]{0:T(128)} %pad_add_fusion.place_ref, bf16[512,1536]{1,0:T(8,128)(2,1)} %get-tuple-element.164.q_ref, ...), custom_call_target="tpu_custom_call" | custom-call | flops 14400000000 | bytes 1000 | tf_op jit(solution)/shard_map/attend_back/pallas_call | solution.py:432
  605.4 15.0 %collective-permute-done.40 = bf16[512,1664]{1,0:T(8,128)(2,1)} collective-permute-done((bf16[512,1664]{1,0:T(8,128)(2,1)}, bf16[512,1664]{1,0:T(8,128)(2,1)}, u32[]{:S(2)}, u32[]{:S(2)}) %collective-permute-start.40) | collective-permute-done | bytes 1703968 | tf_op jit(solution)/shard_map/ppermute | solution.py:39
  639.4 10.5 %collective-permute-done.43 = bf16[512,512]{1,0:T(8,128)(2,1)} collective-permute-done((bf16[512,512]{1,0:T(8,128)(2,1)S(1)}, bf16[512,512]{1,0:T(8,128)(2,1)}, u32[]{:S(2)}, u32[]{:S(2)}) %collective-permute-start.43) | collective-permute-done | bytes 524320 | tf_op jit(solution)/shard_map/ppermute | solution.py:865
  655.4 15.0 %attend_back.3 = (bf16[512,768]{1,0:T(8,128)(2,1)}, bf16[512,256]{1,0:T(8,128)(2,1)}, bf16[512,256]{1,0:T(8,128)(2,1)}, bf16[512,256]{1,0:T(8,128)(2,1)}, bf16[512,256]{1,0:T(8,128)(2,1)}) custom-call(s32[2]{0:T(128)} %pad_add_fusion.place_ref, bf16[512,1536]{1,0:T(8,128)(2,1)} %get-tuple-element.164.q_ref, ...), custom_call_target="tpu_custom_call" | custom-call | flops 14400000000 | bytes 1000 | tf_op jit(solution)/shard_map/attend_back/pallas_call | solution.py:432
  691.8 8.9 %collective-permute-start.60 = (bf16[4,96,1536]{2,1,0:T(8,128)(2,1)}, bf16[4,96,1536]{2,1,0:T(8,128)(2,1)}, u32[]{:S(2)}, u32[]{:S(2)}) collective-permute-start(bf16[4,96,1536]{2,1,0:T(8,128)(2,1)} %bitcast_dynamic-update-slice_fusion.3.refs_0_), channel_id=1, source_target_pairs={{0,16},{16,0},{1,17},{17,1},{2,18},{18,2},{3,19},{19,3},{4,20},{20... | collective-permute-start | bytes 3538952 | tf_op jit(solution)/shard_map/ppermute | solution.py:39
  716.5 11.2 %collective-permute-done.48 = bf16[4,96,2304]{2,1,0:T(8,128)(2,1)} collective-permute-done((bf16[4,96,2304]{2,1,0:T(8,128)(2,1)}, bf16[4,96,2304]{2,1,0:T(8,128)(2,1)}, u32[]{:S(2)}, u32[]{:S(2)}) %collective-permute-start.48) | collective-permute-done | bytes 1769504 | tf_op jit(solution)/shard_map/ppermute | solution.py:39
  756.1 15.4 %collective-permute-done.55 = bf16[4,96,1152]{2,1,0:T(8,128)(2,1)S(1)} collective-permute-done((bf16[4,96,1152]{2,1,0:T(8,128)(2,1)}, bf16[4,96,1152]{2,1,0:T(8,128)(2,1)S(1)}, u32[]{:S(2)}, u32[]{:S(2)}) %collective-permute-start.55) | collective-permute-done | bytes 884768 | tf_op jit(solution)/shard_map/ppermute | solution.py:39
  777.6 8.9 %collective-permute-done.58 = bf16[96,1152]{1,0:T(8,128)(2,1)S(1)} collective-permute-done((bf16[96,1152]{1,0:T(8,128)(2,1)S(1)}, bf16[96,1152]{1,0:T(8,128)(2,1)S(1)}, u32[]{:S(2)}, u32[]{:S(2)}) %collective-permute-start.58) | collective-permute-done | bytes 221216 | tf_op jit(solution)/shard_map/ppermute | solution.py:119
  786.5 11.6 %collective-permute-done.57 = bf16[96,1152]{1,0:T(8,128)(2,1)S(1)} collective-permute-done((bf16[96,1152]{1,0:T(8,128)(2,1)S(1)}, bf16[96,1152]{1,0:T(8,128)(2,1)S(1)}, u32[]{:S(2)}, u32[]{:S(2)}) %collective-permute-start.57) | collective-permute-done | bytes 221216 | tf_op jit(solution)/shard_map/ppermute | solution.py:119
  (348 shorter events, 264.4 us)
Async XLA Ops:
  7.2 97.9 %all-gather.4.cloned.1.call-start = ((), (), s32[]{:S(2)}) async-start(), calls=%async_computation.5 | async-start | bytes 8773632 | tf_op jit(solution)/shard_map/all_gather | solution.py:729
  10.7 224.5 %all-gather.6.cloned.1.call-start = ((), (), s32[]{:S(2)}) async-start(), calls=%async_computation.6 | async-start | bytes 5013504 | tf_op jit(solution)/shard_map/all_gather | solution.py:730
  11.4 382.8 %all-gather.8.cloned.1.call-start = ((), (), s32[]{:S(2)}) async-start(), calls=%async_computation.7 | async-start | bytes 5898240 | tf_op jit(solution)/shard_map/all_gather | solution.py:744
  65.1 57.2 %collective-permute-start.8 = (bf16[512,1664]{1,0:T(8,128)(2,1)}, bf16[512,1664]{1,0:T(8,128)(2,1)S(1)}, u32[]{:S(2)}, u32[]{:S(2)}) collective-permute-start(bf16[512,1664]{1,0:T(8,128)(2,1)} %concatenate.61.refs_2_.refs_0_), channel_id=1, source_target_pairs={{0,2},{1,3},{2,0},{3,1},{4,6},{5,7},{6,4},{7,5},{8,10},{9,11},{10,... | collective-permute-start | bytes 5111816 | tf_op jit(solution)/shard_map/ppermute | solution.py:39
  67.6 54.7 %collective-permute-start.7 = (bf16[512,1664]{1,0:T(8,128)(2,1)}, bf16[512,1664]{1,0:T(8,128)(2,1)S(1)}, u32[]{:S(2)}, u32[]{:S(2)}) collective-permute-start(bf16[512,1664]{1,0:T(8,128)(2,1)} %concatenate.61.refs_2_.refs_0_), channel_id=1, source_target_pairs={{0,16},{16,0},{1,17},{17,1},{2,18},{18,2},{3,19},{19,3},{4,20},{20... | collective-permute-start | bytes 5111816 | tf_op jit(solution)/shard_map/ppermute | solution.py:39
  120.1 535.2 %reduce-scatter.10.cloned.1.call-start = ((), (), s32[]{:S(2)}) async-start(), calls=%async_computation.9 | async-start | bytes 1966080 | tf_op jit(solution)/shard_map/reduce_scatter | solution.py:800
  120.2 124.1 %collective-permute-start.15 = (bf16[384,1536]{1,0:T(8,128)(2,1)}, bf16[384,1536]{1,0:T(8,128)(2,1)}, u32[]{:S(2)}, u32[]{:S(2)}) collective-permute-start(bf16[384,1536]{1,0:T(8,128)(2,1)} %bitcast.15.refs_4_), channel_id=1, source_target_pairs={{0,12},{4,0},{8,4},{12,8},{1,13},{5,1},{9,5},{13,9},{2,14},{6,2},{... | collective-permute-start | bytes 3538952 | tf_op jit(solution)/shard_map/ppermute | solution.py:739
  121.7 131.7 %collective-permute-start.14 = (bf16[384,1536]{1,0:T(8,128)(2,1)}, bf16[384,1536]{1,0:T(8,128)(2,1)}, u32[]{:S(2)}, u32[]{:S(2)}) collective-permute-start(bf16[384,1536]{1,0:T(8,128)(2,1)} %bitcast.15.refs_4_), channel_id=1, source_target_pairs={{0,8},{4,12},{8,0},{12,4},{1,9},{5,13},{9,1},{13,5},{2,10},{6,14},... | collective-permute-start | bytes 3538952 | tf_op jit(solution)/shard_map/ppermute | solution.py:739
  144.6 38.5 %collective-permute-start.9 = (bf16[256,1664]{1,0:T(8,128)(2,1)}, bf16[256,1664]{1,0:T(8,128)(2,1)}, u32[]{:S(2)}, u32[]{:S(2)}) collective-permute-start(bf16[256,1664]{1,0:T(8,128)(2,1)} %slice.93), channel_id=1, source_target_pairs={{0,16},{16,0},{1,17},{17,1},{2,18},{18,2},{3,19},{19,3},{4,20},{20... | collective-permute-start | bytes 2555912 | tf_op jit(solution)/shard_map/ppermute | solution.py:39
  147.0 106.4 %collective-permute-start.13 = (bf16[384,1536]{1,0:T(8,128)(2,1)}, bf16[384,1536]{1,0:T(8,128)(2,1)}, u32[]{:S(2)}, u32[]{:S(2)}) collective-permute-start(bf16[384,1536]{1,0:T(8,128)(2,1)} %bitcast.15.refs_4_), channel_id=1, source_target_pairs={{0,4},{4,8},{8,12},{12,0},{1,5},{5,9},{9,13},{13,1},{2,6},{6,10},{... | collective-permute-start | bytes 3538952 | tf_op jit(solution)/shard_map/ppermute | solution.py:739
  162.8 90.7 %collective-permute-start.12 = (bf16[512,1664]{1,0:T(8,128)(2,1)}, bf16[512,1664]{1,0:T(8,128)(2,1)}, u32[]{:S(2)}, u32[]{:S(2)}) collective-permute-start(bf16[512,1664]{1,0:T(8,128)(2,1)} %concatenate.61.refs_2_.refs_0_), channel_id=1, source_target_pairs={{0,1},{1,0},{2,3},{3,2},{4,5},{5,4},{6,7},{7,6},{8,9},{9,8},{10,11... | collective-permute-start | bytes 5111816 | tf_op jit(solution)/shard_map/ppermute | solution.py:39
  244.3 36.9 %collective-permute-start.17 = (bf16[512,1536]{1,0:T(8,128)(2,1)}, bf16[512,1536]{1,0:T(8,128)(2,1)}, u32[]{:S(2)}, u32[]{:S(2)}) collective-permute-start(bf16[512,1536]{1,0:T(8,128)(2,1)} %get-tuple-element.176.refs_0_), channel_id=1, source_target_pairs={{0,2},{1,3},{2,0},{3,1},{4,6},{5,7},{6,4},{7,5},{8,10},{9,11},{10,... | collective-permute-start | bytes 4718600 | tf_op jit(solution)/shard_map/ppermute | solution.py:39
  253.4 40.3 %collective-permute-start.19 = (bf16[512,1664]{1,0:T(8,128)(2,1)S(1)}, bf16[512,1664]{1,0:T(8,128)(2,1)}, u32[]{:S(2)}, u32[]{:S(2)}) collective-permute-start(bf16[512,1664]{1,0:T(8,128)(2,1)S(1)} %collective-permute-done.7.refs_2_), channel_id=1, source_target_pairs={{0,1},{1,0},{2,3},{3,2},{4,5},{5,4},{6,7},{7,6},{8,9},{9,8},{10,11... | collective-permute-start | bytes 5111816 | tf_op jit(solution)/shard_map/ppermute | solution.py:39
  253.5 63.0 %collective-permute-start.23 = (bf16[512,1664]{1,0:T(8,128)(2,1)}, bf16[512,1664]{1,0:T(8,128)(2,1)}, u32[]{:S(2)}, u32[]{:S(2)}) collective-permute-start(bf16[512,1664]{1,0:T(8,128)(2,1)} %copy-done.7), channel_id=1, source_target_pairs={{0,1},{1,0},{2,3},{3,2},{4,5},{5,4},{6,7},{7,6},{8,9},{9,8},{10,11... | collective-permute-start | bytes 5111816 | tf_op jit(solution)/shard_map/ppermute | solution.py:39
  293.4 41.9 %collective-permute-start.20 = (bf16[256,1536]{1,0:T(8,128)(2,1)}, bf16[256,1536]{1,0:T(8,128)(2,1)}, u32[]{:S(2)}, u32[]{:S(2)}) collective-permute-start(bf16[256,1536]{1,0:T(8,128)(2,1)} %slice.95), channel_id=1, source_target_pairs={{0,16},{16,0},{1,17},{17,1},{2,18},{18,2},{3,19},{19,3},{4,20},{20... | collective-permute-start | bytes 2359304 | tf_op jit(solution)/shard_map/ppermute | solution.py:39
  293.7 41.6 %collective-permute-start.21 = (bf16[256,1536]{1,0:T(8,128)(2,1)}, bf16[256,1536]{1,0:T(8,128)(2,1)}, u32[]{:S(2)}, u32[]{:S(2)}) collective-permute-start(bf16[256,1536]{1,0:T(8,128)(2,1)} %slice.96), channel_id=1, source_target_pairs={{0,2},{1,3},{2,0},{3,1},{4,6},{5,7},{6,4},{7,5},{8,10},{9,11},{10,... | collective-permute-start | bytes 2359304 | tf_op jit(solution)/shard_map/ppermute | solution.py:39
  297.9 40.4 %collective-permute-start.25 = (bf16[512,1664]{1,0:T(8,128)(2,1)S(1)}, bf16[512,1664]{1,0:T(8,128)(2,1)}, u32[]{:S(2)}, u32[]{:S(2)}) collective-permute-start(bf16[512,1664]{1,0:T(8,128)(2,1)S(1)} %constant_dynamic-update-slice_fusion.2.refs_2_.refs_6_), channel_id=1, source_target_pairs={{0,1},{1,0},{2,3},{3,2},{4,5},{5,4},{6,7},{7,6},{8,9},{9,8},{10,11... | collective-permute-start | bytes 5111816 | tf_op jit(solution)/shard_map/ppermute | solution.py:39
  394.2 261.2 %reduce-scatter.8.cloned.1.call-start = ((), (), s32[]{:S(2)}) async-start(), calls=%async_computation.8 | async-start | bytes 3932160 | tf_op jit(solution)/shard_map/reduce_scatter | solution.py:800
  414.4 335.2 %reduce-scatter.14.cloned.1.call-start = ((), (), s32[]{:S(2)}) async-start(), calls=%async_computation.11 | async-start | bytes 1966080 | tf_op jit(solution)/shard_map/reduce_scatter | solution.py:800
  434.2 58.0 %collective-permute-start.36 = (bf16[512,1664]{1,0:T(8,128)(2,1)}, bf16[512,1664]{1,0:T(8,128)(2,1)S(1)}, u32[]{:S(2)}, u32[]{:S(2)}) collective-permute-start(bf16[512,1664]{1,0:T(8,128)(2,1)} %get-tuple-element.250), channel_id=1, source_target_pairs={{0,1},{1,0},{2,3},{3,2},{4,5},{5,4},{6,7},{7,6},{8,9},{9,8},{10,11... | collective-permute-start | bytes 5111816 | tf_op jit(solution)/shard_map/ppermute | solution.py:39
  434.6 52.1 %collective-permute-start.31 = (bf16[512,1664]{1,0:T(8,128)(2,1)}, bf16[512,1664]{1,0:T(8,128)(2,1)S(1)}, u32[]{:S(2)}, u32[]{:S(2)}) collective-permute-start(bf16[512,1664]{1,0:T(8,128)(2,1)} %get-tuple-element.241), channel_id=1, source_target_pairs={{0,1},{1,0},{2,3},{3,2},{4,5},{5,4},{6,7},{7,6},{8,9},{9,8},{10,11... | collective-permute-start | bytes 5111816 | tf_op jit(solution)/shard_map/ppermute | solution.py:39
  486.5 72.7 %collective-permute-start.33 = (bf16[512,1536]{1,0:T(8,128)(2,1)}, bf16[512,1536]{1,0:T(8,128)(2,1)}, u32[]{:S(2)}, u32[]{:S(2)}) collective-permute-start(bf16[512,1536]{1,0:T(8,128)(2,1)} %get-tuple-element.247), channel_id=1, source_target_pairs={{0,1},{1,0},{2,3},{3,2},{4,5},{5,4},{6,7},{7,6},{8,9},{9,8},{10,11... | collective-permute-start | bytes 4718600 | tf_op jit(solution)/shard_map/ppermute | solution.py:39
  486.7 37.0 %collective-permute-start.39 = (bf16[512,1536]{1,0:T(8,128)(2,1)}, bf16[512,1536]{1,0:T(8,128)(2,1)}, u32[]{:S(2)}, u32[]{:S(2)}) collective-permute-start(bf16[512,1536]{1,0:T(8,128)(2,1)} %pad_maximum_fusion.5), channel_id=1, source_target_pairs={{0,16},{16,0},{1,17},{17,1},{2,18},{18,2},{3,19},{19,3},{4,20},{20... | collective-permute-start | bytes 4718600 | tf_op jit(solution)/shard_map/ppermute | solution.py:39
  486.8 72.4 %collective-permute-start.38 = (bf16[512,1664]{1,0:T(8,128)(2,1)}, bf16[512,1664]{1,0:T(8,128)(2,1)}, u32[]{:S(2)}, u32[]{:S(2)}) collective-permute-start(bf16[512,1664]{1,0:T(8,128)(2,1)} %get-tuple-element.252), channel_id=1, source_target_pairs={{0,1},{1,0},{2,3},{3,2},{4,5},{5,4},{6,7},{7,6},{8,9},{9,8},{10,11... | collective-permute-start | bytes 5111816 | tf_op jit(solution)/shard_map/ppermute | solution.py:39
  492.2 67.0 %collective-permute-start.32 = (bf16[512,1536]{1,0:T(8,128)(2,1)}, bf16[512,1536]{1,0:T(8,128)(2,1)}, u32[]{:S(2)}, u32[]{:S(2)}) collective-permute-start(bf16[512,1536]{1,0:T(8,128)(2,1)} %pad_maximum_fusion.6), channel_id=1, source_target_pairs={{0,2},{1,3},{2,0},{3,1},{4,6},{5,7},{6,4},{7,5},{8,10},{9,11},{10,... | collective-permute-start | bytes 4718600 | tf_op jit(solution)/shard_map/ppermute | solution.py:39
  495.2 64.0 %collective-permute-start.35 = (bf16[256,1664]{1,0:T(8,128)(2,1)}, bf16[256,1664]{1,0:T(8,128)(2,1)}, u32[]{:S(2)}, u32[]{:S(2)}) collective-permute-start(bf16[256,1664]{1,0:T(8,128)(2,1)} %get-tuple-element.368), channel_id=1, source_target_pairs={{0,2},{1,3},{2,0},{3,1},{4,6},{5,7},{6,4},{7,5},{8,10},{9,11},{10,... | collective-permute-start | bytes 2555912 | tf_op jit(solution)/shard_map/ppermute | solution.py:39
  559.2 190.4 %reduce-scatter.12.cloned.1.call-start = ((), (), s32[]{:S(2)}) async-start(), calls=%async_computation.10 | async-start | bytes 3932160 | tf_op jit(solution)/shard_map/reduce_scatter | solution.py:800
  581.4 39.0 %collective-permute-start.40 = (bf16[512,1664]{1,0:T(8,128)(2,1)}, bf16[512,1664]{1,0:T(8,128)(2,1)}, u32[]{:S(2)}, u32[]{:S(2)}) collective-permute-start(bf16[512,1664]{1,0:T(8,128)(2,1)} %pad_maximum_fusion.3), channel_id=1, source_target_pairs={{0,16},{16,0},{1,17},{17,1},{2,18},{18,2},{3,19},{19,3},{4,20},{20... | collective-permute-start | bytes 5111816 | tf_op jit(solution)/shard_map/ppermute | solution.py:39
  583.1 38.6 %collective-permute-start.41 = (bf16[512,1664]{1,0:T(8,128)(2,1)}, bf16[512,1664]{1,0:T(8,128)(2,1)}, u32[]{:S(2)}, u32[]{:S(2)}) collective-permute-start(bf16[512,1664]{1,0:T(8,128)(2,1)} %pad_maximum_fusion.4), channel_id=1, source_target_pairs={{0,2},{1,3},{2,0},{3,1},{4,6},{5,7},{6,4},{7,5},{8,10},{9,11},{10,... | collective-permute-start | bytes 5111816 | tf_op jit(solution)/shard_map/ppermute | solution.py:39
  636.0 186.2 %reduce-scatter.16.cloned.1.call-start = ((), (), s32[]{:S(2)}) async-start(), calls=%async_computation.12 | async-start | bytes 5849088
  678.7 48.9 %collective-permute-start.48 = (bf16[4,96,2304]{2,1,0:T(8,128)(2,1)}, bf16[4,96,2304]{2,1,0:T(8,128)(2,1)}, u32[]{:S(2)}, u32[]{:S(2)}) collective-permute-start(bf16[4,96,2304]{2,1,0:T(8,128)(2,1)} %dynamic-slice_bitcast_fusion.2), channel_id=1, source_target_pairs={{0,2},{1,3},{2,0},{3,1},{4,6},{5,7},{6,4},{7,5},{8,10},{9,11},{10,... | collective-permute-start | bytes 5308424 | tf_op jit(solution)/shard_map/ppermute | solution.py:39
  691.8 117.0 %collective-permute-start.60 = (bf16[4,96,1536]{2,1,0:T(8,128)(2,1)}, bf16[4,96,1536]{2,1,0:T(8,128)(2,1)}, u32[]{:S(2)}, u32[]{:S(2)}) collective-permute-start(bf16[4,96,1536]{2,1,0:T(8,128)(2,1)} %bitcast_dynamic-update-slice_fusion.3.refs_0_), channel_id=1, source_target_pairs={{0,16},{16,0},{1,17},{17,1},{2,18},{18,2},{3,19},{19,3},{4,20},{20... | collective-permute-start | bytes 3538952 | tf_op jit(solution)/shard_map/ppermute | solution.py:39
  (84 other events, 1312.6 us)
Sparse Core Ops, SparseCore 0:
  10.9 94.1 all-gather.3
  107.4 127.7 all-gather.5
  236.8 88.4 all-gather.7
  394.3 33.8 reduce-scatter.9
  430.9 59.2 reduce-scatter.7
  559.3 32.8 reduce-scatter.13
  636.1 59.4 reduce-scatter.11
  714.0 101.1 reduce-scatter.15

commit v3 on v2

--- a/solution.py
+++ b/solution.py
@@ -159,7 +159,7 @@
     return lax.dot_general(a, b, (((0,), (0,)), ((), ())), preferred_element_type=F32)
 
 
-def project_in_kernel(token_ref, weight_ref, tail_ref, query_ref, pair_ref, low_ref, gain_ref):
+def project_in_kernel(token_ref, weight_ref, tail_ref, query_ref, paira_ref, pairb_ref, low_ref, gain_ref):
     step = pl.program_id(0)
     queries = HEADS * HEAD_DIM // weight_ref.shape[1]
 
@@ -178,12 +178,17 @@
     def _():
         query_ref[...] = result
 
-    @pl.when(step >= queries)
-    def _():
-        pair_ref[...] = result
-
-
-def project_rows(tokens, weight, qkv):
+    half = result.shape[1] // 2
+    for part in range(2):
+
+        @pl.when(step == queries + part)
+        def _():
+            cols = slice(part * half, (part + 1) * half)
+            paira_ref[:, cols] = result[:, :half]
+            pairb_ref[:, cols] = result[:, half:]
+
+
+def project_rows(tokens, weight, qkv, before):
     count, width = tokens.shape
     tile = 512
     query_width = HEADS * HEAD_DIM
@@ -193,18 +198,20 @@
         grid=(qkv // tile,),
         in_specs=[
             pl.BlockSpec((count, width), lambda j: (0, 0)),
-            pl.BlockSpec((width, tile), lambda j: (0, j)),
-            pl.BlockSpec((width, 128), lambda j: (0, qkv // 128)),
+            pl.BlockSpec((width, tile), lambda j: (0, before // tile + j)),
+            pl.BlockSpec((width, 128), lambda j: (0, (before + qkv) // 128)),
         ],
         out_specs=[
             pl.BlockSpec((count, tile), lambda j: (0, jnp.minimum(j, queries - 1))),
-            pl.BlockSpec((count, tile), lambda j: (0, jnp.maximum(j - queries, 0))),
+            pl.BlockSpec((count, tile), lambda j: (0, 0)),
+            pl.BlockSpec((count, tile), lambda j: (0, 0)),
             pl.BlockSpec((count, width), lambda j: (0, 0)),
             pl.BlockSpec((8, width), lambda j: (0, 0)),
         ],
         out_shape=[
             jax.ShapeDtypeStruct((count, query_width), BF),
-            jax.ShapeDtypeStruct((count, qkv - query_width), BF),
+            jax.ShapeDtypeStruct((count, tile), BF),
+            jax.ShapeDtypeStruct((count, tile), BF),
             jax.ShapeDtypeStruct((count, width), BF),
             jax.ShapeDtypeStruct((8, width), F32),
         ],
@@ -254,7 +261,51 @@
     )(mixed, weight, tokens, gains)
 
 
-def attend_kernel(place_ref, q_ref, k_ref, v_ref, kr_ref, vr_ref, mixed_ref, stat_ref, bias_ref, col_ref):
+def middle_back_kernel(
+    own_ref, got_ref, across_ref, beside_ref, middle_ref, up_ref, gain_ref, weight_ref,
+    grad_ref, low_ref, mixed_ref, sum_ref,
+):
+    @pl.when(pl.program_id(0) == 0)
+    def _():
+        above = own_ref[...].astype(F32) + got_ref[...].astype(F32)
+        above = above + across_ref[...].astype(F32) + beside_ref[...].astype(F32)
+        x = middle_ref[...]
+        inverse = lax.rsqrt(jnp.mean(x * x, axis=-1, keepdims=True) + EPS)
+        normed = x * inverse
+        scaled = above * gain_ref[1:2, :]
+        spread = jnp.mean(scaled * normed, axis=-1, keepdims=True)
+        grad = up_ref[...].astype(F32) + inverse * (scaled - normed * spread)
+        grad_ref[...] = grad
+        low_ref[...] = grad.astype(BF)
+        sum_ref[...] = jnp.broadcast_to(jnp.sum(above * normed, axis=0, keepdims=True), sum_ref.shape)
+
+    mixed_ref[...] = dot_nt(low_ref[...], weight_ref[...]).astype(BF)
+
+
+def middle_back(own, got, across, beside, middle, up, gains, weight, columns):
+    count, width = own.shape
+    tile = 512
+    whole = pl.BlockSpec((count, width), lambda j: (0, 0))
+    row = pl.BlockSpec((8, width), lambda j: (0, 0))
+    return pl.pallas_call(
+        middle_back_kernel,
+        grid=(columns // tile,),
+        in_specs=[whole] * 6 + [row, pl.BlockSpec((tile, width), lambda j: (j, 0))],
+        out_specs=[whole, whole, pl.BlockSpec((count, tile), lambda j: (0, j)), row],
+        out_shape=[
+            jax.ShapeDtypeStruct((count, width), F32),
+            jax.ShapeDtypeStruct((count, width), BF),
+            jax.ShapeDtypeStruct((count, columns), BF),
+            jax.ShapeDtypeStruct((8, width), F32),
+        ],
+        compiler_params=pltpu.CompilerParams(vmem_limit_bytes=VMEM_LIMIT),
+        cost_estimate=cost(1),
+        name="middle_back",
+    )(own, got, across, beside, middle, up, gains, weight)
+
+
+def attend_kernel(place_ref, q_ref, k_ref, v_ref, kr_ref, vr_ref, *refs):
+    mixed_ref, stat_ref, bias_ref, col_ref = refs[-4:]
     count = q_ref.shape[0]
     half = count // 2
     seq_at = place_ref[0]
@@ -307,9 +358,9 @@
     stat_ref[...] = col_ref[...].T[:8, :]
 
 
-def attend(place, query, pair, past):
+def attend(place, query, pair, past, first, held=()):
     count = query.shape[0]
-    steps = KV_HEADS // 2
+    steps = pair.shape[1] // 256
     wide = 2 * GROUP * HEAD_DIM
     return pl.pallas_call(
         attend_kernel,
@@ -317,14 +368,15 @@
             num_scalar_prefetch=1,
             grid=(steps,),
             in_specs=[
-                pl.BlockSpec((count, wide), lambda j, place: (0, j)),
+                pl.BlockSpec((count, wide), lambda j, place: (0, first + j)),
                 pl.BlockSpec((count, 128), lambda j, place: (0, j)),
                 pl.BlockSpec((count, 128), lambda j, place: (0, steps + j)),
                 pl.BlockSpec((count, 128), lambda j, place: (0, j)),
                 pl.BlockSpec((count, 128), lambda j, place: (0, steps + j)),
-            ],
+            ]
+            + [pl.BlockSpec(memory_space=pl.ANY)] * len(held),
             out_specs=[
-                pl.BlockSpec((count, wide), lambda j, place: (0, j)),
+                pl.BlockSpec((count, wide), lambda j, place: (0, first + j)),
                 pl.BlockSpec((None, 8, count), lambda j, place: (j, 0, 0)),
             ],
             scratch_shapes=[pltpu.VMEM((count, count), F32), pltpu.VMEM((count, 128), F32)],
@@ -333,10 +385,11 @@
             jax.ShapeDtypeStruct((count, HEADS * HEAD_DIM), BF),
             jax.ShapeDtypeStruct((steps, 8, count), F32),
         ],
+        input_output_aliases={6: 0} if held else {},
         compiler_params=pltpu.CompilerParams(vmem_limit_bytes=VMEM_LIMIT),
         cost_estimate=cost(0),
         name="attend",
-    )(place, query, pair, pair, past, past)
+    )(place, query, pair, pair, past, past, *held)
 
 
 def attend_back_kernel(
@@ -424,7 +477,6 @@
 
 def attend_back(place, query, pair, past, mixed, mixed_grad, stats, first, steps, us):
     count = query.shape[0]
-    pairs = KV_HEADS // 2
     wide = 2 * GROUP * HEAD_DIM
     narrow = jax.ShapeDtypeStruct((count, steps * 128), BF)
     head_spec = pl.BlockSpec((count, wide), lambda j, place: (0, first + j))
@@ -436,13 +488,13 @@
             grid=(steps,),
             in_specs=[
                 head_spec,
-                pl.BlockSpec((count, 128), lambda j, place: (0, first + j)),
-                pl.BlockSpec((count, 128), lambda j, place: (0, pairs + first + j)),
-                pl.BlockSpec((count, 128), lambda j, place: (0, first + j)),
-                pl.BlockSpec((count, 128), lambda j, place: (0, pairs + first + j)),
+                pl.BlockSpec((count, 128), lambda j, place: (0, j)),
+                pl.BlockSpec((count, 128), lambda j, place: (0, steps + j)),
+                pl.BlockSpec((count, 128), lambda j, place: (0, j)),
+                pl.BlockSpec((count, 128), lambda j, place: (0, steps + j)),
                 head_spec,
                 head_spec,
-                pl.BlockSpec((None, 8, count), lambda j, place: (first + j, 0, 0)),
+                pl.BlockSpec((None, 8, count), lambda j, place: (j, 0, 0)),
             ],
             out_specs=[pl.BlockSpec((count, wide), lambda j, place: (0, j))] + [pair_spec] * 4,
             scratch_shapes=[pltpu.VMEM((count, count), F32)],
@@ -516,50 +568,21 @@
     )(seq, *parts)
 
 
-def expert_kernel(e, has_earlier, n, place_ref, *refs):
+def expert_kernel(e, has_earlier, place_ref, *refs):
     na_ref, nb_ref, ca_ref, cb_ref = refs[:4]
     earlier_refs = refs[4:8] if has_earlier else (None,) * 4
-    begin = 8 if has_earlier else 4
-    block_refs = refs[begin : begin + n]
-    (ch_ref, gl_ref, outa_ref, outb_ref, backa_ref, backb_ref) = refs[-8:-2]
-    wt_ref, sems = refs[-2:]
-    part = block_refs[0].shape[0]
+    wt_ref = refs[8] if has_earlier else refs[4]
+    (ch_ref, gl_ref, outa_ref, outb_ref, backa_ref, backb_ref) = refs[-6:]
     width = na_ref.shape[1]
     ff = wt_ref.shape[1] // 3
-    step_at = pl.program_id(0)
-    fresh = step_at == 0
-    first = step_at < 2
+    first = pl.program_id(0) < 2
     mine = 2 * place_ref[0] + e
-    at = place_ref[1]
-
-    def piece(step, kind):
-        slot = lax.rem(at + n - step, n) if n > 1 else 0
-        rows = pl.ds(pl.multiple_of(slot * part, part), part) if n > 1 else slice(None)
-        cols = slice(kind * ff, (kind + 1) * ff)
-        return pltpu.make_async_copy(block_refs[step].at[:, cols], wt_ref.at[rows, cols], sems.at[kind * n + step])
-
-    @pl.when(fresh)
-    def _():
-        for kind in range(3):
-            for step in range(n):
-                piece(step, kind).start()
-
-    def run(n_ref, c_ref, earlier_out, earlier_back, out_ref, back_ref, is_first):
-        def arrived(kind):
-            if is_first:
-
-                @pl.when(fresh)
-                def _():
-                    for step in range(n):
-                        piece(step, kind).wait()
-
+
+    def run(n_ref, c_ref, earlier_out, earlier_back, out_ref, back_ref):
         packed = c_ref[:, width:].astype(F32)
         lane = lax.broadcasted_iota(jnp.int32, packed.shape, 1)
-        arrived(0)
         g = dot_nn(n_ref[...], wt_ref[:, :ff])
-        arrived(1)
         l = dot_nn(n_ref[...], wt_ref[:, ff : 2 * ff])
-        arrived(2)
         u = dot_nn(c_ref[:, :width], wt_ref[:, 2 * ff :])
         own_lane = (lane == mine) | (lane == EXPERTS + mine)
         weight = jnp.sum(jnp.where(own_lane, packed, 0.0), axis=-1, keepdims=True)
@@ -586,16 +609,16 @@
 
     @pl.when(first)
     def _():
-        run(na_ref, ca_ref, earlier_refs[0], earlier_refs[2], outa_ref, backa_ref, True)
+        run(na_ref, ca_ref, earlier_refs[0], earlier_refs[2], outa_ref, backa_ref)
 
     @pl.when(jnp.logical_not(first))
     def _():
-        run(nb_ref, cb_ref, earlier_refs[1], earlier_refs[3], outb_ref, backb_ref, False)
-
-
-def expert_rows(place, e, rows, up, blocks, chunk, chunks, held, earlier, us):
+        run(nb_ref, cb_ref, earlier_refs[1], earlier_refs[3], outb_ref, backb_ref)
+
+
+def expert_rows(place, e, rows, up, packed, chunk, chunks, held, earlier, us):
     count, width = rows[0].shape
-    ff = blocks[0].shape[1] // 3
+    ff = packed.shape[1] // 3
     tile = count // 2
     more = width + 128
 
@@ -615,20 +638,21 @@
     one = jax.ShapeDtypeStruct((count, width), BF)
     one_more = jax.ShapeDtypeStruct((count, more), BF)
     held, earlier = list(held), list(earlier)
-    begin = 5 + len(earlier) + len(blocks)
+    begin = 6 + len(earlier)
+    packed_spec = pl.BlockSpec((width, 3 * ff), lambda i, place: (0, 0), pipeline_mode=pl.Buffered(1))
     return pl.pallas_call(
-        functools.partial(expert_kernel, e, len(earlier) > 0, len(blocks)),
+        functools.partial(expert_kernel, e, len(earlier) > 0),
         grid_spec=pltpu.PrefetchScalarGridSpec(
             num_scalar_prefetch=1,
             grid=(4,),
             in_specs=wide_specs
             + more_specs
             + (more_specs + wide_specs if earlier else [])
-            + [any_spec] * (len(blocks) + len(held)),
+            + [packed_spec]
+            + [any_spec] * len(held),
             out_specs=[pl.BlockSpec((tile, ff), at_rows), pl.BlockSpec((tile, 2 * ff), at_rows)]
             + more_specs
             + wide_specs,
-            scratch_shapes=[pltpu.VMEM((width, 3 * ff), BF), pltpu.SemaphoreType.DMA((3 * len(blocks),))],
         ),
         out_shape=[jax.ShapeDtypeStruct((total, ff), BF), jax.ShapeDtypeStruct((total, 2 * ff), BF)]
         + [one_more] * 2
@@ -637,12 +661,12 @@
         compiler_params=pltpu.CompilerParams(vmem_limit_bytes=VMEM_LIMIT),
         cost_estimate=cost(us),
         name="expert_rows",
-    )(place, *rows, *up, *earlier, *blocks, *held)
+    )(place, *rows, *up, *earlier, packed, *held)
 
 
 def expert_grad_kernel(*refs):
-    right_ref, out_ref, sum_ref, held_ref, sems = refs[-5:]
-    sources = refs[:-5]
+    out_ref, sum_ref, held_ref, sems = refs[-4:]
+    sources, right_ref = refs[:8], refs[8]
     width = held_ref.shape[2]
     step = pl.program_id(0)
 
@@ -669,24 +693,28 @@
                 out_ref[...] = (sum_ref[...] + product).astype(BF)
 
 
-def expert_grad(lefts, right, width, us):
+def expert_grad(lefts, right, width, total, column, us, held=()):
     count = lefts[0].shape[0]
     columns = right.shape[1]
+    any_spec = pl.BlockSpec(memory_space=pl.ANY)
     return pl.pallas_call(
         expert_grad_kernel,
         grid=(len(lefts),),
-        in_specs=[pl.BlockSpec(memory_space=pl.ANY)] * len(lefts) + [pl.BlockSpec((count, columns), lambda i: (i, 0))],
-        out_specs=pl.BlockSpec((width, columns), lambda i: (0, 0)),
-        out_shape=jax.ShapeDtypeStruct((width, columns), BF),
+        in_specs=[any_spec] * len(lefts)
+        + [pl.BlockSpec((count, columns), lambda i: (i, 0))]
+        + [any_spec] * len(held),
+        out_specs=pl.BlockSpec((width, columns), lambda i: (0, column)),
+        out_shape=jax.ShapeDtypeStruct((width, total), BF),
         scratch_shapes=[
             pltpu.VMEM((width, columns), F32),
             pltpu.VMEM((2, count, width), BF),
             pltpu.SemaphoreType.DMA((2,)),
         ],
+        input_output_aliases={len(lefts) + 1: 0} if held else {},
         compiler_params=pltpu.CompilerParams(vmem_limit_bytes=VMEM_LIMIT),
         cost_estimate=cost(us),
         name="expert_grad",
-    )(*lefts, right)
+    )(*lefts, right, *held)
 
 
 def body(
@@ -726,22 +754,17 @@
     shard = width // (outer_count * inner_count)
     qkv = attention_in.shape[1]
     gains = jnp.concatenate([norm_first[:, None], norm_second[:, None], jnp.zeros((shard, 126), BF)], axis=1)
-    project_in = lax.all_gather(jnp.concatenate([attention_in, gains], axis=1), ROWS, axis=0, tiled=True)
-    project_out = lax.all_gather(attention_out, ROWS, axis=0, tiled=True)
+    projections = lax.all_gather(
+        jnp.concatenate([attention_out, attention_in, gains], axis=1), ROWS, axis=0, tiled=True
+    )
 
     seq_place = seq_at.astype(jnp.int32)[None]
     expert_place = jnp.stack([layer_at.astype(jnp.int32), outer_at.astype(jnp.int32)])
     packed = pack_experts(seq_place, expert_gate, expert_lift, expert_down, inner_count)
     got = [exchange_start(part) for part in packed]
     packed = [exchange_end(*pair).reshape(inner_count * shard, 3 * ff) for pair in zip(packed, got)]
-    if outer_count == 4:
-        blocks_a = [packed[0]] + [
-            lax.ppermute(packed[0], "outer", [(i, (i + step) % outer_count) for i in range(outer_count)])
-            for step in range(1, outer_count)
-        ]
-    else:
-        blocks_a = [lax.all_gather(packed[0], "outer", axis=0, tiled=True)]
-    blocks = (blocks_a, [lax.all_gather(after(packed[1], project_out[:8, :128]), "outer", axis=0, tiled=True)])
+    gathered = [lax.all_gather(packed[0], "outer", axis=0, tiled=True)]
+    gathered.append(lax.all_gather(after(packed[1], gathered[0][:8, :128]), "outer", axis=0, tiled=True))
 
     chosen = (
         routes[0][:, :, None] == jnp.arange(EXPERTS, dtype=jnp.int32)[None, None, :]
@@ -756,20 +779,20 @@
     up_block = after(up_block, packed)
     up_across, up_beside, up_sibling = seq_swap(up_block), side_swap(up_block), core_swap(up_block)
 
-    query, pair, lowered_one, gains = project_rows(tokens[0], project_in, qkv)
-    past = lax.ppermute(pair, "seq", [(0, 1)])
-    past, up_across, up_beside = lax.optimization_barrier((past, up_across, up_beside))
-    up_far_top, up_far_low = seq_swap(up_beside[:half]), side_swap(up_across[half:])
-    mixed, stats = attend(place, query, pair, past)
-    mixed, up_far_top, up_far_low = lax.optimization_barrier((mixed, up_far_top, up_far_low))
     up_pair_across = (up_across, core_swap(up_across))
     up_pair_beside = (up_beside, core_swap(up_beside))
-    middle, lowered_two = merge_rows(mixed, project_out, tokens[0], gains)
+    query, pair_a, pair_b, lowered_one, gains = project_rows(tokens[0], projections, qkv, query_width)
+    past_a = lax.ppermute(pair_a, "seq", [(0, 1)])
+    late_pair, past_a = lax.optimization_barrier((pair_b, past_a))
+    past_b = lax.ppermute(late_pair, "seq", [(0, 1)])
+    mixed, stats_a = attend(place, query, pair_a, past_a, 0)
+    mixed, stats_b = attend(place, query, pair_b, past_b, stats_a.shape[0], (mixed,))
+    middle, lowered_two = merge_rows(mixed, projections, tokens[0], gains)
 
     across, beside, sibling = seq_swap(lowered_two), side_swap(lowered_two), core_swap(lowered_two)
 
     def experts(e, at, rows, up, held, earlier=(), us=1):
-        return expert_rows(expert_place, e, rows, up, blocks[e], at, 4, held, earlier, us)
+        return expert_rows(expert_place, e, rows, up, gathered[e], at, 4, held, earlier, us)
 
     def upper(block, more):
         return jnp.concatenate([low_plus(block[:half], more), block[half:]])
@@ -781,13 +804,17 @@
     made_own = experts(0, 0, row_own, up_own, ())
     across, beside, held = lax.optimization_barrier((across, beside, made_own[:2]))
     far_top, far_low = seq_swap(beside[:half]), side_swap(across[half:])
+    up_beside_far, up_across_far = after((up_beside, up_across), held)
+    up_far_top, up_far_low = seq_swap(up_beside_far[:half]), side_swap(up_across_far[half:])
     row_across = (across, core_swap(across))
     row_beside = (beside, core_swap(beside))
     made_across = experts(0, 1, row_across, up_pair_across, held)
+    made_beside = experts(0, 2, row_beside, up_pair_beside, made_across[:2])
+    far_top, far_low, up_far_top, up_far_low, held = lax.optimization_barrier(
+        (far_top, far_low, up_far_top, up_far_low, made_beside[:2])
+    )
     up_far = jnp.concatenate([up_far_top, up_far_low], axis=0)
     up_pair_far = (up_far, core_swap(up_far))
-    made_beside = experts(0, 2, row_beside, up_pair_beside, made_across[:2])
-    far_top, far_low, held = lax.optimization_barrier((far_top, far_low, made_beside[:2]))
     far = jnp.concatenate([far_top, far_low], axis=0)
     row_far = (far, core_swap(far))
     made_far = experts(0, 3, row_far, up_pair_far, held)
@@ -799,89 +826,93 @@
     def home(total):
         return lax.psum_scatter(total, "outer", scatter_dimension=0, tiled=True)
 
-    def slots(*locals_):
-        local = jnp.concatenate(locals_, axis=1) if len(locals_) > 1 else locals_[0]
+    def slots(local):
         return local.reshape(inner_count, shard, local.shape[1])
 
-    total_a = expert_grad(row_all, grads_a, width, 1)
+    total_a = expert_grad(row_all, grads_a, width, 3 * ff, 0, 1)
+    total_a = expert_grad(up_all, hidden_a, width, 3 * ff, 2, 1, (total_a,))
     home_a = home(total_a)
-    hidden_a = after(hidden_a, total_a)
-    down_a = expert_grad(up_all, hidden_a, width, 1)
-    home_down_a = home(down_a)
-    far_parts = after(made_far[2:], down_a)
+    far_parts = after(made_far[2:], total_a)
 
     made_far = experts(1, 3, row_far, up_pair_far, (), far_parts)
     far_got, far_out_got = core_swap(made_far[5]), core_swap(made_far[3])
     made_across = experts(1, 1, row_across, up_pair_across, made_far[:2], made_across[2:])
     across_got, across_out_got = core_swap(made_across[5]), core_swap(made_across[3])
-    far_got, held = lax.optimization_barrier((far_got, made_across[:2]))
-    far_sum, held = lax.optimization_barrier((low_plus(made_far[4], far_got), held))
+    far_got, far_out_got, held = lax.optimization_barrier((far_got, far_out_got, made_across[:2]))
+    far_sum, far_out, held = lax.optimization_barrier(
+        (low_plus(made_far[4], far_got), low_plus(made_far[2], far_out_got), held)
+    )
     back_low, back_top = side_swap(far_sum[half:]), seq_swap(far_sum[:half])
     made_beside = experts(1, 2, row_beside, up_pair_beside, held, made_beside[2:], 15)
     beside_got, beside_out_got = core_swap(made_beside[5]), core_swap(made_beside[3])
-    across_got, back_low, back_top, held = lax.optimization_barrier(
-        (across_got, back_low, back_top, made_beside[:2])
-    )
-    across_sum, held = lax.optimization_barrier((lower(low_plus(made_across[4], across_got), back_low), held))
+    across_got, across_out_got, back_low, back_top, held = lax.optimization_barrier(
+        (across_got, across_out_got, back_low, back_top, made_beside[:2])
+    )
+    across_sum, out_across, held = lax.optimization_barrier(
+        (lower(low_plus(made_across[4], across_got), back_low), low_plus(made_across[2], across_out_got), held)
+    )
     across_in = seq_swap(across_sum)
     made_own = experts(1, 0, row_own, up_own, held, made_own[2:], 15)
     hidden_b, grads_b = made_own[:2]
-    own_got, own_out_got = core_swap(made_own[5]), core_swap(made_own[3])
-    beside_got, far_out_got, grads_b = lax.optimization_barrier((beside_got, far_out_got, grads_b))
-    beside_sum, grads_b = lax.optimization_barrier((upper(low_plus(made_beside[4], beside_got), back_top), grads_b))
+    own_got = core_swap(made_own[5])
+    beside_got, beside_out_got, grads_b = lax.optimization_barrier((beside_got, beside_out_got, grads_b))
+    beside_sum, out_beside, grads_b = lax.optimization_barrier(
+        (
+            upper(low_plus(made_beside[4], beside_got), back_top),
+            low_plus(made_beside[2], beside_out_got),
+            grads_b,
+        )
+    )
     beside_in = side_swap(beside_sum)
-    far_out = low_plus(made_far[2], far_out_got)
     out_low, out_top = side_swap(far_out[half:]), seq_swap(far_out[:half])
 
-    total_b = expert_grad(row_all, grads_b, width, 1)
+    total_b = expert_grad(row_all, grads_b, width, 3 * ff, 0, 1)
+    total_b = expert_grad(up_all, hidden_b, width, 3 * ff, 2, 1, (total_b,))
     home_b = home(total_b)
-    across_in, hidden_b = lax.optimization_barrier((across_in, after(hidden_b, total_b)))
-    down_b = expert_grad(up_all, hidden_b, width, 1)
-    home_down_b = home(down_b)
-    beside_in, own_got, out_top, out_low, across_out_got, beside_out_got, own_out_got, _ = lax.optimization_barrier(
-        (beside_in, own_got, out_top, out_low, across_out_got, beside_out_got, own_out_got, down_b)
-    )
-    out_across = lower(low_plus(made_across[2], across_out_got), out_low)
-    out_beside = upper(low_plus(made_beside[2], beside_out_got), out_top)
-    normed_grad_two = (
-        made_own[4].astype(F32) + own_got.astype(F32) + across_in.astype(F32) + beside_in.astype(F32)
-    )
-
-    normed_two, inverse_two, _ = norm_rows(middle, gains[1])
-    middle_norm_grad, second_gain_grad = norm_back(normed_grad_two, normed_two, inverse_two, gains[1])
-    middle_grad = upstream + middle_norm_grad
-    branch_grad = middle_grad.astype(BF)
-    mixed_grad = dot_nt(branch_grad, project_out).astype(BF)
-    out_across, out_beside, mixed_grad = lax.optimization_barrier((out_across, out_beside, mixed_grad))
+    across_in, beside_in, own_got, _ = lax.optimization_barrier((across_in, beside_in, own_got, total_b))
+
+    middle_grad, branch_grad, mixed_grad, second_gain_grad = middle_back(
+        made_own[4], own_got, across_in, beside_in, middle, upstream_low, gains, projections, query_width
+    )
+    second_gain_grad = second_gain_grad[0]
+    chain = Chain(mixed_grad)
+    own_out_got = core_swap(chain.enter(made_own[3]))
+    out_top, out_low = chain.enter((out_top, out_low))
+    out_across, out_beside = lower(out_across, out_low), upper(out_beside, out_top)
+    out_across, out_beside = chain.leave(lax.optimization_barrier((out_across, out_beside)))
     out_across_in, out_beside_in = seq_swap(out_across), side_swap(out_beside)
-    chain = Chain(mixed_grad)
-    pairs = KV_HEADS // 2
-    first_pairs = pairs // 2
-
-    def back(first, steps):
-        return attend_back(chain.enter(place), query, pair, past, mixed, mixed_grad, stats, first, steps, 24)
-
-    query_a, key_a, value_a, key_past_a, value_past_a = chain.leave(back(0, first_pairs))
+    def back(pair, past, stats, first):
+        return attend_back(
+            chain.enter(place), query, pair, past, mixed, mixed_grad, stats, first, stats.shape[0], 24
+        )
+
+    query_a, key_a, value_a, key_past_a, value_past_a = chain.leave(back(pair_a, past_a, stats_a, 0))
     late_a = lax.ppermute(jnp.concatenate([key_past_a, value_past_a], axis=1), "seq", [(1, 0)])
-    out_weight_grad = chain.leave(dot_tn(chain.enter(mixed), branch_grad).astype(BF))
-    out_across_in, out_beside_in = chain.enter((out_across_in, out_beside_in))
+    out_home = HomeSum(chain.leave(dot_tn(chain.enter(mixed), branch_grad).astype(BF)))
+    out_across_in, out_beside_in, own_out_got = chain.enter((out_across_in, out_beside_in, own_out_got))
     combined = (
         made_own[2].astype(F32) + own_out_got.astype(F32) + out_across_in.astype(F32) + out_beside_in.astype(F32)
     )
     block_output = chain.leave((middle + combined[:, :width]).astype(BF))[None]
     dots = combined[:, width : width + EXPERTS] + combined[:, width + EXPERTS : width + 2 * EXPERTS]
-    query_weight_a = chain.leave(dot_tn(chain.enter(lowered_one), query_a).astype(BF))
-    early_home = HomeSum(out_weight_grad, query_weight_a)
     grad_gates = chain.leave(jnp.sum(jnp.where(chosen, chain.enter(dots)[:, None, :], 0.0), axis=-1))[None]
-    early_home.got = chain.enter(early_home.got)
-    late_a = chain.enter(late_a)
-    chain.leave((early_home.beside(), late_a))
-    a_slots = slots(chain.enter(home_a), chain.enter(home_down_a))
-    a_got = exchange_start(a_slots)
-    query_b, key_b, value_b, key_past_b, value_past_b = chain.leave(back(first_pairs, pairs - first_pairs))
+    out_home.got = chain.enter(out_home.got)
+    chain.leave(out_home.beside())
+    a_slots = slots(home_a)
+    a_mine = chain.leave(exchange_end(a_slots, chain.enter(exchange_start(a_slots))))
+    late_a = chain.leave(chain.enter(late_a))
+    a_other = seq_swap(a_mine)
+    query_b, key_b, value_b, key_past_b, value_past_b = chain.leave(
+        back(pair_b, past_b, stats_b, stats_a.shape[0])
+    )
     late_b = lax.ppermute(jnp.concatenate([key_past_b, value_past_b], axis=1), "seq", [(1, 0)])
-    query_weight_b = chain.leave(dot_tn(chain.enter(lowered_one), query_b).astype(BF))
-    a_mine = chain.leave(exchange_end(a_slots, chain.enter(a_got)))
+    a_other = chain.enter(a_other)
+    out_home.got = chain.enter(out_home.got)
+    chain.leave((out_home.across(), a_other))
+    query_grad = jnp.concatenate([query_a, query_b], axis=1)
+    query_home = HomeSum(chain.leave(dot_tn(chain.enter(lowered_one), query_grad).astype(BF)))
+    query_home.got = chain.enter(query_home.got)
+    chain.leave(query_home.beside())
     late_b = chain.enter(late_b)
     split_a, split_b = key_past_a.shape[1], key_past_b.shape[1]
     pair_own = jnp.concatenate([key_a, key_b, value_a, value_b], axis=1)
@@ -890,45 +921,49 @@
     )
     pair_grad = low_plus(pair_own, pair_late)
     pair_weight = chain.leave(dot_tn(lowered_one, pair_grad).astype(BF))
-    final_total = chain.leave(jnp.concatenate([query_weight_b, pair_weight], axis=1))
-    final_part = lax.psum_scatter(final_total, ROWS, scatter_dimension=0, tiled=True)
-    early_home.got = chain.enter(early_home.got)
-    chain.leave(early_home.across())
-    projected_grad = jnp.concatenate([query_a, query_b, pair_grad], axis=1)
-    normed_grad_one = chain.leave(dot_nt(chain.enter(projected_grad), project_in[:, :qkv]))
+    pair_part = lax.psum_scatter(pair_weight, ROWS, scatter_dimension=0, tiled=True)
+    projected_grad = jnp.concatenate([query_grad, pair_grad], axis=1)
+    normed_grad_one = chain.leave(
+        dot_nt(chain.enter(projected_grad), projections[:, query_width : query_width + qkv])
+    )
+    query_home.got = chain.enter(query_home.got)
+    chain.leave(query_home.across())
+    out_home.got = chain.enter(out_home.got)
+    chain.leave(out_home.along())
     normed_one, inverse_one, _ = norm_rows(inputs, gains[0])
     input_norm_grad, first_gain_grad = norm_back(chain.enter(normed_grad_one), normed_one, inverse_one, gains[0])
     grad_tokens = chain.leave(middle_grad + input_norm_grad)[None]
     gain_grads = jnp.stack([first_gain_grad, second_gain_grad])
+    gain_grads = gain_grads + core_swap(gain_grads)
+    query_home.got = chain.enter(query_home.got)
+    chain.leave(query_home.along())
+    gain_grads = chain.leave(chain.enter(gain_grads))
     gain_grads = gain_grads + seq_swap(gain_grads)
-    b_slots = slots(chain.enter(home_b), chain.enter(home_down_b))
-    b_got = exchange_start(b_slots)
-    gain_grads = chain.enter(gain_grads)
-    gain_grads = chain.leave(gain_grads + core_swap(gain_grads))
-    early_home.got = chain.enter(early_home.got)
-    chain.leave(early_home.along())
-    b_mine = chain.leave(exchange_end(b_slots, chain.enter(b_got)))
-    a_other, b_other = seq_swap(a_mine), seq_swap(b_mine)
-
-    gain_grads = chain.leave(gain_grads + side_swap(gain_grads))
-    gain_grads = gain_grads.reshape(2, outer_count, inner_count * shard)
+    b_slots = slots(chain.enter(home_b))
+    b_mine = chain.leave(exchange_end(b_slots, chain.enter(exchange_start(b_slots))))
+    gain_grads = chain.leave(chain.enter(gain_grads))
+    b_other = seq_swap(after(b_mine, gain_grads))
+    gain_grads = gain_grads + side_swap(gain_grads)
+    query_home.got = chain.enter(query_home.got)
+    out_home.got = chain.enter(out_home.got)
+    chain.leave((query_home.final(), out_home.final()))
+
+    gain_grads = chain.leave(chain.enter(gain_grads)).reshape(2, outer_count, inner_count * shard)
     gain_sum = pick(gain_grads, outer_at, 1)
     for step in range(1, outer_count):
         piece = pick(gain_grads, lax.rem(outer_at + step, outer_count), 1)
         gain_sum = gain_sum + lax.ppermute(
             piece, "outer", [(i, (i + step) % outer_count) for i in range(outer_count)]
         )
-    gain_sum = pick(gain_sum.reshape(2, inner_count, shard), lax.axis_index("inner"), 1)
-    early_home.got = chain.enter(early_home.got)
-    chain.leave(early_home.final())
-    early_home.other = chain.enter(early_home.other)
-    early = early_home.result()
-    grad_out = chain.leave(early[:, : mixed.shape[1]])
+    gain_sum = chain.leave(pick(gain_sum.reshape(2, inner_count, shard), lax.axis_index("inner"), 1))
     parts = chain.enter((a_mine, a_other, b_mine, b_other))
-    grad_gate, grad_lift, grad_down = [unpack_experts(seq_place, parts, kind, ff) for kind in range(3)]
-    final_part = after(final_part, grad_gate, grad_lift, grad_down)
-    final_sum = final_part.astype(F32) + seq_swap(final_part).astype(F32)
-    grad_in = jnp.concatenate([early[:, mixed.shape[1] :], final_sum], axis=1)
+    grads = [unpack_experts(seq_place, parts, kind, ff) for kind in range(3)]
+    grad_gate, grad_lift, grad_down = chain.leave(lax.optimization_barrier(tuple(grads)))
+    out_home.other, query_home.other = chain.enter((out_home.other, query_home.other))
+    grad_out = chain.leave(out_home.result())
+    pair_part = chain.enter(pair_part)
+    pair_sum = pair_part.astype(F32) + seq_swap(pair_part).astype(F32)
+    grad_in = jnp.concatenate([query_home.result(), pair_sum], axis=1)
     return (
         block_output,
         grad_tokens,

time: 850 us -> 784 us (0.922)
  waiting for transfers between devices: 306 us -> 260 us
  other arithmetic: 63.5 us -> 49.1 us
  Pallas kernels: 309 us -> 318 us
    ppermute x54 -> x58, waiting for transfers between devices: 154 us -> 131 us  [swap(): lax.ppermute(x, axis, [(i, i ^ bit) for i in range(lax.axis_size(axis))])]
    ppermute x4 -> x2, waiting for transfers between devices: 28.1 us -> 12.3 us  [the longest x1 11.9 us: body(): past_a = lax.ppermute(pair_a, 'seq', [(0, 1)])]
    ppermute x1, waiting for transfers between devices: 10.5 us -> 0.01 us  [body(): lax.ppermute(jnp.concatenate([key_past_a, value_past_a], axis=1), 'seq',...]
    ppermute x1, waiting for transfers between devices: 0.01 us -> 10.1 us  [body(): lax.ppermute(jnp.concatenate([key_past_b, value_past_b], axis=1), 'seq',...]
    unnamed x88 -> x125, local copies, waits for them, and re-layouts: 19.1 us -> 10.7 us
    pallas_call x12 -> x13, Pallas kernels: 221 us -> 227 us  [the longest x8 147 us: expert_rows(): pl.pallas_call(functools.partial(expert_kernel, e, len(earlier) > 0), gri...]
    ppermute x54 -> x58, starting transfers between devices: 54.4 us -> 48.5 us  [swap(): lax.ppermute(x, axis, [(i, i ^ bit) for i in range(lax.axis_size(axis))])]
    ppermute x3 -> x6, waiting for transfers between devices: 20.5 us -> 15.8 us  [along(): lax.ppermute(piece, 'outer', [(i, (i + step) % self.n) for i in range(sel...]
  transfers between devices with their start and end apart: 74 -> 77, of which waited for: 25 -> 32; matrix products, arithmetic and copies ran while one was open for 15% -> 13% of each run, Pallas kernels for 37% -> 39%
where the time goes in v3:
time: 784 us; the launch traced here: 777 us
  Pallas kernels  318 us (41%)
  waiting for transfers between devices  260 us (33%)
  starting transfers between devices  65.6 us (8%)
  local copies, waits for them, and re-layouts  51 us (7%)
  other arithmetic  49.1 us (6%)
  matrix products  17.1 us (2%)
  between operations  16.3 us (2%)
    pallas_call x8, Pallas kernels, expert_rows(): pl.pallas_call(functools.partial(expert_kernel, e, len(earlier) > 0), gri...  147 us
    ppermute x58, waiting for transfers between devices, swap(): lax.ppermute(x, axis, [(i, i ^ bit) for i in range(lax.axis_size(axis))])  131 us
    all_gather x1, waiting for transfers between devices, body(): lax.all_gather(jnp.concatenate([attention_out, attention_in, gains], axis...  81.8 us
    pallas_call x4, Pallas kernels, expert_grad(): pl.pallas_call(expert_grad_kernel, grid=(len(lefts),), in_specs=[any_spec...  68.1 us
    ppermute x58, starting transfers between devices, swap(): lax.ppermute(x, axis, [(i, i ^ bit) for i in range(lax.axis_size(axis))])  48.5 us
    pallas_call x2, Pallas kernels, attend_back(): pl.pallas_call(attend_back_kernel, grid_spec=pltpu.PrefetchScalarGridSpec...  30 us
    convert_element_type x17, other arithmetic, low_plus(): return (a.astype(F32) + b.astype(F32)).astype(BF)  25.3 us
    pallas_call x2, Pallas kernels, attend(): pl.pallas_call(attend_kernel, grid_spec=pltpu.PrefetchScalarGridSpec(num_...  22.7 us
  transfers between devices with their start and end apart: 77, of which 32 were waited for; matrix products, arithmetic and copies ran while one was open for 13% of the time, Pallas kernels for 39%

profile of v3, /device:TPU:0, one launch (start us, length us, event | category | flops | bytes accessed | tf_op | source)
XLA Modules:
  0.0 776.7 jit_solution(7307358754248671170)
XLA Ops:
  24.6 13.9 %collective-permute-done.4 = bf16[96,1536]{1,0:T(8,128)(2,1)S(1)} collective-permute-done((bf16[96,1536]{1,0:T(8,128)(2,1)S(1)}, bf16[96,1536]{1,0:T(8,128)(2,1)S(1)}, u32[]{:S(2)}, u32[]{:S(2)}) %collective-permute-start.4) | collective-permute-done | bytes 294944 | tf_op jit(solution)/shard_map/ppermute | solution.py:39
  60.4 7.5 collective-permute-done.8
  69.2 81.8 %all-gather.4.cloned.1.call-done.weight_ref.tail_ref = bf16[1536,4224]{1,0:T(8,128)(2,1)} async-done(((bf16[96,4224]{1,0:T(8,128)(2,1)}), bf16[1536,4224]{1,0:T(8,128)(2,1)}) %all-gather.4.cloned.1.call-update) | async-done | bytes 12976144 | tf_op jit(solution)/shard_map/all_gather | solution.py:757
  151.0 10.9 %project_rows.1 = (bf16[512,1536]{1,0:T(8,128)(2,1)}, bf16[512,512]{1,0:T(8,128)(2,1)}, bf16[512,512]{1,0:T(8,128)(2,1)}, bf16[512,1536]{1,0:T(8,128)(2,1)}, f32[8,1536]{1,0:T(8,128)}) custom-call(bf16[512,1536]{1,0:T(8,128)(2,1)} %bitcast.143, bf16[1536,4224]{1,0:T(8,128)(2,1)} %all-gather.4.cloned.1.call-done.weight_ref.tail_ref, ...), custom_call_target="tpu_custom_call" | custom-call | bytes 1000 | tf_op jit(solution)/shard_map/project_rows/pallas_call | solution.py:196
  165.3 11.9 %collective-permute-done.kr_ref.vr_ref = bf16[512,512]{1,0:T(8,128)(2,1)S(1)} collective-permute-done((bf16[512,512]{1,0:T(8,128)(2,1)}, bf16[512,512]{1,0:T(8,128)(2,1)S(1)}, u32[]{:S(2)}, u32[]{:S(2)}) %collective-permute-start) | collective-permute-done | bytes 524320 | tf_op jit(solution)/shard_map/ppermute | solution.py:785
  182.5 11.1 %attend.2 = (bf16[512,1536]{1,0:T(8,128)(2,1)}, f32[2,8,512]{2,1,0:T(8,128)}) custom-call(s32[2]{0:T(128)} %pad_add_fusion.place_ref, bf16[512,1536]{1,0:T(8,128)(2,1)} %get-tuple-element.182.q_ref, bf16[512,512]{1,0:T(8,128)(2,1)} %get-tuple-element.184.k_ref.v_ref, bf16[512,512]{1,0:T(8,128)(2,1)} %get-tuple-element.184.k_ref.v_ref, ...), custom_call_target="tpu_custom_call" | custom-call | bytes 1000 | tf_op jit(solution)/shard_map/attend/pallas_call | solution.py:365
  194.9 11.5 %attend.3 = (bf16[512,1536]{1,0:T(8,128)(2,1)}, f32[2,8,512]{2,1,0:T(8,128)}) custom-call(s32[2]{0:T(128)} %pad_add_fusion.place_ref, bf16[512,1536]{1,0:T(8,128)(2,1)} %get-tuple-element.182.q_ref, bf16[512,512]{1,0:T(8,128)(2,1)} %get-tuple-element.185.k_ref.v_ref, ...), custom_call_target="tpu_custom_call", output_to_operand_aliasing={{0}: (6, {})} | custom-call | bytes 1000 | tf_op jit(solution)/shard_map/attend/pallas_call | solution.py:365
  206.4 8.9 %merge_rows.1 = (f32[512,1536]{1,0:T(8,128)}, bf16[512,1536]{1,0:T(8,128)(2,1)}) custom-call(bf16[512,1536]{1,0:T(8,128)(2,1)} %get-tuple-element.299.mixed_ref, bf16[1536,4224]{1,0:T(8,128)(2,1)} %all-gather.4.cloned.1.call-done.weight_ref.tail_ref, bf16[512,1536]{1,0:T(8,128)(2,1)} %bitcast.144, f32[8,1536]{1,0:T(8,128)} %get-tuple-element.189.gain_ref), custom_call_target="tpu_custom_call" | custom-call | bytes 1000 | tf_op jit(solution)/shard_map/merge_rows/pallas_call | solution.py:247
  215.4 9.4 %collective-permute-start.10 = (bf16[512,1536]{1,0:T(8,128)(2,1)}, bf16[512,1536]{1,0:T(8,128)(2,1)S(1)}, u32[]{:S(2)}, u32[]{:S(2)}) collective-permute-start(bf16[512,1536]{1,0:T(8,128)(2,1)} %get-tuple-element.191.refs_0_), channel_id=1, source_target_pairs={{0,16},{16,0},{1,17},{17,1},{2,18},{18,2},{3,19},{19,3},{4,20},{20... | collective-permute-start | bytes 4718600 | tf_op jit(solution)/shard_map/ppermute | solution.py:39
  231.8 9.0 %all-gather.6.cloned.1.call-done.refs_4_ = bf16[1536,1536]{1,0:T(8,128)(2,1)} async-done(((bf16[384,1536]{1,0:T(8,128)(2,1)}), bf16[1536,1536]{1,0:T(8,128)(2,1)}) %all-gather.6.cloned.1.call-update) | async-done | bytes 4718608 | tf_op jit(solution)/shard_map/all_gather | solution.py:766
  240.8 17.9 %expert_rows.8 = (bf16[4096,512]{1,0:T(8,128)(2,1)}, bf16[4096,1024]{1,0:T(8,128)(2,1)}, bf16[512,1664]{1,0:T(8,128)(2,1)}, bf16[512,1664]{1,0:T(8,128)(2,1)}, b...) custom-call(s32[2]{0:T(128)} %pad_add_fusion.1.place_ref, bf16[512,1536]{1,0:T(8,128)(2,1)} %get-tuple-element.191.refs_0_, ...), custom_call_target="tpu_custom_call" | custom-call | flops 600000000 | bytes 1000 | tf_op jit(solution)/shard_map/expert_rows/pallas_call | solution.py:643
  275.2 17.8 %expert_rows.9 = (bf16[4096,512]{1,0:T(8,128)(2,1)}, bf16[4096,1024]{1,0:T(8,128)(2,1)}, bf16[512,1664]{1,0:T(8,128)(2,1)}, bf16[512,1664]{1,0:T(8,128)(2,1)}, b...) custom-call(s32[2]{0:T(128)} %pad_add_fusion.1.place_ref, ...), custom_call_target="tpu_custom_call", output_to_operand_aliasing={{0}: (6, {}), {1}: (7, {})} | custom-call | flops 600000000 | bytes 1000 | tf_op jit(solution)/shard_map/expert_rows/pallas_call | solution.py:643
  293.0 18.0 %expert_rows.10 = (bf16[4096,512]{1,0:T(8,128)(2,1)}, bf16[4096,1024]{1,0:T(8,128)(2,1)}, bf16[512,1664]{1,0:T(8,128)(2,1)}, bf16[512,1664]{1,0:T(8,128)(2,1)}, ...) custom-call(s32[2]{0:T(128)} %pad_add_fusion.1.place_ref, ...), custom_call_target="tpu_custom_call", output_to_operand_aliasing={{0}: (6, {}), {1}: (7, {})} | custom-call | flops 600000000 | bytes 1000 | tf_op jit(solution)/shard_map/expert_rows/pallas_call | solution.py:643
  321.5 17.8 %expert_rows.11 = (bf16[4096,512]{1,0:T(8,128)(2,1)}, bf16[4096,1024]{1,0:T(8,128)(2,1)}, bf16[512,1664]{1,0:T(8,128)(2,1)}, bf16[512,1664]{1,0:T(8,128)(2,1)}, ...) custom-call(s32[2]{0:T(128)} %pad_add_fusion.1.place_ref, ...), custom_call_target="tpu_custom_call", output_to_operand_aliasing={{0}: (6, {}), {1}: (7, {})} | custom-call | flops 600000000 | bytes 1000 | tf_op jit(solution)/shard_map/expert_rows/pallas_call | solution.py:643
  339.3 19.9 %expert_grad.4.refs_9_ = bf16[1536,1536]{1,0:T(8,128)(2,1)} custom-call(bf16[512,1536]{1,0:T(8,128)(2,1)} %get-tuple-element.191.refs_0_, bf16[512,1536]{1,0:T(8,128)(2,1)} %collective-permute-done.2.refs_1_, bf16[512,1536]{1,0:T(8,128)(2,1)} %copy-done.3, bf16[512,1536]{1,0:T(8,128)(2,1)} %copy-done.5, ...), custom_call_target="tpu_custom_call" | custom-call | flops 600000000 | bytes 1000 | tf_op jit(solution)/shard_map/expert_grad/pallas_call | solution.py:700
  359.2 14.2 %expert_grad.5 = bf16[1536,1536]{1,0:T(8,128)(2,1)} custom-call(bf16[512,1664]{1,0:T(8,128)(2,1)} %concatenate.50.refs_2_.refs_0_, bf16[512,1664]{1,0:T(8,128)(2,1)} %collective-permute-done.9.refs_3_.refs_1_, bf16[512,1664]{1,0:T(8,128)(2,1)} %copy-done.2, bf16[512,1664]{1,0:T(8,128)(2,1)} %collective-permute-done.14.refs_3_, ...), custom_call_target="tpu_custom_call", output_to_operand_aliasing={{}: (9, {})} | custom-call | flops 600000000 | bytes 1000 | tf_op jit(solution)/shard_map/expert_grad/pallas_call | solution.py:700
  373.4 18.4 %expert_rows.12 = (bf16[4096,512]{1,0:T(8,128)(2,1)}, bf16[4096,1024]{1,0:T(8,128)(2,1)}, bf16[512,1664]{1,0:T(8,128)(2,1)}, bf16[512,1664]{1,0:T(8,128)(2,1)}, ...) custom-call(s32[2]{0:T(128)} %pad_add_fusion.1.place_ref, bf16[512,1536]{1,0:T(8,128)(2,1)} %copy-done.4, ...), custom_call_target="tpu_custom_call" | custom-call | flops 600000000 | bytes 1000 | tf_op jit(solution)/shard_map/expert_rows/pallas_call | solution.py:643
  392.4 19.5 %expert_rows.13 = (bf16[4096,512]{1,0:T(8,128)(2,1)}, bf16[4096,1024]{1,0:T(8,128)(2,1)}, bf16[512,1664]{1,0:T(8,128)(2,1)}, bf16[512,1664]{1,0:T(8,128)(2,1)}, ...) custom-call(s32[2]{0:T(128)} %pad_add_fusion.1.place_ref, ...), custom_call_target="tpu_custom_call", output_to_operand_aliasing={{0}: (10, {}), {1}: (11, {})} | custom-call | flops 600000000 | bytes 1000 | tf_op jit(solution)/shard_map/expert_rows/pallas_call | solution.py:643
  419.9 18.6 %expert_rows.14 = (bf16[4096,512]{1,0:T(8,128)(2,1)}, bf16[4096,1024]{1,0:T(8,128)(2,1)}, bf16[512,1664]{1,0:T(8,128)(2,1)}, bf16[512,1664]{1,0:T(8,128)(2,1)}, ...) custom-call(s32[2]{0:T(128)} %pad_add_fusion.1.place_ref, ...), custom_call_target="tpu_custom_call", output_to_operand_aliasing={{0}: (10, {}), {1}: (11, {})} | custom-call | flops 8999999488 | bytes 1000 | tf_op jit(solution)/shard_map/expert_rows/pallas_call | solution.py:643
  445.1 18.6 %expert_rows.15 = (bf16[4096,512]{1,0:T(8,128)(2,1)}, bf16[4096,1024]{1,0:T(8,128)(2,1)}, bf16[512,1664]{1,0:T(8,128)(2,1)}, bf16[512,1664]{1,0:T(8,128)(2,1)}, ...) custom-call(s32[2]{0:T(128)} %pad_add_fusion.1.place_ref, ...), custom_call_target="tpu_custom_call", output_to_operand_aliasing={{0}: (10, {}), {1}: (11, {})} | custom-call | flops 8999999488 | bytes 1000 | tf_op jit(solution)/shard_map/expert_rows/pallas_call | solution.py:643
  477.6 19.6 %expert_grad.6.refs_9_ = bf16[1536,1536]{1,0:T(8,128)(2,1)} custom-call(bf16[512,1536]{1,0:T(8,128)(2,1)} %get-tuple-element.191.refs_0_, bf16[512,1536]{1,0:T(8,128)(2,1)} %collective-permute-done.2.refs_1_, bf16[512,1536]{1,0:T(8,128)(2,1)} %copy-done.3, bf16[512,1536]{1,0:T(8,128)(2,1)} %copy-done.5, ...), custom_call_target="tpu_custom_call" | custom-call | flops 600000000 | bytes 1000 | tf_op jit(solution)/shard_map/expert_grad/pallas_call | solution.py:700
  497.2 14.4 %expert_grad.7 = bf16[1536,1536]{1,0:T(8,128)(2,1)} custom-call(bf16[512,1664]{1,0:T(8,128)(2,1)} %concatenate.50.refs_2_.refs_0_, bf16[512,1664]{1,0:T(8,128)(2,1)} %collective-permute-done.9.refs_3_.refs_1_, bf16[512,1664]{1,0:T(8,128)(2,1)} %copy-done.2, bf16[512,1664]{1,0:T(8,128)(2,1)} %collective-permute-done.14.refs_3_, ...), custom_call_target="tpu_custom_call", output_to_operand_aliasing={{}: (9, {})} | custom-call | flops 600000000 | bytes 1000 | tf_op jit(solution)/shard_map/expert_grad/pallas_call | solution.py:700
  511.6 12.7 %middle_back.1 = (f32[512,1536]{1,0:T(8,128)}, bf16[512,1536]{1,0:T(8,128)(2,1)}, bf16[512,1536]{1,0:T(8,128)(2,1)}, f32[8,1536]{1,0:T(8,128)}) custom-call(bf16[512,1536]{1,0:T(8,128)(2,1)} %get-tuple-element.266.own_ref, bf16[512,1536]{1,0:T(8,128)(2,1)} %collective-permute-done.36.got_ref, bf16[512,1536]{1,0:T(8,128)(2,1)} %collective-permute-done.32.across_ref, ...), custom_call_target="tpu_custom_call" | custom-call | flops 600000000 | bytes 1000 | tf_op jit(solution)/shard_map/middle_back/pallas_call | solution.py:290
  535.1 14.8 %attend_back.2 = (bf16[512,768]{1,0:T(8,128)(2,1)}, bf16[512,256]{1,0:T(8,128)(2,1)}, bf16[512,256]{1,0:T(8,128)(2,1)}, bf16[512,256]{1,0:T(8,128)(2,1)}, bf16[512,256]{1,0:T(8,128)(2,1)}) custom-call(s32[2]{0:T(128)} %pad_add_fusion.place_ref, bf16[512,1536]{1,0:T(8,128)(2,1)} %get-tuple-element.182.q_ref, bf16[512,512]{1,0:T(8,128)(2,1)} %get-tuple-element.184.k_ref.v_ref, ...), custom_call_target="tpu_custom_call" | custom-call | flops 14400000000 | bytes 1000 | tf_op jit(solution)/shard_map/attend_back/pallas_call | solution.py:484
  558.5 12.9 %collective-permute-done.37 = bf16[512,1664]{1,0:T(8,128)(2,1)} collective-permute-done((bf16[512,1664]{1,0:T(8,128)(2,1)}, bf16[512,1664]{1,0:T(8,128)(2,1)}, u32[]{:S(2)}, u32[]{:S(2)}) %collective-permute-start.37) | collective-permute-done | bytes 1703968 | tf_op jit(solution)/shard_map/ppermute | solution.py:39
  598.0 15.2 %attend_back.3 = (bf16[512,768]{1,0:T(8,128)(2,1)}, bf16[512,256]{1,0:T(8,128)(2,1)}, bf16[512,256]{1,0:T(8,128)(2,1)}, bf16[512,256]{1,0:T(8,128)(2,1)}, bf16[512,256]{1,0:T(8,128)(2,1)}) custom-call(s32[2]{0:T(128)} %pad_add_fusion.place_ref, bf16[512,1536]{1,0:T(8,128)(2,1)} %get-tuple-element.182.q_ref, bf16[512,512]{1,0:T(8,128)(2,1)} %get-tuple-element.185.k_ref.v_ref, ...), custom_call_target="tpu_custom_call" | custom-call | flops 14400000000 | bytes 1000 | tf_op jit(solution)/shard_map/attend_back/pallas_call | solution.py:484
  640.9 10.1 %collective-permute-done.45 = bf16[512,512]{1,0:T(8,128)(2,1)S(1)} collective-permute-done((bf16[512,512]{1,0:T(8,128)(2,1)S(1)}, bf16[512,512]{1,0:T(8,128)(2,1)S(1)}, u32[]{:S(2)}, u32[]{:S(2)}) %collective-permute-start.45) | collective-permute-done | bytes 524320 | tf_op jit(solution)/shard_map/ppermute | solution.py:908
  660.1 7.7 fusion
  667.8 11.2 %collective-permute-done.50 = bf16[4,96,1536]{2,1,0:T(8,128)(2,1)} collective-permute-done((bf16[4,96,1536]{2,1,0:T(8,128)(2,1)}, bf16[4,96,1536]{2,1,0:T(8,128)(2,1)}, u32[]{:S(2)}, u32[]{:S(2)}) %collective-permute-start.50) | collective-permute-done | bytes 1179680 | tf_op jit(solution)/shard_map/ppermute | solution.py:39
  687.0 11.6 %collective-permute-done.52 = bf16[4,96,768]{2,1,0:T(8,128)(2,1)S(1)} collective-permute-done((bf16[4,96,768]{2,1,0:T(8,128)(2,1)S(1)}, bf16[4,96,768]{2,1,0:T(8,128)(2,1)S(1)}, u32[]{:S(2)}, u32[]{:S(2)}) %collective-permute-start.52) | collective-permute-done | bytes 589856 | tf_op jit(solution)/shard_map/ppermute | solution.py:39
  709.5 8.4 %collective-permute-done.55 = bf16[96,1536]{1,0:T(8,128)(2,1)} collective-permute-done((bf16[96,1536]{1,0:T(8,128)(2,1)S(1)}, bf16[96,1536]{1,0:T(8,128)(2,1)}, u32[]{:S(2)}, u32[]{:S(2)}) %collective-permute-start.55) | collective-permute-done | bytes 294944 | tf_op jit(solution)/shard_map/ppermute | solution.py:39
  727.2 9.8 %collective-permute-done.59 = bf16[96,768]{1,0:T(8,128)(2,1)S(1)} collective-permute-done((bf16[96,768]{1,0:T(8,128)(2,1)S(1)}, bf16[96,768]{1,0:T(8,128)(2,1)S(1)}, u32[]{:S(2)}, u32[]{:S(2)}) %collective-permute-start.59) | collective-permute-done | bytes 147488 | tf_op jit(solution)/shard_map/ppermute | solution.py:119
  (388 shorter events, 255.4 us)
Async XLA Ops:
  7.2 143.8 %all-gather.4.cloned.1.call-start = ((), (), s32[]{:S(2)}) async-start(), calls=%async_computation.3 | async-start | bytes 13787136 | tf_op jit(solution)/shard_map/all_gather | solution.py:757
  10.9 229.9 %all-gather.6.cloned.1.call-start = ((), (), s32[]{:S(2)}) async-start(), calls=%async_computation.4 | async-start | bytes 5898240 | tf_op jit(solution)/shard_map/all_gather | solution.py:766
  46.5 326.9 %all-gather.8.cloned.1.call-start = ((), (), s32[]{:S(2)}) async-start(), calls=%async_computation.5 | async-start | bytes 5898240 | tf_op jit(solution)/shard_map/all_gather | solution.py:767
  67.9 147.5 %collective-permute-start.17 = (bf16[512,1664]{1,0:T(8,128)(2,1)}, bf16[512,1664]{1,0:T(8,128)(2,1)}, u32[]{:S(2)}, u32[]{:S(2)}) collective-permute-start(bf16[512,1664]{1,0:T(8,128)(2,1)} %concatenate.50.refs_2_.refs_0_), channel_id=1, source_target_pairs={{0,2},{1,3},{2,0},{3,1},{4,6},{5,7},{6,4},{7,5},{8,10},{9,11},{10,... | collective-permute-start | bytes 5111816 | tf_op jit(solution)/shard_map/ppermute | solution.py:39
  181.5 396.6 %reduce-scatter.4.cloned.1.call-start = ((), (), s32[]{:S(2)}) async-start(), calls=%async_computation.6 | async-start | bytes 5898240 | tf_op jit(solution)/shard_map/reduce_scatter | solution.py:827
  181.8 48.9 %collective-permute-start.13 = (bf16[512,1664]{1,0:T(8,128)(2,1)}, bf16[512,1664]{1,0:T(8,128)(2,1)S(1)}, u32[]{:S(2)}, u32[]{:S(2)}) collective-permute-start(bf16[512,1664]{1,0:T(8,128)(2,1)} %concatenate.50.refs_2_.refs_0_), channel_id=1, source_target_pairs={{0,16},{16,0},{1,17},{17,1},{2,18},{18,2},{3,19},{19,3},{4,20},{20... | collective-permute-start | bytes 5111816 | tf_op jit(solution)/shard_map/ppermute | solution.py:39
  181.8 48.8 %collective-permute-start.9 = (bf16[512,1664]{1,0:T(8,128)(2,1)}, bf16[512,1664]{1,0:T(8,128)(2,1)}, u32[]{:S(2)}, u32[]{:S(2)}) collective-permute-start(bf16[512,1664]{1,0:T(8,128)(2,1)} %concatenate.50.refs_2_.refs_0_), channel_id=1, source_target_pairs={{0,1},{1,0},{2,3},{3,2},{4,5},{5,4},{6,7},{7,6},{8,9},{9,8},{10,11... | collective-permute-start | bytes 5111816 | tf_op jit(solution)/shard_map/ppermute | solution.py:39
  215.4 43.3 %collective-permute-start.11 = (bf16[512,1536]{1,0:T(8,128)(2,1)}, bf16[512,1536]{1,0:T(8,128)(2,1)}, u32[]{:S(2)}, u32[]{:S(2)}) collective-permute-start(bf16[512,1536]{1,0:T(8,128)(2,1)} %get-tuple-element.191.refs_0_), channel_id=1, source_target_pairs={{0,2},{1,3},{2,0},{3,1},{4,6},{5,7},{6,4},{7,5},{8,10},{9,11},{10,... | collective-permute-start | bytes 4718600 | tf_op jit(solution)/shard_map/ppermute | solution.py:39
  215.4 47.5 %collective-permute-start.10 = (bf16[512,1536]{1,0:T(8,128)(2,1)}, bf16[512,1536]{1,0:T(8,128)(2,1)S(1)}, u32[]{:S(2)}, u32[]{:S(2)}) collective-permute-start(bf16[512,1536]{1,0:T(8,128)(2,1)} %get-tuple-element.191.refs_0_), channel_id=1, source_target_pairs={{0,16},{16,0},{1,17},{17,1},{2,18},{18,2},{3,19},{19,3},{4,20},{20... | collective-permute-start | bytes 4718600 | tf_op jit(solution)/shard_map/ppermute | solution.py:39
  230.6 35.9 %collective-permute-start.21 = (bf16[512,1664]{1,0:T(8,128)(2,1)}, bf16[512,1664]{1,0:T(8,128)(2,1)}, u32[]{:S(2)}, u32[]{:S(2)}) collective-permute-start(bf16[512,1664]{1,0:T(8,128)(2,1)} %collective-permute-done.17.refs_2_.refs_4_), channel_id=1, source_target_pairs={{0,1},{1,0},{2,3},{3,2},{4,5},{5,4},{6,7},{7,6},{8,9},{9,8},{10,11... | collective-permute-start | bytes 5111816 | tf_op jit(solution)/shard_map/ppermute | solution.py:39
  230.6 41.3 %collective-permute-start.14 = (bf16[512,1664]{1,0:T(8,128)(2,1)S(1)}, bf16[512,1664]{1,0:T(8,128)(2,1)}, u32[]{:S(2)}, u32[]{:S(2)}) collective-permute-start(bf16[512,1664]{1,0:T(8,128)(2,1)S(1)} %collective-permute-done.13.refs_2_), channel_id=1, source_target_pairs={{0,1},{1,0},{2,3},{3,2},{4,5},{5,4},{6,7},{7,6},{8,9},{9,8},{10,11... | collective-permute-start | bytes 5111816 | tf_op jit(solution)/shard_map/ppermute | solution.py:39
  262.9 30.1 %collective-permute-start.20 = (bf16[512,1536]{1,0:T(8,128)(2,1)}, bf16[512,1536]{1,0:T(8,128)(2,1)}, u32[]{:S(2)}, u32[]{:S(2)}) collective-permute-start(bf16[512,1536]{1,0:T(8,128)(2,1)} %collective-permute-done.11.refs_0_.refs_4_), channel_id=1, source_target_pairs={{0,1},{1,0},{2,3},{3,2},{4,5},{5,4},{6,7},{7,6},{8,9},{9,8},{10,11... | collective-permute-start | bytes 4718600 | tf_op jit(solution)/shard_map/ppermute | solution.py:39
  266.5 44.5 %collective-permute-start.19 = (bf16[256,1664]{1,0:T(8,128)(2,1)}, bf16[256,1664]{1,0:T(8,128)(2,1)}, u32[]{:S(2)}, u32[]{:S(2)}) collective-permute-start(bf16[256,1664]{1,0:T(8,128)(2,1)} %slice.90), channel_id=1, source_target_pairs={{0,2},{1,3},{2,0},{3,1},{4,6},{5,7},{6,4},{7,5},{8,10},{9,11},{10,... | collective-permute-start | bytes 2555912 | tf_op jit(solution)/shard_map/ppermute | solution.py:39
  266.5 44.5 %collective-permute-start.18 = (bf16[256,1664]{1,0:T(8,128)(2,1)}, bf16[256,1664]{1,0:T(8,128)(2,1)}, u32[]{:S(2)}, u32[]{:S(2)}) collective-permute-start(bf16[256,1664]{1,0:T(8,128)(2,1)} %slice.89), channel_id=1, source_target_pairs={{0,16},{16,0},{1,17},{17,1},{2,18},{18,2},{3,19},{19,3},{4,20},{20... | collective-permute-start | bytes 2555912 | tf_op jit(solution)/shard_map/ppermute | solution.py:39
  271.9 39.0 %collective-permute-start.15 = (bf16[256,1536]{1,0:T(8,128)(2,1)}, bf16[256,1536]{1,0:T(8,128)(2,1)S(1)}, u32[]{:S(2)}, u32[]{:S(2)}) collective-permute-start(bf16[256,1536]{1,0:T(8,128)(2,1)} %slice.87), channel_id=1, source_target_pairs={{0,16},{16,0},{1,17},{17,1},{2,18},{18,2},{3,19},{19,3},{4,20},{20... | collective-permute-start | bytes 2359304 | tf_op jit(solution)/shard_map/ppermute | solution.py:39
  273.2 37.8 %collective-permute-start.16 = (bf16[256,1536]{1,0:T(8,128)(2,1)}, bf16[256,1536]{1,0:T(8,128)(2,1)S(1)}, u32[]{:S(2)}, u32[]{:S(2)}) collective-permute-start(bf16[256,1536]{1,0:T(8,128)(2,1)} %slice.88), channel_id=1, source_target_pairs={{0,2},{1,3},{2,0},{3,1},{4,6},{5,7},{6,4},{7,5},{8,10},{9,11},{10,... | collective-permute-start | bytes 2359304 | tf_op jit(solution)/shard_map/ppermute | solution.py:39
  392.4 306.4 %reduce-scatter.6.cloned.1.call-start = ((), (), s32[]{:S(2)}) async-start(), calls=%async_computation.7 | async-start | bytes 5898240 | tf_op jit(solution)/shard_map/reduce_scatter | solution.py:827
  412.0 27.1 %collective-permute-start.25 = (bf16[512,1664]{1,0:T(8,128)(2,1)}, bf16[512,1664]{1,0:T(8,128)(2,1)S(1)}, u32[]{:S(2)}, u32[]{:S(2)}) collective-permute-start(bf16[512,1664]{1,0:T(8,128)(2,1)} %get-tuple-element.235), channel_id=1, source_target_pairs={{0,1},{1,0},{2,3},{3,2},{4,5},{5,4},{6,7},{7,6},{8,9},{9,8},{10,11... | collective-permute-start | bytes 5111816 | tf_op jit(solution)/shard_map/ppermute | solution.py:39
  463.7 47.9 %collective-permute-start.36 = (bf16[512,1536]{1,0:T(8,128)(2,1)}, bf16[512,1536]{1,0:T(8,128)(2,1)}, u32[]{:S(2)}, u32[]{:S(2)}) collective-permute-start(bf16[512,1536]{1,0:T(8,128)(2,1)} %get-tuple-element.278), channel_id=1, source_target_pairs={{0,1},{1,0},{2,3},{3,2},{4,5},{5,4},{6,7},{7,6},{8,9},{9,8},{10,11... | collective-permute-start | bytes 4718600 | tf_op jit(solution)/shard_map/ppermute | solution.py:39
  463.8 47.8 %collective-permute-start.32 = (bf16[512,1536]{1,0:T(8,128)(2,1)}, bf16[512,1536]{1,0:T(8,128)(2,1)}, u32[]{:S(2)}, u32[]{:S(2)}) collective-permute-start(bf16[512,1536]{1,0:T(8,128)(2,1)} %pad_maximum_fusion.3), channel_id=1, source_target_pairs={{0,16},{16,0},{1,17},{17,1},{2,18},{18,2},{3,19},{19,3},{4,20},{20... | collective-permute-start | bytes 4718600 | tf_op jit(solution)/shard_map/ppermute | solution.py:39
  471.4 40.2 %collective-permute-start.35 = (bf16[512,1536]{1,0:T(8,128)(2,1)}, bf16[512,1536]{1,0:T(8,128)(2,1)}, u32[]{:S(2)}, u32[]{:S(2)}) collective-permute-start(bf16[512,1536]{1,0:T(8,128)(2,1)} %pad_maximum_fusion.4), channel_id=1, source_target_pairs={{0,2},{1,3},{2,0},{3,1},{4,6},{5,7},{6,4},{7,5},{8,10},{9,11},{10,... | collective-permute-start | bytes 4718600 | tf_op jit(solution)/shard_map/ppermute | solution.py:39
  474.3 52.2 %collective-permute-start.31 = (bf16[256,1664]{1,0:T(8,128)(2,1)}, bf16[256,1664]{1,0:T(8,128)(2,1)}, u32[]{:S(2)}, u32[]{:S(2)}) collective-permute-start(bf16[256,1664]{1,0:T(8,128)(2,1)} %get-tuple-element.360), channel_id=1, source_target_pairs={{0,2},{1,3},{2,0},{3,1},{4,6},{5,7},{6,4},{7,5},{8,10},{9,11},{10,... | collective-permute-start | bytes 2555912 | tf_op jit(solution)/shard_map/ppermute | solution.py:39
  474.8 51.7 %collective-permute-start.30 = (bf16[256,1664]{1,0:T(8,128)(2,1)}, bf16[256,1664]{1,0:T(8,128)(2,1)}, u32[]{:S(2)}, u32[]{:S(2)}) collective-permute-start(bf16[256,1664]{1,0:T(8,128)(2,1)} %get-tuple-element.361), channel_id=1, source_target_pairs={{0,16},{16,0},{1,17},{17,1},{2,18},{18,2},{3,19},{19,3},{4,20},{20... | collective-permute-start | bytes 2555912 | tf_op jit(solution)/shard_map/ppermute | solution.py:39
  531.6 39.8 %collective-permute-start.37 = (bf16[512,1664]{1,0:T(8,128)(2,1)}, bf16[512,1664]{1,0:T(8,128)(2,1)}, u32[]{:S(2)}, u32[]{:S(2)}) collective-permute-start(bf16[512,1664]{1,0:T(8,128)(2,1)} %get-tuple-element.288), channel_id=1, source_target_pairs={{0,16},{16,0},{1,17},{17,1},{2,18},{18,2},{3,19},{19,3},{4,20},{20... | collective-permute-start | bytes 5111816 | tf_op jit(solution)/shard_map/ppermute | solution.py:39
  533.3 38.4 %collective-permute-start.38 = (bf16[512,1664]{1,0:T(8,128)(2,1)}, bf16[512,1664]{1,0:T(8,128)(2,1)}, u32[]{:S(2)}, u32[]{:S(2)}) collective-permute-start(bf16[512,1664]{1,0:T(8,128)(2,1)} %get-tuple-element.289), channel_id=1, source_target_pairs={{0,2},{1,3},{2,0},{3,1},{4,6},{5,7},{6,4},{7,5},{8,10},{9,11},{10,... | collective-permute-start | bytes 5111816 | tf_op jit(solution)/shard_map/ppermute | solution.py:39
  535.1 36.7 %collective-permute-start.39 = (bf16[512,1664]{1,0:T(8,128)(2,1)}, bf16[512,1664]{1,0:T(8,128)(2,1)}, u32[]{:S(2)}, u32[]{:S(2)}) collective-permute-start(bf16[512,1664]{1,0:T(8,128)(2,1)} %get-tuple-element.291), channel_id=1, source_target_pairs={{0,1},{1,0},{2,3},{3,2},{4,5},{5,4},{6,7},{7,6},{8,9},{9,8},{10,11... | collective-permute-start | bytes 5111816 | tf_op jit(solution)/shard_map/ppermute | solution.py:39
  555.4 206.3 %reduce-scatter.8.cloned.1.call-start = ((), (), s32[]{:S(2)}) async-start(), calls=%async_computation.8 | async-start | bytes 3342336 | tf_op jit(solution)/shard_map/reduce_scatter | solution.py:924
  557.2 40.8 %collective-permute-start.40 = (bf16[512,512]{1,0:T(8,128)(2,1)}, bf16[512,512]{1,0:T(8,128)(2,1)S(1)}, u32[]{:S(2)}, u32[]{:S(2)}) collective-permute-start(bf16[512,512]{1,0:T(8,128)(2,1)} %pad_maximum_fusion.7), channel_id=1, source_target_pairs={{16,0},{17,1},{18,2},{19,3},{20,4},{21,5},{22,6},{23,7},{24,8},{25... | collective-permute-start | bytes 1572872 | tf_op jit(solution)/shard_map/ppermute | solution.py:890
  583.9 36.5 %collective-permute-start.46 = (bf16[4,96,1536]{2,1,0:T(8,128)(2,1)S(1)}, bf16[4,96,1536]{2,1,0:T(8,128)(2,1)}, u32[]{:S(2)}, u32[]{:S(2)}) collective-permute-start(bf16[4,96,1536]{2,1,0:T(8,128)(2,1)S(1)} %dynamic-slice_bitcast_fusion.1), channel_id=1, source_target_pairs={{0,2},{1,3},{2,0},{3,1},{4,6},{5,7},{6,4},{7,5},{8,10},{9,11},{10,... | collective-permute-start | bytes 3538952 | tf_op jit(solution)/shard_map/ppermute | solution.py:39
  597.7 27.5 %collective-permute-start.47 = (bf16[4,96,1536]{2,1,0:T(8,128)(2,1)}, bf16[4,96,1536]{2,1,0:T(8,128)(2,1)}, u32[]{:S(2)}, u32[]{:S(2)}) collective-permute-start(bf16[4,96,1536]{2,1,0:T(8,128)(2,1)} %bitcast_dynamic-update-slice_fusion.3.refs_0_), channel_id=1, source_target_pairs={{0,16},{16,0},{1,17},{17,1},{2,18},{18,2},{3,19},{19,3},{4,20},{20... | collective-permute-start | bytes 3538952 | tf_op jit(solution)/shard_map/ppermute | solution.py:39
  635.7 44.9 %collective-permute-start.49 = (bf16[4,96,768]{2,1,0:T(8,128)(2,1)S(1)}, bf16[4,96,768]{2,1,0:T(8,128)(2,1)}, u32[]{:S(2)}, u32[]{:S(2)}) collective-permute-start(bf16[4,96,768]{2,1,0:T(8,128)(2,1)S(1)} %constant_dynamic-slice_fusion.7), channel_id=1, source_target_pairs={{0,16},{16,0},{1,17},{17,1},{2,18},{18,2},{3,19},{19,3},{4,20},{20... | collective-permute-start | bytes 1769480 | tf_op jit(solution)/shard_map/ppermute | solution.py:39
  719.9 29.0 %collective-permute-start.69 = (bf16[4,96,1536]{2,1,0:T(8,128)(2,1)S(1)}, bf16[4,96,1536]{2,1,0:T(8,128)(2,1)}, u32[]{:S(2)}, u32[]{:S(2)}) collective-permute-start(bf16[4,96,1536]{2,1,0:T(8,128)(2,1)S(1)} %bitcast_dynamic-update-slice_fusion.refs_2_), channel_id=1, source_target_pairs={{0,16},{16,0},{1,17},{17,1},{2,18},{18,2},{3,19},{19,3},{4,20},{20... | collective-permute-start | bytes 3538952 | tf_op jit(solution)/shard_map/ppermute | solution.py:39
  (106 other events, 1376.9 us)
Sparse Core Ops, SparseCore 0:
  11.0 139.9 all-gather.3
  153.1 87.5 all-gather.5
  242.3 87.8 all-gather.7
  392.5 83.8 reduce-scatter.3
  555.5 90.6 reduce-scatter.5
  660.2 67.7 reduce-scatter.7

commit v4 on v3

--- a/solution.py
+++ b/solution.py
@@ -506,6 +506,45 @@
     )(place, query, pair, pair, past, past, mixed, mixed_grad, stats)
 
 
+def pair_kernel(low_ref, keya_ref, keyb_ref, valuea_ref, valueb_ref, latea_ref, lateb_ref, pair_ref, grad_ref):
+    half = keya_ref.shape[1]
+    for part, (a_ref, b_ref) in enumerate(((keya_ref, keyb_ref), (valuea_ref, valueb_ref))):
+
+        @pl.when(pl.program_id(0) == part)
+        def _():
+            cols = slice(part * half, (part + 1) * half)
+            pair_ref[:, :half] = (a_ref[...].astype(F32) + latea_ref[:, cols].astype(F32)).astype(BF)
+            pair_ref[:, half:] = (b_ref[...].astype(F32) + lateb_ref[:, cols].astype(F32)).astype(BF)
+
+    grad_ref[...] = dot_tn(low_ref[...], pair_ref[...]).astype(BF)
+
+
+def pair_back(low, key_a, key_b, value_a, value_b, late_a, late_b):
+    count, width = low.shape
+    half = key_a.shape[1]
+
+    def whole(x):
+        return pl.BlockSpec(x.shape, lambda j: (0, 0))
+
+    args = (low, key_a, key_b, value_a, value_b, late_a, late_b)
+    return pl.pallas_call(
+        pair_kernel,
+        grid=(2,),
+        in_specs=[whole(x) for x in args],
+        out_specs=[
+            pl.BlockSpec((count, 2 * half), lambda j: (0, j)),
+            pl.BlockSpec((width, 2 * half), lambda j: (0, j)),
+        ],
+        out_shape=[
+            jax.ShapeDtypeStruct((count, 4 * half), BF),
+            jax.ShapeDtypeStruct((width, 4 * half), BF),
+        ],
+        compiler_params=pltpu.CompilerParams(vmem_limit_bytes=VMEM_LIMIT),
+        cost_estimate=cost(0),
+        name="pair_back",
+    )(*args)
+
+
 def pack_kernel(seq_ref, gate_ref, lift_ref, down_ref, *out_refs):
     owners, _, columns = out_refs[0].shape
     ff = columns // 3
@@ -754,9 +793,8 @@
     shard = width // (outer_count * inner_count)
     qkv = attention_in.shape[1]
     gains = jnp.concatenate([norm_first[:, None], norm_second[:, None], jnp.zeros((shard, 126), BF)], axis=1)
-    projections = lax.all_gather(
-        jnp.concatenate([attention_out, attention_in, gains], axis=1), ROWS, axis=0, tiled=True
-    )
+    project_in = lax.all_gather(jnp.concatenate([attention_in, gains], axis=1), ROWS, axis=0, tiled=True)
+    project_out = lax.all_gather(attention_out, ROWS, axis=0, tiled=True)
 
     seq_place = seq_at.astype(jnp.int32)[None]
     expert_place = jnp.stack([layer_at.astype(jnp.int32), outer_at.astype(jnp.int32)])
@@ -781,13 +819,13 @@
 
     up_pair_across = (up_across, core_swap(up_across))
     up_pair_beside = (up_beside, core_swap(up_beside))
-    query, pair_a, pair_b, lowered_one, gains = project_rows(tokens[0], projections, qkv, query_width)
+    query, pair_a, pair_b, lowered_one, gains = project_rows(tokens[0], project_in, qkv, 0)
     past_a = lax.ppermute(pair_a, "seq", [(0, 1)])
     late_pair, past_a = lax.optimization_barrier((pair_b, past_a))
     past_b = lax.ppermute(late_pair, "seq", [(0, 1)])
     mixed, stats_a = attend(place, query, pair_a, past_a, 0)
     mixed, stats_b = attend(place, query, pair_b, past_b, stats_a.shape[0], (mixed,))
-    middle, lowered_two = merge_rows(mixed, projections, tokens[0], gains)
+    middle, lowered_two = merge_rows(mixed, project_out, tokens[0], gains)
 
     across, beside, sibling = seq_swap(lowered_two), side_swap(lowered_two), core_swap(lowered_two)
 
@@ -800,15 +838,16 @@
     def lower(block, more):
         return jnp.concatenate([block[:half], low_plus(block[half:], more)])
 
+    lowered_two, across, beside, up_beside, up_across = lax.optimization_barrier(
+        (lowered_two, across, beside, up_beside, up_across)
+    )
     row_own, up_own = (lowered_two, sibling), (up_block, up_sibling)
-    made_own = experts(0, 0, row_own, up_own, ())
-    across, beside, held = lax.optimization_barrier((across, beside, made_own[:2]))
     far_top, far_low = seq_swap(beside[:half]), side_swap(across[half:])
-    up_beside_far, up_across_far = after((up_beside, up_across), held)
-    up_far_top, up_far_low = seq_swap(up_beside_far[:half]), side_swap(up_across_far[half:])
+    up_far_top, up_far_low = seq_swap(up_beside[:half]), side_swap(up_across[half:])
     row_across = (across, core_swap(across))
     row_beside = (beside, core_swap(beside))
-    made_across = experts(0, 1, row_across, up_pair_across, held)
+    made_own = experts(0, 0, row_own, up_own, ())
+    made_across = experts(0, 1, row_across, up_pair_across, made_own[:2])
     made_beside = experts(0, 2, row_beside, up_pair_beside, made_across[:2])
     far_top, far_low, up_far_top, up_far_low, held = lax.optimization_barrier(
         (far_top, far_low, up_far_top, up_far_low, made_beside[:2])
@@ -872,7 +911,7 @@
     across_in, beside_in, own_got, _ = lax.optimization_barrier((across_in, beside_in, own_got, total_b))
 
     middle_grad, branch_grad, mixed_grad, second_gain_grad = middle_back(
-        made_own[4], own_got, across_in, beside_in, middle, upstream_low, gains, projections, query_width
+        made_own[4], own_got, across_in, beside_in, middle, upstream_low, gains, project_out, query_width
     )
     second_gain_grad = second_gain_grad[0]
     chain = Chain(mixed_grad)
@@ -914,40 +953,32 @@
     query_home.got = chain.enter(query_home.got)
     chain.leave(query_home.beside())
     late_b = chain.enter(late_b)
-    split_a, split_b = key_past_a.shape[1], key_past_b.shape[1]
-    pair_own = jnp.concatenate([key_a, key_b, value_a, value_b], axis=1)
-    pair_late = jnp.concatenate(
-        [late_a[:, :split_a], late_b[:, :split_b], late_a[:, split_a:], late_b[:, split_b:]], axis=1
-    )
-    pair_grad = low_plus(pair_own, pair_late)
-    pair_weight = chain.leave(dot_tn(lowered_one, pair_grad).astype(BF))
+    pair_grad, pair_weight = chain.leave(
+        pair_back(chain.enter(lowered_one), key_a, key_b, value_a, value_b, late_a, late_b)
+    )
     pair_part = lax.psum_scatter(pair_weight, ROWS, scatter_dimension=0, tiled=True)
-    projected_grad = jnp.concatenate([query_grad, pair_grad], axis=1)
-    normed_grad_one = chain.leave(
-        dot_nt(chain.enter(projected_grad), projections[:, query_width : query_width + qkv])
-    )
     query_home.got = chain.enter(query_home.got)
     chain.leave(query_home.across())
-    out_home.got = chain.enter(out_home.got)
-    chain.leave(out_home.along())
+    b_slots = slots(chain.enter(home_b))
+    b_got = exchange_start(b_slots)
+    projected_grad = jnp.concatenate([query_grad, pair_grad], axis=1)
+    normed_grad_one = chain.leave(dot_nt(chain.enter(projected_grad), project_in[:, :qkv]))
+    query_home.got = chain.enter(query_home.got)
+    chain.leave(query_home.along())
+    b_mine = chain.leave(exchange_end(b_slots, chain.enter(b_got)))
     normed_one, inverse_one, _ = norm_rows(inputs, gains[0])
     input_norm_grad, first_gain_grad = norm_back(chain.enter(normed_grad_one), normed_one, inverse_one, gains[0])
     grad_tokens = chain.leave(middle_grad + input_norm_grad)[None]
+    b_other = seq_swap(b_mine)
+
     gain_grads = jnp.stack([first_gain_grad, second_gain_grad])
     gain_grads = gain_grads + core_swap(gain_grads)
-    query_home.got = chain.enter(query_home.got)
-    chain.leave(query_home.along())
+    out_home.got = chain.enter(out_home.got)
+    chain.leave(out_home.along())
     gain_grads = chain.leave(chain.enter(gain_grads))
-    gain_grads = gain_grads + seq_swap(gain_grads)
-    b_slots = slots(chain.enter(home_b))
-    b_mine = chain.leave(exchange_end(b_slots, chain.enter(exchange_start(b_slots))))
-    gain_grads = chain.leave(chain.enter(gain_grads))
-    b_other = seq_swap(after(b_mine, gain_grads))
     gain_grads = gain_grads + side_swap(gain_grads)
     query_home.got = chain.enter(query_home.got)
-    out_home.got = chain.enter(out_home.got)
-    chain.leave((query_home.final(), out_home.final()))
-
+    chain.leave(query_home.final())
     gain_grads = chain.leave(chain.enter(gain_grads)).reshape(2, outer_count, inner_count * shard)
     gain_sum = pick(gain_grads, outer_at, 1)
     for step in range(1, outer_count):
@@ -955,7 +986,10 @@
         gain_sum = gain_sum + lax.ppermute(
             piece, "outer", [(i, (i + step) % outer_count) for i in range(outer_count)]
         )
-    gain_sum = chain.leave(pick(gain_sum.reshape(2, inner_count, shard), lax.axis_index("inner"), 1))
+    out_home.got = chain.enter(out_home.got)
+    chain.leave(out_home.final())
+    gain_sum = chain.leave(pick(chain.enter(gain_sum).reshape(2, inner_count, shard), lax.axis_index("inner"), 1))
+    gain_sum = gain_sum + seq_swap(gain_sum)
     parts = chain.enter((a_mine, a_other, b_mine, b_other))
     grads = [unpack_experts(seq_place, parts, kind, ff) for kind in range(3)]
     grad_gate, grad_lift, grad_down = chain.leave(lax.optimization_barrier(tuple(grads)))

time: 784 us -> 763 us (0.973)
  waiting for transfers between devices: 260 us -> 226 us
  starting transfers between devices: 65.6 us -> 77.7 us
    all_gather x1 -> x2, waiting for transfers between devices: 81.8 us -> 53.3 us  [the longest x1 51.1 us: body(): lax.all_gather(jnp.concatenate([attention_in, gains], axis=1), ROWS, axis...]
    ppermute x58, waiting for transfers between devices: 131 us -> 109 us  [swap(): lax.ppermute(x, axis, [(i, i ^ bit) for i in range(lax.axis_size(axis))])]
    all_gather x1, waiting for transfers between devices: 8.98 us -> 25.7 us  [body(): gathered = [lax.all_gather(packed[0], 'outer', axis=0, tiled=True)]]
    convert_element_type x17 -> x16, other arithmetic: 25.3 us -> 23.3 us  [low_plus(): return (a.astype(F32) + b.astype(F32)).astype(BF)]
  transfers between devices with their start and end apart: 77 -> 78, of which waited for: 32 -> 27; matrix products, arithmetic and copies ran while one was open for 13% -> 13% of each run, Pallas kernels for 39% -> 40%
where the time goes in v4:
time: 763 us; the launch traced here: 756 us
  Pallas kernels  323 us (42%)
  waiting for transfers between devices  226 us (30%)
  starting transfers between devices  77.7 us (10%)
  local copies, waits for them, and re-layouts  51.1 us (7%)
  other arithmetic  48.4 us (6%)
  between operations  16.1 us (2%)
  matrix products  13.5 us (2%)
    pallas_call x8, Pallas kernels, expert_rows(): pl.pallas_call(functools.partial(expert_kernel, e, len(earlier) > 0), gri...  146 us
    ppermute x58, waiting for transfers between devices, swap(): lax.ppermute(x, axis, [(i, i ^ bit) for i in range(lax.axis_size(axis))])  109 us
    pallas_call x4, Pallas kernels, expert_grad(): pl.pallas_call(expert_grad_kernel, grid=(len(lefts),), in_specs=[any_spec...  67.9 us
    ppermute x58, starting transfers between devices, swap(): lax.ppermute(x, axis, [(i, i ^ bit) for i in range(lax.axis_size(axis))])  52.3 us
    all_gather x1, waiting for transfers between devices, body(): lax.all_gather(jnp.concatenate([attention_in, gains], axis=1), ROWS, axis...  51.1 us
    pallas_call x2, Pallas kernels, attend_back(): pl.pallas_call(attend_back_kernel, grid_spec=pltpu.PrefetchScalarGridSpec...  30 us
    all_gather x1, waiting for transfers between devices, body(): gathered = [lax.all_gather(packed[0], 'outer', axis=0, tiled=True)]  25.7 us
    convert_element_type x16, other arithmetic, low_plus(): return (a.astype(F32) + b.astype(F32)).astype(BF)  23.3 us
  transfers between devices with their start and end apart: 78, of which 27 were waited for; matrix products, arithmetic and copies ran while one was open for 13% of the time, Pallas kernels for 40%

profile of v4, /device:TPU:0, one launch (start us, length us, event | category | flops | bytes accessed | tf_op | source)
XLA Modules:
  0.0 755.9 jit_solution(13138613905339358928)
XLA Ops:
  11.5 6.2 pack_experts.1
  25.1 11.3 %collective-permute-done.5 = bf16[96,1536]{1,0:T(8,128)(2,1)S(1)} collective-permute-done((bf16[96,1536]{1,0:T(8,128)(2,1)S(1)}, bf16[96,1536]{1,0:T(8,128)(2,1)S(1)}, u32[]{:S(2)}, u32[]{:S(2)}) %collective-permute-start.5) | collective-permute-done | bytes 294944 | tf_op jit(solution)/shard_map/ppermute | solution.py:39
  49.2 51.1 %all-gather.5.cloned.1.call-done.weight_ref.tail_ref = bf16[1536,2688]{1,0:T(8,128)(2,1)} async-done(((bf16[96,2688]{1,0:T(8,128)(2,1)}), bf16[1536,2688]{1,0:T(8,128)(2,1)}) %all-gather.5.cloned.1.call-update) | async-done | bytes 8257552 | tf_op jit(solution)/shard_map/all_gather | solution.py:796
  100.4 10.8 %project_rows.1 = (bf16[512,1536]{1,0:T(8,128)(2,1)}, bf16[512,512]{1,0:T(8,128)(2,1)}, bf16[512,512]{1,0:T(8,128)(2,1)}, bf16[512,1536]{1,0:T(8,128)(2,1)}, f32[8,1536]{1,0:T(8,128)}) custom-call(bf16[512,1536]{1,0:T(8,128)(2,1)} %bitcast.142, bf16[1536,2688]{1,0:T(8,128)(2,1)} %all-gather.5.cloned.1.call-done.weight_ref.tail_ref, ...), custom_call_target="tpu_custom_call" | custom-call | bytes 1000 | tf_op jit(solution)/shard_map/project_rows/pallas_call | solution.py:196
  117.8 8.8 %collective-permute-done.kr_ref.vr_ref = bf16[512,512]{1,0:T(8,128)(2,1)S(1)} collective-permute-done((bf16[512,512]{1,0:T(8,128)(2,1)}, bf16[512,512]{1,0:T(8,128)(2,1)S(1)}, u32[]{:S(2)}, u32[]{:S(2)}) %collective-permute-start) | collective-permute-done | bytes 524320 | tf_op jit(solution)/shard_map/ppermute | solution.py:823
  135.2 11.1 %attend.2 = (bf16[512,1536]{1,0:T(8,128)(2,1)}, f32[2,8,512]{2,1,0:T(8,128)}) custom-call(s32[2]{0:T(128)} %pad_add_fusion.place_ref, bf16[512,1536]{1,0:T(8,128)(2,1)} %get-tuple-element.183.q_ref, bf16[512,512]{1,0:T(8,128)(2,1)} %get-tuple-element.185.k_ref.v_ref, bf16[512,512]{1,0:T(8,128)(2,1)} %get-tuple-element.185.k_ref.v_ref, ...), custom_call_target="tpu_custom_call" | custom-call | bytes 1000 | tf_op jit(solution)/shard_map/attend/pallas_call | solution.py:365
  147.2 11.6 %attend.3 = (bf16[512,1536]{1,0:T(8,128)(2,1)}, f32[2,8,512]{2,1,0:T(8,128)}) custom-call(s32[2]{0:T(128)} %pad_add_fusion.place_ref, bf16[512,1536]{1,0:T(8,128)(2,1)} %get-tuple-element.183.q_ref, bf16[512,512]{1,0:T(8,128)(2,1)} %get-tuple-element.186.k_ref.v_ref, ...), custom_call_target="tpu_custom_call", output_to_operand_aliasing={{0}: (6, {})} | custom-call | bytes 1000 | tf_op jit(solution)/shard_map/attend/pallas_call | solution.py:365
  160.9 9.0 %merge_rows.1 = (f32[512,1536]{1,0:T(8,128)}, bf16[512,1536]{1,0:T(8,128)(2,1)}) custom-call(bf16[512,1536]{1,0:T(8,128)(2,1)} %get-tuple-element.299.mixed_ref, bf16[1536,1536]{1,0:T(8,128)(2,1)} %all-gather.7.cloned.1.call-done.weight_ref, bf16[512,1536]{1,0:T(8,128)(2,1)} %bitcast.143, f32[8,1536]{1,0:T(8,128)} %get-tuple-element.190.gain_ref), custom_call_target="tpu_custom_call" | custom-call | bytes 1000 | tf_op jit(solution)/shard_map/merge_rows/pallas_call | solution.py:247
  170.5 8.7 %collective-permute-start.2 = (bf16[512,1536]{1,0:T(8,128)(2,1)}, bf16[512,1536]{1,0:T(8,128)(2,1)S(1)}, u32[]{:S(2)}, u32[]{:S(2)}) collective-permute-start(bf16[512,1536]{1,0:T(8,128)(2,1)} %get-tuple-element.196.refs_0_), channel_id=1, source_target_pairs={{0,16},{16,0},{1,17},{17,1},{2,18},{18,2},{3,19},{19,3},{4,20},{20... | collective-permute-start | bytes 4718600 | tf_op jit(solution)/shard_map/ppermute | solution.py:39
  180.2 33.1 %collective-permute-done.3.refs_0_.refs_4_ = bf16[512,1536]{1,0:T(8,128)(2,1)} collective-permute-done((bf16[512,1536]{1,0:T(8,128)(2,1)}, bf16[512,1536]{1,0:T(8,128)(2,1)}, u32[]{:S(2)}, u32[]{:S(2)}) %collective-permute-start.3) | collective-permute-done | bytes 1572896 | tf_op jit(solution)/shard_map/ppermute | solution.py:39
  226.1 25.7 %all-gather.9.cloned.1.call-done.refs_4_ = bf16[1536,1536]{1,0:T(8,128)(2,1)} async-done(((bf16[384,1536]{1,0:T(8,128)(2,1)}), bf16[1536,1536]{1,0:T(8,128)(2,1)}) %all-gather.9.cloned.1.call-update) | async-done | bytes 4718608 | tf_op jit(solution)/shard_map/all_gather | solution.py:804
  251.8 17.7 %expert_rows.8 = (bf16[4096,512]{1,0:T(8,128)(2,1)}, bf16[4096,1024]{1,0:T(8,128)(2,1)}, bf16[512,1664]{1,0:T(8,128)(2,1)}, bf16[512,1664]{1,0:T(8,128)(2,1)}, b...) custom-call(s32[2]{0:T(128)} %pad_add_fusion.1.place_ref, bf16[512,1536]{1,0:T(8,128)(2,1)} %get-tuple-element.196.refs_0_, ...), custom_call_target="tpu_custom_call" | custom-call | flops 600000000 | bytes 1000 | tf_op jit(solution)/shard_map/expert_rows/pallas_call | solution.py:682
  269.5 17.8 %expert_rows.9 = (bf16[4096,512]{1,0:T(8,128)(2,1)}, bf16[4096,1024]{1,0:T(8,128)(2,1)}, bf16[512,1664]{1,0:T(8,128)(2,1)}, bf16[512,1664]{1,0:T(8,128)(2,1)}, b...) custom-call(s32[2]{0:T(128)} %pad_add_fusion.1.place_ref, ...), custom_call_target="tpu_custom_call", output_to_operand_aliasing={{0}: (6, {}), {1}: (7, {})} | custom-call | flops 600000000 | bytes 1000 | tf_op jit(solution)/shard_map/expert_rows/pallas_call | solution.py:682
  287.3 18.0 %expert_rows.10 = (bf16[4096,512]{1,0:T(8,128)(2,1)}, bf16[4096,1024]{1,0:T(8,128)(2,1)}, bf16[512,1664]{1,0:T(8,128)(2,1)}, bf16[512,1664]{1,0:T(8,128)(2,1)}, ...) custom-call(s32[2]{0:T(128)} %pad_add_fusion.1.place_ref, ...), custom_call_target="tpu_custom_call", output_to_operand_aliasing={{0}: (6, {}), {1}: (7, {})} | custom-call | flops 600000000 | bytes 1000 | tf_op jit(solution)/shard_map/expert_rows/pallas_call | solution.py:682
  315.7 17.8 %expert_rows.11 = (bf16[4096,512]{1,0:T(8,128)(2,1)}, bf16[4096,1024]{1,0:T(8,128)(2,1)}, bf16[512,1664]{1,0:T(8,128)(2,1)}, bf16[512,1664]{1,0:T(8,128)(2,1)}, ...) custom-call(s32[2]{0:T(128)} %pad_add_fusion.1.place_ref, ...), custom_call_target="tpu_custom_call", output_to_operand_aliasing={{0}: (6, {}), {1}: (7, {})} | custom-call | flops 600000000 | bytes 1000 | tf_op jit(solution)/shard_map/expert_rows/pallas_call | solution.py:682
  333.5 19.8 %expert_grad.4.refs_9_ = bf16[1536,1536]{1,0:T(8,128)(2,1)} custom-call(bf16[512,1536]{1,0:T(8,128)(2,1)} %get-tuple-element.196.refs_0_, bf16[512,1536]{1,0:T(8,128)(2,1)} %copy-done.9, bf16[512,1536]{1,0:T(8,128)(2,1)} %copy-done.3, bf16[512,1536]{1,0:T(8,128)(2,1)} %copy-done.6, bf16[512,1536]{1,0:T(8,128)(2,1)} %collective-permute-done.3.refs_0_.refs_4_, ...), custom_call_target="tpu_custom_call" | custom-call | flops 600000000 | bytes 1000 | tf_op jit(solution)/shard_map/expert_grad/pallas_call | solution.py:739
  353.4 14.1 %expert_grad.5 = bf16[1536,1536]{1,0:T(8,128)(2,1)} custom-call(bf16[512,1664]{1,0:T(8,128)(2,1)} %concatenate.44.refs_2_.refs_0_, bf16[512,1664]{1,0:T(8,128)(2,1)} %collective-permute-done.13.refs_3_.refs_1_, bf16[512,1664]{1,0:T(8,128)(2,1)} %copy-done.2, bf16[512,1664]{1,0:T(8,128)(2,1)} %copy-done.5, ...), custom_call_target="tpu_custom_call", output_to_operand_aliasing={{}: (9, {})} | custom-call | flops 600000000 | bytes 1000 | tf_op jit(solution)/shard_map/expert_grad/pallas_call | solution.py:739
  367.5 18.4 %expert_rows.12 = (bf16[4096,512]{1,0:T(8,128)(2,1)}, bf16[4096,1024]{1,0:T(8,128)(2,1)}, bf16[512,1664]{1,0:T(8,128)(2,1)}, bf16[512,1664]{1,0:T(8,128)(2,1)}, ...) custom-call(s32[2]{0:T(128)} %pad_add_fusion.1.place_ref, bf16[512,1536]{1,0:T(8,128)(2,1)} %copy-done.4, ...), custom_call_target="tpu_custom_call" | custom-call | flops 600000000 | bytes 1000 | tf_op jit(solution)/shard_map/expert_rows/pallas_call | solution.py:682
  386.6 19.6 %expert_rows.13 = (bf16[4096,512]{1,0:T(8,128)(2,1)}, bf16[4096,1024]{1,0:T(8,128)(2,1)}, bf16[512,1664]{1,0:T(8,128)(2,1)}, bf16[512,1664]{1,0:T(8,128)(2,1)}, ...) custom-call(s32[2]{0:T(128)} %pad_add_fusion.1.place_ref, ...), custom_call_target="tpu_custom_call", output_to_operand_aliasing={{0}: (10, {}), {1}: (11, {})} | custom-call | flops 600000000 | bytes 1000 | tf_op jit(solution)/shard_map/expert_rows/pallas_call | solution.py:682
  414.7 18.5 %expert_rows.14 = (bf16[4096,512]{1,0:T(8,128)(2,1)}, bf16[4096,1024]{1,0:T(8,128)(2,1)}, bf16[512,1664]{1,0:T(8,128)(2,1)}, bf16[512,1664]{1,0:T(8,128)(2,1)}, ...) custom-call(s32[2]{0:T(128)} %pad_add_fusion.1.place_ref, ...), custom_call_target="tpu_custom_call", output_to_operand_aliasing={{0}: (10, {}), {1}: (11, {})} | custom-call | flops 8999999488 | bytes 1000 | tf_op jit(solution)/shard_map/expert_rows/pallas_call | solution.py:682
  439.5 18.6 %expert_rows.15 = (bf16[4096,512]{1,0:T(8,128)(2,1)}, bf16[4096,1024]{1,0:T(8,128)(2,1)}, bf16[512,1664]{1,0:T(8,128)(2,1)}, bf16[512,1664]{1,0:T(8,128)(2,1)}, ...) custom-call(s32[2]{0:T(128)} %pad_add_fusion.1.place_ref, ...), custom_call_target="tpu_custom_call", output_to_operand_aliasing={{0}: (10, {}), {1}: (11, {})} | custom-call | flops 8999999488 | bytes 1000 | tf_op jit(solution)/shard_map/expert_rows/pallas_call | solution.py:682
  472.1 19.6 %expert_grad.6.refs_9_ = bf16[1536,1536]{1,0:T(8,128)(2,1)} custom-call(bf16[512,1536]{1,0:T(8,128)(2,1)} %get-tuple-element.196.refs_0_, bf16[512,1536]{1,0:T(8,128)(2,1)} %copy-done.9, bf16[512,1536]{1,0:T(8,128)(2,1)} %copy-done.3, bf16[512,1536]{1,0:T(8,128)(2,1)} %copy-done.6, bf16[512,1536]{1,0:T(8,128)(2,1)} %collective-permute-done.3.refs_0_.refs_4_, ...), custom_call_target="tpu_custom_call" | custom-call | flops 600000000 | bytes 1000 | tf_op jit(solution)/shard_map/expert_grad/pallas_call | solution.py:739
  491.7 14.4 %expert_grad.7 = bf16[1536,1536]{1,0:T(8,128)(2,1)} custom-call(bf16[512,1664]{1,0:T(8,128)(2,1)} %concatenate.44.refs_2_.refs_0_, bf16[512,1664]{1,0:T(8,128)(2,1)} %collective-permute-done.13.refs_3_.refs_1_, bf16[512,1664]{1,0:T(8,128)(2,1)} %copy-done.2, bf16[512,1664]{1,0:T(8,128)(2,1)} %copy-done.5, ...), custom_call_target="tpu_custom_call", output_to_operand_aliasing={{}: (9, {})} | custom-call | flops 600000000 | bytes 1000 | tf_op jit(solution)/shard_map/expert_grad/pallas_call | solution.py:739
  506.1 12.7 %middle_back.1 = (f32[512,1536]{1,0:T(8,128)}, bf16[512,1536]{1,0:T(8,128)(2,1)}, bf16[512,1536]{1,0:T(8,128)(2,1)}, f32[8,1536]{1,0:T(8,128)}) custom-call(bf16[512,1536]{1,0:T(8,128)(2,1)} %get-tuple-element.266.own_ref, bf16[512,1536]{1,0:T(8,128)(2,1)} %collective-permute-done.36.got_ref, bf16[512,1536]{1,0:T(8,128)(2,1)} %collective-permute-done.32.across_ref, ...), custom_call_target="tpu_custom_call" | custom-call | flops 600000000 | bytes 1000 | tf_op jit(solution)/shard_map/middle_back/pallas_call | solution.py:290
  528.3 14.8 %attend_back.2 = (bf16[512,768]{1,0:T(8,128)(2,1)}, bf16[512,256]{1,0:T(8,128)(2,1)}, bf16[512,256]{1,0:T(8,128)(2,1)}, bf16[512,256]{1,0:T(8,128)(2,1)}, bf16[512,256]{1,0:T(8,128)(2,1)}) custom-call(s32[2]{0:T(128)} %pad_add_fusion.place_ref, bf16[512,1536]{1,0:T(8,128)(2,1)} %get-tuple-element.183.q_ref, bf16[512,512]{1,0:T(8,128)(2,1)} %get-tuple-element.185.k_ref.v_ref, ...), custom_call_target="tpu_custom_call" | custom-call | flops 14400000000 | bytes 1000 | tf_op jit(solution)/shard_map/attend_back/pallas_call | solution.py:484
  551.7 14.9 %collective-permute-done.37 = bf16[512,1664]{1,0:T(8,128)(2,1)} collective-permute-done((bf16[512,1664]{1,0:T(8,128)(2,1)}, bf16[512,1664]{1,0:T(8,128)(2,1)}, u32[]{:S(2)}, u32[]{:S(2)}) %collective-permute-start.37) | collective-permute-done | bytes 1703968 | tf_op jit(solution)/shard_map/ppermute | solution.py:39
  590.9 15.2 %attend_back.3 = (bf16[512,768]{1,0:T(8,128)(2,1)}, bf16[512,256]{1,0:T(8,128)(2,1)}, bf16[512,256]{1,0:T(8,128)(2,1)}, bf16[512,256]{1,0:T(8,128)(2,1)}, bf16[512,256]{1,0:T(8,128)(2,1)}) custom-call(s32[2]{0:T(128)} %pad_add_fusion.place_ref, bf16[512,1536]{1,0:T(8,128)(2,1)} %get-tuple-element.183.q_ref, bf16[512,512]{1,0:T(8,128)(2,1)} %get-tuple-element.186.k_ref.v_ref, ...), custom_call_target="tpu_custom_call" | custom-call | flops 14400000000 | bytes 1000 | tf_op jit(solution)/shard_map/attend_back/pallas_call | solution.py:484
  606.1 7.0 collective-permute-done.45
  638.5 10.1 %collective-permute-done.48.lateb_ref = bf16[512,512]{1,0:T(8,128)(2,1)} collective-permute-done((bf16[512,512]{1,0:T(8,128)(2,1)}, bf16[512,512]{1,0:T(8,128)(2,1)}, u32[]{:S(2)}, u32[]{:S(2)}) %collective-permute-start.48) | collective-permute-done | bytes 524320 | tf_op jit(solution)/shard_map/ppermute | solution.py:947
  648.6 5.5 pair_back.1
  665.8 7.6 %fusion = f32[512,1536]{1,0:T(8,128)S(1)} fusion(bf16[512,2560]{1,0:T(8,128)(2,1)} %pad_maximum_fusion, bf16[1536,2688]{1,0:T(8,128)(2,1)} %all-gather.5.cloned.1.call-done.weight_ref.tail_ref), kind=kOutput, calls=%fused_computation | convolution fusion | flops 4026531840 | bytes 13631488 | tf_op jit(solution)/shard_map/dot_general | solution.py:151
  696.2 11.0 %collective-permute-done.58 = bf16[96,768]{1,0:T(8,128)(2,1)S(1)} collective-permute-done((bf16[96,768]{1,0:T(8,128)(2,1)S(1)}, bf16[96,768]{1,0:T(8,128)(2,1)S(1)}, u32[]{:S(2)}, u32[]{:S(2)}) %collective-permute-start.58) | collective-permute-done | bytes 147488 | tf_op jit(solution)/shard_map/ppermute | solution.py:119
  (367 shorter events, 239.1 us)
Async XLA Ops:
  7.2 93.2 %all-gather.5.cloned.1.call-start = ((), (), s32[]{:S(2)}) async-start(), calls=%async_computation.3 | async-start | bytes 8773632 | tf_op jit(solution)/shard_map/all_gather | solution.py:796
  10.7 150.3 %all-gather.7.cloned.1.call-start = ((), (), s32[]{:S(2)}) async-start(), calls=%async_computation.4 | async-start | bytes 5013504 | tf_op jit(solution)/shard_map/all_gather | solution.py:797
  11.4 240.4 %all-gather.9.cloned.1.call-start = ((), (), s32[]{:S(2)}) async-start(), calls=%async_computation.5 | async-start | bytes 5898240 | tf_op jit(solution)/shard_map/all_gather | solution.py:804
  43.1 324.4 %all-gather.11.cloned.1.call-start = ((), (), s32[]{:S(2)}) async-start(), calls=%async_computation.6 | async-start | bytes 5898240 | tf_op jit(solution)/shard_map/all_gather | solution.py:805
  45.8 68.9 %collective-permute-start.8 = (bf16[96,1536]{1,0:T(8,128)(2,1)}, bf16[96,1536]{1,0:T(8,128)(2,1)}, u32[]{:S(2)}, u32[]{:S(2)}) collective-permute-start(bf16[96,1536]{1,0:T(8,128)(2,1)} %get-tuple-element.373), channel_id=1, source_target_pairs={{0,2},{1,3},{2,0},{3,1},{4,6},{5,7},{6,4},{7,5},{8,10},{9,11},{10,... | collective-permute-start | bytes 884744 | tf_op jit(solution)/shard_map/ppermute | solution.py:39
  47.8 67.9 %collective-permute-start.9 = (bf16[96,1536]{1,0:T(8,128)(2,1)}, bf16[96,1536]{1,0:T(8,128)(2,1)}, u32[]{:S(2)}, u32[]{:S(2)}) collective-permute-start(bf16[96,1536]{1,0:T(8,128)(2,1)} %get-tuple-element.372), channel_id=1, source_target_pairs={{0,3},{1,2},{2,1},{3,0},{4,7},{5,6},{6,5},{7,4},{8,11},{9,10},{10,... | collective-permute-start | bytes 884744 | tf_op jit(solution)/shard_map/ppermute | solution.py:39
  117.8 455.2 %reduce-scatter.4.cloned.1.call-start = ((), (), s32[]{:S(2)}) async-start(), calls=%async_computation.7 | async-start | bytes 5898240 | tf_op jit(solution)/shard_map/reduce_scatter | solution.py:866
  134.2 45.0 %collective-permute-start.11 = (bf16[512,1664]{1,0:T(8,128)(2,1)}, bf16[512,1664]{1,0:T(8,128)(2,1)S(1)}, u32[]{:S(2)}, u32[]{:S(2)}) collective-permute-start(bf16[512,1664]{1,0:T(8,128)(2,1)} %concatenate.44.refs_2_.refs_0_), channel_id=1, source_target_pairs={{0,16},{16,0},{1,17},{17,1},{2,18},{18,2},{3,19},{19,3},{4,20},{20... | collective-permute-start | bytes 5111816 | tf_op jit(solution)/shard_map/ppermute | solution.py:39
  134.2 46.0 %collective-permute-start.10 = (bf16[512,1664]{1,0:T(8,128)(2,1)}, bf16[512,1664]{1,0:T(8,128)(2,1)}, u32[]{:S(2)}, u32[]{:S(2)}) collective-permute-start(bf16[512,1664]{1,0:T(8,128)(2,1)} %concatenate.44.refs_2_.refs_0_), channel_id=1, source_target_pairs={{0,2},{1,3},{2,0},{3,1},{4,6},{5,7},{6,4},{7,5},{8,10},{9,11},{10,... | collective-permute-start | bytes 5111816 | tf_op jit(solution)/shard_map/ppermute | solution.py:39
  169.9 43.4 %collective-permute-start.3 = (bf16[512,1536]{1,0:T(8,128)(2,1)}, bf16[512,1536]{1,0:T(8,128)(2,1)}, u32[]{:S(2)}, u32[]{:S(2)}) collective-permute-start(bf16[512,1536]{1,0:T(8,128)(2,1)} %get-tuple-element.196.refs_0_), channel_id=1, source_target_pairs={{0,2},{1,3},{2,0},{3,1},{4,6},{5,7},{6,4},{7,5},{8,10},{9,11},{10,... | collective-permute-start | bytes 4718600 | tf_op jit(solution)/shard_map/ppermute | solution.py:39
  170.5 42.9 %collective-permute-start.2 = (bf16[512,1536]{1,0:T(8,128)(2,1)}, bf16[512,1536]{1,0:T(8,128)(2,1)S(1)}, u32[]{:S(2)}, u32[]{:S(2)}) collective-permute-start(bf16[512,1536]{1,0:T(8,128)(2,1)} %get-tuple-element.196.refs_0_), channel_id=1, source_target_pairs={{0,16},{16,0},{1,17},{17,1},{2,18},{18,2},{3,19},{19,3},{4,20},{20... | collective-permute-start | bytes 4718600 | tf_op jit(solution)/shard_map/ppermute | solution.py:39
  179.2 34.7 %collective-permute-start.13 = (bf16[512,1664]{1,0:T(8,128)(2,1)}, bf16[512,1664]{1,0:T(8,128)(2,1)}, u32[]{:S(2)}, u32[]{:S(2)}) collective-permute-start(bf16[512,1664]{1,0:T(8,128)(2,1)} %concatenate.44.refs_2_.refs_0_), channel_id=1, source_target_pairs={{0,1},{1,0},{2,3},{3,2},{4,5},{5,4},{6,7},{7,6},{8,9},{9,8},{10,11... | collective-permute-start | bytes 5111816 | tf_op jit(solution)/shard_map/ppermute | solution.py:39
  179.2 37.9 %collective-permute-start.15 = (bf16[512,1664]{1,0:T(8,128)(2,1)S(1)}, bf16[512,1664]{1,0:T(8,128)(2,1)S(1)}, u32[]{:S(2)}, u32[]{:S(2)}) collective-permute-start(bf16[512,1664]{1,0:T(8,128)(2,1)S(1)} %collective-permute-done.11.refs_2_), channel_id=1, source_target_pairs={{0,1},{1,0},{2,3},{3,2},{4,5},{5,4},{6,7},{7,6},{8,9},{9,8},{10,11... | collective-permute-start | bytes 5111816 | tf_op jit(solution)/shard_map/ppermute | solution.py:39
  180.2 37.2 %collective-permute-start.21 = (bf16[512,1664]{1,0:T(8,128)(2,1)}, bf16[512,1664]{1,0:T(8,128)(2,1)S(1)}, u32[]{:S(2)}, u32[]{:S(2)}) collective-permute-start(bf16[512,1664]{1,0:T(8,128)(2,1)} %collective-permute-done.10.refs_2_.refs_4_), channel_id=1, source_target_pairs={{0,1},{1,0},{2,3},{3,2},{4,5},{5,4},{6,7},{7,6},{8,9},{9,8},{10,11... | collective-permute-start | bytes 5111816 | tf_op jit(solution)/shard_map/ppermute | solution.py:39
  213.9 73.5 %collective-permute-start.20 = (bf16[512,1536]{1,0:T(8,128)(2,1)}, bf16[512,1536]{1,0:T(8,128)(2,1)}, u32[]{:S(2)}, u32[]{:S(2)}) collective-permute-start(bf16[512,1536]{1,0:T(8,128)(2,1)} %collective-permute-done.3.refs_0_.refs_4_), channel_id=1, source_target_pairs={{0,1},{1,0},{2,3},{3,2},{4,5},{5,4},{6,7},{7,6},{8,9},{9,8},{10,11... | collective-permute-start | bytes 4718600 | tf_op jit(solution)/shard_map/ppermute | solution.py:39
  217.1 88.2 %collective-permute-start.19 = (bf16[256,1664]{1,0:T(8,128)(2,1)}, bf16[256,1664]{1,0:T(8,128)(2,1)S(1)}, u32[]{:S(2)}, u32[]{:S(2)}) collective-permute-start(bf16[256,1664]{1,0:T(8,128)(2,1)} %slice.76), channel_id=1, source_target_pairs={{0,2},{1,3},{2,0},{3,1},{4,6},{5,7},{6,4},{7,5},{8,10},{9,11},{10,... | collective-permute-start | bytes 2555912 | tf_op jit(solution)/shard_map/ppermute | solution.py:39
  217.5 87.9 %collective-permute-start.18 = (bf16[256,1664]{1,0:T(8,128)(2,1)}, bf16[256,1664]{1,0:T(8,128)(2,1)S(1)}, u32[]{:S(2)}, u32[]{:S(2)}) collective-permute-start(bf16[256,1664]{1,0:T(8,128)(2,1)} %slice.75), channel_id=1, source_target_pairs={{0,16},{16,0},{1,17},{17,1},{2,18},{18,2},{3,19},{19,3},{4,20},{20... | collective-permute-start | bytes 2555912 | tf_op jit(solution)/shard_map/ppermute | solution.py:39
  222.2 83.1 %collective-permute-start.16 = (bf16[256,1536]{1,0:T(8,128)(2,1)}, bf16[256,1536]{1,0:T(8,128)(2,1)}, u32[]{:S(2)}, u32[]{:S(2)}) collective-permute-start(bf16[256,1536]{1,0:T(8,128)(2,1)} %slice.73), channel_id=1, source_target_pairs={{0,16},{16,0},{1,17},{17,1},{2,18},{18,2},{3,19},{19,3},{4,20},{20... | collective-permute-start | bytes 2359304 | tf_op jit(solution)/shard_map/ppermute | solution.py:39
  223.9 81.4 %collective-permute-start.17 = (bf16[256,1536]{1,0:T(8,128)(2,1)}, bf16[256,1536]{1,0:T(8,128)(2,1)}, u32[]{:S(2)}, u32[]{:S(2)}) collective-permute-start(bf16[256,1536]{1,0:T(8,128)(2,1)} %slice.74), channel_id=1, source_target_pairs={{0,2},{1,3},{2,0},{3,1},{4,6},{5,7},{6,4},{7,5},{8,10},{9,11},{10,... | collective-permute-start | bytes 2359304 | tf_op jit(solution)/shard_map/ppermute | solution.py:39
  386.5 274.7 %reduce-scatter.6.cloned.1.call-start = ((), (), s32[]{:S(2)}) async-start(), calls=%async_computation.8 | async-start | bytes 5898240 | tf_op jit(solution)/shard_map/reduce_scatter | solution.py:866
  458.2 47.9 %collective-permute-start.36 = (bf16[512,1536]{1,0:T(8,128)(2,1)}, bf16[512,1536]{1,0:T(8,128)(2,1)}, u32[]{:S(2)}, u32[]{:S(2)}) collective-permute-start(bf16[512,1536]{1,0:T(8,128)(2,1)} %get-tuple-element.278), channel_id=1, source_target_pairs={{0,1},{1,0},{2,3},{3,2},{4,5},{5,4},{6,7},{7,6},{8,9},{9,8},{10,11... | collective-permute-start | bytes 4718600 | tf_op jit(solution)/shard_map/ppermute | solution.py:39
  458.4 47.7 %collective-permute-start.32 = (bf16[512,1536]{1,0:T(8,128)(2,1)}, bf16[512,1536]{1,0:T(8,128)(2,1)}, u32[]{:S(2)}, u32[]{:S(2)}) collective-permute-start(bf16[512,1536]{1,0:T(8,128)(2,1)} %pad_maximum_fusion.3), channel_id=1, source_target_pairs={{0,16},{16,0},{1,17},{17,1},{2,18},{18,2},{3,19},{19,3},{4,20},{20... | collective-permute-start | bytes 4718600 | tf_op jit(solution)/shard_map/ppermute | solution.py:39
  466.1 40.0 %collective-permute-start.35 = (bf16[512,1536]{1,0:T(8,128)(2,1)}, bf16[512,1536]{1,0:T(8,128)(2,1)}, u32[]{:S(2)}, u32[]{:S(2)}) collective-permute-start(bf16[512,1536]{1,0:T(8,128)(2,1)} %pad_maximum_fusion.4), channel_id=1, source_target_pairs={{0,2},{1,3},{2,0},{3,1},{4,6},{5,7},{6,4},{7,5},{8,10},{9,11},{10,... | collective-permute-start | bytes 4718600 | tf_op jit(solution)/shard_map/ppermute | solution.py:39
  468.2 52.9 %collective-permute-start.31 = (bf16[256,1664]{1,0:T(8,128)(2,1)}, bf16[256,1664]{1,0:T(8,128)(2,1)}, u32[]{:S(2)}, u32[]{:S(2)}) collective-permute-start(bf16[256,1664]{1,0:T(8,128)(2,1)} %get-tuple-element.362), channel_id=1, source_target_pairs={{0,2},{1,3},{2,0},{3,1},{4,6},{5,7},{6,4},{7,5},{8,10},{9,11},{10,... | collective-permute-start | bytes 2555912 | tf_op jit(solution)/shard_map/ppermute | solution.py:39
  469.5 51.6 %collective-permute-start.30 = (bf16[256,1664]{1,0:T(8,128)(2,1)}, bf16[256,1664]{1,0:T(8,128)(2,1)}, u32[]{:S(2)}, u32[]{:S(2)}) collective-permute-start(bf16[256,1664]{1,0:T(8,128)(2,1)} %get-tuple-element.363), channel_id=1, source_target_pairs={{0,16},{16,0},{1,17},{17,1},{2,18},{18,2},{3,19},{19,3},{4,20},{20... | collective-permute-start | bytes 2555912 | tf_op jit(solution)/shard_map/ppermute | solution.py:39
  526.2 40.5 %collective-permute-start.37 = (bf16[512,1664]{1,0:T(8,128)(2,1)}, bf16[512,1664]{1,0:T(8,128)(2,1)}, u32[]{:S(2)}, u32[]{:S(2)}) collective-permute-start(bf16[512,1664]{1,0:T(8,128)(2,1)} %get-tuple-element.288), channel_id=1, source_target_pairs={{0,16},{16,0},{1,17},{17,1},{2,18},{18,2},{3,19},{19,3},{4,20},{20... | collective-permute-start | bytes 5111816 | tf_op jit(solution)/shard_map/ppermute | solution.py:39
  527.8 38.8 %collective-permute-start.38 = (bf16[512,1664]{1,0:T(8,128)(2,1)}, bf16[512,1664]{1,0:T(8,128)(2,1)}, u32[]{:S(2)}, u32[]{:S(2)}) collective-permute-start(bf16[512,1664]{1,0:T(8,128)(2,1)} %get-tuple-element.289), channel_id=1, source_target_pairs={{0,2},{1,3},{2,0},{3,1},{4,6},{5,7},{6,4},{7,5},{8,10},{9,11},{10,... | collective-permute-start | bytes 5111816 | tf_op jit(solution)/shard_map/ppermute | solution.py:39
  528.3 38.3 %collective-permute-start.39 = (bf16[512,1664]{1,0:T(8,128)(2,1)}, bf16[512,1664]{1,0:T(8,128)(2,1)}, u32[]{:S(2)}, u32[]{:S(2)}) collective-permute-start(bf16[512,1664]{1,0:T(8,128)(2,1)} %get-tuple-element.291), channel_id=1, source_target_pairs={{0,1},{1,0},{2,3},{3,2},{4,5},{5,4},{6,7},{7,6},{8,9},{9,8},{10,11... | collective-permute-start | bytes 5111816 | tf_op jit(solution)/shard_map/ppermute | solution.py:39
  548.6 192.3 %reduce-scatter.8.cloned.1.call-start = ((), (), s32[]{:S(2)}) async-start(), calls=%async_computation.9 | async-start | bytes 3342336 | tf_op jit(solution)/shard_map/reduce_scatter | solution.py:959
  550.5 40.4 %collective-permute-start.40 = (bf16[512,512]{1,0:T(8,128)(2,1)}, bf16[512,512]{1,0:T(8,128)(2,1)S(1)}, u32[]{:S(2)}, u32[]{:S(2)}) collective-permute-start(bf16[512,512]{1,0:T(8,128)(2,1)} %pad_maximum_fusion.7), channel_id=1, source_target_pairs={{16,0},{17,1},{18,2},{19,3},{20,4},{21,5},{22,6},{23,7},{24,8},{25... | collective-permute-start | bytes 1572872 | tf_op jit(solution)/shard_map/ppermute | solution.py:929
  635.0 52.7 %collective-permute-start.55 = (bf16[4,96,768]{2,1,0:T(8,128)(2,1)S(1)}, bf16[4,96,768]{2,1,0:T(8,128)(2,1)}, u32[]{:S(2)}, u32[]{:S(2)}) collective-permute-start(bf16[4,96,768]{2,1,0:T(8,128)(2,1)S(1)} %constant_dynamic-slice_fusion.5), channel_id=1, source_target_pairs={{0,16},{16,0},{1,17},{17,1},{2,18},{18,2},{3,19},{19,3},{4,20},{20... | collective-permute-start | bytes 1769480 | tf_op jit(solution)/shard_map/ppermute | solution.py:39
  680.7 47.3 %collective-permute-start.69 = (bf16[4,96,1536]{2,1,0:T(8,128)(2,1)}, bf16[4,96,1536]{2,1,0:T(8,128)(2,1)}, u32[]{:S(2)}, u32[]{:S(2)}) collective-permute-start(bf16[4,96,1536]{2,1,0:T(8,128)(2,1)} %bitcast_dynamic-update-slice_fusion.refs_2_), channel_id=1, source_target_pairs={{0,16},{16,0},{1,17},{17,1},{2,18},{18,2},{3,19},{19,3},{4,20},{20... | collective-permute-start | bytes 3538952 | tf_op jit(solution)/shard_map/ppermute | solution.py:39
  (96 other events, 1166.5 us)
Sparse Core Ops, SparseCore 0:
  10.9 89.4 all-gather.4
  102.6 58.2 all-gather.6
  163.1 88.7 all-gather.8
  253.3 87.8 all-gather.10
  386.6 83.7 reduce-scatter.3
  548.7 91.7 reduce-scatter.5
  654.3 76.7 reduce-scatter.7

commit v5 on v4

--- a/solution.py
+++ b/solution.py
@@ -607,95 +607,140 @@
     )(seq, *parts)
 
 
-def expert_kernel(e, has_earlier, place_ref, *refs):
-    na_ref, nb_ref, ca_ref, cb_ref = refs[:4]
-    earlier_refs = refs[4:8] if has_earlier else (None,) * 4
-    wt_ref = refs[8] if has_earlier else refs[4]
-    (ch_ref, gl_ref, outa_ref, outb_ref, backa_ref, backb_ref) = refs[-6:]
-    width = na_ref.shape[1]
+def expert_kernel(e, blocks, has_earlier, place_ref, *refs):
+    rows_refs, up_refs = refs[:blocks], refs[blocks : 2 * blocks]
+    if has_earlier:
+        earlier_out, earlier_back, wt_ref = refs[2 * blocks : 2 * blocks + 3]
+        (ch_ref, gl_ref, outa_ref, outb_ref, backa_ref, backb_ref) = refs[-12:-6]
+        n_buf, c_buf, sems, out_buf, back_buf, out_sems = refs[-6:]
+    else:
+        wt_ref = refs[2 * blocks]
+        ch_ref, gl_ref, out_ref, back_ref, n_buf, c_buf, sems = refs[-7:]
+    tile, width = n_buf.shape[1:]
+    tiles = 2 * blocks
     ff = wt_ref.shape[1] // 3
-    first = pl.program_id(0) < 2
+    step = pl.program_id(0)
+    slot = lax.rem(step, 2)
     mine = 2 * place_ref[0] + e
-
-    def run(n_ref, c_ref, earlier_out, earlier_back, out_ref, back_ref):
-        packed = c_ref[:, width:].astype(F32)
-        lane = lax.broadcasted_iota(jnp.int32, packed.shape, 1)
-        g = dot_nn(n_ref[...], wt_ref[:, :ff])
-        l = dot_nn(n_ref[...], wt_ref[:, ff : 2 * ff])
-        u = dot_nn(c_ref[:, :width], wt_ref[:, 2 * ff :])
-        own_lane = (lane == mine) | (lane == EXPERTS + mine)
-        weight = jnp.sum(jnp.where(own_lane, packed, 0.0), axis=-1, keepdims=True)
-        sig = 1.0 / (1.0 + jnp.exp(-g))
-        silu = g * sig
-        hidden = silu * l
-        dot = jnp.sum(hidden * u, axis=-1, keepdims=True)
-        dot_high = dot.astype(BF).astype(F32)
-        dots = jnp.where(lane == mine, dot_high, 0.0)
-        dots = jnp.where(lane == EXPERTS + mine, dot - dot_high, dots)
-        grad = u * weight
-        ch_ref[...] = (hidden * weight).astype(BF)
-        gl_ref[:, :ff] = (grad * l * (sig + silu * (1.0 - sig))).astype(BF)
-        gl_ref[:, ff:] = (grad * silu).astype(BF)
-        back = dot_nt(gl_ref[...], wt_ref[:, : 2 * ff])
-        out = dot_nt(ch_ref[...], wt_ref[:, 2 * ff :])
-        if has_earlier:
-            out = out + earlier_out[:, :width].astype(F32)
-            dots = dots + earlier_out[:, width:].astype(F32)
-            back = back + earlier_back[...].astype(F32)
-        back_ref[...] = back.astype(BF)
-        out_ref[:, :width] = out.astype(BF)
-        out_ref[:, width:] = dots.astype(BF)
-
-    @pl.when(first)
-    def _():
-        run(na_ref, ca_ref, earlier_refs[0], earlier_refs[2], outa_ref, backa_ref)
-
-    @pl.when(jnp.logical_not(first))
-    def _():
-        run(nb_ref, cb_ref, earlier_refs[1], earlier_refs[3], outb_ref, backb_ref)
-
-
-def expert_rows(place, e, rows, up, packed, chunk, chunks, held, earlier, us):
+    if has_earlier:
+        out_ref, back_ref = out_buf.at[step], back_buf.at[step]
+
+    def fetch(t):
+        part = pl.ds((t % 2) * tile, tile)
+        return (
+            pltpu.make_async_copy(rows_refs[t // 2].at[part], n_buf.at[t % 2], sems.at[0, t % 2]),
+            pltpu.make_async_copy(up_refs[t // 2].at[part], c_buf.at[t % 2], sems.at[1, t % 2]),
+        )
+
+    @pl.when(step == 0)
+    def _():
+        for copy in fetch(0):
+            copy.start()
+
+    for t in range(tiles):
+
+        @pl.when(step == t)
+        def _():
+            if t + 1 < tiles:
+                for copy in fetch(t + 1):
+                    copy.start()
+            for copy in fetch(t):
+                copy.wait()
+
+    n_ref, c_ref = n_buf.at[slot], c_buf.at[slot]
+    packed = c_ref[:, width:].astype(F32)
+    lane = lax.broadcasted_iota(jnp.int32, packed.shape, 1)
+    g = dot_nn(n_ref[...], wt_ref[:, :ff])
+    l = dot_nn(n_ref[...], wt_ref[:, ff : 2 * ff])
+    u = dot_nn(c_ref[:, :width], wt_ref[:, 2 * ff :])
+    own_lane = (lane == mine) | (lane == EXPERTS + mine)
+    weight = jnp.sum(jnp.where(own_lane, packed, 0.0), axis=-1, keepdims=True)
+    sig = 1.0 / (1.0 + jnp.exp(-g))
+    silu = g * sig
+    hidden = silu * l
+    dot = jnp.sum(hidden * u, axis=-1, keepdims=True)
+    dot_high = dot.astype(BF).astype(F32)
+    dots = jnp.where(lane == mine, dot_high, 0.0)
+    dots = jnp.where(lane == EXPERTS + mine, dot - dot_high, dots)
+    grad = u * weight
+    ch_ref[...] = (hidden * weight).astype(BF)
+    gl_ref[:, :ff] = (grad * l * (sig + silu * (1.0 - sig))).astype(BF)
+    gl_ref[:, ff:] = (grad * silu).astype(BF)
+    back = dot_nt(gl_ref[...], wt_ref[:, : 2 * ff])
+    out = dot_nt(ch_ref[...], wt_ref[:, 2 * ff :])
+    if has_earlier:
+        out = out + earlier_out[:, :width].astype(F32)
+        dots = dots + earlier_out[:, width:].astype(F32)
+        back = back + earlier_back[...].astype(F32)
+    back_ref[...] = back.astype(BF)
+    out_ref[:, :width] = out.astype(BF)
+    out_ref[:, width:] = dots.astype(BF)
+    if has_earlier:
+
+        def send(t):
+            part = pl.ds((t % 2) * tile, tile)
+            to_out, to_back = (outa_ref, backa_ref) if t < 2 else (outb_ref, backb_ref)
+            return (
+                pltpu.make_async_copy(out_buf.at[t], to_out.at[part], out_sems.at[0, t]),
+                pltpu.make_async_copy(back_buf.at[t], to_back.at[part], out_sems.at[1, t]),
+            )
+
+        for t in range(tiles):
+
+            @pl.when(step == t)
+            def _():
+                for copy in send(t):
+                    copy.start()
+
+        @pl.when(step == tiles - 1)
+        def _():
+            for t in range(tiles):
+                for copy in send(t):
+                    copy.wait()
+
+
+def expert_rows(place, e, rows, up, packed, chunk, total, held, earlier, us):
     count, width = rows[0].shape
+    blocks = len(rows)
     ff = packed.shape[1] // 3
     tile = count // 2
     more = width + 128
 
-    def early(i, place):
-        return (jnp.minimum(i, 1), 0)
-
-    def late(i, place):
-        return (jnp.maximum(i - 2, 0), 0)
-
     def at_rows(i, place):
         return (4 * chunk + i, 0)
 
     any_spec = pl.BlockSpec(memory_space=pl.ANY)
-    wide_specs = [pl.BlockSpec((tile, width), early), pl.BlockSpec((tile, width), late)]
-    more_specs = [pl.BlockSpec((tile, more), early), pl.BlockSpec((tile, more), late)]
-    total = 2 * count * chunks
+    sum_specs = [pl.BlockSpec((tile, more), at_rows), pl.BlockSpec((tile, width), at_rows)]
+    packed_spec = pl.BlockSpec((width, 3 * ff), lambda i, place: (0, 0), pipeline_mode=pl.Buffered(1))
     one = jax.ShapeDtypeStruct((count, width), BF)
     one_more = jax.ShapeDtypeStruct((count, more), BF)
+    scratch = [pltpu.VMEM((2, tile, width), BF), pltpu.VMEM((2, tile, more), BF), pltpu.SemaphoreType.DMA((2, 2))]
     held, earlier = list(held), list(earlier)
-    begin = 6 + len(earlier)
-    packed_spec = pl.BlockSpec((width, 3 * ff), lambda i, place: (0, 0), pipeline_mode=pl.Buffered(1))
+    begin = 2 + 2 * blocks + len(earlier)
+    if earlier:
+        sums = [one_more] * 2 + [one] * 2
+        out_sums = [any_spec] * 4
+        scratch += [
+            pltpu.VMEM((2 * blocks, tile, more), BF),
+            pltpu.VMEM((2 * blocks, tile, width), BF),
+            pltpu.SemaphoreType.DMA((2, 2 * blocks)),
+        ]
+    else:
+        sums = [jax.ShapeDtypeStruct((total, more), BF), jax.ShapeDtypeStruct((total, width), BF)]
+        out_sums = sum_specs
     return pl.pallas_call(
-        functools.partial(expert_kernel, e, len(earlier) > 0),
+        functools.partial(expert_kernel, e, blocks, len(earlier) > 0),
         grid_spec=pltpu.PrefetchScalarGridSpec(
             num_scalar_prefetch=1,
-            grid=(4,),
-            in_specs=wide_specs
-            + more_specs
-            + (more_specs + wide_specs if earlier else [])
+            grid=(2 * blocks,),
+            in_specs=[any_spec] * (2 * blocks)
+            + (sum_specs if earlier else [])
             + [packed_spec]
             + [any_spec] * len(held),
-            out_specs=[pl.BlockSpec((tile, ff), at_rows), pl.BlockSpec((tile, 2 * ff), at_rows)]
-            + more_specs
-            + wide_specs,
+            out_specs=[pl.BlockSpec((tile, ff), at_rows), pl.BlockSpec((tile, 2 * ff), at_rows)] + out_sums,
+            scratch_shapes=scratch,
         ),
-        out_shape=[jax.ShapeDtypeStruct((total, ff), BF), jax.ShapeDtypeStruct((total, 2 * ff), BF)]
-        + [one_more] * 2
-        + [one] * 2,
+        out_shape=[jax.ShapeDtypeStruct((total, ff), BF), jax.ShapeDtypeStruct((total, 2 * ff), BF)] + sums,
         input_output_aliases={begin + at: at for at in range(len(held))},
         compiler_params=pltpu.CompilerParams(vmem_limit_bytes=VMEM_LIMIT),
         cost_estimate=cost(us),
@@ -817,20 +862,28 @@
     up_block = after(up_block, packed)
     up_across, up_beside, up_sibling = seq_swap(up_block), side_swap(up_block), core_swap(up_block)
 
-    up_pair_across = (up_across, core_swap(up_across))
-    up_pair_beside = (up_beside, core_swap(up_beside))
     query, pair_a, pair_b, lowered_one, gains = project_rows(tokens[0], project_in, qkv, 0)
     past_a = lax.ppermute(pair_a, "seq", [(0, 1)])
     late_pair, past_a = lax.optimization_barrier((pair_b, past_a))
     past_b = lax.ppermute(late_pair, "seq", [(0, 1)])
     mixed, stats_a = attend(place, query, pair_a, past_a, 0)
     mixed, stats_b = attend(place, query, pair_b, past_b, stats_a.shape[0], (mixed,))
+    up_across, up_beside, stats_a = lax.optimization_barrier((up_across, up_beside, stats_a))
+    up_far_top, up_far_low = seq_swap(up_beside[:half]), side_swap(up_across[half:])
+    up_across_other, up_beside_other = core_swap(up_across), core_swap(up_beside)
+    mixed, up_far_top, up_far_low, up_sibling, up_across_other, up_beside_other = lax.optimization_barrier(
+        (mixed, up_far_top, up_far_low, up_sibling, up_across_other, up_beside_other)
+    )
+    up_pair_across, up_pair_beside = (up_across, up_across_other), (up_beside, up_beside_other)
+    up_far = jnp.concatenate([up_far_top, up_far_low], axis=0)
+    up_pair_far = (up_far, core_swap(up_far))
     middle, lowered_two = merge_rows(mixed, project_out, tokens[0], gains)
 
+    chips = 4
     across, beside, sibling = seq_swap(lowered_two), side_swap(lowered_two), core_swap(lowered_two)
 
     def experts(e, at, rows, up, held, earlier=(), us=1):
-        return expert_rows(expert_place, e, rows, up, gathered[e], at, 4, held, earlier, us)
+        return expert_rows(expert_place, e, rows, up, gathered[e], at, 2 * chips * count, held, earlier, us)
 
     def upper(block, more):
         return jnp.concatenate([low_plus(block[:half], more), block[half:]])
@@ -838,29 +891,16 @@
     def lower(block, more):
         return jnp.concatenate([block[:half], low_plus(block[half:], more)])
 
-    lowered_two, across, beside, up_beside, up_across = lax.optimization_barrier(
-        (lowered_two, across, beside, up_beside, up_across)
-    )
+    lowered_two, across, beside, sibling = lax.optimization_barrier((lowered_two, across, beside, sibling))
     row_own, up_own = (lowered_two, sibling), (up_block, up_sibling)
     far_top, far_low = seq_swap(beside[:half]), side_swap(across[half:])
-    up_far_top, up_far_low = seq_swap(up_beside[:half]), side_swap(up_across[half:])
     row_across = (across, core_swap(across))
     row_beside = (beside, core_swap(beside))
-    made_own = experts(0, 0, row_own, up_own, ())
-    made_across = experts(0, 1, row_across, up_pair_across, made_own[:2])
-    made_beside = experts(0, 2, row_beside, up_pair_beside, made_across[:2])
-    far_top, far_low, up_far_top, up_far_low, held = lax.optimization_barrier(
-        (far_top, far_low, up_far_top, up_far_low, made_beside[:2])
-    )
-    up_far = jnp.concatenate([up_far_top, up_far_low], axis=0)
-    up_pair_far = (up_far, core_swap(up_far))
     far = jnp.concatenate([far_top, far_low], axis=0)
     row_far = (far, core_swap(far))
-    made_far = experts(0, 3, row_far, up_pair_far, held)
-    hidden_a, grads_a = made_far[:2]
-
     row_all = (*row_own, *row_across, *row_beside, *row_far)
     up_all = (*up_own, *up_pair_across, *up_pair_beside, *up_pair_far)
+    hidden_a, grads_a, *sums_a = experts(0, 0, row_all, up_all, ())
 
     def home(total):
         return lax.psum_scatter(total, "outer", scatter_dimension=0, tiled=True)
@@ -871,18 +911,18 @@
     total_a = expert_grad(row_all, grads_a, width, 3 * ff, 0, 1)
     total_a = expert_grad(up_all, hidden_a, width, 3 * ff, 2, 1, (total_a,))
     home_a = home(total_a)
-    far_parts = after(made_far[2:], total_a)
-
-    made_far = experts(1, 3, row_far, up_pair_far, (), far_parts)
+    sums_a = after(sums_a, total_a)
+
+    made_far = experts(1, 3, row_far, up_pair_far, (), sums_a)
     far_got, far_out_got = core_swap(made_far[5]), core_swap(made_far[3])
-    made_across = experts(1, 1, row_across, up_pair_across, made_far[:2], made_across[2:])
+    made_across = experts(1, 1, row_across, up_pair_across, made_far[:2], sums_a)
     across_got, across_out_got = core_swap(made_across[5]), core_swap(made_across[3])
     far_got, far_out_got, held = lax.optimization_barrier((far_got, far_out_got, made_across[:2]))
     far_sum, far_out, held = lax.optimization_barrier(
         (low_plus(made_far[4], far_got), low_plus(made_far[2], far_out_got), held)
     )
     back_low, back_top = side_swap(far_sum[half:]), seq_swap(far_sum[:half])
-    made_beside = experts(1, 2, row_beside, up_pair_beside, held, made_beside[2:], 15)
+    made_beside = experts(1, 2, row_beside, up_pair_beside, held, sums_a, 15)
     beside_got, beside_out_got = core_swap(made_beside[5]), core_swap(made_beside[3])
     across_got, across_out_got, back_low, back_top, held = lax.optimization_barrier(
         (across_got, across_out_got, back_low, back_top, made_beside[:2])
@@ -891,7 +931,7 @@
         (lower(low_plus(made_across[4], across_got), back_low), low_plus(made_across[2], across_out_got), held)
     )
     across_in = seq_swap(across_sum)
-    made_own = experts(1, 0, row_own, up_own, held, made_own[2:], 15)
+    made_own = experts(1, 0, row_own, up_own, held, sums_a, 15)
     hidden_b, grads_b = made_own[:2]
     own_got = core_swap(made_own[5])
     beside_got, beside_out_got, grads_b = lax.optimization_barrier((beside_got, beside_out_got, grads_b))

time: 763 us -> 743 us (0.974)
  Pallas kernels: 323 us -> 305 us
    ppermute x58, waiting for transfers between devices: 109 us -> 156 us  [swap(): lax.ppermute(x, axis, [(i, i ^ bit) for i in range(lax.axis_size(axis))])]
    all_gather x1, waiting for transfers between devices: 25.7 us -> 0.01 us  [body(): gathered = [lax.all_gather(packed[0], 'outer', axis=0, tiled=True)]]
    all_gather x1, waiting for transfers between devices: 51.1 us -> 28.6 us  [body(): lax.all_gather(jnp.concatenate([attention_in, gains], axis=1), ROWS, axis...]
    pallas_call x8 -> x5, Pallas kernels: 146 us -> 128 us  [expert_rows(): pl.pallas_call(functools.partial(expert_kernel, e, blocks, len(earlier) >...]
    ppermute x58, starting transfers between devices: 52.3 us -> 44.3 us  [swap(): lax.ppermute(x, axis, [(i, i ^ bit) for i in range(lax.axis_size(axis))])]
  transfers between devices with their start and end apart: 78 -> 78, of which waited for: 27 -> 33; matrix products, arithmetic and copies ran while one was open for 13% -> 13% of each run, Pallas kernels for 40% -> 39%
where the time goes in v5:
time: 743 us; the launch traced here: 736 us
  Pallas kernels  305 us (41%)
  waiting for transfers between devices  231 us (31%)
  starting transfers between devices  76.6 us (10%)
  other arithmetic  47.6 us (6%)
  local copies, waits for them, and re-layouts  45.9 us (6%)
  between operations  16.1 us (2%)
  matrix products  13.6 us (2%)
    ppermute x58, waiting for transfers between devices, swap(): lax.ppermute(x, axis, [(i, i ^ bit) for i in range(lax.axis_size(axis))])  156 us
    pallas_call x5, Pallas kernels, expert_rows(): pl.pallas_call(functools.partial(expert_kernel, e, blocks, len(earlier) >...  128 us
    pallas_call x4, Pallas kernels, expert_grad(): pl.pallas_call(expert_grad_kernel, grid=(len(lefts),), in_specs=[any_spec...  68.2 us
    ppermute x58, starting transfers between devices, swap(): lax.ppermute(x, axis, [(i, i ^ bit) for i in range(lax.axis_size(axis))])  44.3 us
    pallas_call x2, Pallas kernels, attend_back(): pl.pallas_call(attend_back_kernel, grid_spec=pltpu.PrefetchScalarGridSpec...  30.1 us
    all_gather x1, waiting for transfers between devices, body(): lax.all_gather(jnp.concatenate([attention_in, gains], axis=1), ROWS, axis...  28.6 us
    convert_element_type x16, other arithmetic, low_plus(): return (a.astype(F32) + b.astype(F32)).astype(BF)  23.4 us
    pallas_call x2, Pallas kernels, attend(): pl.pallas_call(attend_kernel, grid_spec=pltpu.PrefetchScalarGridSpec(num_...  22.5 us
  transfers between devices with their start and end apart: 78, of which 33 were waited for; matrix products, arithmetic and copies ran while one was open for 13% of the time, Pallas kernels for 39%

profile of v5, /device:TPU:0, one launch (start us, length us, event | category | flops | bytes accessed | tf_op | source)
XLA Modules:
  0.0 735.7 jit_solution(11692654841560523390)
XLA Ops:
  11.5 6.2 pack_experts.1
  25.2 11.3 %collective-permute-done.3 = bf16[96,1536]{1,0:T(8,128)(2,1)S(1)} collective-permute-done((bf16[96,1536]{1,0:T(8,128)(2,1)S(1)}, bf16[96,1536]{1,0:T(8,128)(2,1)S(1)}, u32[]{:S(2)}, u32[]{:S(2)}) %collective-permute-start.3) | collective-permute-done | bytes 294944 | tf_op jit(solution)/shard_map/ppermute | solution.py:39
  51.6 11.1 %collective-permute-done.6 = bf16[96,1536]{1,0:T(8,128)(2,1)} collective-permute-done((bf16[96,1536]{1,0:T(8,128)(2,1)}, bf16[96,1536]{1,0:T(8,128)(2,1)}, u32[]{:S(2)}, u32[]{:S(2)}) %collective-permute-start.6) | collective-permute-done | bytes 294944 | tf_op jit(solution)/shard_map/ppermute | solution.py:39
  64.4 10.3 %collective-permute-done.7 = bf16[96,1536]{1,0:T(8,128)(2,1)S(1)} collective-permute-done((bf16[96,1536]{1,0:T(8,128)(2,1)}, bf16[96,1536]{1,0:T(8,128)(2,1)S(1)}, u32[]{:S(2)}, u32[]{:S(2)}) %collective-permute-start.7) | collective-permute-done | bytes 294944 | tf_op jit(solution)/shard_map/ppermute | solution.py:39
  77.5 28.6 %all-gather.5.cloned.1.call-done.weight_ref.tail_ref = bf16[1536,2688]{1,0:T(8,128)(2,1)} async-done(((bf16[96,2688]{1,0:T(8,128)(2,1)}), bf16[1536,2688]{1,0:T(8,128)(2,1)}) %all-gather.5.cloned.1.call-update) | async-done | bytes 8257552 | tf_op jit(solution)/shard_map/all_gather | solution.py:841
  106.1 10.8 %project_rows.1 = (bf16[512,1536]{1,0:T(8,128)(2,1)}, bf16[512,512]{1,0:T(8,128)(2,1)}, bf16[512,512]{1,0:T(8,128)(2,1)}, bf16[512,1536]{1,0:T(8,128)(2,1)}, f32[8,1536]{1,0:T(8,128)}) custom-call(bf16[512,1536]{1,0:T(8,128)(2,1)} %bitcast.142, bf16[1536,2688]{1,0:T(8,128)(2,1)} %all-gather.5.cloned.1.call-done.weight_ref.tail_ref, ...), custom_call_target="tpu_custom_call" | custom-call | bytes 1000 | tf_op jit(solution)/shard_map/project_rows/pallas_call | solution.py:196
  122.2 10.0 %collective-permute-done.kr_ref.vr_ref = bf16[512,512]{1,0:T(8,128)(2,1)} collective-permute-done((bf16[512,512]{1,0:T(8,128)(2,1)}, bf16[512,512]{1,0:T(8,128)(2,1)}, u32[]{:S(2)}, u32[]{:S(2)}) %collective-permute-start) | collective-permute-done | bytes 524320 | tf_op jit(solution)/shard_map/ppermute | solution.py:866
  132.2 11.3 %attend.2 = (bf16[512,1536]{1,0:T(8,128)(2,1)}, f32[2,8,512]{2,1,0:T(8,128)}) custom-call(s32[2]{0:T(128)} %pad_add_fusion.place_ref, bf16[512,1536]{1,0:T(8,128)(2,1)} %get-tuple-element.163.q_ref, bf16[512,512]{1,0:T(8,128)(2,1)} %get-tuple-element.165.k_ref.v_ref, bf16[512,512]{1,0:T(8,128)(2,1)} %get-tuple-element.165.k_ref.v_ref, ...), custom_call_target="tpu_custom_call" | custom-call | bytes 1000 | tf_op jit(solution)/shard_map/attend/pallas_call | solution.py:365
  144.1 8.3 %collective-permute-start.1 = (bf16[512,512]{1,0:T(8,128)(2,1)S(1)}, bf16[512,512]{1,0:T(8,128)(2,1)S(1)}, u32[]{:S(2)}, u32[]{:S(2)}) collective-permute-start(bf16[512,512]{1,0:T(8,128)(2,1)S(1)} %copy-done.21), channel_id=1, source_target_pairs={{0,16},{1,17},{2,18},{3,19},{4,20},{5,21},{6,22},{7,23},{8,24},{9,... | collective-permute-start | bytes 1572872 | tf_op jit(solution)/shard_map/ppermute | solution.py:868
  156.3 7.3 collective-permute-done.1.kr_ref.vr_ref
  166.9 11.2 %attend.3 = (bf16[512,1536]{1,0:T(8,128)(2,1)}, f32[2,8,512]{2,1,0:T(8,128)}) custom-call(s32[2]{0:T(128)} %pad_add_fusion.place_ref, bf16[512,1536]{1,0:T(8,128)(2,1)} %get-tuple-element.163.q_ref, bf16[512,512]{1,0:T(8,128)(2,1)} %get-tuple-element.166.k_ref.v_ref, ...), custom_call_target="tpu_custom_call", output_to_operand_aliasing={{0}: (6, {})} | custom-call | bytes 1000 | tf_op jit(solution)/shard_map/attend/pallas_call | solution.py:365
  178.1 7.6 %collective-permute-done.10 = bf16[256,1664]{1,0:T(8,128)(2,1)} collective-permute-done((bf16[256,1664]{1,0:T(8,128)(2,1)}, bf16[256,1664]{1,0:T(8,128)(2,1)}, u32[]{:S(2)}, u32[]{:S(2)}) %collective-permute-start.10) | collective-permute-done | bytes 852000 | tf_op jit(solution)/shard_map/ppermute | solution.py:39
  185.7 8.9 %merge_rows.1 = (f32[512,1536]{1,0:T(8,128)}, bf16[512,1536]{1,0:T(8,128)(2,1)}) custom-call(bf16[512,1536]{1,0:T(8,128)(2,1)} %get-tuple-element.259.mixed_ref, bf16[1536,1536]{1,0:T(8,128)(2,1)} %all-gather.7.cloned.1.call-done.weight_ref, bf16[512,1536]{1,0:T(8,128)(2,1)} %bitcast.143, f32[8,1536]{1,0:T(8,128)} %get-tuple-element.177.gain_ref), custom_call_target="tpu_custom_call" | custom-call | bytes 1000 | tf_op jit(solution)/shard_map/merge_rows/pallas_call | solution.py:247
  198.2 33.4 %collective-permute-done.16.refs_4_.refs_0_ = bf16[512,1536]{1,0:T(8,128)(2,1)S(1)} collective-permute-done((bf16[512,1536]{1,0:T(8,128)(2,1)}, bf16[512,1536]{1,0:T(8,128)(2,1)S(1)}, u32[]{:S(2)}, u32[]{:S(2)}) %collective-permute-start.16) | collective-permute-done | bytes 1572896 | tf_op jit(solution)/shard_map/ppermute | solution.py:39
  239.7 11.6 %collective-permute-done.20 = bf16[256,1536]{1,0:T(8,128)(2,1)S(1)} collective-permute-done((bf16[256,1536]{1,0:T(8,128)(2,1)S(1)}, bf16[256,1536]{1,0:T(8,128)(2,1)S(1)}, u32[]{:S(2)}, u32[]{:S(2)}) %collective-permute-start.20) | collective-permute-done | bytes 786464 | tf_op jit(solution)/shard_map/ppermute | solution.py:39
  258.7 52.9 %expert_rows.5 = (bf16[4096,512]{1,0:T(8,128)(2,1)}, bf16[4096,1024]{1,0:T(8,128)(2,1)}, bf16[4096,1664]{1,0:T(8,128)(2,1)}, bf16[4096,1536]{1,0:T(8,128)(2,1)}) custom-call(s32[2]{0:T(128)} %pad_add_fusion.1.place_ref, bf16[512,1536]{1,0:T(8,128)(2,1)} %get-tuple-element.180.refs_0_, bf16[512,1536]{1,0:T(8,128)(2,1)} %copy-done.5, ...), custom_call_target="tpu_custom_call" | custom-call | flops 600000000 | bytes 1000 | tf_op jit(solution)/shard_map/expert_rows/pallas_call | solution.py:731
  311.6 19.7 %expert_grad.4.refs_9_ = bf16[1536,1536]{1,0:T(8,128)(2,1)} custom-call(bf16[512,1536]{1,0:T(8,128)(2,1)} %get-tuple-element.180.refs_0_, bf16[512,1536]{1,0:T(8,128)(2,1)} %copy-done.5, bf16[512,1536]{1,0:T(8,128)(2,1)} %collective-permute-done.15.refs_2_.refs_0_, bf16[512,1536]{1,0:T(8,128)(2,1)} %collective-permute-done.18.refs_3_.refs_1_, ...), custom_call_target="tpu_custom_call" | custom-call | flops 600000000 | bytes 1000 | tf_op jit(solution)/shard_map/expert_grad/pallas_call | solution.py:784
  331.4 14.3 %expert_grad.5 = bf16[1536,1536]{1,0:T(8,128)(2,1)} custom-call(bf16[512,1664]{1,0:T(8,128)(2,1)} %copy-done, bf16[512,1664]{1,0:T(8,128)(2,1)} %collective-permute-done.12.refs_9_.refs_1_.refs_3_, bf16[512,1664]{1,0:T(8,128)(2,1)} %collective-permute-done.8.refs_10_.refs_2_, ...), custom_call_target="tpu_custom_call", output_to_operand_aliasing={{}: (9, {})} | custom-call | flops 600000000 | bytes 1000 | tf_op jit(solution)/shard_map/expert_grad/pallas_call | solution.py:784
  345.7 18.5 %expert_rows.6 = (bf16[4096,512]{1,0:T(8,128)(2,1)}, bf16[4096,1024]{1,0:T(8,128)(2,1)}, bf16[512,1664]{1,0:T(8,128)(2,1)}, bf16[512,1664]{1,0:T(8,128)(2,1)}, b...) custom-call(s32[2]{0:T(128)} %pad_add_fusion.1.place_ref, ...), custom_call_target="tpu_custom_call" | custom-call | flops 600000000 | bytes 1000 | tf_op jit(solution)/shard_map/expert_rows/pallas_call | solution.py:731
  364.9 19.2 %expert_rows.7 = (bf16[4096,512]{1,0:T(8,128)(2,1)}, bf16[4096,1024]{1,0:T(8,128)(2,1)}, bf16[512,1664]{1,0:T(8,128)(2,1)}, bf16[512,1664]{1,0:T(8,128)(2,1)}, b...) custom-call(s32[2]{0:T(128)} %pad_add_fusion.1.place_ref, ...), custom_call_target="tpu_custom_call", output_to_operand_aliasing={{0}: (8, {}), {1}: (9, {})} | custom-call | flops 600000000 | bytes 1000 | tf_op jit(solution)/shard_map/expert_rows/pallas_call | solution.py:731
  391.5 18.7 %expert_rows.8 = (bf16[4096,512]{1,0:T(8,128)(2,1)}, bf16[4096,1024]{1,0:T(8,128)(2,1)}, bf16[512,1664]{1,0:T(8,128)(2,1)}, bf16[512,1664]{1,0:T(8,128)(2,1)}, b...) custom-call(s32[2]{0:T(128)} %pad_add_fusion.1.place_ref, ...), custom_call_target="tpu_custom_call", output_to_operand_aliasing={{0}: (8, {}), {1}: (9, {})} | custom-call | flops 8999999488 | bytes 1000 | tf_op jit(solution)/shard_map/expert_rows/pallas_call | solution.py:731
  416.5 18.8 %expert_rows.9 = (bf16[4096,512]{1,0:T(8,128)(2,1)}, bf16[4096,1024]{1,0:T(8,128)(2,1)}, bf16[512,1664]{1,0:T(8,128)(2,1)}, bf16[512,1664]{1,0:T(8,128)(2,1)}, b...) custom-call(s32[2]{0:T(128)} %pad_add_fusion.1.place_ref, ...), custom_call_target="tpu_custom_call", output_to_operand_aliasing={{0}: (8, {}), {1}: (9, {})} | custom-call | flops 8999999488 | bytes 1000 | tf_op jit(solution)/shard_map/expert_rows/pallas_call | solution.py:731
  449.2 19.7 %expert_grad.6.refs_9_ = bf16[1536,1536]{1,0:T(8,128)(2,1)} custom-call(bf16[512,1536]{1,0:T(8,128)(2,1)} %get-tuple-element.180.refs_0_, bf16[512,1536]{1,0:T(8,128)(2,1)} %copy-done.5, bf16[512,1536]{1,0:T(8,128)(2,1)} %collective-permute-done.15.refs_2_.refs_0_, bf16[512,1536]{1,0:T(8,128)(2,1)} %collective-permute-done.18.refs_3_.refs_1_, ...), custom_call_target="tpu_custom_call" | custom-call | flops 600000000 | bytes 1000 | tf_op jit(solution)/shard_map/expert_grad/pallas_call | solution.py:784
  468.9 14.4 %expert_grad.7 = bf16[1536,1536]{1,0:T(8,128)(2,1)} custom-call(bf16[512,1664]{1,0:T(8,128)(2,1)} %copy-done, bf16[512,1664]{1,0:T(8,128)(2,1)} %collective-permute-done.12.refs_9_.refs_1_.refs_3_, bf16[512,1664]{1,0:T(8,128)(2,1)} %collective-permute-done.8.refs_10_.refs_2_, ...), custom_call_target="tpu_custom_call", output_to_operand_aliasing={{}: (9, {})} | custom-call | flops 600000000 | bytes 1000 | tf_op jit(solution)/shard_map/expert_grad/pallas_call | solution.py:784
  483.4 12.7 %middle_back.1 = (f32[512,1536]{1,0:T(8,128)}, bf16[512,1536]{1,0:T(8,128)(2,1)}, bf16[512,1536]{1,0:T(8,128)(2,1)}, f32[8,1536]{1,0:T(8,128)}) custom-call(bf16[512,1536]{1,0:T(8,128)(2,1)} %get-tuple-element.226.own_ref, bf16[512,1536]{1,0:T(8,128)(2,1)} %collective-permute-done.36.got_ref, bf16[512,1536]{1,0:T(8,128)(2,1)} %collective-permute-done.32.across_ref, ...), custom_call_target="tpu_custom_call" | custom-call | flops 600000000 | bytes 1000 | tf_op jit(solution)/shard_map/middle_back/pallas_call | solution.py:290
  505.9 14.8 %attend_back.2 = (bf16[512,768]{1,0:T(8,128)(2,1)}, bf16[512,256]{1,0:T(8,128)(2,1)}, bf16[512,256]{1,0:T(8,128)(2,1)}, bf16[512,256]{1,0:T(8,128)(2,1)}, bf16[512,256]{1,0:T(8,128)(2,1)}) custom-call(s32[2]{0:T(128)} %pad_add_fusion.place_ref, bf16[512,1536]{1,0:T(8,128)(2,1)} %get-tuple-element.163.q_ref, bf16[512,512]{1,0:T(8,128)(2,1)} %get-tuple-element.165.k_ref.v_ref, ...), custom_call_target="tpu_custom_call" | custom-call | flops 14400000000 | bytes 1000 | tf_op jit(solution)/shard_map/attend_back/pallas_call | solution.py:484
  529.3 16.1 %collective-permute-done.37 = bf16[512,1664]{1,0:T(8,128)(2,1)} collective-permute-done((bf16[512,1664]{1,0:T(8,128)(2,1)}, bf16[512,1664]{1,0:T(8,128)(2,1)}, u32[]{:S(2)}, u32[]{:S(2)}) %collective-permute-start.37) | collective-permute-done | bytes 1703968 | tf_op jit(solution)/shard_map/ppermute | solution.py:39
  569.0 15.3 %attend_back.3 = (bf16[512,768]{1,0:T(8,128)(2,1)}, bf16[512,256]{1,0:T(8,128)(2,1)}, bf16[512,256]{1,0:T(8,128)(2,1)}, bf16[512,256]{1,0:T(8,128)(2,1)}, bf16[512,256]{1,0:T(8,128)(2,1)}) custom-call(s32[2]{0:T(128)} %pad_add_fusion.place_ref, bf16[512,1536]{1,0:T(8,128)(2,1)} %get-tuple-element.163.q_ref, bf16[512,512]{1,0:T(8,128)(2,1)} %get-tuple-element.166.k_ref.v_ref, ...), custom_call_target="tpu_custom_call" | custom-call | flops 14400000000 | bytes 1000 | tf_op jit(solution)/shard_map/attend_back/pallas_call | solution.py:484
  584.3 7.1 collective-permute-done.45
  616.5 10.1 %collective-permute-done.48.lateb_ref = bf16[512,512]{1,0:T(8,128)(2,1)} collective-permute-done((bf16[512,512]{1,0:T(8,128)(2,1)}, bf16[512,512]{1,0:T(8,128)(2,1)}, u32[]{:S(2)}, u32[]{:S(2)}) %collective-permute-start.48) | collective-permute-done | bytes 524320 | tf_op jit(solution)/shard_map/ppermute | solution.py:987
  644.7 7.7 %fusion = f32[512,1536]{1,0:T(8,128)S(1)} fusion(bf16[512,2560]{1,0:T(8,128)(2,1)} %pad_maximum_fusion, bf16[1536,2688]{1,0:T(8,128)(2,1)} %all-gather.5.cloned.1.call-done.weight_ref.tail_ref), kind=kOutput, calls=%fused_computation | convolution fusion | flops 4026531840 | bytes 13631488 | tf_op jit(solution)/shard_map/dot_general | solution.py:151
  676.0 11.2 %collective-permute-done.58 = bf16[96,768]{1,0:T(8,128)(2,1)S(1)} collective-permute-done((bf16[96,768]{1,0:T(8,128)(2,1)S(1)}, bf16[96,768]{1,0:T(8,128)(2,1)S(1)}, u32[]{:S(2)}, u32[]{:S(2)}) %collective-permute-start.58) | collective-permute-done | bytes 147488 | tf_op jit(solution)/shard_map/ppermute | solution.py:119
  (350 shorter events, 240.4 us)
Async XLA Ops:
  7.2 99.0 %all-gather.5.cloned.1.call-start = ((), (), s32[]{:S(2)}) async-start(), calls=%async_computation.3 | async-start | bytes 8773632 | tf_op jit(solution)/shard_map/all_gather | solution.py:841
  10.7 175.0 %all-gather.7.cloned.1.call-start = ((), (), s32[]{:S(2)}) async-start(), calls=%async_computation.4 | async-start | bytes 5013504 | tf_op jit(solution)/shard_map/all_gather | solution.py:842
  11.4 244.1 %all-gather.9.cloned.1.call-start = ((), (), s32[]{:S(2)}) async-start(), calls=%async_computation.5 | async-start | bytes 5898240 | tf_op jit(solution)/shard_map/all_gather | solution.py:849
  43.1 302.6 %all-gather.11.cloned.1.call-start = ((), (), s32[]{:S(2)}) async-start(), calls=%async_computation.6 | async-start | bytes 5898240 | tf_op jit(solution)/shard_map/all_gather | solution.py:850
  75.4 68.1 %collective-permute-start.9 = (bf16[512,1664]{1,0:T(8,128)(2,1)S(1)}, bf16[512,1664]{1,0:T(8,128)(2,1)S(1)}, u32[]{:S(2)}, u32[]{:S(2)}) collective-permute-start(bf16[512,1664]{1,0:T(8,128)(2,1)S(1)} %concatenate.44.refs_8_.refs_0_.refs_2_), channel_id=1, source_target_pairs={{0,2},{1,3},{2,0},{3,1},{4,6},{5,7},{6,4},{7,5},{8,10},{9,11},{10,... | collective-permute-start | bytes 5111816 | tf_op jit(solution)/shard_map/ppermute | solution.py:39
  75.5 68.0 %collective-permute-start.8 = (bf16[512,1664]{1,0:T(8,128)(2,1)S(1)}, bf16[512,1664]{1,0:T(8,128)(2,1)}, u32[]{:S(2)}, u32[]{:S(2)}) collective-permute-start(bf16[512,1664]{1,0:T(8,128)(2,1)S(1)} %concatenate.44.refs_8_.refs_0_.refs_2_), channel_id=1, source_target_pairs={{0,16},{16,0},{1,17},{17,1},{2,18},{18,2},{3,19},{19,3},{4,20},{20... | collective-permute-start | bytes 5111816 | tf_op jit(solution)/shard_map/ppermute | solution.py:39
  77.5 474.2 %reduce-scatter.4.cloned.1.call-start = ((), (), s32[]{:S(2)}) async-start(), calls=%async_computation.7 | async-start | bytes 5898240 | tf_op jit(solution)/shard_map/reduce_scatter | solution.py:906
  122.2 55.9 %collective-permute-start.12 = (bf16[512,1664]{1,0:T(8,128)(2,1)S(1)}, bf16[512,1664]{1,0:T(8,128)(2,1)}, u32[]{:S(2)}, u32[]{:S(2)}) collective-permute-start(bf16[512,1664]{1,0:T(8,128)(2,1)S(1)} %concatenate.44.refs_8_.refs_0_.refs_2_), channel_id=1, source_target_pairs={{0,1},{1,0},{2,3},{3,2},{4,5},{5,4},{6,7},{7,6},{8,9},{9,8},{10,11... | collective-permute-start | bytes 5111816 | tf_op jit(solution)/shard_map/ppermute | solution.py:39
  143.5 42.1 %collective-permute-start.14 = (bf16[512,1664]{1,0:T(8,128)(2,1)S(1)}, bf16[512,1664]{1,0:T(8,128)(2,1)}, u32[]{:S(2)}, u32[]{:S(2)}) collective-permute-start(bf16[512,1664]{1,0:T(8,128)(2,1)S(1)} %collective-permute-done.9.refs_12_.refs_4_.refs_2_), channel_id=1, source_target_pairs={{0,1},{1,0},{2,3},{3,2},{4,5},{5,4},{6,7},{7,6},{8,9},{9,8},{10,11... | collective-permute-start | bytes 5111816 | tf_op jit(solution)/shard_map/ppermute | solution.py:39
  143.6 42.0 %collective-permute-start.13 = (bf16[512,1664]{1,0:T(8,128)(2,1)}, bf16[512,1664]{1,0:T(8,128)(2,1)}, u32[]{:S(2)}, u32[]{:S(2)}) collective-permute-start(bf16[512,1664]{1,0:T(8,128)(2,1)} %collective-permute-done.8.refs_10_.refs_2_), channel_id=1, source_target_pairs={{0,1},{1,0},{2,3},{3,2},{4,5},{5,4},{6,7},{7,6},{8,9},{9,8},{10,11... | collective-permute-start | bytes 5111816 | tf_op jit(solution)/shard_map/ppermute | solution.py:39
  194.6 37.0 %collective-permute-start.16 = (bf16[512,1536]{1,0:T(8,128)(2,1)}, bf16[512,1536]{1,0:T(8,128)(2,1)S(1)}, u32[]{:S(2)}, u32[]{:S(2)}) collective-permute-start(bf16[512,1536]{1,0:T(8,128)(2,1)} %get-tuple-element.180.refs_0_), channel_id=1, source_target_pairs={{0,2},{1,3},{2,0},{3,1},{4,6},{5,7},{6,4},{7,5},{8,10},{9,11},{10,... | collective-permute-start | bytes 4718600 | tf_op jit(solution)/shard_map/ppermute | solution.py:39
  195.4 36.9 %collective-permute-start.15 = (bf16[512,1536]{1,0:T(8,128)(2,1)}, bf16[512,1536]{1,0:T(8,128)(2,1)}, u32[]{:S(2)}, u32[]{:S(2)}) collective-permute-start(bf16[512,1536]{1,0:T(8,128)(2,1)} %get-tuple-element.180.refs_0_), channel_id=1, source_target_pairs={{0,16},{16,0},{1,17},{17,1},{2,18},{18,2},{3,19},{19,3},{4,20},{20... | collective-permute-start | bytes 4718600 | tf_op jit(solution)/shard_map/ppermute | solution.py:39
  364.9 275.0 %reduce-scatter.6.cloned.1.call-start = ((), (), s32[]{:S(2)}) async-start(), calls=%async_computation.8 | async-start | bytes 5898240 | tf_op jit(solution)/shard_map/reduce_scatter | solution.py:906
  384.1 26.1 %collective-permute-start.24 = (bf16[512,1536]{1,0:T(8,128)(2,1)}, bf16[512,1536]{1,0:T(8,128)(2,1)}, u32[]{:S(2)}, u32[]{:S(2)}) collective-permute-start(bf16[512,1536]{1,0:T(8,128)(2,1)} %get-tuple-element.198), channel_id=1, source_target_pairs={{0,1},{1,0},{2,3},{3,2},{4,5},{5,4},{6,7},{7,6},{8,9},{9,8},{10,11... | collective-permute-start | bytes 4718600 | tf_op jit(solution)/shard_map/ppermute | solution.py:39
  384.4 26.3 %collective-permute-start.25 = (bf16[512,1664]{1,0:T(8,128)(2,1)}, bf16[512,1664]{1,0:T(8,128)(2,1)S(1)}, u32[]{:S(2)}, u32[]{:S(2)}) collective-permute-start(bf16[512,1664]{1,0:T(8,128)(2,1)} %get-tuple-element.199), channel_id=1, source_target_pairs={{0,1},{1,0},{2,3},{3,2},{4,5},{5,4},{6,7},{7,6},{8,9},{9,8},{10,11... | collective-permute-start | bytes 5111816 | tf_op jit(solution)/shard_map/ppermute | solution.py:39
  410.2 27.3 %collective-permute-start.33 = (bf16[512,1536]{1,0:T(8,128)(2,1)}, bf16[512,1536]{1,0:T(8,128)(2,1)}, u32[]{:S(2)}, u32[]{:S(2)}) collective-permute-start(bf16[512,1536]{1,0:T(8,128)(2,1)} %get-tuple-element.229), channel_id=1, source_target_pairs={{0,1},{1,0},{2,3},{3,2},{4,5},{5,4},{6,7},{7,6},{8,9},{9,8},{10,11... | collective-permute-start | bytes 4718600 | tf_op jit(solution)/shard_map/ppermute | solution.py:39
  410.3 27.2 %collective-permute-start.34 = (bf16[512,1664]{1,0:T(8,128)(2,1)}, bf16[512,1664]{1,0:T(8,128)(2,1)}, u32[]{:S(2)}, u32[]{:S(2)}) collective-permute-start(bf16[512,1664]{1,0:T(8,128)(2,1)} %get-tuple-element.230), channel_id=1, source_target_pairs={{0,1},{1,0},{2,3},{3,2},{4,5},{5,4},{6,7},{7,6},{8,9},{9,8},{10,11... | collective-permute-start | bytes 5111816 | tf_op jit(solution)/shard_map/ppermute | solution.py:39
  435.3 48.1 %collective-permute-start.36 = (bf16[512,1536]{1,0:T(8,128)(2,1)}, bf16[512,1536]{1,0:T(8,128)(2,1)}, u32[]{:S(2)}, u32[]{:S(2)}) collective-permute-start(bf16[512,1536]{1,0:T(8,128)(2,1)} %get-tuple-element.238), channel_id=1, source_target_pairs={{0,1},{1,0},{2,3},{3,2},{4,5},{5,4},{6,7},{7,6},{8,9},{9,8},{10,11... | collective-permute-start | bytes 4718600 | tf_op jit(solution)/shard_map/ppermute | solution.py:39
  435.4 47.9 %collective-permute-start.32 = (bf16[512,1536]{1,0:T(8,128)(2,1)}, bf16[512,1536]{1,0:T(8,128)(2,1)}, u32[]{:S(2)}, u32[]{:S(2)}) collective-permute-start(bf16[512,1536]{1,0:T(8,128)(2,1)} %pad_maximum_fusion.3), channel_id=1, source_target_pairs={{0,16},{16,0},{1,17},{17,1},{2,18},{18,2},{3,19},{19,3},{4,20},{20... | collective-permute-start | bytes 4718600 | tf_op jit(solution)/shard_map/ppermute | solution.py:39
  444.7 38.6 %collective-permute-start.35 = (bf16[512,1536]{1,0:T(8,128)(2,1)}, bf16[512,1536]{1,0:T(8,128)(2,1)}, u32[]{:S(2)}, u32[]{:S(2)}) collective-permute-start(bf16[512,1536]{1,0:T(8,128)(2,1)} %pad_maximum_fusion.4), channel_id=1, source_target_pairs={{0,2},{1,3},{2,0},{3,1},{4,6},{5,7},{6,4},{7,5},{8,10},{9,11},{10,... | collective-permute-start | bytes 4718600 | tf_op jit(solution)/shard_map/ppermute | solution.py:39
  446.9 52.9 %collective-permute-start.31 = (bf16[256,1664]{1,0:T(8,128)(2,1)}, bf16[256,1664]{1,0:T(8,128)(2,1)}, u32[]{:S(2)}, u32[]{:S(2)}) collective-permute-start(bf16[256,1664]{1,0:T(8,128)(2,1)} %get-tuple-element.322), channel_id=1, source_target_pairs={{0,2},{1,3},{2,0},{3,1},{4,6},{5,7},{6,4},{7,5},{8,10},{9,11},{10,... | collective-permute-start | bytes 2555912 | tf_op jit(solution)/shard_map/ppermute | solution.py:39
  448.1 51.7 %collective-permute-start.30 = (bf16[256,1664]{1,0:T(8,128)(2,1)}, bf16[256,1664]{1,0:T(8,128)(2,1)}, u32[]{:S(2)}, u32[]{:S(2)}) collective-permute-start(bf16[256,1664]{1,0:T(8,128)(2,1)} %get-tuple-element.323), channel_id=1, source_target_pairs={{0,16},{16,0},{1,17},{17,1},{2,18},{18,2},{3,19},{19,3},{4,20},{20... | collective-permute-start | bytes 2555912 | tf_op jit(solution)/shard_map/ppermute | solution.py:39
  504.9 40.5 %collective-permute-start.37 = (bf16[512,1664]{1,0:T(8,128)(2,1)}, bf16[512,1664]{1,0:T(8,128)(2,1)}, u32[]{:S(2)}, u32[]{:S(2)}) collective-permute-start(bf16[512,1664]{1,0:T(8,128)(2,1)} %get-tuple-element.248), channel_id=1, source_target_pairs={{0,16},{16,0},{1,17},{17,1},{2,18},{18,2},{3,19},{19,3},{4,20},{20... | collective-permute-start | bytes 5111816 | tf_op jit(solution)/shard_map/ppermute | solution.py:39
  505.2 40.2 %collective-permute-start.38 = (bf16[512,1664]{1,0:T(8,128)(2,1)}, bf16[512,1664]{1,0:T(8,128)(2,1)}, u32[]{:S(2)}, u32[]{:S(2)}) collective-permute-start(bf16[512,1664]{1,0:T(8,128)(2,1)} %get-tuple-element.249), channel_id=1, source_target_pairs={{0,2},{1,3},{2,0},{3,1},{4,6},{5,7},{6,4},{7,5},{8,10},{9,11},{10,... | collective-permute-start | bytes 5111816 | tf_op jit(solution)/shard_map/ppermute | solution.py:39
  505.9 39.5 %collective-permute-start.39 = (bf16[512,1664]{1,0:T(8,128)(2,1)}, bf16[512,1664]{1,0:T(8,128)(2,1)}, u32[]{:S(2)}, u32[]{:S(2)}) collective-permute-start(bf16[512,1664]{1,0:T(8,128)(2,1)} %get-tuple-element.251), channel_id=1, source_target_pairs={{0,1},{1,0},{2,3},{3,2},{4,5},{5,4},{6,7},{7,6},{8,9},{9,8},{10,11... | collective-permute-start | bytes 5111816 | tf_op jit(solution)/shard_map/ppermute | solution.py:39
  526.1 194.6 %reduce-scatter.8.cloned.1.call-start = ((), (), s32[]{:S(2)}) async-start(), calls=%async_computation.9 | async-start | bytes 3342336 | tf_op jit(solution)/shard_map/reduce_scatter | solution.py:999
  528.0 41.0 %collective-permute-start.40 = (bf16[512,512]{1,0:T(8,128)(2,1)}, bf16[512,512]{1,0:T(8,128)(2,1)S(1)}, u32[]{:S(2)}, u32[]{:S(2)}) collective-permute-start(bf16[512,512]{1,0:T(8,128)(2,1)} %pad_maximum_fusion.7), channel_id=1, source_target_pairs={{16,0},{17,1},{18,2},{19,3},{20,4},{21,5},{22,6},{23,7},{24,8},{25... | collective-permute-start | bytes 1572872 | tf_op jit(solution)/shard_map/ppermute | solution.py:969
  557.3 34.2 %collective-permute-start.45 = (bf16[4,96,1536]{2,1,0:T(8,128)(2,1)S(1)}, bf16[4,96,1536]{2,1,0:T(8,128)(2,1)}, u32[]{:S(2)}, u32[]{:S(2)}) collective-permute-start(bf16[4,96,1536]{2,1,0:T(8,128)(2,1)S(1)} %dynamic-slice_bitcast_fusion.1), channel_id=1, source_target_pairs={{0,2},{1,3},{2,0},{3,1},{4,6},{5,7},{6,4},{7,5},{8,10},{9,11},{10,... | collective-permute-start | bytes 3538952 | tf_op jit(solution)/shard_map/ppermute | solution.py:39
  568.9 27.8 %collective-permute-start.46 = (bf16[4,96,1536]{2,1,0:T(8,128)(2,1)}, bf16[4,96,1536]{2,1,0:T(8,128)(2,1)}, u32[]{:S(2)}, u32[]{:S(2)}) collective-permute-start(bf16[4,96,1536]{2,1,0:T(8,128)(2,1)} %bitcast_dynamic-update-slice_fusion.3.refs_0_), channel_id=1, source_target_pairs={{0,16},{16,0},{1,17},{17,1},{2,18},{18,2},{3,19},{19,3},{4,20},{20... | collective-permute-start | bytes 3538952 | tf_op jit(solution)/shard_map/ppermute | solution.py:39
  607.8 28.6 %collective-permute-start.49 = (bf16[4,96,1536]{2,1,0:T(8,128)(2,1)}, bf16[4,96,1536]{2,1,0:T(8,128)(2,1)}, u32[]{:S(2)}, u32[]{:S(2)}) collective-permute-start(bf16[4,96,1536]{2,1,0:T(8,128)(2,1)} %dynamic-slice_bitcast_fusion), channel_id=1, source_target_pairs={{0,2},{1,3},{2,0},{3,1},{4,6},{5,7},{6,4},{7,5},{8,10},{9,11},{10,... | collective-permute-start | bytes 3538952 | tf_op jit(solution)/shard_map/ppermute | solution.py:39
  613.0 54.5 %collective-permute-start.55 = (bf16[4,96,768]{2,1,0:T(8,128)(2,1)S(1)}, bf16[4,96,768]{2,1,0:T(8,128)(2,1)}, u32[]{:S(2)}, u32[]{:S(2)}) collective-permute-start(bf16[4,96,768]{2,1,0:T(8,128)(2,1)S(1)} %constant_dynamic-slice_fusion.5), channel_id=1, source_target_pairs={{0,16},{16,0},{1,17},{17,1},{2,18},{18,2},{3,19},{19,3},{4,20},{20... | collective-permute-start | bytes 1769480 | tf_op jit(solution)/shard_map/ppermute | solution.py:39
  659.5 48.1 %collective-permute-start.69 = (bf16[4,96,1536]{2,1,0:T(8,128)(2,1)}, bf16[4,96,1536]{2,1,0:T(8,128)(2,1)}, u32[]{:S(2)}, u32[]{:S(2)}) collective-permute-start(bf16[4,96,1536]{2,1,0:T(8,128)(2,1)} %bitcast_dynamic-update-slice_fusion.refs_2_), channel_id=1, source_target_pairs={{0,16},{16,0},{1,17},{17,1},{2,18},{18,2},{3,19},{19,3},{4,20},{20... | collective-permute-start | bytes 3538952 | tf_op jit(solution)/shard_map/ppermute | solution.py:39
  (89 other events, 1097.8 us)
Sparse Core Ops, SparseCore 0:
  10.9 95.2 all-gather.4
  108.4 54.2 all-gather.6
  164.3 87.9 all-gather.8
  253.7 87.8 all-gather.10
  365.0 83.5 reduce-scatter.3
  526.3 93.6 reduce-scatter.5
  632.4 78.5 reduce-scatter.7

commit v6 on v5

--- a/solution.py
+++ b/solution.py
@@ -1030,13 +1030,13 @@
     chain.leave(out_home.final())
     gain_sum = chain.leave(pick(chain.enter(gain_sum).reshape(2, inner_count, shard), lax.axis_index("inner"), 1))
     gain_sum = gain_sum + seq_swap(gain_sum)
+    pair_other = seq_swap(chain.enter(pair_part))
     parts = chain.enter((a_mine, a_other, b_mine, b_other))
     grads = [unpack_experts(seq_place, parts, kind, ff) for kind in range(3)]
     grad_gate, grad_lift, grad_down = chain.leave(lax.optimization_barrier(tuple(grads)))
     out_home.other, query_home.other = chain.enter((out_home.other, query_home.other))
     grad_out = chain.leave(out_home.result())
-    pair_part = chain.enter(pair_part)
-    pair_sum = pair_part.astype(F32) + seq_swap(pair_part).astype(F32)
+    pair_sum = pair_part.astype(F32) + chain.enter(pair_other).astype(F32)
     grad_in = jnp.concatenate([query_home.result(), pair_sum], axis=1)
     return (
         block_output,

time: 743 us -> 742 us (level)
  no operation moved by 1% of the time
where the time goes in v6:
time: 742 us; the launch traced here: 735 us
  Pallas kernels  305 us (41%)
  waiting for transfers between devices  230 us (31%)
  starting transfers between devices  76.7 us (10%)
  other arithmetic  47.6 us (6%)
  local copies, waits for them, and re-layouts  45.9 us (6%)
  between operations  16.1 us (2%)
  matrix products  13.6 us (2%)
    ppermute x58, waiting for transfers between devices, swap(): lax.ppermute(x, axis, [(i, i ^ bit) for i in range(lax.axis_size(axis))])  155 us
    pallas_call x5, Pallas kernels, expert_rows(): pl.pallas_call(functools.partial(expert_kernel, e, blocks, len(earlier) >...  128 us
    pallas_call x4, Pallas kernels, expert_grad(): pl.pallas_call(expert_grad_kernel, grid=(len(lefts),), in_specs=[any_spec...  68.2 us
    ppermute x58, starting transfers between devices, swap(): lax.ppermute(x, axis, [(i, i ^ bit) for i in range(lax.axis_size(axis))])  44.4 us
    pallas_call x2, Pallas kernels, attend_back(): pl.pallas_call(attend_back_kernel, grid_spec=pltpu.PrefetchScalarGridSpec...  30.1 us
    all_gather x1, waiting for transfers between devices, body(): lax.all_gather(jnp.concatenate([attention_in, gains], axis=1), ROWS, axis...  28.6 us
    convert_element_type x16, other arithmetic, low_plus(): return (a.astype(F32) + b.astype(F32)).astype(BF)  23.4 us
    pallas_call x2, Pallas kernels, attend(): pl.pallas_call(attend_kernel, grid_spec=pltpu.PrefetchScalarGridSpec(num_...  22.5 us
  transfers between devices with their start and end apart: 78, of which 33 were waited for; matrix products, arithmetic and copies ran while one was open for 13% of the time, Pallas kernels for 39%

profile of v6, /device:TPU:0, one launch (start us, length us, event | category | flops | bytes accessed | tf_op | source)
XLA Modules:
  0.0 734.9 jit_solution(9299894197283216867)
XLA Ops:
  11.5 6.2 pack_experts.1
  25.2 11.3 %collective-permute-done.3 = bf16[96,1536]{1,0:T(8,128)(2,1)S(1)} collective-permute-done((bf16[96,1536]{1,0:T(8,128)(2,1)S(1)}, bf16[96,1536]{1,0:T(8,128)(2,1)S(1)}, u32[]{:S(2)}, u32[]{:S(2)}) %collective-permute-start.3) | collective-permute-done | bytes 294944 | tf_op jit(solution)/shard_map/ppermute | solution.py:39
  51.6 11.1 %collective-permute-done.6 = bf16[96,1536]{1,0:T(8,128)(2,1)} collective-permute-done((bf16[96,1536]{1,0:T(8,128)(2,1)}, bf16[96,1536]{1,0:T(8,128)(2,1)}, u32[]{:S(2)}, u32[]{:S(2)}) %collective-permute-start.6) | collective-permute-done | bytes 294944 | tf_op jit(solution)/shard_map/ppermute | solution.py:39
  64.4 10.3 %collective-permute-done.7 = bf16[96,1536]{1,0:T(8,128)(2,1)S(1)} collective-permute-done((bf16[96,1536]{1,0:T(8,128)(2,1)}, bf16[96,1536]{1,0:T(8,128)(2,1)S(1)}, u32[]{:S(2)}, u32[]{:S(2)}) %collective-permute-start.7) | collective-permute-done | bytes 294944 | tf_op jit(solution)/shard_map/ppermute | solution.py:39
  77.5 28.6 %all-gather.5.cloned.1.call-done.weight_ref.tail_ref = bf16[1536,2688]{1,0:T(8,128)(2,1)} async-done(((bf16[96,2688]{1,0:T(8,128)(2,1)}), bf16[1536,2688]{1,0:T(8,128)(2,1)}) %all-gather.5.cloned.1.call-update) | async-done | bytes 8257552 | tf_op jit(solution)/shard_map/all_gather | solution.py:841
  106.1 10.8 %project_rows.1 = (bf16[512,1536]{1,0:T(8,128)(2,1)}, bf16[512,512]{1,0:T(8,128)(2,1)}, bf16[512,512]{1,0:T(8,128)(2,1)}, bf16[512,1536]{1,0:T(8,128)(2,1)}, f32[8,1536]{1,0:T(8,128)}) custom-call(bf16[512,1536]{1,0:T(8,128)(2,1)} %bitcast.142, bf16[1536,2688]{1,0:T(8,128)(2,1)} %all-gather.5.cloned.1.call-done.weight_ref.tail_ref, ...), custom_call_target="tpu_custom_call" | custom-call | bytes 1000 | tf_op jit(solution)/shard_map/project_rows/pallas_call | solution.py:196
  122.2 10.0 %collective-permute-done.kr_ref.vr_ref = bf16[512,512]{1,0:T(8,128)(2,1)} collective-permute-done((bf16[512,512]{1,0:T(8,128)(2,1)}, bf16[512,512]{1,0:T(8,128)(2,1)}, u32[]{:S(2)}, u32[]{:S(2)}) %collective-permute-start) | collective-permute-done | bytes 524320 | tf_op jit(solution)/shard_map/ppermute | solution.py:866
  132.2 11.3 %attend.2 = (bf16[512,1536]{1,0:T(8,128)(2,1)}, f32[2,8,512]{2,1,0:T(8,128)}) custom-call(s32[2]{0:T(128)} %pad_add_fusion.place_ref, bf16[512,1536]{1,0:T(8,128)(2,1)} %get-tuple-element.164.q_ref, bf16[512,512]{1,0:T(8,128)(2,1)} %get-tuple-element.166.k_ref.v_ref, bf16[512,512]{1,0:T(8,128)(2,1)} %get-tuple-element.166.k_ref.v_ref, ...), custom_call_target="tpu_custom_call" | custom-call | bytes 1000 | tf_op jit(solution)/shard_map/attend/pallas_call | solution.py:365
  144.1 8.3 %collective-permute-start.1 = (bf16[512,512]{1,0:T(8,128)(2,1)S(1)}, bf16[512,512]{1,0:T(8,128)(2,1)S(1)}, u32[]{:S(2)}, u32[]{:S(2)}) collective-permute-start(bf16[512,512]{1,0:T(8,128)(2,1)S(1)} %copy-done.21), channel_id=1, source_target_pairs={{0,16},{1,17},{2,18},{3,19},{4,20},{5,21},{6,22},{7,23},{8,24},{9,... | collective-permute-start | bytes 1572872 | tf_op jit(solution)/shard_map/ppermute | solution.py:868
  156.3 7.3 collective-permute-done.1.kr_ref.vr_ref
  166.9 11.2 %attend.3 = (bf16[512,1536]{1,0:T(8,128)(2,1)}, f32[2,8,512]{2,1,0:T(8,128)}) custom-call(s32[2]{0:T(128)} %pad_add_fusion.place_ref, bf16[512,1536]{1,0:T(8,128)(2,1)} %get-tuple-element.164.q_ref, bf16[512,512]{1,0:T(8,128)(2,1)} %get-tuple-element.167.k_ref.v_ref, ...), custom_call_target="tpu_custom_call", output_to_operand_aliasing={{0}: (6, {})} | custom-call | bytes 1000 | tf_op jit(solution)/shard_map/attend/pallas_call | solution.py:365
  178.1 7.6 %collective-permute-done.10 = bf16[256,1664]{1,0:T(8,128)(2,1)} collective-permute-done((bf16[256,1664]{1,0:T(8,128)(2,1)}, bf16[256,1664]{1,0:T(8,128)(2,1)}, u32[]{:S(2)}, u32[]{:S(2)}) %collective-permute-start.10) | collective-permute-done | bytes 852000 | tf_op jit(solution)/shard_map/ppermute | solution.py:39
  185.7 8.9 %merge_rows.1 = (f32[512,1536]{1,0:T(8,128)}, bf16[512,1536]{1,0:T(8,128)(2,1)}) custom-call(bf16[512,1536]{1,0:T(8,128)(2,1)} %get-tuple-element.260.mixed_ref, bf16[1536,1536]{1,0:T(8,128)(2,1)} %all-gather.7.cloned.1.call-done.weight_ref, bf16[512,1536]{1,0:T(8,128)(2,1)} %bitcast.143, f32[8,1536]{1,0:T(8,128)} %get-tuple-element.178.gain_ref), custom_call_target="tpu_custom_call" | custom-call | bytes 1000 | tf_op jit(solution)/shard_map/merge_rows/pallas_call | solution.py:247
  198.2 33.4 %collective-permute-done.16.refs_4_.refs_0_ = bf16[512,1536]{1,0:T(8,128)(2,1)S(1)} collective-permute-done((bf16[512,1536]{1,0:T(8,128)(2,1)}, bf16[512,1536]{1,0:T(8,128)(2,1)S(1)}, u32[]{:S(2)}, u32[]{:S(2)}) %collective-permute-start.16) | collective-permute-done | bytes 1572896 | tf_op jit(solution)/shard_map/ppermute | solution.py:39
  239.7 11.6 %collective-permute-done.20 = bf16[256,1536]{1,0:T(8,128)(2,1)S(1)} collective-permute-done((bf16[256,1536]{1,0:T(8,128)(2,1)S(1)}, bf16[256,1536]{1,0:T(8,128)(2,1)S(1)}, u32[]{:S(2)}, u32[]{:S(2)}) %collective-permute-start.20) | collective-permute-done | bytes 786464 | tf_op jit(solution)/shard_map/ppermute | solution.py:39
  258.7 52.9 %expert_rows.5 = (bf16[4096,512]{1,0:T(8,128)(2,1)}, bf16[4096,1024]{1,0:T(8,128)(2,1)}, bf16[4096,1664]{1,0:T(8,128)(2,1)}, bf16[4096,1536]{1,0:T(8,128)(2,1)}) custom-call(s32[2]{0:T(128)} %pad_add_fusion.1.place_ref, bf16[512,1536]{1,0:T(8,128)(2,1)} %get-tuple-element.181.refs_0_, bf16[512,1536]{1,0:T(8,128)(2,1)} %copy-done.5, ...), custom_call_target="tpu_custom_call" | custom-call | flops 600000000 | bytes 1000 | tf_op jit(solution)/shard_map/expert_rows/pallas_call | solution.py:731
  311.6 19.7 %expert_grad.4.refs_9_ = bf16[1536,1536]{1,0:T(8,128)(2,1)} custom-call(bf16[512,1536]{1,0:T(8,128)(2,1)} %get-tuple-element.181.refs_0_, bf16[512,1536]{1,0:T(8,128)(2,1)} %copy-done.5, bf16[512,1536]{1,0:T(8,128)(2,1)} %collective-permute-done.15.refs_2_.refs_0_, bf16[512,1536]{1,0:T(8,128)(2,1)} %collective-permute-done.18.refs_3_.refs_1_, ...), custom_call_target="tpu_custom_call" | custom-call | flops 600000000 | bytes 1000 | tf_op jit(solution)/shard_map/expert_grad/pallas_call | solution.py:784
  331.4 14.3 %expert_grad.5 = bf16[1536,1536]{1,0:T(8,128)(2,1)} custom-call(bf16[512,1664]{1,0:T(8,128)(2,1)} %copy-done, bf16[512,1664]{1,0:T(8,128)(2,1)} %collective-permute-done.12.refs_9_.refs_1_.refs_3_, bf16[512,1664]{1,0:T(8,128)(2,1)} %collective-permute-done.8.refs_10_.refs_2_, ...), custom_call_target="tpu_custom_call", output_to_operand_aliasing={{}: (9, {})} | custom-call | flops 600000000 | bytes 1000 | tf_op jit(solution)/shard_map/expert_grad/pallas_call | solution.py:784
  345.7 18.5 %expert_rows.6 = (bf16[4096,512]{1,0:T(8,128)(2,1)}, bf16[4096,1024]{1,0:T(8,128)(2,1)}, bf16[512,1664]{1,0:T(8,128)(2,1)}, bf16[512,1664]{1,0:T(8,128)(2,1)}, b...) custom-call(s32[2]{0:T(128)} %pad_add_fusion.1.place_ref, ...), custom_call_target="tpu_custom_call" | custom-call | flops 600000000 | bytes 1000 | tf_op jit(solution)/shard_map/expert_rows/pallas_call | solution.py:731
  364.9 19.2 %expert_rows.7 = (bf16[4096,512]{1,0:T(8,128)(2,1)}, bf16[4096,1024]{1,0:T(8,128)(2,1)}, bf16[512,1664]{1,0:T(8,128)(2,1)}, bf16[512,1664]{1,0:T(8,128)(2,1)}, b...) custom-call(s32[2]{0:T(128)} %pad_add_fusion.1.place_ref, ...), custom_call_target="tpu_custom_call", output_to_operand_aliasing={{0}: (8, {}), {1}: (9, {})} | custom-call | flops 600000000 | bytes 1000 | tf_op jit(solution)/shard_map/expert_rows/pallas_call | solution.py:731
  391.5 18.7 %expert_rows.8 = (bf16[4096,512]{1,0:T(8,128)(2,1)}, bf16[4096,1024]{1,0:T(8,128)(2,1)}, bf16[512,1664]{1,0:T(8,128)(2,1)}, bf16[512,1664]{1,0:T(8,128)(2,1)}, b...) custom-call(s32[2]{0:T(128)} %pad_add_fusion.1.place_ref, ...), custom_call_target="tpu_custom_call", output_to_operand_aliasing={{0}: (8, {}), {1}: (9, {})} | custom-call | flops 8999999488 | bytes 1000 | tf_op jit(solution)/shard_map/expert_rows/pallas_call | solution.py:731
  416.5 18.8 %expert_rows.9 = (bf16[4096,512]{1,0:T(8,128)(2,1)}, bf16[4096,1024]{1,0:T(8,128)(2,1)}, bf16[512,1664]{1,0:T(8,128)(2,1)}, bf16[512,1664]{1,0:T(8,128)(2,1)}, b...) custom-call(s32[2]{0:T(128)} %pad_add_fusion.1.place_ref, ...), custom_call_target="tpu_custom_call", output_to_operand_aliasing={{0}: (8, {}), {1}: (9, {})} | custom-call | flops 8999999488 | bytes 1000 | tf_op jit(solution)/shard_map/expert_rows/pallas_call | solution.py:731
  449.2 19.7 %expert_grad.6.refs_9_ = bf16[1536,1536]{1,0:T(8,128)(2,1)} custom-call(bf16[512,1536]{1,0:T(8,128)(2,1)} %get-tuple-element.181.refs_0_, bf16[512,1536]{1,0:T(8,128)(2,1)} %copy-done.5, bf16[512,1536]{1,0:T(8,128)(2,1)} %collective-permute-done.15.refs_2_.refs_0_, bf16[512,1536]{1,0:T(8,128)(2,1)} %collective-permute-done.18.refs_3_.refs_1_, ...), custom_call_target="tpu_custom_call" | custom-call | flops 600000000 | bytes 1000 | tf_op jit(solution)/shard_map/expert_grad/pallas_call | solution.py:784
  468.9 14.4 %expert_grad.7 = bf16[1536,1536]{1,0:T(8,128)(2,1)} custom-call(bf16[512,1664]{1,0:T(8,128)(2,1)} %copy-done, bf16[512,1664]{1,0:T(8,128)(2,1)} %collective-permute-done.12.refs_9_.refs_1_.refs_3_, bf16[512,1664]{1,0:T(8,128)(2,1)} %collective-permute-done.8.refs_10_.refs_2_, ...), custom_call_target="tpu_custom_call", output_to_operand_aliasing={{}: (9, {})} | custom-call | flops 600000000 | bytes 1000 | tf_op jit(solution)/shard_map/expert_grad/pallas_call | solution.py:784
  483.4 12.7 %middle_back.1 = (f32[512,1536]{1,0:T(8,128)}, bf16[512,1536]{1,0:T(8,128)(2,1)}, bf16[512,1536]{1,0:T(8,128)(2,1)}, f32[8,1536]{1,0:T(8,128)}) custom-call(bf16[512,1536]{1,0:T(8,128)(2,1)} %get-tuple-element.227.own_ref, bf16[512,1536]{1,0:T(8,128)(2,1)} %collective-permute-done.36.got_ref, bf16[512,1536]{1,0:T(8,128)(2,1)} %collective-permute-done.32.across_ref, ...), custom_call_target="tpu_custom_call" | custom-call | flops 600000000 | bytes 1000 | tf_op jit(solution)/shard_map/middle_back/pallas_call | solution.py:290
  505.9 14.8 %attend_back.2 = (bf16[512,768]{1,0:T(8,128)(2,1)}, bf16[512,256]{1,0:T(8,128)(2,1)}, bf16[512,256]{1,0:T(8,128)(2,1)}, bf16[512,256]{1,0:T(8,128)(2,1)}, bf16[512,256]{1,0:T(8,128)(2,1)}) custom-call(s32[2]{0:T(128)} %pad_add_fusion.place_ref, bf16[512,1536]{1,0:T(8,128)(2,1)} %get-tuple-element.164.q_ref, bf16[512,512]{1,0:T(8,128)(2,1)} %get-tuple-element.166.k_ref.v_ref, ...), custom_call_target="tpu_custom_call" | custom-call | flops 14400000000 | bytes 1000 | tf_op jit(solution)/shard_map/attend_back/pallas_call | solution.py:484
  529.3 16.1 %collective-permute-done.37 = bf16[512,1664]{1,0:T(8,128)(2,1)} collective-permute-done((bf16[512,1664]{1,0:T(8,128)(2,1)}, bf16[512,1664]{1,0:T(8,128)(2,1)}, u32[]{:S(2)}, u32[]{:S(2)}) %collective-permute-start.37) | collective-permute-done | bytes 1703968 | tf_op jit(solution)/shard_map/ppermute | solution.py:39
  569.0 15.3 %attend_back.3 = (bf16[512,768]{1,0:T(8,128)(2,1)}, bf16[512,256]{1,0:T(8,128)(2,1)}, bf16[512,256]{1,0:T(8,128)(2,1)}, bf16[512,256]{1,0:T(8,128)(2,1)}, bf16[512,256]{1,0:T(8,128)(2,1)}) custom-call(s32[2]{0:T(128)} %pad_add_fusion.place_ref, bf16[512,1536]{1,0:T(8,128)(2,1)} %get-tuple-element.164.q_ref, bf16[512,512]{1,0:T(8,128)(2,1)} %get-tuple-element.167.k_ref.v_ref, ...), custom_call_target="tpu_custom_call" | custom-call | flops 14400000000 | bytes 1000 | tf_op jit(solution)/shard_map/attend_back/pallas_call | solution.py:484
  584.3 7.1 collective-permute-done.45
  616.5 10.1 %collective-permute-done.48.lateb_ref = bf16[512,512]{1,0:T(8,128)(2,1)} collective-permute-done((bf16[512,512]{1,0:T(8,128)(2,1)}, bf16[512,512]{1,0:T(8,128)(2,1)}, u32[]{:S(2)}, u32[]{:S(2)}) %collective-permute-start.48) | collective-permute-done | bytes 524320 | tf_op jit(solution)/shard_map/ppermute | solution.py:987
  644.7 7.7 %fusion = f32[512,1536]{1,0:T(8,128)S(1)} fusion(bf16[512,2560]{1,0:T(8,128)(2,1)} %pad_maximum_fusion, bf16[1536,2688]{1,0:T(8,128)(2,1)} %all-gather.5.cloned.1.call-done.weight_ref.tail_ref), kind=kOutput, calls=%fused_computation | convolution fusion | flops 4026531840 | bytes 13631488 | tf_op jit(solution)/shard_map/dot_general | solution.py:151
  676.0 11.2 %collective-permute-done.58 = bf16[96,768]{1,0:T(8,128)(2,1)S(1)} collective-permute-done((bf16[96,768]{1,0:T(8,128)(2,1)S(1)}, bf16[96,768]{1,0:T(8,128)(2,1)S(1)}, u32[]{:S(2)}, u32[]{:S(2)}) %collective-permute-start.58) | collective-permute-done | bytes 147488 | tf_op jit(solution)/shard_map/ppermute | solution.py:119
  (350 shorter events, 239.7 us)
Async XLA Ops:
  7.2 99.0 %all-gather.5.cloned.1.call-start = ((), (), s32[]{:S(2)}) async-start(), calls=%async_computation.3 | async-start | bytes 8773632 | tf_op jit(solution)/shard_map/all_gather | solution.py:841
  10.7 175.0 %all-gather.7.cloned.1.call-start = ((), (), s32[]{:S(2)}) async-start(), calls=%async_computation.4 | async-start | bytes 5013504 | tf_op jit(solution)/shard_map/all_gather | solution.py:842
  11.4 244.1 %all-gather.9.cloned.1.call-start = ((), (), s32[]{:S(2)}) async-start(), calls=%async_computation.5 | async-start | bytes 5898240 | tf_op jit(solution)/shard_map/all_gather | solution.py:849
  43.1 302.6 %all-gather.11.cloned.1.call-start = ((), (), s32[]{:S(2)}) async-start(), calls=%async_computation.6 | async-start | bytes 5898240 | tf_op jit(solution)/shard_map/all_gather | solution.py:850
  75.4 68.1 %collective-permute-start.9 = (bf16[512,1664]{1,0:T(8,128)(2,1)S(1)}, bf16[512,1664]{1,0:T(8,128)(2,1)S(1)}, u32[]{:S(2)}, u32[]{:S(2)}) collective-permute-start(bf16[512,1664]{1,0:T(8,128)(2,1)S(1)} %concatenate.44.refs_8_.refs_0_.refs_2_), channel_id=1, source_target_pairs={{0,2},{1,3},{2,0},{3,1},{4,6},{5,7},{6,4},{7,5},{8,10},{9,11},{10,... | collective-permute-start | bytes 5111816 | tf_op jit(solution)/shard_map/ppermute | solution.py:39
  75.5 68.0 %collective-permute-start.8 = (bf16[512,1664]{1,0:T(8,128)(2,1)S(1)}, bf16[512,1664]{1,0:T(8,128)(2,1)}, u32[]{:S(2)}, u32[]{:S(2)}) collective-permute-start(bf16[512,1664]{1,0:T(8,128)(2,1)S(1)} %concatenate.44.refs_8_.refs_0_.refs_2_), channel_id=1, source_target_pairs={{0,16},{16,0},{1,17},{17,1},{2,18},{18,2},{3,19},{19,3},{4,20},{20... | collective-permute-start | bytes 5111816 | tf_op jit(solution)/shard_map/ppermute | solution.py:39
  77.5 474.2 %reduce-scatter.4.cloned.1.call-start = ((), (), s32[]{:S(2)}) async-start(), calls=%async_computation.7 | async-start | bytes 5898240 | tf_op jit(solution)/shard_map/reduce_scatter | solution.py:906
  122.2 55.9 %collective-permute-start.12 = (bf16[512,1664]{1,0:T(8,128)(2,1)S(1)}, bf16[512,1664]{1,0:T(8,128)(2,1)}, u32[]{:S(2)}, u32[]{:S(2)}) collective-permute-start(bf16[512,1664]{1,0:T(8,128)(2,1)S(1)} %concatenate.44.refs_8_.refs_0_.refs_2_), channel_id=1, source_target_pairs={{0,1},{1,0},{2,3},{3,2},{4,5},{5,4},{6,7},{7,6},{8,9},{9,8},{10,11... | collective-permute-start | bytes 5111816 | tf_op jit(solution)/shard_map/ppermute | solution.py:39
  143.5 42.1 %collective-permute-start.14 = (bf16[512,1664]{1,0:T(8,128)(2,1)S(1)}, bf16[512,1664]{1,0:T(8,128)(2,1)}, u32[]{:S(2)}, u32[]{:S(2)}) collective-permute-start(bf16[512,1664]{1,0:T(8,128)(2,1)S(1)} %collective-permute-done.9.refs_12_.refs_4_.refs_2_), channel_id=1, source_target_pairs={{0,1},{1,0},{2,3},{3,2},{4,5},{5,4},{6,7},{7,6},{8,9},{9,8},{10,11... | collective-permute-start | bytes 5111816 | tf_op jit(solution)/shard_map/ppermute | solution.py:39
  143.6 42.0 %collective-permute-start.13 = (bf16[512,1664]{1,0:T(8,128)(2,1)}, bf16[512,1664]{1,0:T(8,128)(2,1)}, u32[]{:S(2)}, u32[]{:S(2)}) collective-permute-start(bf16[512,1664]{1,0:T(8,128)(2,1)} %collective-permute-done.8.refs_10_.refs_2_), channel_id=1, source_target_pairs={{0,1},{1,0},{2,3},{3,2},{4,5},{5,4},{6,7},{7,6},{8,9},{9,8},{10,11... | collective-permute-start | bytes 5111816 | tf_op jit(solution)/shard_map/ppermute | solution.py:39
  194.6 37.0 %collective-permute-start.16 = (bf16[512,1536]{1,0:T(8,128)(2,1)}, bf16[512,1536]{1,0:T(8,128)(2,1)S(1)}, u32[]{:S(2)}, u32[]{:S(2)}) collective-permute-start(bf16[512,1536]{1,0:T(8,128)(2,1)} %get-tuple-element.181.refs_0_), channel_id=1, source_target_pairs={{0,2},{1,3},{2,0},{3,1},{4,6},{5,7},{6,4},{7,5},{8,10},{9,11},{10,... | collective-permute-start | bytes 4718600 | tf_op jit(solution)/shard_map/ppermute | solution.py:39
  195.4 36.9 %collective-permute-start.15 = (bf16[512,1536]{1,0:T(8,128)(2,1)}, bf16[512,1536]{1,0:T(8,128)(2,1)}, u32[]{:S(2)}, u32[]{:S(2)}) collective-permute-start(bf16[512,1536]{1,0:T(8,128)(2,1)} %get-tuple-element.181.refs_0_), channel_id=1, source_target_pairs={{0,16},{16,0},{1,17},{17,1},{2,18},{18,2},{3,19},{19,3},{4,20},{20... | collective-permute-start | bytes 4718600 | tf_op jit(solution)/shard_map/ppermute | solution.py:39
  364.9 275.0 %reduce-scatter.6.cloned.1.call-start = ((), (), s32[]{:S(2)}) async-start(), calls=%async_computation.8 | async-start | bytes 5898240 | tf_op jit(solution)/shard_map/reduce_scatter | solution.py:906
  384.1 26.1 %collective-permute-start.24 = (bf16[512,1536]{1,0:T(8,128)(2,1)}, bf16[512,1536]{1,0:T(8,128)(2,1)}, u32[]{:S(2)}, u32[]{:S(2)}) collective-permute-start(bf16[512,1536]{1,0:T(8,128)(2,1)} %get-tuple-element.199), channel_id=1, source_target_pairs={{0,1},{1,0},{2,3},{3,2},{4,5},{5,4},{6,7},{7,6},{8,9},{9,8},{10,11... | collective-permute-start | bytes 4718600 | tf_op jit(solution)/shard_map/ppermute | solution.py:39
  384.4 26.3 %collective-permute-start.25 = (bf16[512,1664]{1,0:T(8,128)(2,1)}, bf16[512,1664]{1,0:T(8,128)(2,1)S(1)}, u32[]{:S(2)}, u32[]{:S(2)}) collective-permute-start(bf16[512,1664]{1,0:T(8,128)(2,1)} %get-tuple-element.200), channel_id=1, source_target_pairs={{0,1},{1,0},{2,3},{3,2},{4,5},{5,4},{6,7},{7,6},{8,9},{9,8},{10,11... | collective-permute-start | bytes 5111816 | tf_op jit(solution)/shard_map/ppermute | solution.py:39
  410.2 27.3 %collective-permute-start.33 = (bf16[512,1536]{1,0:T(8,128)(2,1)}, bf16[512,1536]{1,0:T(8,128)(2,1)}, u32[]{:S(2)}, u32[]{:S(2)}) collective-permute-start(bf16[512,1536]{1,0:T(8,128)(2,1)} %get-tuple-element.230), channel_id=1, source_target_pairs={{0,1},{1,0},{2,3},{3,2},{4,5},{5,4},{6,7},{7,6},{8,9},{9,8},{10,11... | collective-permute-start | bytes 4718600 | tf_op jit(solution)/shard_map/ppermute | solution.py:39
  410.3 27.2 %collective-permute-start.34 = (bf16[512,1664]{1,0:T(8,128)(2,1)}, bf16[512,1664]{1,0:T(8,128)(2,1)}, u32[]{:S(2)}, u32[]{:S(2)}) collective-permute-start(bf16[512,1664]{1,0:T(8,128)(2,1)} %get-tuple-element.231), channel_id=1, source_target_pairs={{0,1},{1,0},{2,3},{3,2},{4,5},{5,4},{6,7},{7,6},{8,9},{9,8},{10,11... | collective-permute-start | bytes 5111816 | tf_op jit(solution)/shard_map/ppermute | solution.py:39
  435.3 48.1 %collective-permute-start.36 = (bf16[512,1536]{1,0:T(8,128)(2,1)}, bf16[512,1536]{1,0:T(8,128)(2,1)}, u32[]{:S(2)}, u32[]{:S(2)}) collective-permute-start(bf16[512,1536]{1,0:T(8,128)(2,1)} %get-tuple-element.239), channel_id=1, source_target_pairs={{0,1},{1,0},{2,3},{3,2},{4,5},{5,4},{6,7},{7,6},{8,9},{9,8},{10,11... | collective-permute-start | bytes 4718600 | tf_op jit(solution)/shard_map/ppermute | solution.py:39
  435.4 47.9 %collective-permute-start.32 = (bf16[512,1536]{1,0:T(8,128)(2,1)}, bf16[512,1536]{1,0:T(8,128)(2,1)}, u32[]{:S(2)}, u32[]{:S(2)}) collective-permute-start(bf16[512,1536]{1,0:T(8,128)(2,1)} %pad_maximum_fusion.3), channel_id=1, source_target_pairs={{0,16},{16,0},{1,17},{17,1},{2,18},{18,2},{3,19},{19,3},{4,20},{20... | collective-permute-start | bytes 4718600 | tf_op jit(solution)/shard_map/ppermute | solution.py:39
  444.7 38.6 %collective-permute-start.35 = (bf16[512,1536]{1,0:T(8,128)(2,1)}, bf16[512,1536]{1,0:T(8,128)(2,1)}, u32[]{:S(2)}, u32[]{:S(2)}) collective-permute-start(bf16[512,1536]{1,0:T(8,128)(2,1)} %pad_maximum_fusion.4), channel_id=1, source_target_pairs={{0,2},{1,3},{2,0},{3,1},{4,6},{5,7},{6,4},{7,5},{8,10},{9,11},{10,... | collective-permute-start | bytes 4718600 | tf_op jit(solution)/shard_map/ppermute | solution.py:39
  446.9 52.9 %collective-permute-start.31 = (bf16[256,1664]{1,0:T(8,128)(2,1)}, bf16[256,1664]{1,0:T(8,128)(2,1)}, u32[]{:S(2)}, u32[]{:S(2)}) collective-permute-start(bf16[256,1664]{1,0:T(8,128)(2,1)} %get-tuple-element.324), channel_id=1, source_target_pairs={{0,2},{1,3},{2,0},{3,1},{4,6},{5,7},{6,4},{7,5},{8,10},{9,11},{10,... | collective-permute-start | bytes 2555912 | tf_op jit(solution)/shard_map/ppermute | solution.py:39
  448.1 51.7 %collective-permute-start.30 = (bf16[256,1664]{1,0:T(8,128)(2,1)}, bf16[256,1664]{1,0:T(8,128)(2,1)}, u32[]{:S(2)}, u32[]{:S(2)}) collective-permute-start(bf16[256,1664]{1,0:T(8,128)(2,1)} %get-tuple-element.325), channel_id=1, source_target_pairs={{0,16},{16,0},{1,17},{17,1},{2,18},{18,2},{3,19},{19,3},{4,20},{20... | collective-permute-start | bytes 2555912 | tf_op jit(solution)/shard_map/ppermute | solution.py:39
  504.9 40.5 %collective-permute-start.37 = (bf16[512,1664]{1,0:T(8,128)(2,1)}, bf16[512,1664]{1,0:T(8,128)(2,1)}, u32[]{:S(2)}, u32[]{:S(2)}) collective-permute-start(bf16[512,1664]{1,0:T(8,128)(2,1)} %get-tuple-element.249), channel_id=1, source_target_pairs={{0,16},{16,0},{1,17},{17,1},{2,18},{18,2},{3,19},{19,3},{4,20},{20... | collective-permute-start | bytes 5111816 | tf_op jit(solution)/shard_map/ppermute | solution.py:39
  505.2 40.2 %collective-permute-start.38 = (bf16[512,1664]{1,0:T(8,128)(2,1)}, bf16[512,1664]{1,0:T(8,128)(2,1)}, u32[]{:S(2)}, u32[]{:S(2)}) collective-permute-start(bf16[512,1664]{1,0:T(8,128)(2,1)} %get-tuple-element.250), channel_id=1, source_target_pairs={{0,2},{1,3},{2,0},{3,1},{4,6},{5,7},{6,4},{7,5},{8,10},{9,11},{10,... | collective-permute-start | bytes 5111816 | tf_op jit(solution)/shard_map/ppermute | solution.py:39
  505.9 39.5 %collective-permute-start.39 = (bf16[512,1664]{1,0:T(8,128)(2,1)}, bf16[512,1664]{1,0:T(8,128)(2,1)}, u32[]{:S(2)}, u32[]{:S(2)}) collective-permute-start(bf16[512,1664]{1,0:T(8,128)(2,1)} %get-tuple-element.252), channel_id=1, source_target_pairs={{0,1},{1,0},{2,3},{3,2},{4,5},{5,4},{6,7},{7,6},{8,9},{9,8},{10,11... | collective-permute-start | bytes 5111816 | tf_op jit(solution)/shard_map/ppermute | solution.py:39
  526.1 193.8 %reduce-scatter.8.cloned.1.call-start = ((), (), s32[]{:S(2)}) async-start(), calls=%async_computation.9 | async-start | bytes 3342336 | tf_op jit(solution)/shard_map/reduce_scatter | solution.py:999
  528.0 41.0 %collective-permute-start.40 = (bf16[512,512]{1,0:T(8,128)(2,1)}, bf16[512,512]{1,0:T(8,128)(2,1)S(1)}, u32[]{:S(2)}, u32[]{:S(2)}) collective-permute-start(bf16[512,512]{1,0:T(8,128)(2,1)} %pad_maximum_fusion.7), channel_id=1, source_target_pairs={{16,0},{17,1},{18,2},{19,3},{20,4},{21,5},{22,6},{23,7},{24,8},{25... | collective-permute-start | bytes 1572872 | tf_op jit(solution)/shard_map/ppermute | solution.py:969
  557.3 34.2 %collective-permute-start.45 = (bf16[4,96,1536]{2,1,0:T(8,128)(2,1)S(1)}, bf16[4,96,1536]{2,1,0:T(8,128)(2,1)}, u32[]{:S(2)}, u32[]{:S(2)}) collective-permute-start(bf16[4,96,1536]{2,1,0:T(8,128)(2,1)S(1)} %dynamic-slice_bitcast_fusion.1), channel_id=1, source_target_pairs={{0,2},{1,3},{2,0},{3,1},{4,6},{5,7},{6,4},{7,5},{8,10},{9,11},{10,... | collective-permute-start | bytes 3538952 | tf_op jit(solution)/shard_map/ppermute | solution.py:39
  568.9 27.8 %collective-permute-start.46 = (bf16[4,96,1536]{2,1,0:T(8,128)(2,1)}, bf16[4,96,1536]{2,1,0:T(8,128)(2,1)}, u32[]{:S(2)}, u32[]{:S(2)}) collective-permute-start(bf16[4,96,1536]{2,1,0:T(8,128)(2,1)} %bitcast_dynamic-update-slice_fusion.3.refs_0_), channel_id=1, source_target_pairs={{0,16},{16,0},{1,17},{17,1},{2,18},{18,2},{3,19},{19,3},{4,20},{20... | collective-permute-start | bytes 3538952 | tf_op jit(solution)/shard_map/ppermute | solution.py:39
  607.8 28.6 %collective-permute-start.49 = (bf16[4,96,1536]{2,1,0:T(8,128)(2,1)}, bf16[4,96,1536]{2,1,0:T(8,128)(2,1)}, u32[]{:S(2)}, u32[]{:S(2)}) collective-permute-start(bf16[4,96,1536]{2,1,0:T(8,128)(2,1)} %dynamic-slice_bitcast_fusion), channel_id=1, source_target_pairs={{0,2},{1,3},{2,0},{3,1},{4,6},{5,7},{6,4},{7,5},{8,10},{9,11},{10,... | collective-permute-start | bytes 3538952 | tf_op jit(solution)/shard_map/ppermute | solution.py:39
  613.0 54.5 %collective-permute-start.55 = (bf16[4,96,768]{2,1,0:T(8,128)(2,1)S(1)}, bf16[4,96,768]{2,1,0:T(8,128)(2,1)}, u32[]{:S(2)}, u32[]{:S(2)}) collective-permute-start(bf16[4,96,768]{2,1,0:T(8,128)(2,1)S(1)} %constant_dynamic-slice_fusion.5), channel_id=1, source_target_pairs={{0,16},{16,0},{1,17},{17,1},{2,18},{18,2},{3,19},{19,3},{4,20},{20... | collective-permute-start | bytes 1769480 | tf_op jit(solution)/shard_map/ppermute | solution.py:39
  659.5 48.1 %collective-permute-start.69 = (bf16[4,96,1536]{2,1,0:T(8,128)(2,1)}, bf16[4,96,1536]{2,1,0:T(8,128)(2,1)}, u32[]{:S(2)}, u32[]{:S(2)}) collective-permute-start(bf16[4,96,1536]{2,1,0:T(8,128)(2,1)} %bitcast_dynamic-update-slice_fusion.refs_2_), channel_id=1, source_target_pairs={{0,16},{16,0},{1,17},{17,1},{2,18},{18,2},{3,19},{19,3},{4,20},{20... | collective-permute-start | bytes 3538952 | tf_op jit(solution)/shard_map/ppermute | solution.py:39
  (89 other events, 1097.8 us)
Sparse Core Ops, SparseCore 0:
  10.9 95.2 all-gather.4
  108.4 54.2 all-gather.6
  164.3 87.9 all-gather.8
  253.7 87.8 all-gather.10
  365.0 83.5 reduce-scatter.3
  526.3 93.6 reduce-scatter.5
  632.4 78.5 reduce-scatter.7
